TPU v7x, 32 devices: a whole 2x2x4 slice. The times are simulated.
32 devices in a mesh: dp: 4 (over z), seq: 8 (over y, x, core).
Axes of the slice: x: 2, y: 2, z: 4, core: 2. Of those that a mesh axis runs over, the one named last changes fastest.
Arguments:
- inputs: bfloat16 [32, 1024, 512], P('dp', 'seq'), may hold values from -6 to 6
- doc_start: int32 [32, 1024], P('dp', 'seq'), may hold values from 0 to 1, as said below
- norm1_gain: float32 [512], replicated, may hold values from 0.5 to 1.5
- conv_weight: float32 [512, 4], replicated, may hold values from -3 to 3
- gate_bias: float32 [1024], replicated, may hold values from -20 to -2
- w_in: bfloat16 [512, 2048], replicated, may hold values from -0.25 to 0.25
- w_out: bfloat16 [1024, 512], replicated, may hold values from -3 to 3
- norm2_gain: float32 [512], replicated, may hold values from 0.5 to 1.5
- w_up: bfloat16 [512, 2048], replicated, may hold values from -0.25 to 0.25
- w_down: bfloat16 [2048, 512], replicated, may hold values from -0.125 to 0.125
- out_grad: bfloat16 [32, 1024, 512], P('dp', 'seq'), may hold values from -6 to 6
Outputs:
- result: bfloat16 [32, 1024, 512], P('dp', 'seq')
- grad_inputs: float32 [32, 1024, 512], P('dp', 'seq')
- grad_norm1: float32 [512], P('seq')
- grad_conv: float32 [512, 4], P('seq')
- grad_bias: float32 [1024], P('seq')
- grad_w_in: float32 [512, 2048], P('seq')
- grad_w_out: float32 [1024, 512], P('seq')
- grad_norm2: float32 [512], P('seq')
- grad_w_up: float32 [512, 2048], P('seq')
- grad_w_down: float32 [2048, 512], P('seq')
Inputs may be any that keep to these rules, and one draw needn't show every extreme that they name: `doc_start`: each row's first token is 1. In every aligned block of 8 rows, one row drawn from the seed holds a single document over all 1024 tokens. In the other rows every later token begins a document independently with chance 1 / 384, so such a row holds documents of random, uneven lengths, or now and then a single one.
All inputs are finite; a program needn't handle non-finite values.
Results may differ from a plain program's by a relative error of at most 0.0085.
Values may be sent and summed in bfloat16 or wider, within the bound.
No kernel may reach another device: no remote copies, remote signals or barrier semaphores. Data moves between devices by JAX's collectives and lax.ppermute only.
A program may use at most 192 MiB of HBM per device.

v0:
```python
import functools

import jax
import jax.numpy as jnp
from jax import lax
from jax.experimental import pallas as pl
from jax.experimental.pallas import tpu as pltpu
from jax.sharding import PartitionSpec as P

KW = 4
EPS = 1e-05
EDGE = 8
LANES = 128
LIMITS = (16, 30, 16, 16, 24)
F32 = jnp.float32
BF16 = jnp.bfloat16
GELU_C = 0.7978845608028654
GELU_A = 0.044715

VMEM_SPEC = pl.BlockSpec(memory_space=pltpu.VMEM)
SMEM_SPEC = pl.BlockSpec(memory_space=pltpu.SMEM)


def dot(left, right):
    return jnp.dot(left, right, preferred_element_type=F32)


def dot_nt(left, right):
    return lax.dot_general(left, right, (((1,), (1,)), ((), ())), preferred_element_type=F32)


def dot_tn(left, right):
    return lax.dot_general(left, right, (((0,), (0,)), ((), ())), preferred_element_type=F32)


def widen(column, lanes):
    return jnp.concatenate([column] * (lanes // column.shape[1]), axis=1)


def rms(values):
    return lax.rsqrt(jnp.mean(values * values, axis=-1, keepdims=True) + EPS)


def rows_of(index, count):
    return pl.ds(pl.multiple_of(index * count, count), count)


def interleave(buf, row, batch, values):
    for lane in range(buf.shape[0]):
        cols = slice(lane * LANES, (lane + 1) * LANES)
        buf[lane, pl.ds(row, values.shape[0], stride=batch), :] = values[:, cols].astype(F32)


def deinterleave(buf, row, batch, span):
    parts = [buf[lane, pl.ds(row, span, stride=batch), :] for lane in range(buf.shape[0])]
    return jnp.concatenate(parts, axis=1)


def read(buf, rows):
    return jnp.concatenate([buf[lane, rows, :] for lane in range(buf.shape[0])], axis=1)


def write(buf, rows, values):
    for lane in range(buf.shape[0]):
        buf[lane, rows, :] = values[:, lane * LANES : (lane + 1) * LANES]


def front_kernel(
    x_ref, halo_ref, keep_ref, gain_ref, taps_ref, bias_ref, w_ref,
    xt_ref, conv_ref, gate_ref, cand_ref, total_ref, norm_buf,
    *, steps,
):
    batch, span, width = x_ref.shape
    hidden = gate_ref.shape[1]
    size = steps * batch
    lead = EDGE * batch
    for row in range(batch):
        interleave(norm_buf, row, batch, halo_ref[row])
        interleave(xt_ref, row, batch, x_ref[row])
    gain = gain_ref[...]

    def normed_of(values):
        return (values * rms(values) * gain).astype(BF16).astype(F32)

    write(norm_buf, slice(0, lead), normed_of(read(norm_buf, slice(0, lead))))

    def chunk(index, carry):
        rows = rows_of(index, size)
        here = normed_of(read(xt_ref, rows))
        write(norm_buf, pl.ds(pl.multiple_of(index * size + lead, 8), size), here)
        mixing = here * taps_ref[0:1, :]
        for tap in range(1, KW):
            start = pl.multiple_of(index * size + lead - tap * batch, 8)
            mixing = mixing + read(norm_buf, pl.ds(start, size)) * taps_ref[tap : tap + 1, :]
        conv_low = mixing.astype(BF16)
        conv_ref[rows, :] = conv_low
        gate_ref[rows, :] = jax.nn.sigmoid(dot(conv_low, w_ref[:, :hidden]) + bias_ref[...])
        cand_ref[rows, :] = dot(conv_low, w_ref[:, hidden:])

        def step(offset, carry):
            prod, state = carry
            here = rows_of(index * steps + offset, batch)
            gate = gate_ref[here, :]
            decay = (1.0 - gate) * widen(keep_ref[here, :], hidden)
            return decay * prod, decay * state + gate * cand_ref[here, :]

        return lax.fori_loop(0, steps, step, carry, unroll=8)

    first = (jnp.ones((batch, hidden), F32), jnp.zeros((batch, hidden), F32))
    prod, state = lax.fori_loop(0, span // steps, chunk, first)
    total_ref[0] = prod
    total_ref[1] = state


def middle_kernel(
    place_ref, totals_ref, g_ref, xt_ref, keep_ref, gate_ref, cand_ref, gain_ref,
    w_out_ref, w_up_ref, w_down_ref,
    result_ref, gt_ref, prev_ref, held_ref, nmid_ref, act_ref, gup_ref, gmid_ref, gbranch_ref, gheld_ref,
    outgoing_ref, gnorm2_ref, wide_buf,
    *, steps, block,
):
    batch, span, width = g_ref.shape
    hidden = gate_ref.shape[1]
    inner = w_up_ref.shape[1]
    size = steps * batch
    place = place_ref[0]
    for row in range(batch):
        interleave(wide_buf, row, batch, g_ref[row])

    def fold(source, state):
        return jnp.where(source < place, totals_ref[source, 0] * state + totals_ref[source, 1], state)

    carry_in = lax.fori_loop(0, totals_ref.shape[0], fold, jnp.zeros((batch, hidden), F32))
    gain = gain_ref[...]

    def chunk(index, carry):
        state, gnorm2 = carry
        rows = rows_of(index, size)

        def two_steps(pair, state):
            out = []
            for side in range(2):
                here = pl.ds(pl.multiple_of((index * steps + 2 * pair + side) * batch, batch), batch)
                gate = gate_ref[here, :]
                prev_ref[here, :] = state
                decay = (1.0 - gate) * widen(keep_ref[here, :], hidden)
                state = decay * state + gate * cand_ref[here, :]
                out.append(state)
            both = rows_of(index * (steps // 2) + pair, 2 * batch)
            held_ref[both, :] = jnp.concatenate(out, axis=0).astype(BF16)
            return state

        state = lax.fori_loop(0, steps // 2, two_steps, state, unroll=4)
        middle = read(xt_ref, rows) + dot(held_ref[rows, :], w_out_ref[...])
        scale = rms(middle)
        unit = middle * scale
        nmid = (unit * gain).astype(BF16)
        nmid_ref[rows, :] = nmid
        g_wide = read(wide_buf, rows)
        g_low = g_wide.astype(BF16)
        gt_ref[rows, :] = g_low
        result = middle
        gnmid = jnp.zeros((size, width), F32)
        for part in range(inner // block):
            cols = slice(part * block, (part + 1) * block)
            up = dot(nmid, w_up_ref[:, cols])
            gact = dot_nt(g_low, w_down_ref[cols, :])
            square = up * up
            half = 0.5 + 0.5 * jnp.tanh(up * (GELU_C + (GELU_C * GELU_A) * square))
            act = up * half
            slope = half + act * (1.0 - half) * (2.0 * GELU_C + (6.0 * GELU_C * GELU_A) * square)
            act_low = act.astype(BF16)
            gup = (slope * gact).astype(BF16)
            act_ref[rows, cols] = act_low
            gup_ref[rows, cols] = gup
            result = result + dot(act_low, w_down_ref[cols, :])
            gnmid = gnmid + dot_nt(gup, w_up_ref[:, cols])
        write(wide_buf, rows, result)
        gnorm2 = gnorm2 + jnp.sum(gnmid * unit, axis=0, keepdims=True)
        pulled = gnmid * gain
        gmid = g_wide + scale * (pulled - unit * jnp.mean(pulled * unit, axis=-1, keepdims=True))
        gmid_ref[rows, :] = gmid
        gbranch = gmid.astype(BF16)
        gbranch_ref[rows, :] = gbranch
        gheld_ref[rows, :] = dot_nt(gbranch, w_out_ref[...])
        return state, gnorm2

    _, gnorm2 = lax.fori_loop(0, span // steps, chunk, (carry_in, jnp.zeros((1, width), F32)))
    gnorm2_ref[...] = gnorm2

    def back(offset, carry):
        here = rows_of(span - 1 - offset, batch)
        decay = (1.0 - gate_ref[here, :]) * widen(keep_ref[here, :], hidden)
        return decay * (gheld_ref[here, :] + carry)

    outgoing_ref[...] = lax.fori_loop(0, span, back, jnp.zeros((batch, hidden), F32), unroll=8)
    for row in range(batch):
        result_ref[row] = deinterleave(wide_buf, row, batch, span).astype(BF16)


def back_kernel(
    place_ref, totals_ref, outs_ref, keep_ref, gate_ref, cand_ref, prev_ref, gheld_ref, conv_ref,
    gproj_ref, gbias_ref, stay_ref, send_ref,
):
    count, batch, hidden = outs_ref.shape
    span = gate_ref.shape[0] // batch
    place = place_ref[0]

    def fold(offset, state):
        source = count - 1 - offset
        return jnp.where(source > place, totals_ref[source, 0] * state + outs_ref[source], state)

    carry_in = lax.fori_loop(0, count, fold, jnp.zeros((batch, hidden), F32))

    def two_steps(offset, carry):
        arriving, gbias = carry
        pair = span // 2 - 1 - offset
        logits = [None, None]
        cands = [None, None]
        for side in (1, 0):
            here = pl.ds(pl.multiple_of((2 * pair + side) * batch, batch), batch)
            gate = gate_ref[here, :]
            keep = widen(keep_ref[here, :], hidden)
            gstate = gheld_ref[here, :] + arriving
            rest = 1.0 - gate
            cands[side] = gstate * gate
            logits[side] = cands[side] * (cand_ref[here, :] - prev_ref[here, :] * keep) * rest
            arriving = rest * keep * gstate
            gbias = gbias + logits[side]
        both = rows_of(pair, 2 * batch)
        gproj_ref[both, :hidden] = jnp.concatenate(logits, axis=0).astype(BF16)
        gproj_ref[both, hidden:] = jnp.concatenate(cands, axis=0).astype(BF16)
        return arriving, gbias

    _, gbias = lax.fori_loop(
        0, span // 2, two_steps, (carry_in, jnp.zeros((batch, hidden), F32)), unroll=4
    )
    gbias_ref[...] = jnp.sum(gbias, axis=0, keepdims=True)
    odd = place_ref[0] % 2 == 1
    wide_gradient(conv_ref, gproj_ref, stay_ref, send_ref, 0, odd)


def deal(tile, shards, first, stay_ref, send_ref, row, odd):
    size = tile.shape[0] // shards
    for even in range(0, shards, 2):
        pair = [tile[(even + k) * size : (even + k + 1) * size].astype(BF16) for k in range(2)]
        index = (first + even) // 2
        stay_ref[index, row : row + size, :] = jnp.where(odd, pair[1], pair[0])
        send_ref[index, row : row + size, :] = jnp.where(odd, pair[0], pair[1])


def wide_gradient(left_ref, right_ref, stay_ref, send_ref, row, odd):
    shards = 2 * stay_ref.shape[0]
    width = stay_ref.shape[2]
    size = left_ref.shape[1] // shards
    for part in range(right_ref.shape[1] // width):
        tile = dot_tn(left_ref[...], right_ref[:, part * width : (part + 1) * width])
        deal(tile, shards, 0, stay_ref, send_ref, row + part * size, odd)


def tall_gradient(left_ref, right_ref, stay_ref, send_ref, row, odd, block=512):
    shards = 2 * stay_ref.shape[0]
    count = left_ref.shape[1] // block
    for part in range(count):
        tile = dot_tn(left_ref[:, part * block : (part + 1) * block], right_ref[...])
        deal(tile, shards // count, part * (shards // count), stay_ref, send_ref, row, odd)


def weights_kernel(
    place_ref, nmid_ref, gup_ref, act_ref, gt_ref, held_ref, gbranch_ref, stay_ref, send_ref
):
    odd = place_ref[0] % 2 == 1
    shards = 2 * stay_ref.shape[0]
    wide_gradient(nmid_ref, gup_ref, stay_ref, send_ref, 0, odd)
    row = nmid_ref.shape[1] // shards * (gup_ref.shape[1] // stay_ref.shape[2])
    tall_gradient(act_ref, gt_ref, stay_ref, send_ref, row, odd)
    row = row + act_ref.shape[1] // shards
    tall_gradient(held_ref, gbranch_ref, stay_ref, send_ref, row, odd)


def chunks(count, size, body):
    def step(index, carry):
        body(pl.ds(pl.multiple_of(index * size, size), size))
        return carry

    lax.fori_loop(0, count // size, step, 0)


def core_sum_kernel(bits_ref, stay_ref, come_ref, stay_a, send_a, stay_b, send_b, *, plan):
    half = stay_a.shape[1]
    for out_stay, out_send, base, axis in ((stay_a, send_a, 0, plan[0]), (stay_b, send_b, half, plan[1])):
        low = 1 << axis
        for group in range(out_stay.shape[0]):
            fixed = (group >> axis) * 2 * low + (group & (low - 1))
            mine = fixed + low * bits_ref[axis]
            other = fixed + low * (1 - bits_ref[axis])

            def body(rows):
                source = pl.ds(pl.multiple_of(rows.start + base, 16), rows.size)
                out_stay[group, rows, :] = stay_ref[mine, source, :].astype(F32) + come_ref[
                    mine, source, :
                ].astype(F32)
                out_send[group, rows, :] = (
                    stay_ref[other, source, :].astype(F32) + come_ref[other, source, :].astype(F32)
                ).astype(BF16)

            chunks(half, 16, body)


def split_sum_kernel(bits_ref, *refs, plan):
    for part, (which, axis) in enumerate(plan):
        stay_ref, come_ref = refs[2 * part], refs[2 * part + 1]
        out_stay, out_send = refs[2 * len(plan) + 2 * part], refs[2 * len(plan) + 2 * part + 1]
        low = 1 << axis
        for group in range(out_stay.shape[0]):
            fixed = (group >> axis) * 2 * low + (group & (low - 1))
            mine = fixed + low * bits_ref[which]
            other = fixed + low * (1 - bits_ref[which])

            def body(rows):
                out_stay[group, rows, :] = stay_ref[mine, rows, :] + come_ref[mine, rows, :].astype(F32)
                out_send[group, rows, :] = (
                    stay_ref[other, rows, :] + come_ref[other, rows, :].astype(F32)
                ).astype(BF16)

            chunks(out_stay.shape[1], 16, body)


def join_sum_kernel(bits_ref, stay_a, come_a, stay_b, come_b, out_stay, out_send):
    half = stay_a.shape[1]
    width = out_stay.shape[1]
    here = pl.ds(pl.multiple_of(bits_ref[0] * width, width), width)
    there = pl.ds(pl.multiple_of((1 - bits_ref[0]) * width, width), width)
    for stay_ref, come_ref, base in ((stay_a, come_a, 0), (stay_b, come_b, half)):

        def body(rows):
            goal = pl.ds(pl.multiple_of(rows.start + base, 16), rows.size)
            out_stay[goal, :] = stay_ref[0, rows, here] + come_ref[0, rows, here].astype(F32)
            out_send[goal, :] = (
                stay_ref[0, rows, there] + come_ref[0, rows, there].astype(F32)
            ).astype(BF16)

        chunks(half, 16, body)


def column_sum_kernel(bits_ref, stay_ref, come_ref, out_stay, out_send, *, bit):
    width = out_stay.shape[1]
    here = pl.ds(pl.multiple_of(bits_ref[bit] * width, width), width)
    there = pl.ds(pl.multiple_of((1 - bits_ref[bit]) * width, width), width)

    def body(rows):
        out_stay[rows, :] = stay_ref[rows, here] + come_ref[rows, here].astype(F32)
        out_send[rows, :] = (stay_ref[rows, there] + come_ref[rows, there].astype(F32)).astype(BF16)

    chunks(out_stay.shape[0], 16, body)


def round_sum_kernel(stay_ref, come_ref, out_ref):
    def body(rows):
        out_ref[rows, :] = (stay_ref[rows, :].astype(F32) + come_ref[rows, :].astype(F32)).astype(BF16)

    chunks(out_ref.shape[0], 16, body)


def tail_kernel(
    gconv_ref, after_ref, xt_ref, halo_ref, gmid_ref, gain_ref, taps_ref,
    ginput_ref, gnorm1_ref, gtaps_ref, norm_buf, gconv_buf, wide_buf,
    *, steps,
):
    batch, span, width = ginput_ref.shape
    size = steps * batch
    lead = EDGE * batch
    gain = gain_ref[...]
    for row in range(batch):
        interleave(norm_buf, row, batch, halo_ref[row])
    edge = read(norm_buf, slice(0, lead))
    write(norm_buf, slice(0, lead), (edge * rms(edge) * gain).astype(BF16).astype(F32))
    gconv_buf[pl.ds(span * batch, after_ref.shape[0]), :] = after_ref[...].astype(F32)

    def spread(index, carry):
        rows = rows_of(index, size)
        values = read(xt_ref, rows)
        normed = (values * rms(values) * gain).astype(BF16).astype(F32)
        write(norm_buf, pl.ds(pl.multiple_of(index * size + lead, 8), size), normed)
        gconv_buf[rows, :] = gconv_ref[rows, :].astype(F32)
        return carry

    lax.fori_loop(0, span // steps, spread, 0)

    def chunk(index, carry):
        gnorm1, gtaps = carry
        rows = rows_of(index, size)
        here = gconv_buf[rows, :]
        gnormed = here * taps_ref[0:1, :]
        sums = []
        for tap in range(KW):
            if tap:
                later = pl.ds(pl.multiple_of(index * size + tap * batch, 8), size)
                gnormed = gnormed + gconv_buf[later, :] * taps_ref[tap : tap + 1, :]
            earlier = pl.ds(pl.multiple_of(index * size + lead - tap * batch, 8), size)
            sums.append(gtaps[tap] + jnp.sum(read(norm_buf, earlier) * here, axis=0, keepdims=True))
        values = read(xt_ref, rows)
        scale = rms(values)
        unit = values * scale
        gnorm1 = gnorm1 + jnp.sum(gnormed * unit, axis=0, keepdims=True)
        pulled = gnormed * gain
        ginput = gmid_ref[rows, :] + scale * (
            pulled - unit * jnp.mean(pulled * unit, axis=-1, keepdims=True)
        )
        write(wide_buf, rows, ginput)
        return gnorm1, tuple(sums)

    zero = jnp.zeros((1, width), F32)
    gnorm1, gtaps = lax.fori_loop(0, span // steps, chunk, (zero, (zero,) * KW))
    gnorm1_ref[...] = gnorm1
    for tap in range(KW):
        gtaps_ref[tap : tap + 1, :] = gtaps[tap]
    for row in range(batch):
        ginput_ref[row] = deinterleave(wide_buf, row, batch, span)


def call(kernel, name, out_shapes, in_specs, args, scratch=(), limit=16, flops=0, moved=0):
    return pl.pallas_call(
        kernel,
        name=name,
        out_shape=[jax.ShapeDtypeStruct(shape, kind) for shape, kind in out_shapes],
        in_specs=in_specs,
        out_specs=[VMEM_SPEC] * len(out_shapes),
        scratch_shapes=list(scratch),
        compiler_params=pltpu.CompilerParams(vmem_limit_bytes=limit * 2**20),
        cost_estimate=pl.CostEstimate(flops=flops, bytes_accessed=moved, transcendentals=0),
    )(*args)


def shifted(block, axis, distance):
    devices = range(lax.axis_size(axis))
    route = [(i - distance, i) for i in devices if i - distance in devices]
    return lax.ppermute(block, axis, route)


def swap(block, axis, bit):
    return lax.ppermute(block, axis, [(i, i ^ (1 << bit)) for i in range(lax.axis_size(axis))])


def spread_sum(name, stay, come, seq_bits, dp_bits):
    places, rows, width = stay.shape
    levels = places.bit_length() - 1
    order_a = list(range(levels))
    order_b = order_a[::-1]
    half = rows // 2

    def shapes(count):
        return [((count, half, width), F32), ((count, half, width), BF16)] * 2

    stay_a, send_a, stay_b, send_b = call(
        functools.partial(core_sum_kernel, plan=(order_a[0], order_b[0])), name + "_core",
        shapes(places // 2), [SMEM_SPEC] + [VMEM_SPEC] * 2, (seq_bits, stay, come),
    )
    for level in range(levels):
        come_a = swap(send_a, "seq", order_a[level] + 1)
        come_b = swap(send_b, "seq", order_b[level] + 1)
        if level + 1 == levels:
            break
        plan = []
        for order in (order_a, order_b):
            bit = order[level + 1]
            plan.append((bit, bit - sum(done < bit for done in order[: level + 1])))
        stay_a, send_a, stay_b, send_b = call(
            functools.partial(split_sum_kernel, plan=tuple(plan)), name + "_seq",
            shapes(places // 4 >> level), [SMEM_SPEC] + [VMEM_SPEC] * 4,
            (seq_bits, stay_a, come_a, stay_b, come_b),
        )
    depth = lax.axis_size("dp").bit_length() - 1
    wide = width // 2
    stay, send = call(
        join_sum_kernel, name + "_join", [((rows, wide), F32), ((rows, wide), BF16)],
        [SMEM_SPEC] + [VMEM_SPEC] * 4, (dp_bits, stay_a, come_a, stay_b, come_b),
    )
    for bit in range(1, depth - 1):
        wide = wide // 2
        come = swap(send, "dp", bit - 1)
        stay, send = call(
            functools.partial(column_sum_kernel, bit=bit), name + "_dp",
            [((rows, wide), F32), ((rows, wide), BF16)], [SMEM_SPEC] + [VMEM_SPEC] * 2,
            (dp_bits, stay, come),
        )
    come = swap(send, "dp", depth - 2)
    (low,) = call(
        round_sum_kernel, name + "_last", [((rows, wide), BF16)], [VMEM_SPEC] * 2, (stay, come)
    )
    come = swap(low, "dp", depth - 1)
    (total,) = call(
        round_sum_kernel, name + "_total", [((rows, wide), BF16)], [VMEM_SPEC] * 2, (low, come)
    )
    for bit in range(depth - 2, -1, -1):
        come = swap(total, "dp", bit)
        upper = dp_bits[bit] == 1
        total = jnp.concatenate(
            [jnp.where(upper, come, total), jnp.where(upper, total, come)], axis=1
        )
    return total.astype(F32)


def on_device(
    inputs, doc_start, norm1_gain, conv_weight, gate_bias, w_in, w_out, norm2_gain, w_up, w_down, out_grad
):
    batch, span, width = inputs.shape
    hidden = w_out.shape[0]
    inner = w_up.shape[1]
    tokens = batch * span
    lanes = width // LANES
    seq_count, dp_count = lax.axis_size("seq"), lax.axis_size("dp")
    pairs = seq_count // 2
    seq_at = lax.axis_index("seq").astype(jnp.int32)
    dp_at = lax.axis_index("dp").astype(jnp.int32)
    place = seq_at[None]
    seq_bits = jnp.stack([(seq_at >> bit) & 1 for bit in range(1, seq_count.bit_length() - 1)])
    dp_bits = jnp.stack([(dp_at >> bit) & 1 for bit in range(dp_count.bit_length() - 1)])
    halo = shifted(inputs[:, span - EDGE :, :], "seq", 1)
    keep = 1.0 - jnp.transpose(doc_start).astype(F32)
    keep = jnp.broadcast_to(keep[:, :, None], (span, batch, 128)).reshape(tokens, 128)
    taps = jnp.transpose(conv_weight)
    gain1, gain2, bias = norm1_gain[None], norm2_gain[None], gate_bias[None]

    xt, conv_out, gate, cand, totals = call(
        functools.partial(front_kernel, steps=16), "front",
        [
            ((lanes, tokens, LANES), F32), ((tokens, width), BF16), ((tokens, hidden), F32),
            ((tokens, hidden), F32), ((2, batch, hidden), F32),
        ],
        [VMEM_SPEC] * 7,
        (inputs, halo, keep, gain1, taps, bias, w_in),
        [pltpu.VMEM((lanes, tokens + EDGE * batch, LANES), F32)],
        limit=LIMITS[0], flops=2 * tokens * width * 2 * hidden, moved=10 * 2**20,
    )
    all_totals = lax.all_gather(totals[None], "seq", axis=0, tiled=True)
    (
        result, gt, prev, held, nmid, act, gup, gmid, gbranch, gheld, outgoing, gnorm2,
    ) = call(
        functools.partial(middle_kernel, steps=32, block=512), "middle",
        [
            ((batch, span, width), BF16), ((tokens, width), BF16), ((tokens, hidden), F32),
            ((tokens, hidden), BF16), ((tokens, width), BF16), ((tokens, inner), BF16),
            ((tokens, inner), BF16), ((tokens, width), F32), ((tokens, width), BF16),
            ((tokens, hidden), F32), ((batch, hidden), F32), ((1, width), F32),
        ],
        [SMEM_SPEC] + [VMEM_SPEC] * 10,
        (place, all_totals, out_grad, xt, keep, gate, cand, gain2, w_out, w_up, w_down),
        [pltpu.VMEM((lanes, tokens, LANES), F32)],
        limit=LIMITS[1], flops=10 * tokens * width * inner, moved=40 * 2**20,
    )
    all_outs = lax.all_gather(outgoing[None], "seq", axis=0, tiled=True)
    up_rows = inner // seq_count
    rows = up_rows + inner // seq_count + hidden // seq_count
    stay1, send1 = call(
        weights_kernel, "weights", [((pairs, rows, width), BF16)] * 2,
        [SMEM_SPEC] + [VMEM_SPEC] * 6,
        (place, nmid, gup, act, gt, held, gbranch),
        limit=LIMITS[2], flops=5 * tokens * width * inner, moved=10 * 2**20,
    )
    come1 = swap(send1, "seq", 0)
    gproj, gbias, stay2, send2 = call(
        back_kernel, "back",
        [((tokens, 2 * hidden), BF16), ((1, hidden), F32)]
        + [((pairs, 2 * hidden // seq_count, width), BF16)] * 2,
        [SMEM_SPEC] + [VMEM_SPEC] * 8,
        (place, all_totals, all_outs, keep, gate, cand, prev, gheld, conv_out),
        limit=LIMITS[3], flops=2 * tokens * width * inner, moved=20 * 2**20,
    )
    come2 = swap(send2, "seq", 0)
    total1 = spread_sum("first", stay1, come1, seq_bits, dp_bits)
    total2 = spread_sum("second", stay2, come2, seq_bits, dp_bits)
    gconv = dot_nt(gproj, w_in).astype(BF16)
    after = shifted(gconv[: EDGE * batch], "seq", -1)
    ginput, gnorm1, gtaps = call(
        functools.partial(tail_kernel, steps=16), "tail",
        [((batch, span, width), F32), ((1, width), F32), ((KW, width), F32)],
        [VMEM_SPEC] * 7,
        (gconv, after, xt, halo, gmid, gain1, taps),
        [
            pltpu.VMEM((lanes, tokens + EDGE * batch, LANES), F32),
            pltpu.VMEM((tokens + EDGE * batch, width), F32),
            pltpu.VMEM((lanes, tokens, LANES), F32),
        ],
        limit=LIMITS[4], flops=0, moved=10 * 2**20,
    )
    small = lax.psum(
        jnp.concatenate([gnorm1[0], gnorm2[0], gbias[0], jnp.transpose(gtaps).reshape(-1)]),
        ("dp", "seq"),
    )

    def own(values):
        size = values.shape[0] // seq_count
        return lax.dynamic_slice_in_dim(values, seq_at * size, size, 0)

    def sides(block):
        blocks = block.reshape(inner // width, -1, width)
        return jnp.concatenate([blocks[k] for k in range(inner // width)], axis=1)

    return (
        result, ginput, own(small[:width]), own(small[2 * width + hidden :].reshape(width, KW)),
        own(small[2 * width : 2 * width + hidden]), sides(total2),
        total1[2 * up_rows :], own(small[width : 2 * width]), sides(total1[:up_rows]),
        total1[up_rows : 2 * up_rows],
    )


def solution(mesh):
    rows, flat = P("dp", "seq", None), P()
    in_specs = (rows, P("dp", "seq")) + (flat,) * 8 + (rows,)
    vec, mat = P("seq"), P("seq", None)
    out_specs = (rows, rows, vec, mat, vec, mat, mat, vec, mat, mat)
    return jax.shard_map(
        on_device, mesh=mesh, in_specs=in_specs, out_specs=out_specs, check_vma=False
    )
```

profile of v0, /device:TPU:0, one launch (start us, length us, event | category | flops | bytes accessed | tf_op | source)
XLA Modules:
  0.0 243.2 jit_solution(16316415771538040245)
XLA Ops:
  0.6 0.8 slice.71
  1.5 2.3 collective-permute-start
  3.8 0.7 subtract_bitcast_fusion
  5.0 0.7 copy-done.25
  5.7 1.2 copy-done.27
  6.9 0.7 copy-done.29
  7.6 1.6 copy-done.39
  9.2 0.7 copy-done.42
  9.9 6.0 %front.1 = (f32[4,1024,128]{2,1,0:T(8,128)S(1)}, bf16[1024,512]{1,0:T(8,128)(2,1)S(1)}, f32[1024,1024]{1,0:T(8,128)S(1)}, f32[1024,1024]{1,0:T(8,128)S(1)}, f32[2,8,1024]{2,1,0:T(8,128)S(1)}) custom-call(bf16[8,128,512]{2,1,0:T(8,128)(2,1)S(1)} %copy-done.27, bf16[8,8,512]{2,1,0:T(8,128)(2,1)S(1)} %collective-permute-done.halo_ref, ...), custom_call_target="tpu_custom_call" | custom-call | flops 2147483648 | bytes 10485760 | tf_op jit(solution)/shard_map/front/pallas_call | solution.py:423
  15.9 2.0 copy-done
  17.9 2.0 copy-done.2
  19.9 14.5 %all-gather = f32[16,8,1024]{2,1,0:T(8,128)S(1)} all-gather(f32[2,8,1024]{2,1,0:T(8,128)S(1)} %get-tuple-element.56), channel_id=2, replica_groups=mesh['dp'=4,'seq'=8] {'seq'}, dimensions={0}, use_global_device_ids=true | all-gather | bytes 589824 | tf_op jit(solution)/shard_map/all_gather | solution.py:536
  34.4 26.4 %middle.1 = (bf16[8,128,512]{2,1,0:T(8,128)(2,1)}, bf16[1024,512]{1,0:T(8,128)(2,1)S(1)}, f32[1024,1024]{1,0:T(8,128)S(1)}, bf16[1024,1024]{1,0:T(8,128)(2,1)S(1...) custom-call(s32[1]{0:T(128)} %bitcast.place_ref, ...), custom_call_target="tpu_custom_call" | custom-call | flops 10737418240 | bytes 41943040 | tf_op jit(solution)/shard_map/middle/pallas_call | solution.py:423
  60.9 1.4 copy-done.7
  62.2 2.2 copy-done.44
  64.4 2.2 copy-done.45
  66.6 7.1 %weights.1 = (bf16[4,640,512]{2,1,0:T(8,128)(2,1)S(1)}, bf16[4,640,512]{2,1,0:T(8,128)(2,1)}) custom-call(s32[1]{0:T(128)} %bitcast.place_ref, bf16[1024,512]{1,0:T(8,128)(2,1)S(1)} %get-tuple-element.84.nmid_ref, bf16[1024,2048]{1,0:T(8,128)(2,1)S(1)} %copy-done.45, bf16[1024,2048]{1,0:T(8,128)(2,1)S(1)} %copy-done.44, ...), custom_call_target="tpu_custom_call" | custom-call | flops 5368709120 | bytes 10485760 | tf_op jit(solution)/shard_map/weights/pallas_call | solution.py:423
  74.1 8.6 %all-gather.1 = f32[64,1024]{1,0:T(8,128)S(1)} all-gather(f32[8,1024]{1,0:T(8,128)S(1)} %get-tuple-element.61), channel_id=3, replica_groups=mesh['dp'=4,'seq'=8] {'seq'}, dimensions={0}, use_global_device_ids=true | all-gather | bytes 294912 | tf_op jit(solution)/shard_map/all_gather | solution.py:552
  82.7 5.3 %back.1 = (bf16[1024,2048]{1,0:T(8,128)(2,1)S(1)}, f32[1,1024]{1,0:T(1,128)S(1)}, bf16[4,256,512]{2,1,0:T(8,128)(2,1)S(1)}, bf16[4,256,512]{2,1,0:T(8,128)(2,1)}) custom-call(s32[1]{0:T(128)} %bitcast.place_ref, f32[8,2,8,1024]{3,2,1,0:T(8,128)S(1)} %bitcast.20, f32[8,8,1024]{2,1,0:T(8,128)S(1)} %bitcast.21, f32[1024,128]{1,0:T(8,128)S(1)} %broadcast_in_dim.28.keep_ref, ...), custom_call_target="tpu_custom_call" | custom-call | flops 2147483648 | bytes 20971520 | tf_op jit(solution)/shard_map/back/pallas_call | solution.py:423
  87.9 1.0 copy-done.13
  89.5 2.0 copy-done.35
  92.0 4.0 %first_core.1 = (f32[2,320,512]{2,1,0:T(8,128)S(1)}, bf16[2,320,512]{2,1,0:T(8,128)(2,1)}, f32[2,320,512]{2,1,0:T(8,128)S(1)}, bf16[2,320,512]{2,1,0:T(8,128)(2,1)}) custom-call(s32[2]{0:T(128)S(1)} %pad_add_fusion.1.bits_ref, bf16[4,640,512]{2,1,0:T(8,128)(2,1)S(1)} %get-tuple-element.90.stay_ref, bf16[4,640,512]{2,1,0:T(8,128)(2,1)} %collective-permute-done.10.come_ref), custom_call_target="tpu_custom_call" | custom-call | tf_op jit(solution)/shard_map/first_core/pallas_call | solution.py:423
  96.0 1.1 copy-done.9
  97.1 1.1 copy-done.11
  98.1 1.4 collective-permute-start.11
  100.2 1.8 second_core.1
  102.0 1.5 collective-permute-start.3
  104.1 16.6 %collective-permute-done.3.refs_1_ = bf16[2,128,512]{2,1,0:T(8,128)(2,1)S(1)} collective-permute-done((bf16[2,128,512]{2,1,0:T(8,128)(2,1)S(1)}, bf16[2,128,512]{2,1,0:T(8,128)(2,1)S(1)}, u32[]{:S(2)}, u32[]{:S(2)}) %collective-permute-start.3) | collective-permute-done | bytes 262176 | tf_op jit(solution)/shard_map/ppermute | solution.py:442
  120.8 1.2 collective-permute-done.4.refs_3_
  121.9 1.4 second_seq.1
  123.4 0.7 copy-done.21
  124.6 1.4 collective-permute-start.6
  126.2 3.2 %collective-permute-done.5.come_a = bf16[1,128,512]{2,1,0:T(8,128)(2,1)} collective-permute-done((bf16[1,128,512]{2,1,0:T(8,128)(2,1)}, bf16[1,128,512]{2,1,0:T(8,128)(2,1)}, u32[]{:S(2)}, u32[]{:S(2)}) %collective-permute-start.5) | collective-permute-done | bytes 131104 | tf_op jit(solution)/shard_map/ppermute | solution.py:442
  129.9 0.9 copy-done.22
  130.9 1.9 second_join.1
  132.8 1.6 collective-permute-start.7
  134.4 2.4 first_seq.1
  136.9 0.9 copy-done.15
  137.7 0.8 copy-done.17
  138.6 1.5 collective-permute-start.13
  140.6 4.1 %convolution_convert_fusion.gconv_ref = bf16[1024,512]{1,0:T(8,128)(2,1)S(1)} fusion(bf16[1024,2048]{1,0:T(8,128)(2,1)S(1)} %copy-done.36, bf16[512,2048]{1,0:T(8,128)(2,1)} %w_ref.1), kind=kOutput, calls=%fused_computation | convolution fusion | flops 2148007936 | bytes 7340032 | tf_op jit(solution)/shard_map/dot_general | solution.py:29
  145.4 1.3 collective-permute-start.1
  146.7 2.2 collective-permute-done.1.after_ref
  148.9 1.6 copy-done.8
  150.5 0.7 copy-done.30
  151.2 6.3 %tail.1 = (f32[8,128,512]{2,1,0:T(8,128)}, f32[1,512]{1,0:T(1,128)S(1)}, f32[4,512]{1,0:T(4,128)S(1)}) custom-call(bf16[1024,512]{1,0:T(8,128)(2,1)S(1)} %convolution_convert_fusion.gconv_ref, bf16[64,512]{1,0:T(8,128)(2,1)} %collective-permute-done.1.after_ref, f32[4,1024,128]{2,1,0:T(8,128)S(1)} %copy-done.6, bf16[8,8,512]{2,1,0:T(8,128)(2,1)S(1)} %copy-done.24, ...), custom_call_target="tpu_custom_call" | custom-call | bytes 10485760 | tf_op jit(solution)/shard_map/tail/pallas_call | solution.py:423
  158.4 0.9 copy-done.20
  159.3 1.0 second_last.1.stay_ref
  160.3 2.7 %collective-permute-start.8 = (bf16[256,256]{1,0:T(8,128)(2,1)S(1)}, bf16[256,256]{1,0:T(8,128)(2,1)S(1)}, u32[]{:S(2)}, u32[]{:S(2)}) collective-permute-start(bf16[256,256]{1,0:T(8,128)(2,1)S(1)} %second_last.1.stay_ref), channel_id=1, source_target_pairs={{0,16},{8,24},{16,0},{24,8},{1,17},{9,25},{17,1},{25,9},{2,18},{10... | collective-permute-start | bytes 393224 | tf_op jit(solution)/shard_map/ppermute | solution.py:442
  163.0 0.7 pad_maximum_fusion.2
  163.7 39.6 %psum.7 = f32[4096]{0:T(1024)S(1)} all-reduce(f32[4096]{0:T(1024)S(1)} %pad_maximum_fusion.2), channel_id=1, replica_groups=mesh['dp'=4,'seq'=8] {'dp','seq'}, use_global_device_ids=true, to_apply=%region_0.1 | all-reduce | flops 4096 | bytes 32768 | tf_op jit(solution)/shard_map/psum | solution.py:587
  203.6 1.1 copy-done.16
  204.7 1.1 copy-done.18
  206.4 1.4 first_join.1
  207.8 1.6 collective-permute-start.15
  212.5 5.5 %collective-permute-done.15.come_ref = bf16[640,256]{1,0:T(8,128)(2,1)S(1)} collective-permute-done((bf16[640,256]{1,0:T(8,128)(2,1)S(1)}, bf16[640,256]{1,0:T(8,128)(2,1)S(1)}, u32[]{:S(2)}, u32[]{:S(2)}) %collective-permute-start.15) | collective-permute-done | bytes 327712 | tf_op jit(solution)/shard_map/ppermute | solution.py:442
  218.2 1.7 collective-permute-start.16
  219.9 1.3 collective-permute-done.9
  221.3 11.3 %collective-permute-done.16.come_ref = bf16[640,256]{1,0:T(8,128)(2,1)S(1)} collective-permute-done((bf16[640,256]{1,0:T(8,128)(2,1)S(1)}, bf16[640,256]{1,0:T(8,128)(2,1)S(1)}, u32[]{:S(2)}, u32[]{:S(2)}) %collective-permute-start.16) | collective-permute-done | bytes 327712 | tf_op jit(solution)/shard_map/ppermute | solution.py:442
  232.9 0.8 pad_maximum_fusion
  233.7 6.8 %collective-permute-done.17 = bf16[640,256]{1,0:T(8,128)(2,1)S(1)} collective-permute-done((bf16[640,256]{1,0:T(8,128)(2,1)S(1)}, bf16[640,256]{1,0:T(8,128)(2,1)S(1)}, u32[]{:S(2)}, u32[]{:S(2)}) %collective-permute-start.17) | collective-permute-done | bytes 327712 | tf_op jit(solution)/shard_map/ppermute | solution.py:442
  240.6 0.9 maximum_convert_fusion.1
  241.6 0.7 slice.96
  242.4 0.8 pad_maximum_fusion.1
  (113 shorter events, 11.3 us)
Async XLA Ops:
  1.5 3.3 %collective-permute-start = (bf16[8,8,512]{2,1,0:T(8,128)(2,1)S(1)}, bf16[8,8,512]{2,1,0:T(8,128)(2,1)S(1)}, u32[]{:S(2)}, u32[]{:S(2)}) collective-permute-start(bf16[8,8,512]{2,1,0:T(8,128)(2,1)S(1)} %slice.71), channel_id=1, source_target_pairs={{0,1},{1,2},{2,3},{3,4},{4,5},{5,6},{6,7},{8,9},{9,10},{10,11},{11... | collective-permute-start | bytes 196616 | tf_op jit(solution)/shard_map/ppermute | solution.py:438
  4.7 11.1 %copy-start.23 = (bf16[8,8,512]{2,1,0:T(8,128)(2,1)}, bf16[8,8,512]{2,1,0:T(8,128)(2,1)S(1)}, u32[]{:S(2)}) copy-start(bf16[8,8,512]{2,1,0:T(8,128)(2,1)S(1)} %collective-permute-done.halo_ref) | copy-start | bytes 196612
  5.0 0.7 copy-start.25
  5.7 1.2 copy-start.27
  6.9 0.7 copy-start.29
  7.6 1.6 copy-start.39
  9.2 0.7 copy-start.42
  9.8 24.6 %copy-start.37 = (bf16[512,2048]{1,0:T(8,128)(2,1)S(1)}, bf16[512,2048]{1,0:T(8,128)(2,1)}, u32[]{:S(2)}) copy-start(bf16[512,2048]{1,0:T(8,128)(2,1)} %w_up_ref.1) | copy-start | bytes 6291460
  9.8 24.6 %copy-start.38 = (bf16[2048,512]{1,0:T(8,128)(2,1)S(1)}, bf16[2048,512]{1,0:T(8,128)(2,1)}, u32[]{:S(2)}) copy-start(bf16[2048,512]{1,0:T(8,128)(2,1)} %w_down_ref.1) | copy-start | bytes 6291460
  9.9 24.6 %copy-start.40 = (bf16[8,128,512]{2,1,0:T(8,128)(2,1)S(1)}, bf16[8,128,512]{2,1,0:T(8,128)(2,1)}, u32[]{:S(2)}) copy-start(bf16[8,128,512]{2,1,0:T(8,128)(2,1)} %g_ref.1) | copy-start | bytes 3145732
  9.9 24.6 %copy-start.41 = (bf16[1024,512]{1,0:T(8,128)(2,1)S(1)}, bf16[1024,512]{1,0:T(8,128)(2,1)}, u32[]{:S(2)}) copy-start(bf16[1024,512]{1,0:T(8,128)(2,1)} %w_out_ref.1) | copy-start | bytes 3145732
  9.9 24.6 %copy-start.43 = (f32[512]{0:T(512)S(1)}, f32[512]{0:T(512)}, u32[]{:S(2)}) copy-start(f32[512]{0:T(512)} %param.18) | copy-start | bytes 6148
  15.9 2.0 copy-start
  17.9 2.0 copy-start.2
  19.9 41.0 %copy-start.5 = (f32[4,1024,128]{2,1,0:T(8,128)}, f32[4,1024,128]{2,1,0:T(8,128)S(1)}, u32[]{:S(2)}) copy-start(f32[4,1024,128]{2,1,0:T(8,128)S(1)} %get-tuple-element.57.xt_ref) | copy-start | bytes 6291460
  60.8 1.4 copy-start.7
  62.2 11.5 %copy-start.31 = (f32[1,512]{1,0:T(1,128)}, f32[1,512]{1,0:T(1,128)S(1)}, u32[]{:S(2)}) copy-start(f32[1,512]{1,0:T(1,128)S(1)} %get-tuple-element.69) | copy-start | bytes 6148
  62.2 2.2 copy-start.44
  64.4 2.2 copy-start.45
  66.6 16.1 %copy-start.1 = (f32[1024,1024]{1,0:T(8,128)S(1)}, f32[1024,1024]{1,0:T(8,128)}, u32[]{:S(2)}) copy-start(f32[1024,1024]{1,0:T(8,128)} %copy-done) | copy-start | bytes 12582916
  66.6 16.1 %copy-start.3 = (f32[1024,1024]{1,0:T(8,128)S(1)}, f32[1024,1024]{1,0:T(8,128)}, u32[]{:S(2)}) copy-start(f32[1024,1024]{1,0:T(8,128)} %copy-done.2) | copy-start | bytes 12582916
  66.6 16.1 %copy-start.4 = (f32[1024,1024]{1,0:T(8,128)S(1)}, f32[1024,1024]{1,0:T(8,128)}, u32[]{:S(2)}) copy-start(f32[1024,1024]{1,0:T(8,128)} %get-tuple-element.63.gheld_ref) | copy-start | bytes 12582916
  73.7 18.2 %collective-permute-start.10 = (bf16[4,640,512]{2,1,0:T(8,128)(2,1)}, bf16[4,640,512]{2,1,0:T(8,128)(2,1)}, u32[]{:S(2)}, u32[]{:S(2)}) collective-permute-start(bf16[4,640,512]{2,1,0:T(8,128)(2,1)} %get-tuple-element.91), channel_id=1, source_target_pairs={{0,1},{1,0},{2,3},{3,2},{4,5},{5,4},{6,7},{7,6},{8,9},{9,8},{10,11... | collective-permute-start | bytes 7864328 | tf_op jit(solution)/shard_map/ppermute | solution.py:442
  87.9 1.0 copy-start.13
  88.9 0.6 copy-start.28
  89.5 2.0 copy-start.35
  91.5 8.7 %collective-permute-start.2 = (bf16[4,256,512]{2,1,0:T(8,128)(2,1)}, bf16[4,256,512]{2,1,0:T(8,128)(2,1)}, u32[]{:S(2)}, u32[]{:S(2)}) collective-permute-start(bf16[4,256,512]{2,1,0:T(8,128)(2,1)} %get-tuple-element.73), channel_id=1, source_target_pairs={{0,1},{1,0},{2,3},{3,2},{4,5},{5,4},{6,7},{7,6},{8,9},{9,8},{10,11... | collective-permute-start | bytes 3145736 | tf_op jit(solution)/shard_map/ppermute | solution.py:442
  92.0 8.2 %copy-start.14 = (bf16[4,256,512]{2,1,0:T(8,128)(2,1)S(1)}, bf16[4,256,512]{2,1,0:T(8,128)(2,1)}, u32[]{:S(2)}) copy-start(bf16[4,256,512]{2,1,0:T(8,128)(2,1)} %copy-done.13) | copy-start | bytes 3145732
  96.0 1.1 copy-start.9
  97.1 1.1 copy-start.11
  98.1 36.3 %collective-permute-start.11 = (bf16[2,320,512]{2,1,0:T(8,128)(2,1)}, bf16[2,320,512]{2,1,0:T(8,128)(2,1)S(1)}, u32[]{:S(2)}, u32[]{:S(2)}) collective-permute-start(bf16[2,320,512]{2,1,0:T(8,128)(2,1)} %get-tuple-element.93), channel_id=1, source_target_pairs={{0,2},{1,3},{2,0},{3,1},{4,6},{5,7},{6,4},{7,5},{8,10},{9,11},{10,... | collective-permute-start | bytes 1966088 | tf_op jit(solution)/shard_map/ppermute | solution.py:442
  99.6 34.8 %collective-permute-start.12 = (bf16[2,320,512]{2,1,0:T(8,128)(2,1)}, bf16[2,320,512]{2,1,0:T(8,128)(2,1)}, u32[]{:S(2)}, u32[]{:S(2)}) collective-permute-start(bf16[2,320,512]{2,1,0:T(8,128)(2,1)} %get-tuple-element.95), channel_id=1, source_target_pairs={{0,4},{1,5},{2,6},{3,7},{4,0},{5,1},{6,2},{7,3},{8,12},{9,13},{10,... | collective-permute-start | bytes 1966088 | tf_op jit(solution)/shard_map/ppermute | solution.py:442
  100.2 34.2 %copy-start.10 = (f32[2,320,512]{2,1,0:T(8,128)S(1)}, f32[2,320,512]{2,1,0:T(8,128)}, u32[]{:S(2)}) copy-start(f32[2,320,512]{2,1,0:T(8,128)} %copy-done.9) | copy-start | bytes 3932164
  100.2 34.3 %copy-start.12 = (f32[2,320,512]{2,1,0:T(8,128)S(1)}, f32[2,320,512]{2,1,0:T(8,128)}, u32[]{:S(2)}) copy-start(f32[2,320,512]{2,1,0:T(8,128)} %copy-done.11) | copy-start | bytes 3932164
  102.0 18.7 %collective-permute-start.3 = (bf16[2,128,512]{2,1,0:T(8,128)(2,1)S(1)}, bf16[2,128,512]{2,1,0:T(8,128)(2,1)S(1)}, u32[]{:S(2)}, u32[]{:S(2)}) collective-permute-start(bf16[2,128,512]{2,1,0:T(8,128)(2,1)S(1)} %get-tuple-element.75), channel_id=1, source_target_pairs={{0,2},{1,3},{2,0},{3,1},{4,6},{5,7},{6,4},{7,5},{8,10},{9,11},{10,... | collective-permute-start | bytes 786440 | tf_op jit(solution)/shard_map/ppermute | solution.py:442
  103.5 18.4 %collective-permute-start.4 = (bf16[2,128,512]{2,1,0:T(8,128)(2,1)S(1)}, bf16[2,128,512]{2,1,0:T(8,128)(2,1)S(1)}, u32[]{:S(2)}, u32[]{:S(2)}) collective-permute-start(bf16[2,128,512]{2,1,0:T(8,128)(2,1)S(1)} %get-tuple-element.77), channel_id=1, source_target_pairs={{0,4},{1,5},{2,6},{3,7},{4,0},{5,1},{6,2},{7,3},{8,12},{9,13},{10,... | collective-permute-start | bytes 786440 | tf_op jit(solution)/shard_map/ppermute | solution.py:442
  123.4 0.7 copy-start.21
  124.1 5.3 %collective-permute-start.5 = (bf16[1,128,512]{2,1,0:T(8,128)(2,1)}, bf16[1,128,512]{2,1,0:T(8,128)(2,1)}, u32[]{:S(2)}, u32[]{:S(2)}) collective-permute-start(bf16[1,128,512]{2,1,0:T(8,128)(2,1)} %get-tuple-element.79), channel_id=1, source_target_pairs={{0,4},{1,5},{2,6},{3,7},{4,0},{5,1},{6,2},{7,3},{8,12},{9,13},{10,... | collective-permute-start | bytes 393224 | tf_op jit(solution)/shard_map/ppermute | solution.py:442
  124.6 5.3 %collective-permute-start.6 = (bf16[1,128,512]{2,1,0:T(8,128)(2,1)}, bf16[1,128,512]{2,1,0:T(8,128)(2,1)}, u32[]{:S(2)}, u32[]{:S(2)}) collective-permute-start(bf16[1,128,512]{2,1,0:T(8,128)(2,1)} %get-tuple-element.81), channel_id=1, source_target_pairs={{0,2},{1,3},{2,0},{3,1},{4,6},{5,7},{6,4},{7,5},{8,10},{9,11},{10,... | collective-permute-start | bytes 393224 | tf_op jit(solution)/shard_map/ppermute | solution.py:442
  126.2 8.3 %copy-start.33 = (s32[2]{0:T(128)}, s32[2]{0:T(128)S(1)}, u32[]{:S(2)}) copy-start(s32[2]{0:T(128)S(1)} %pad_add_fusion.bits_ref) | copy-start | bytes 28
  129.9 1.0 copy-start.22
  130.9 9.7 %copy-start.36 = (bf16[1024,2048]{1,0:T(8,128)(2,1)S(1)}, bf16[1024,2048]{1,0:T(8,128)(2,1)}, u32[]{:S(2)}) copy-start(bf16[1024,2048]{1,0:T(8,128)(2,1)} %copy-done.35) | copy-start | bytes 12582916
  132.8 7.8 %copy-start.19 = (f32[256,256]{1,0:T(8,128)}, f32[256,256]{1,0:T(8,128)S(1)}, u32[]{:S(2)}) copy-start(f32[256,256]{1,0:T(8,128)S(1)} %get-tuple-element.82.stay_ref) | copy-start | bytes 786436
  132.8 25.5 %collective-permute-start.7 = (bf16[256,256]{1,0:T(8,128)(2,1)}, bf16[256,256]{1,0:T(8,128)(2,1)}, u32[]{:S(2)}, u32[]{:S(2)}) collective-permute-start(bf16[256,256]{1,0:T(8,128)(2,1)} %get-tuple-element.83), channel_id=1, source_target_pairs={{0,8},{8,0},{16,24},{24,16},{1,9},{9,1},{17,25},{25,17},{2,10},{10... | collective-permute-start | bytes 393224 | tf_op jit(solution)/shard_map/ppermute | solution.py:442
  136.9 0.9 copy-start.15
  137.7 0.8 copy-start.17
  138.6 65.0 %collective-permute-start.13 = (bf16[1,320,512]{2,1,0:T(8,128)(2,1)}, bf16[1,320,512]{2,1,0:T(8,128)(2,1)S(1)}, u32[]{:S(2)}, u32[]{:S(2)}) collective-permute-start(bf16[1,320,512]{2,1,0:T(8,128)(2,1)} %get-tuple-element.97), channel_id=1, source_target_pairs={{0,4},{1,5},{2,6},{3,7},{4,0},{5,1},{6,2},{7,3},{8,12},{9,13},{10,... | collective-permute-start | bytes 983048 | tf_op jit(solution)/shard_map/ppermute | solution.py:442
  140.1 63.5 %collective-permute-start.14 = (bf16[1,320,512]{2,1,0:T(8,128)(2,1)}, bf16[1,320,512]{2,1,0:T(8,128)(2,1)}, u32[]{:S(2)}, u32[]{:S(2)}) collective-permute-start(bf16[1,320,512]{2,1,0:T(8,128)(2,1)} %get-tuple-element.99), channel_id=1, source_target_pairs={{0,2},{1,3},{2,0},{3,1},{4,6},{5,7},{6,4},{7,5},{8,10},{9,11},{10,... | collective-permute-start | bytes 983048 | tf_op jit(solution)/shard_map/ppermute | solution.py:442
  140.6 8.3 %copy-start.6 = (f32[4,1024,128]{2,1,0:T(8,128)S(1)}, f32[4,1024,128]{2,1,0:T(8,128)}, u32[]{:S(2)}) copy-start(f32[4,1024,128]{2,1,0:T(8,128)} %copy-done.5) | copy-start | bytes 6291460
  140.6 8.3 %copy-start.24 = (bf16[8,8,512]{2,1,0:T(8,128)(2,1)S(1)}, bf16[8,8,512]{2,1,0:T(8,128)(2,1)}, u32[]{:S(2)}) copy-start(bf16[8,8,512]{2,1,0:T(8,128)(2,1)} %copy-done.23) | copy-start | bytes 196612
  140.6 8.3 %copy-start.26 = (f32[512,4]{0,1:T(4,128)S(1)}, f32[512,4]{0,1:T(4,128)}, u32[]{:S(2)}) copy-start(f32[512,4]{0,1:T(4,128)} %param.14) | copy-start | bytes 24580
  145.4 3.5 %collective-permute-start.1 = (bf16[64,512]{1,0:T(8,128)(2,1)}, bf16[64,512]{1,0:T(8,128)(2,1)}, u32[]{:S(2)}, u32[]{:S(2)}) collective-permute-start(bf16[64,512]{1,0:T(8,128)(2,1)} %slice.88), channel_id=1, source_target_pairs={{1,0},{2,1},{3,2},{4,3},{5,4},{6,5},{7,6},{9,8},{10,9},{11,10},{12... | collective-permute-start | bytes 196616 | tf_op jit(solution)/shard_map/ppermute | solution.py:438
  148.9 1.6 copy-start.8
  150.5 0.7 copy-start.30
  157.5 0.6 copy-start.32
  158.4 1.0 copy-start.20
  160.3 49.8 %collective-permute-start.8 = (bf16[256,256]{1,0:T(8,128)(2,1)S(1)}, bf16[256,256]{1,0:T(8,128)(2,1)S(1)}, u32[]{:S(2)}, u32[]{:S(2)}) collective-permute-start(bf16[256,256]{1,0:T(8,128)(2,1)S(1)} %second_last.1.stay_ref), channel_id=1, source_target_pairs={{0,16},{8,24},{16,0},{24,8},{1,17},{9,25},{17,1},{25,9},{2,18},{10... | collective-permute-start | bytes 393224 | tf_op jit(solution)/shard_map/ppermute | solution.py:442
  203.6 1.1 copy-start.16
  204.7 1.1 copy-start.18
  205.7 0.7 copy-start.34
  207.8 10.1 %collective-permute-start.15 = (bf16[640,256]{1,0:T(8,128)(2,1)S(1)}, bf16[640,256]{1,0:T(8,128)(2,1)S(1)}, u32[]{:S(2)}, u32[]{:S(2)}) collective-permute-start(bf16[640,256]{1,0:T(8,128)(2,1)S(1)} %get-tuple-element.101), channel_id=1, source_target_pairs={{0,8},{8,0},{16,24},{24,16},{1,9},{9,1},{17,25},{25,17},{2,10},{10... | collective-permute-start | bytes 983048 | tf_op jit(solution)/shard_map/ppermute | solution.py:442
  210.2 11.0 %collective-permute-start.9 = (bf16[256,256]{1,0:T(8,128)(2,1)S(1)}, bf16[256,256]{1,0:T(8,128)(2,1)S(1)}, u32[]{:S(2)}, u32[]{:S(2)}) collective-permute-start(bf16[256,256]{1,0:T(8,128)(2,1)S(1)} %second_total.1), channel_id=1, source_target_pairs={{0,8},{8,0},{16,24},{24,16},{1,9},{9,1},{17,25},{25,17},{2,10},{10... | collective-permute-start | bytes 393224 | tf_op jit(solution)/shard_map/ppermute | solution.py:442
  218.2 14.4 %collective-permute-start.16 = (bf16[640,256]{1,0:T(8,128)(2,1)S(1)}, bf16[640,256]{1,0:T(8,128)(2,1)S(1)}, u32[]{:S(2)}, u32[]{:S(2)}) collective-permute-start(bf16[640,256]{1,0:T(8,128)(2,1)S(1)} %first_last.1.stay_ref), channel_id=1, source_target_pairs={{0,16},{8,24},{16,0},{24,8},{1,17},{9,25},{17,1},{25,9},{2,18},{10... | collective-permute-start | bytes 983048 | tf_op jit(solution)/shard_map/ppermute | solution.py:442
  232.8 7.7 %collective-permute-start.17 = (bf16[640,256]{1,0:T(8,128)(2,1)S(1)}, bf16[640,256]{1,0:T(8,128)(2,1)S(1)}, u32[]{:S(2)}, u32[]{:S(2)}) collective-permute-start(bf16[640,256]{1,0:T(8,128)(2,1)S(1)} %first_total.1), channel_id=1, source_target_pairs={{0,8},{8,0},{16,24},{24,16},{1,9},{9,1},{17,25},{25,17},{2,10},{10... | collective-permute-start | bytes 983048 | tf_op jit(solution)/shard_map/ppermute | solution.py:442
where the time goes:
time: 244 us; the launch traced here: 243 us
  Pallas kernels  65.7 us (27%)
  blocking collectives  62.6 us (26%)
  waiting for transfers between devices  48.6 us (20%)
  local copies, waits for them, and re-layouts  36 us (15%)
  starting transfers between devices  20.7 us (8%)
  other arithmetic  4.39 us (2%)
  matrix products  4.14 us (2%)
    pallas_call x15, Pallas kernels, call(): pl.pallas_call(kernel, name=name, out_shape=[jax.ShapeDtypeStruct(shape,...  65.7 us
    ppermute x16, waiting for transfers between devices, swap(): lax.ppermute(block, axis, [(i, i ^ 1 << bit) for i in range(lax.axis_size...  46.4 us
    psum x1, blocking collectives, on_device(): lax.psum(jnp.concatenate([gnorm1[0], gnorm2[0], gbias[0], jnp.transpose(g...  39.6 us
    unnamed x93, local copies, waits for them, and re-layouts  31.1 us
    ppermute x16, starting transfers between devices, swap(): lax.ppermute(block, axis, [(i, i ^ 1 << bit) for i in range(lax.axis_size...  17.1 us
    all_gather x1, blocking collectives, on_device(): all_totals = lax.all_gather(totals[None], 'seq', axis=0, tiled=True)  14.5 us
    all_gather x1, blocking collectives, on_device(): all_outs = lax.all_gather(outgoing[None], 'seq', axis=0, tiled=True)  8.55 us
  transfers between devices with their start and end apart: 18, of which 9 were waited for; matrix products, arithmetic and copies ran while one was open for 4% of the time, Pallas kernels for 11%

commit v1 on v0

v1 whole, which is shorter than its diff:
```python
import functools

import jax
import jax.numpy as jnp
from jax import lax
from jax.experimental import pallas as pl
from jax.experimental.pallas import tpu as pltpu
from jax.sharding import PartitionSpec as P

KW = 4
EPS = 1e-05
EDGE = 8
LANES = 128
WORK = {"first_seq": 10**10, "back": 10**10}
LIMITS = {"ingest": 2, "prepare": 3, "prepare_rest": 1, "front": 4, "forward": 3, "weights": 3, "reverse": 2, "back": 3, "gconv": 1, "tail": 10, "result": 4}
F32 = jnp.float32
BF16 = jnp.bfloat16
GELU_C = 0.7978845608028654
GELU_A = 0.044715

VMEM_SPEC = pl.BlockSpec(memory_space=pltpu.VMEM)


def dot(left, right):
    return jnp.dot(left, right, preferred_element_type=F32)


def dot_nt(left, right):
    return lax.dot_general(left, right, (((1,), (1,)), ((), ())), preferred_element_type=F32)


def dot_tn(left, right):
    return lax.dot_general(left, right, (((0,), (0,)), ((), ())), preferred_element_type=F32)


def widen(column, lanes):
    return jnp.concatenate([column] * (lanes // column.shape[1]), axis=1)


def rms(values):
    return lax.rsqrt(jnp.mean(values * values, axis=-1, keepdims=True) + EPS)


def rows_of(index, count):
    return pl.ds(pl.multiple_of(index * count, count), count)


def interleave(buf, row, batch, values):
    for lane in range(buf.shape[0]):
        cols = slice(lane * LANES, (lane + 1) * LANES)
        buf[lane, pl.ds(row, values.shape[0], stride=batch), :] = values[:, cols].astype(F32)


def deinterleave(buf, row, batch, span):
    parts = [buf[lane, pl.ds(row, span, stride=batch), :] for lane in range(buf.shape[0])]
    return jnp.concatenate(parts, axis=1)


def read(buf, rows):
    return jnp.concatenate([buf[lane, rows, :] for lane in range(buf.shape[0])], axis=1)


def write(buf, rows, values):
    for lane in range(buf.shape[0]):
        buf[lane, rows, :] = values[:, lane * LANES : (lane + 1) * LANES]


def ingest_kernel(x_ref, start_ref, gain_ref, xt_ref, normed_ref, edge_ref, keep_ref, x_buf, sems, *, steps):
    batch, span, width = x_ref.shape
    size = steps * batch
    copies = [pltpu.make_async_copy(x_ref.at[row], x_buf.at[row], sems.at[row]) for row in range(batch)]
    for copy in copies:
        copy.start()
    keep = 1.0 - start_ref[...].astype(F32)
    for token in range(span):
        keep_ref[token * batch : (token + 1) * batch, :] = jnp.broadcast_to(
            keep[:, token : token + 1], (batch, LANES)
        )
    for row, copy in enumerate(copies):
        copy.wait()
        interleave(xt_ref, row, batch, x_buf[row])

    def chunk(index, carry):
        rows = rows_of(index, size)
        values = read(xt_ref, rows)
        normed_ref[rows, :] = (values * rms(values) * gain_ref[...]).astype(BF16)
        return carry

    lax.fori_loop(0, span // steps, chunk, 0)
    edge_ref[...] = normed_ref[(span - EDGE) * batch :, :]


def prepare_kernel(g_ref, w_down_ref, gt_ref, gact_ref, wide_buf, *, steps, block):
    batch, span, width = g_ref.shape
    size = steps * batch
    for row in range(batch):
        interleave(wide_buf, row, batch, g_ref[row])

    def chunk(index, carry):
        rows = rows_of(index, size)
        g_low = read(wide_buf, rows).astype(BF16)
        gt_ref[rows, :] = g_low
        for part in range(gact_ref.shape[1] // block):
            cols = slice(part * block, (part + 1) * block)
            gact_ref[rows, cols] = dot_nt(g_low, w_down_ref[cols, :]).astype(BF16)
        return carry

    lax.fori_loop(0, span // steps, chunk, 0)


def prepare_rest_kernel(gt_ref, w_down_ref, gact_ref, *, size, block):
    first = w_down_ref.shape[0] - gact_ref.shape[1]

    def chunk(index, carry):
        rows = rows_of(index, size)
        for part in range(gact_ref.shape[1] // block):
            cols = slice(part * block, (part + 1) * block)
            weights = w_down_ref[first + part * block : first + (part + 1) * block, :]
            gact_ref[rows, cols] = dot_nt(gt_ref[rows, :], weights).astype(BF16)
        return carry

    lax.fori_loop(0, gt_ref.shape[0] // size, chunk, 0)


def chip_totals_kernel(mine_ref, mate_ref, chip_ref):
    odd = bit_of("seq", 0) == 1
    prod, state = mine_ref[0], mine_ref[1]
    mate_prod, mate_state = mate_ref[0], mate_ref[1]
    chip_ref[0] = prod * mate_prod
    chip_ref[1] = jnp.where(odd, prod * mate_state + state, mate_prod * state + mate_state)


def chip_outgoing_kernel(mine_ref, mate_ref, totals_ref, mate_totals_ref, chip_ref):
    odd = bit_of("seq", 0) == 1
    mine, mate = mine_ref[...], mate_ref[...]
    chip_ref[...] = jnp.where(odd, mate_totals_ref[0] * mine + mate, totals_ref[0] * mate + mine)


def from_chip(refs, source, chip, part):
    value = refs[0][part]
    for mask in range(2, len(refs) + 1):
        value = jnp.where((source ^ chip) == mask, refs[mask - 1][part], value)
    return value


def front_kernel(
    normed_ref, halo_ref, keep_ref, taps_ref, bias_ref, w_ref,
    conv_ref, gate_ref, cand_ref, total_ref, norm_buf,
    *, steps, block,
):
    batch, hidden = total_ref.shape[1:]
    tokens, width = normed_ref.shape
    span = tokens // batch
    size = steps * batch
    lead = EDGE * batch
    norm_buf[:lead, :] = halo_ref[...].astype(F32)

    def chunk(index, carry):
        rows = rows_of(index, size)
        here = normed_ref[rows, :].astype(F32)
        norm_buf[pl.ds(pl.multiple_of(index * size + lead, 8), size), :] = here
        mixing = here * taps_ref[0:1, :]
        for tap in range(1, KW):
            start = pl.multiple_of(index * size + lead - tap * batch, 8)
            mixing = mixing + norm_buf[pl.ds(start, size), :] * taps_ref[tap : tap + 1, :]
        conv_low = mixing.astype(BF16)
        conv_ref[rows, :] = conv_low
        for part in range(hidden // block):
            cols = slice(part * block, (part + 1) * block)
            more = slice(hidden + part * block, hidden + (part + 1) * block)
            gate_ref[rows, cols] = jax.nn.sigmoid(dot(conv_low, w_ref[:, cols]) + bias_ref[:, cols])
            cand_ref[rows, cols] = dot(conv_low, w_ref[:, more])

        def step(offset, carry):
            prod, state = carry
            here = rows_of(index * steps + offset, batch)
            gate = gate_ref[here, :]
            decay = (1.0 - gate) * widen(keep_ref[here, :], hidden)
            return decay * prod, decay * state + gate * cand_ref[here, :]

        return lax.fori_loop(0, steps, step, carry, unroll=8)

    first = (jnp.ones((batch, hidden), F32), jnp.zeros((batch, hidden), F32))
    prod, state = lax.fori_loop(0, span // steps, chunk, first)
    total_ref[0] = prod
    total_ref[1] = state


def forward_kernel(
    mate_ref, *refs, chips, steps, block,
):
    chip_refs = refs[: chips - 1]
    (
        xt_ref, keep_ref, gate_ref, cand_ref, gact_ref, more_ref, gain_ref, w_out_ref, w_up_ref,
        prev_ref, held_ref, mid_ref, nmid_ref, act_ref, gup_ref,
    ) = refs[chips - 1 :]
    batch, hidden = mate_ref.shape[1:]
    inner = w_up_ref.shape[1]
    span = gate_ref.shape[0] // batch
    size = steps * batch
    chip = lax.shift_right_logical(lax.axis_index("seq"), 1)
    carry_in = jnp.zeros((batch, hidden), F32)
    for source in range(chips - 1):
        prod = from_chip(chip_refs, source, chip, 0)
        state = from_chip(chip_refs, source, chip, 1)
        carry_in = jnp.where(source < chip, prod * carry_in + state, carry_in)
    carry_in = jnp.where(bit_of("seq", 0) == 1, mate_ref[0] * carry_in + mate_ref[1], carry_in)
    gain = gain_ref[...]

    def chunk(index, state):
        rows = rows_of(index, size)

        def two_steps(pair, state):
            out = []
            for side in range(2):
                here = pl.ds(pl.multiple_of((index * steps + 2 * pair + side) * batch, batch), batch)
                gate = gate_ref[here, :]
                prev_ref[here, :] = state
                decay = (1.0 - gate) * widen(keep_ref[here, :], hidden)
                state = decay * state + gate * cand_ref[here, :]
                out.append(state)
            both = rows_of(index * (steps // 2) + pair, 2 * batch)
            held_ref[both, :] = jnp.concatenate(out, axis=0).astype(BF16)
            return state

        state = lax.fori_loop(0, steps // 2, two_steps, state, unroll=4)
        middle = read(xt_ref, rows) + dot(held_ref[rows, :], w_out_ref[...])
        mid_ref[rows, :] = middle
        nmid = (middle * rms(middle) * gain).astype(BF16)
        nmid_ref[rows, :] = nmid
        for part in range(inner // block):
            cols = slice(part * block, (part + 1) * block)
            up = dot(nmid, w_up_ref[:, cols])
            square = up * up
            half = 0.5 + 0.5 * jnp.tanh(up * (GELU_C + (GELU_C * GELU_A) * square))
            act = up * half
            slope = half + act * (1.0 - half) * (2.0 * GELU_C + (6.0 * GELU_C * GELU_A) * square)
            act_ref[rows, cols] = act.astype(BF16)
            start = part * block
            source, start = (gact_ref, start) if start < gact_ref.shape[1] else (more_ref, start - gact_ref.shape[1])
            gact = source[rows, start : start + block].astype(F32)
            gup_ref[rows, cols] = (slope * gact).astype(BF16)
        return state

    lax.fori_loop(0, span // steps, chunk, carry_in)


def result_kernel(act_ref, mid_ref, w_down_ref, result_ref, wide_buf, *, steps):
    batch, span, width = result_ref.shape

    def chunk(index, carry):
        rows = rows_of(index, steps * batch)
        write(wide_buf, rows, mid_ref[rows, :] + dot(act_ref[rows, :], w_down_ref[...]))
        return carry

    lax.fori_loop(0, span // steps, chunk, 0)
    for row in range(batch):
        result_ref[row] = deinterleave(wide_buf, row, batch, span).astype(BF16)


def gconv_kernel(gproj_ref, w_in_ref, gconv_ref, *, steps):
    size = steps * 8

    def chunk(index, carry):
        rows = rows_of(index, size)
        gconv_ref[rows, :] = dot_nt(gproj_ref[rows, :], w_in_ref[...]).astype(BF16)
        return carry

    lax.fori_loop(0, gproj_ref.shape[0] // size, chunk, 0)


def reverse_kernel(
    gup_ref, mid_ref, gt_ref, gain_ref, keep_ref, gate_ref, w_out_ref, w_up_ref,
    gmid_ref, gbranch_ref, gheld_ref, outgoing_ref, gnorm2_ref,
    *, steps,
):
    tokens, width = mid_ref.shape
    batch, hidden = outgoing_ref.shape
    span = tokens // batch
    size = steps * batch
    gain = gain_ref[...]

    def chunk(offset, carry):
        arriving, gnorm2 = carry
        index = span // steps - 1 - offset
        rows = rows_of(index, size)
        gnmid = dot_nt(gup_ref[rows, :], w_up_ref[...])
        middle = mid_ref[rows, :]
        scale = rms(middle)
        unit = middle * scale
        gnorm2 = gnorm2 + jnp.sum(gnmid * unit, axis=0, keepdims=True)
        pulled = gnmid * gain
        gmid = gt_ref[rows, :].astype(F32) + scale * (
            pulled - unit * jnp.mean(pulled * unit, axis=-1, keepdims=True)
        )
        gmid_ref[rows, :] = gmid
        gbranch = gmid.astype(BF16)
        gbranch_ref[rows, :] = gbranch
        gheld_ref[rows, :] = dot_nt(gbranch, w_out_ref[...])

        def back(offset, arriving):
            here = rows_of(index * steps + steps - 1 - offset, batch)
            decay = (1.0 - gate_ref[here, :]) * widen(keep_ref[here, :], hidden)
            return decay * (gheld_ref[here, :] + arriving)

        return lax.fori_loop(0, steps, back, arriving, unroll=8), gnorm2

    first = (jnp.zeros((batch, hidden), F32), jnp.zeros((1, width), F32))
    outgoing, gnorm2 = lax.fori_loop(0, span // steps, chunk, first)
    outgoing_ref[...] = outgoing
    gnorm2_ref[...] = gnorm2


def back_kernel(*refs, chips):
    chip_refs, out_refs = refs[: chips - 1], refs[chips - 1 : 2 * chips - 2]
    (
        mate_ref, mate_out_ref, keep_ref, gate_ref, cand_ref, prev_ref, gheld_ref, conv_ref,
        gproj_ref, gbias_ref, stay_ref, send_ref,
    ) = refs[2 * chips - 2 :]
    batch, hidden = mate_out_ref.shape
    span = gate_ref.shape[0] // batch
    chip = lax.shift_right_logical(lax.axis_index("seq"), 1)
    carry_in = jnp.zeros((batch, hidden), F32)
    for source in range(chips - 1, 0, -1):
        prod = from_chip(chip_refs, source, chip, 0)
        state = from_chip(out_refs, source, chip, slice(None))
        carry_in = jnp.where(source > chip, prod * carry_in + state, carry_in)
    carry_in = jnp.where(bit_of("seq", 0) == 0, mate_ref[0] * carry_in + mate_out_ref[...], carry_in)

    def two_steps(offset, carry):
        arriving, gbias = carry
        pair = span // 2 - 1 - offset
        logits = [None, None]
        cands = [None, None]
        for side in (1, 0):
            here = pl.ds(pl.multiple_of((2 * pair + side) * batch, batch), batch)
            gate = gate_ref[here, :]
            keep = widen(keep_ref[here, :], hidden)
            gstate = gheld_ref[here, :] + arriving
            rest = 1.0 - gate
            cands[side] = gstate * gate
            logits[side] = cands[side] * (cand_ref[here, :] - prev_ref[here, :] * keep) * rest
            arriving = rest * keep * gstate
            gbias = gbias + logits[side]
        both = rows_of(pair, 2 * batch)
        gproj_ref[both, :hidden] = jnp.concatenate(logits, axis=0).astype(BF16)
        gproj_ref[both, hidden:] = jnp.concatenate(cands, axis=0).astype(BF16)
        return arriving, gbias

    _, gbias = lax.fori_loop(
        0, span // 2, two_steps, (carry_in, jnp.zeros((batch, hidden), F32)), unroll=4
    )
    gbias_ref[...] = jnp.sum(gbias, axis=0, keepdims=True)
    odd = bit_of("seq", 0) == 1
    wide_gradient(conv_ref, gproj_ref, stay_ref, send_ref, odd)


def deal(tile, shards, first, stay_ref, send_ref, row, odd):
    size = tile.shape[0] // shards
    for even in range(0, shards, 2):
        pair = [tile[(even + k) * size : (even + k + 1) * size].astype(BF16) for k in range(2)]
        index = (first + even) // 2
        stay_ref[index, row : row + size, :] = jnp.where(odd, pair[1], pair[0])
        send_ref[index, row : row + size, :] = jnp.where(odd, pair[0], pair[1])


def wide_gradient(left_ref, right_ref, stay_ref, send_ref, odd):
    shards = 2 * stay_ref.shape[0]
    width = stay_ref.shape[2]
    size = left_ref.shape[1] // shards
    for part in range(right_ref.shape[1] // width):
        tile = dot_tn(left_ref[...], right_ref[:, part * width : (part + 1) * width])
        deal(tile, shards, 0, stay_ref, send_ref, part * size, odd)


def tall_gradient(left_ref, right_ref, stay_ref, send_ref, odd, block=512):
    shards = 2 * stay_ref.shape[0]
    count = left_ref.shape[1] // block
    for part in range(count):
        tile = dot_tn(left_ref[:, part * block : (part + 1) * block], right_ref[...])
        deal(tile, shards // count, part * (shards // count), stay_ref, send_ref, 0, odd)


def weights_kernel(nmid_ref, gup_ref, act_ref, gt_ref, stay_up, send_up, stay_down, send_down):
    odd = bit_of("seq", 0) == 1
    wide_gradient(nmid_ref, gup_ref, stay_up, send_up, odd)
    tall_gradient(act_ref, gt_ref, stay_down, send_down, odd)


def weights_out_kernel(held_ref, gbranch_ref, stay_ref, send_ref):
    tall_gradient(held_ref, gbranch_ref, stay_ref, send_ref, bit_of("seq", 0) == 1)


def bit_of(axis, bit):
    return lax.shift_right_logical(lax.axis_index(axis), bit) & 1


def chunks(count, size, body):
    def step(index, carry):
        body(pl.ds(pl.multiple_of(index * size, size), size))
        return carry

    lax.fori_loop(0, count // size, step, 0)


def core_sum_kernel(*refs, plan):
    sources, (stay_a, send_a, stay_b, send_b) = refs[:-4], refs[-4:]
    base = 0
    for stay_ref, come_ref in zip(sources[::2], sources[1::2]):
        half = stay_ref.shape[1] // 2
        for out_stay, out_send, first, axis in ((stay_a, send_a, 0, plan[0]), (stay_b, send_b, half, plan[1])):
            low = 1 << axis
            for group in range(out_stay.shape[0]):
                fixed = (group >> axis) * 2 * low + (group & (low - 1))
                mine = fixed + low * bit_of("seq", axis + 1)
                other = fixed + low * (1 - bit_of("seq", axis + 1))

                def body(rows):
                    source = pl.ds(pl.multiple_of(rows.start + first, 16), rows.size)
                    goal = pl.ds(pl.multiple_of(rows.start + base, 16), rows.size)
                    out_stay[group, goal, :] = stay_ref[mine, source, :].astype(F32) + come_ref[
                        mine, source, :
                    ].astype(F32)
                    out_send[group, goal, :] = (
                        stay_ref[other, source, :].astype(F32) + come_ref[other, source, :].astype(F32)
                    ).astype(BF16)

                chunks(half, 16, body)
        base += half


def split_sum_kernel(*refs, plan):
    for part, (which, axis) in enumerate(plan):
        stay_ref, come_ref = refs[2 * part], refs[2 * part + 1]
        out_stay, out_send = refs[2 * len(plan) + 2 * part], refs[2 * len(plan) + 2 * part + 1]
        low = 1 << axis
        for group in range(out_stay.shape[0]):
            fixed = (group >> axis) * 2 * low + (group & (low - 1))
            mine = fixed + low * bit_of("seq", which + 1)
            other = fixed + low * (1 - bit_of("seq", which + 1))

            def body(rows):
                out_stay[group, rows, :] = stay_ref[mine, rows, :] + come_ref[mine, rows, :].astype(F32)
                out_send[group, rows, :] = (
                    stay_ref[other, rows, :] + come_ref[other, rows, :].astype(F32)
                ).astype(BF16)

            chunks(out_stay.shape[1], 16, body)


def join_sum_kernel(stay_a, come_a, stay_b, come_b, out_stay, out_send):
    half = stay_a.shape[1]
    width = out_stay.shape[1]
    here = pl.ds(pl.multiple_of(bit_of("dp", 0) * width, width), width)
    there = pl.ds(pl.multiple_of((1 - bit_of("dp", 0)) * width, width), width)
    for stay_ref, come_ref, base in ((stay_a, come_a, 0), (stay_b, come_b, half)):

        def body(rows):
            goal = pl.ds(pl.multiple_of(rows.start + base, 16), rows.size)
            out_stay[goal, :] = stay_ref[0, rows, here] + come_ref[0, rows, here].astype(F32)
            out_send[goal, :] = (
                stay_ref[0, rows, there] + come_ref[0, rows, there].astype(F32)
            ).astype(BF16)

        chunks(half, 16, body)


def column_sum_kernel(stay_ref, come_ref, out_stay, out_send, *, bit):
    width = out_stay.shape[1]
    here = pl.ds(pl.multiple_of(bit_of("dp", bit) * width, width), width)
    there = pl.ds(pl.multiple_of((1 - bit_of("dp", bit)) * width, width), width)

    def body(rows):
        out_stay[rows, :] = stay_ref[rows, here] + come_ref[rows, here].astype(F32)
        out_send[rows, :] = (stay_ref[rows, there] + come_ref[rows, there].astype(F32)).astype(BF16)

    chunks(out_stay.shape[0], 16, body)


def round_sum_kernel(stay_ref, come_ref, out_ref):
    def body(rows):
        out_ref[rows, :] = (stay_ref[rows, :].astype(F32) + come_ref[rows, :].astype(F32)).astype(BF16)

    chunks(out_ref.shape[0], 16, body)


def tail_kernel(
    gconv_ref, after_ref, xt_ref, normed_ref, halo_ref, gmid_ref, gain_ref, taps_ref, gnorm2_ref, gbias_ref,
    ginput_ref, small_ref, norm_buf, gconv_buf, wide_buf,
    *, steps,
):
    batch, span, width = ginput_ref.shape
    size = steps * batch
    lead = EDGE * batch
    gain = gain_ref[...]
    norm_buf[:lead, :] = halo_ref[...].astype(F32)
    gconv_buf[pl.ds(span * batch, after_ref.shape[0]), :] = after_ref[...].astype(F32)

    def spread(index, carry):
        rows = rows_of(index, size)
        norm_buf[pl.ds(pl.multiple_of(index * size + lead, 8), size), :] = normed_ref[rows, :].astype(F32)
        gconv_buf[rows, :] = gconv_ref[rows, :].astype(F32)
        return carry

    lax.fori_loop(0, span // steps, spread, 0)

    def chunk(index, carry):
        gnorm1, gtaps = carry
        rows = rows_of(index, size)
        here = gconv_buf[rows, :]
        gnormed = here * taps_ref[0:1, :]
        sums = []
        for tap in range(KW):
            if tap:
                later = pl.ds(pl.multiple_of(index * size + tap * batch, 8), size)
                gnormed = gnormed + gconv_buf[later, :] * taps_ref[tap : tap + 1, :]
            earlier = pl.ds(pl.multiple_of(index * size + lead - tap * batch, 8), size)
            sums.append(gtaps[tap] + jnp.sum(norm_buf[earlier, :] * here, axis=0, keepdims=True))
        values = read(xt_ref, rows)
        scale = rms(values)
        unit = values * scale
        gnorm1 = gnorm1 + jnp.sum(gnormed * unit, axis=0, keepdims=True)
        pulled = gnormed * gain
        ginput = gmid_ref[rows, :] + scale * (
            pulled - unit * jnp.mean(pulled * unit, axis=-1, keepdims=True)
        )
        write(wide_buf, rows, ginput)
        return gnorm1, tuple(sums)

    zero = jnp.zeros((1, width), F32)
    gnorm1, gtaps = lax.fori_loop(0, span // steps, chunk, (zero, (zero,) * KW))
    small_ref[0:1, :] = gnorm1
    small_ref[1:2, :] = gnorm2_ref[...]
    for tap in range(KW):
        small_ref[2 + tap : 3 + tap, :] = gtaps[tap]
    for part in range(gbias_ref.shape[1] // width):
        row = 2 + KW + part
        small_ref[row : row + 1, :] = gbias_ref[:, part * width : (part + 1) * width]
    for row in range(batch):
        ginput_ref[row] = deinterleave(wide_buf, row, batch, span)


def finish_kernel(total_ref, come_ref, *outs, sizes):
    wide = total_ref.shape[1]
    width = 2 * wide
    for source, bit in ((total_ref, bit_of("dp", 0)), (come_ref, 1 - bit_of("dp", 0))):
        row = 0
        for half in range(2):
            for out, rows in zip(outs, sizes):
                size = out.shape[0]
                for start in range(half * rows // 2, (half + 1) * rows // 2, min(size, rows // 2)):
                    count = min(size, rows // 2)
                    part, low = start // size, start % size
                    cols = pl.ds(pl.multiple_of(part * width + bit * wide, wide), wide)
                    out[low : low + count, cols] = source[row : row + count, :].astype(F32)
                    row += count


def call(
    kernel, name, out_shapes, in_specs, args, scratch=(), limit=2, after=None, rider=None, work=1
):
    ins, outs = len(args), len(out_shapes)

    def body(*refs):
        inner = list(refs[:ins])
        rest = refs[ins:]
        if rider is not None:
            mine, other, rest = rest[0], rest[1], rest[2:]
        if after is not None:
            rest = rest[1:]
        inner += rest[:outs]
        rest = rest[outs:]
        if rider is not None:
            rest[0][...] = mine[...] + other[...]
            rest = rest[1:]
        kernel(*inner, *rest)

    args, in_specs, out_shapes = list(args), list(in_specs), list(out_shapes)
    if rider is not None:
        args += rider
        in_specs += [VMEM_SPEC] * 2
        out_shapes.append((rider[0].shape, rider[0].dtype))
    if after is not None:
        args.append(after)
        in_specs.append(pl.BlockSpec(memory_space=pl.ANY))
    return pl.pallas_call(
        body,
        name=name,
        out_shape=[jax.ShapeDtypeStruct(shape, kind) for shape, kind in out_shapes],
        in_specs=in_specs,
        out_specs=[VMEM_SPEC] * len(out_shapes),
        scratch_shapes=list(scratch),
        compiler_params=pltpu.CompilerParams(vmem_limit_bytes=limit * 2**20),
        cost_estimate=pl.CostEstimate(flops=work, bytes_accessed=1, transcendentals=0),
    )(*args)


def shifted(block, axis, distance):
    devices = range(lax.axis_size(axis))
    route = [(i - distance, i) for i in devices if i - distance in devices]
    return lax.ppermute(block, axis, route)


def swap_by(block, axis, mask):
    return lax.ppermute(block, axis, [(i, i ^ mask) for i in range(lax.axis_size(axis))])


def swap(block, axis, bit):
    return swap_by(block, axis, 1 << bit)


class Order:
    def __init__(self):
        self.last = None
        self.small = None
        self.come = None
        self.hops = []
        self.turn = 0

    def ride(self, small, hops):
        self.small, self.hops, self.turn = small, list(hops), 0
        self.send()

    def send(self):
        self.come = swap(self.small, *self.hops.pop(0)) if self.hops else None

    def call(self, *args, **kwargs):
        self.turn += 1
        rider = None if self.come is None or self.turn < 2 else [self.small, self.come]
        kwargs.setdefault("work", WORK.get(args[1], 1))
        outs = list(call(*args, **kwargs, after=self.last, rider=rider))
        if rider is not None:
            self.small = outs.pop()
            self.turn = 0
            self.send()
        self.last = min(outs, key=lambda out: out.size * out.dtype.itemsize)
        return outs


def spread_sum(order, name, sources, out_shapes):
    places, _, width = sources[0][0].shape
    sizes = tuple(stay.shape[1] for stay, _ in sources)
    rows = sum(sizes)
    levels = places.bit_length() - 1
    order_a = list(range(levels))
    order_b = order_a[::-1]
    half = rows // 2

    def shapes(count):
        return [((count, half, width), F32), ((count, half, width), BF16)] * 2

    stay_a, send_a, stay_b, send_b = order.call(
        functools.partial(core_sum_kernel, plan=(order_a[0], order_b[0])), name + "_core",
        shapes(places // 2), [VMEM_SPEC] * (2 * len(sources)), [part for pair in sources for part in pair],
        limit=1,
    )
    for level in range(levels):
        come_a = swap(send_a, "seq", order_a[level] + 1)
        come_b = swap(send_b, "seq", order_b[level] + 1)
        yield None
        if level + 1 == levels:
            break
        plan = []
        for bits in (order_a, order_b):
            bit = bits[level + 1]
            plan.append((bit, bit - sum(done < bit for done in bits[: level + 1])))
        stay_a, send_a, stay_b, send_b = order.call(
            functools.partial(split_sum_kernel, plan=tuple(plan)), name + "_seq",
            shapes(places // 4 >> level), [VMEM_SPEC] * 4,
            (stay_a, come_a, stay_b, come_b),
        )
    depth = lax.axis_size("dp").bit_length() - 1
    wide = width // 2
    stay, send = order.call(
        join_sum_kernel, name + "_join", [((rows, wide), F32), ((rows, wide), BF16)],
        [VMEM_SPEC] * 4, (stay_a, come_a, stay_b, come_b),
    )
    for bit in range(1, depth - 1):
        wide = wide // 2
        come = swap(send, "dp", bit - 1)
        yield None
        stay, send = order.call(
            functools.partial(column_sum_kernel, bit=bit), name + "_dp",
            [((rows, wide), F32), ((rows, wide), BF16)], [VMEM_SPEC] * 2,
            (stay, come),
        )
    come = swap(send, "dp", depth - 2)
    yield None
    (low,) = order.call(
        round_sum_kernel, name + "_last", [((rows, wide), BF16)], [VMEM_SPEC] * 2, (stay, come)
    )
    come = swap(low, "dp", depth - 1)
    yield None
    (total,) = order.call(
        round_sum_kernel, name + "_total", [((rows, wide), BF16)], [VMEM_SPEC] * 2, (low, come)
    )
    for bit in range(depth - 2, 0, -1):
        come = swap(total, "dp", bit)
        upper = bit_of("dp", bit) == 1
        total = jnp.concatenate(
            [jnp.where(upper, come, total), jnp.where(upper, total, come)], axis=1
        )
    come = swap(total, "dp", 0)
    yield None
    yield order.call(
        functools.partial(finish_kernel, sizes=sizes), name + "_finish", [(shape, F32) for shape in out_shapes],
        [VMEM_SPEC] * 2, (total, come),
    )


def on_device(
    inputs, doc_start, norm1_gain, conv_weight, gate_bias, w_in, w_out, norm2_gain, w_up, w_down, out_grad
):
    batch, span, width = inputs.shape
    hidden = w_out.shape[0]
    inner = w_up.shape[1]
    tokens = batch * span
    lanes = width // LANES
    seq_count, dp_count = lax.axis_size("seq"), lax.axis_size("dp")
    seq_depth, dp_depth = seq_count.bit_length() - 1, dp_count.bit_length() - 1
    pairs = seq_count // 2
    seq_at = lax.axis_index("seq").astype(jnp.int32)
    taps = jnp.transpose(conv_weight)
    gain1, gain2, bias = norm1_gain[None], norm2_gain[None], gate_bias[None]
    order = Order()

    xt, normed, edge, keep = order.call(
        functools.partial(ingest_kernel, steps=16), "ingest",
        [
            ((lanes, tokens, LANES), F32), ((tokens, width), BF16), ((EDGE * batch, width), BF16),
            ((tokens, LANES), F32),
        ],
        [pl.BlockSpec(memory_space=pltpu.HBM)] + [VMEM_SPEC] * 2, (inputs, doc_start, gain1),
        [pltpu.VMEM((batch, span, width), BF16), pltpu.SemaphoreType.DMA((batch,))],
        limit=LIMITS["ingest"],
    )
    halo = shifted(edge, "seq", 1)
    gt, gact = order.call(
        functools.partial(prepare_kernel, steps=64, block=512), "prepare",
        [((tokens, width), BF16), ((tokens, inner // 2), BF16)],
        [VMEM_SPEC] * 2, (out_grad, w_down), [pltpu.VMEM((lanes, tokens, LANES), F32)],
        limit=LIMITS["prepare"],
    )
    conv_out, gate, cand, totals = order.call(
        functools.partial(front_kernel, steps=64, block=512), "front",
        [
            ((tokens, width), BF16), ((tokens, hidden), F32), ((tokens, hidden), F32),
            ((2, batch, hidden), F32),
        ],
        [VMEM_SPEC] * 6, (normed, halo, keep, taps, bias, w_in),
        [pltpu.VMEM((tokens + EDGE * batch, width), F32)],
        limit=LIMITS["front"],
    )
    chips = seq_count // 2
    mate_totals = swap(totals, "seq", 0)
    (chip_totals,) = order.call(
        chip_totals_kernel, "chip_totals", [(totals.shape, F32)], [VMEM_SPEC] * 2, (totals, mate_totals)
    )
    all_totals = [swap_by(chip_totals, "seq", 2 * mask) for mask in range(1, chips)]
    (more,) = order.call(
        functools.partial(prepare_rest_kernel, size=512, block=512), "prepare_rest",
        [((tokens, inner // 2), BF16)], [VMEM_SPEC] * 2, (gt, w_down), limit=LIMITS["prepare_rest"],
    )
    prev, held, mid, nmid, act, gup = order.call(
        functools.partial(forward_kernel, chips=chips, steps=64, block=512), "forward",
        [
            ((tokens, hidden), F32), ((tokens, hidden), BF16), ((tokens, width), F32),
            ((tokens, width), BF16), ((tokens, inner), BF16), ((tokens, inner), BF16),
        ],
        [VMEM_SPEC] * (9 + chips),
        (mate_totals, *all_totals, xt, keep, gate, cand, gact, more, gain2, w_out, w_up),
        limit=LIMITS["forward"],
    )
    up_rows = inner // seq_count
    stay_up, send_up, stay_down, send_down = order.call(
        weights_kernel, "weights", [((pairs, up_rows, width), BF16)] * 4,
        [VMEM_SPEC] * 4, (nmid, gup, act, gt), limit=LIMITS["weights"],
    )
    come_up, come_down = swap(send_up, "seq", 0), swap(send_down, "seq", 0)
    gmid, gbranch, gheld, outgoing, gnorm2 = order.call(
        functools.partial(reverse_kernel, steps=64), "reverse",
        [
            ((tokens, width), F32), ((tokens, width), BF16), ((tokens, hidden), F32),
            ((batch, hidden), F32), ((1, width), F32),
        ],
        [VMEM_SPEC] * 8, (gup, mid, gt, gain2, keep, gate, w_out, w_up),
        limit=LIMITS["reverse"],
    )
    mate_outgoing = swap(outgoing, "seq", 0)
    out_rows = hidden // seq_count
    in_rows = 2 * hidden // seq_count
    stay_out, send_out = order.call(
        weights_out_kernel, "weights_out", [((pairs, out_rows, width), BF16)] * 2,
        [VMEM_SPEC] * 2, (held, gbranch), limit=LIMITS["weights"],
    )
    come_out = swap(send_out, "seq", 0)
    (chip_outgoing,) = order.call(
        chip_outgoing_kernel, "chip_outgoing", [(outgoing.shape, F32)], [VMEM_SPEC] * 4,
        (outgoing, mate_outgoing, totals, mate_totals),
    )
    all_outgoing = [swap_by(chip_outgoing, "seq", 2 * mask) for mask in range(1, chips)]
    first = spread_sum(
        order, "first", [(stay_up, come_up), (stay_down, come_down)],
        [(width // seq_count, inner), (up_rows, width)],
    )
    next(first)
    gproj, gbias, stay_in, send_in = order.call(
        functools.partial(back_kernel, chips=chips), "back",
        [((tokens, 2 * hidden), BF16), ((1, hidden), F32)] + [((pairs, in_rows, width), BF16)] * 2,
        [VMEM_SPEC] * (6 + 2 * chips),
        (
            *all_totals, *all_outgoing, mate_totals, mate_outgoing, keep, gate, cand, prev, gheld, conv_out,
        ),
        limit=LIMITS["back"],
    )
    come_in = swap(send_in, "seq", 0)
    (gconv,) = order.call(
        functools.partial(gconv_kernel, steps=64), "gconv", [((tokens, width), BF16)],
        [VMEM_SPEC] * 2, (gproj, w_in), limit=LIMITS["gconv"],
    )
    after = shifted(gconv[: EDGE * batch], "seq", -1)
    order.last = after
    second = spread_sum(
        order, "second", [(stay_in, come_in), (stay_out, come_out)],
        [(width // seq_count, 2 * hidden), (out_rows, width)],
    )
    next(first)
    next(second)
    bias_rows = hidden // width
    ginput, small = order.call(
        functools.partial(tail_kernel, steps=16), "tail",
        [((batch, span, width), F32), ((2 + KW + bias_rows, width), F32)],
        [VMEM_SPEC] * 10,
        (gconv, after, xt, normed, halo, gmid, gain1, taps, gnorm2, gbias),
        [
            pltpu.VMEM((tokens + EDGE * batch, width), F32),
            pltpu.VMEM((tokens + EDGE * batch, width), F32),
            pltpu.VMEM((lanes, tokens, LANES), F32),
        ],
        limit=LIMITS["tail"],
    )
    order.ride(
        small, [("seq", bit) for bit in range(seq_depth)] + [("dp", bit) for bit in range(dp_depth)]
    )
    next(first)
    next(second)
    (result,) = order.call(
        functools.partial(result_kernel, steps=64), "result", [((batch, span, width), BF16)],
        [VMEM_SPEC] * 3, (act, mid, w_down), [pltpu.VMEM((lanes, tokens, LANES), F32)],
        limit=LIMITS["result"],
    )
    next(first)
    next(second)
    next(first)
    next(second)
    done = {}
    while len(done) < 2:
        for part in (first, second):
            if part not in done:
                outs = next(part)
                if outs is not None:
                    done[part] = outs
    while order.come is not None:
        order.small = order.small + order.come
        order.send()
    small = order.small
    gw_up, gw_down = done[first]
    gw_in, gw_out = done[second]

    def own(values):
        size = values.shape[0] // seq_count
        return lax.dynamic_slice_in_dim(values, seq_at * size, size, 0)

    return (
        result, ginput, own(small[0]), own(jnp.transpose(small[2 : 2 + KW])),
        own(small[2 + KW :].reshape(-1)), gw_in, gw_out, own(small[1]), gw_up, gw_down,
    )


def solution(mesh):
    rows, flat = P("dp", "seq", None), P()
    in_specs = (rows, P("dp", "seq")) + (flat,) * 8 + (rows,)
    vec, mat = P("seq"), P("seq", None)
    out_specs = (rows, rows, vec, mat, vec, mat, mat, vec, mat, mat)
    return jax.shard_map(
        on_device, mesh=mesh, in_specs=in_specs, out_specs=out_specs, check_vma=False
    )
```

time: 244 us -> 135 us (0.55)
  blocking collectives: 62.6 us -> 0 us
  local copies, waits for them, and re-layouts: 36 us -> 9.55 us
  starting transfers between devices: 20.7 us -> 41.2 us
  waiting for transfers between devices: 48.6 us -> 30 us
  Pallas kernels: 65.7 us -> 51.4 us
  other arithmetic: 4.39 us -> 0 us
  matrix products: 4.14 us -> 0 us
    psum x1 -> x0, blocking collectives: 39.6 us -> none  [on_device(): lax.psum(jnp.concatenate([gnorm1[0], gnorm2[0], gbias[0], jnp.transpose(g...]
    unnamed x93 -> x32, local copies, waits for them, and re-layouts: 31.1 us -> 7.71 us
    all_gather x2 -> x0, blocking collectives: 23.1 us -> none  [the longest x1 14.5 us: on_device(): all_totals = lax.all_gather(totals[None], 'seq', axis=0, tiled=True)]
    ppermute x16 -> x31, starting transfers between devices: 17.1 us -> 37.6 us  [swap_by(): lax.ppermute(block, axis, [(i, i ^ mask) for i in range(lax.axis_size(axi...]
    ppermute x16 -> x31, waiting for transfers between devices: 46.4 us -> 29.5 us  [swap_by(): lax.ppermute(block, axis, [(i, i ^ mask) for i in range(lax.axis_size(axi...]
    pallas_call x15 -> x26, Pallas kernels: 65.7 us -> 51.4 us  [call(): pl.pallas_call(body, name=name, out_shape=[jax.ShapeDtypeStruct(shape, ki...]
    dot_general x1 -> x0, matrix products: 4.14 us -> none  [dot_nt(): lax.dot_general(left, right, (((1,), (1,)), ((), ())), preferred_element_...]
  transfers between devices with their start and end apart: 18 -> 33, of which waited for: 9 -> 14; matrix products, arithmetic and copies ran while one was open for 4% -> 0% of each run, Pallas kernels for 11% -> 22%
where the time goes in v1:
time: 135 us; the launch traced here: 133 us
  Pallas kernels  51.4 us (38%)
  starting transfers between devices  41.2 us (31%)
  waiting for transfers between devices  30 us (22%)
  local copies, waits for them, and re-layouts  9.55 us (7%)
    pallas_call x26, Pallas kernels, call(): pl.pallas_call(body, name=name, out_shape=[jax.ShapeDtypeStruct(shape, ki...  51.4 us
    ppermute x31, starting transfers between devices, swap_by(): lax.ppermute(block, axis, [(i, i ^ mask) for i in range(lax.axis_size(axi...  37.6 us
    ppermute x31, waiting for transfers between devices, swap_by(): lax.ppermute(block, axis, [(i, i ^ mask) for i in range(lax.axis_size(axi...  29.5 us
    unnamed x32, local copies, waits for them, and re-layouts  7.71 us
    ppermute x2, starting transfers between devices, shifted(): return lax.ppermute(block, axis, route)  3.65 us
  transfers between devices with their start and end apart: 33, of which 14 were waited for; matrix products, arithmetic and copies ran while one was open for 0% of the time, Pallas kernels for 22%

profile of v1, /device:TPU:0, one launch (start us, length us, event | category | flops | bytes accessed | tf_op | source)
XLA Modules:
  0.0 133.2 jit_solution(12396616304418940891)
XLA Ops:
  0.7 1.2 copy-done.7
  1.9 0.7 copy-done.10
  2.6 0.7 copy-done.13
  3.2 3.2 %ingest.1 = (f32[4,1024,128]{2,1,0:T(8,128)S(1)}, bf16[1024,512]{1,0:T(8,128)(2,1)S(1)}, bf16[64,512]{1,0:T(8,128)(2,1)S(1)}, f32[1024,128]{1,0:T(8,128)S(1)}) custom-call(bf16[8,128,512]{2,1,0:T(8,128)(2,1)S(1)} %copy-done.7, s32[8,128]{1,0:T(8,128)S(1)} %copy-done.13, f32[1,512]{1,0:T(1,128)S(1)} %bitcast.15), custom_call_target="tpu_custom_call" | custom-call | flops 1 | bytes 1 | tf_op jit(solution)/shard_map/ingest/pallas_call | solution.py:586
  6.5 2.4 %collective-permute-start = (bf16[64,512]{1,0:T(8,128)(2,1)S(1)}, bf16[64,512]{1,0:T(8,128)(2,1)S(1)}, u32[]{:S(2)}, u32[]{:S(2)}) collective-permute-start(bf16[64,512]{1,0:T(8,128)(2,1)S(1)} %get-tuple-element.75.refs_2_), channel_id=1, source_target_pairs={{0,1},{1,2},{2,3},{3,4},{4,5},{5,6},{6,7},{8,9},{9,10},{10,11},{11... | collective-permute-start | bytes 196616 | tf_op jit(solution)/shard_map/ppermute | solution.py:601
  8.8 1.6 %copy-done = bf16[2048,512]{1,0:T(8,128)(2,1)S(1)} copy-done((bf16[2048,512]{1,0:T(8,128)(2,1)S(1)}, bf16[2048,512]{1,0:T(8,128)(2,1)}, u32[]{:S(2)}) %copy-start) | copy-done | bytes 2097176
  10.4 1.2 copy-done.6
  11.7 2.1 %prepare.1 = (bf16[1024,512]{1,0:T(8,128)(2,1)S(1)}, bf16[1024,1024]{1,0:T(8,128)(2,1)S(1)}) custom-call(bf16[8,128,512]{2,1,0:T(8,128)(2,1)S(1)} %copy-done.6, bf16[2048,512]{1,0:T(8,128)(2,1)S(1)} %copy-done, bf16[64,512]{1,0:T(8,128)(2,1)S(1)} %get-tuple-element.75.refs_2_), custom_call_target="tpu_custom_call" | custom-call | flops 1 | bytes 1 | tf_op jit(solution)/shard_map/prepare/pallas_call | solution.py:586
  13.8 3.8 %front.1 = (bf16[1024,512]{1,0:T(8,128)(2,1)S(1)}, f32[1024,1024]{1,0:T(8,128)S(1)}, f32[1024,1024]{1,0:T(8,128)S(1)}, f32[2,8,1024]{2,1,0:T(8,128)S(1)}) custom-call(bf16[1024,512]{1,0:T(8,128)(2,1)S(1)} %get-tuple-element.74.refs_0_.refs_3_, bf16[64,512]{1,0:T(8,128)(2,1)S(1)} %collective-permute-done.refs_1_.refs_4_, ...), custom_call_target="tpu_custom_call" | custom-call | flops 1 | bytes 1 | tf_op jit(solution)/shard_map/front/pallas_call | solution.py:586
  17.6 2.7 %collective-permute-start.1 = (f32[2,8,1024]{2,1,0:T(8,128)S(1)}, f32[2,8,1024]{2,1,0:T(8,128)S(1)}, u32[]{:S(2)}, u32[]{:S(2)}) collective-permute-start(f32[2,8,1024]{2,1,0:T(8,128)S(1)} %get-tuple-element.78.refs_0_.refs_2_), channel_id=1, source_target_pairs={{0,1},{1,0},{2,3},{3,2},{4,5},{5,4},{6,7},{7,6},{8,9},{9,8},{10,11... | collective-permute-start | bytes 196616 | tf_op jit(solution)/shard_map/ppermute | solution.py:605
  20.3 0.9 collective-permute-done.1.refs_1_.refs_0_.refs_3_.refs_6_
  21.2 1.6 %collective-permute-start.2 = (f32[2,8,1024]{2,1,0:T(8,128)S(1)}, f32[2,8,1024]{2,1,0:T(8,128)S(1)}, u32[]{:S(2)}, u32[]{:S(2)}) collective-permute-start(f32[2,8,1024]{2,1,0:T(8,128)S(1)} %chip_totals.1.refs_2_), channel_id=1, source_target_pairs={{0,2},{1,3},{2,0},{3,1},{4,6},{5,7},{6,4},{7,5},{8,10},{9,11},{10,... | collective-permute-start | bytes 196616 | tf_op jit(solution)/shard_map/ppermute | solution.py:605
  23.1 1.7 %collective-permute-start.4 = (f32[2,8,1024]{2,1,0:T(8,128)S(1)}, f32[2,8,1024]{2,1,0:T(8,128)S(1)}, u32[]{:S(2)}, u32[]{:S(2)}) collective-permute-start(f32[2,8,1024]{2,1,0:T(8,128)S(1)} %chip_totals.1.refs_2_), channel_id=1, source_target_pairs={{0,6},{1,7},{2,4},{3,5},{4,2},{5,3},{6,0},{7,1},{8,14},{9,15},{10,... | collective-permute-start | bytes 196616 | tf_op jit(solution)/shard_map/ppermute | solution.py:605
  24.8 1.5 %prepare_rest.1.refs_9_.refs_13_ = bf16[1024,1024]{1,0:T(8,128)(2,1)S(1)} custom-call(bf16[1024,512]{1,0:T(8,128)(2,1)S(1)} %get-tuple-element.77.refs_6_.refs_0_.refs_3_.refs_2_, bf16[2048,512]{1,0:T(8,128)(2,1)S(1)} %copy-done.1, f32[2,8,1024]{2,1,0:T(8,128)S(1)} %chip_totals.1.refs_2_), custom_call_target="tpu_custom_call" | custom-call | flops 1 | bytes 1 | tf_op jit(solution)/shard_map/prepare_rest/pallas_call | solution.py:586
  26.3 2.2 %collective-permute-done.3.refs_2_.refs_1_ = f32[2,8,1024]{2,1,0:T(8,128)S(1)} collective-permute-done((f32[2,8,1024]{2,1,0:T(8,128)S(1)}, f32[2,8,1024]{2,1,0:T(8,128)S(1)}, u32[]{:S(2)}, u32[]{:S(2)}) %collective-permute-start.3) | collective-permute-done | bytes 65568 | tf_op jit(solution)/shard_map/ppermute | solution.py:605
  28.5 8.8 %forward.1 = (f32[1024,1024]{1,0:T(8,128)S(1)}, bf16[1024,1024]{1,0:T(8,128)(2,1)S(1)}, f32[1024,512]{1,0:T(8,128)S(1)}, bf16[1024,512]{1,0:T(8,128)(2,1)S(1)}, ...) custom-call(f32[2,8,1024]{2,1,0:T(8,128)S(1)} %collective-permute-done.1.refs_1_.refs_0_.refs_3_.refs_6_, ...), custom_call_target="tpu_custom_call" | custom-call | flops 1 | bytes 1 | tf_op jit(solution)/shard_map/forward/pallas_call | solution.py:586
  37.3 4.6 %weights.1 = (bf16[4,256,512]{2,1,0:T(8,128)(2,1)S(1)}, bf16[4,256,512]{2,1,0:T(8,128)(2,1)S(1)}, bf16[4,256,512]{2,1,0:T(8,128)(2,1)S(1)}, bf16[4,256,512]{2,1,0:T(8,128)(2,1)S(1)}) custom-call(bf16[1024,512]{1,0:T(8,128)(2,1)S(1)} %get-tuple-element.86.refs_0_.refs_4_, bf16[1024,2048]{1,0:T(8,128)(2,1)S(1)} %get-tuple-element.85.refs_1_.refs_0_, ...), custom_call_target="tpu_custom_call" | custom-call | flops 1 | bytes 1 | tf_op jit(solution)/shard_map/weights/pallas_call | solution.py:586
  42.0 0.5 collective-permute-start.9
  42.5 5.1 %reverse.1 = (f32[1024,512]{1,0:T(8,128)S(1)}, bf16[1024,512]{1,0:T(8,128)(2,1)S(1)}, f32[1024,1024]{1,0:T(8,128)S(1)}, f32[8,1024]{1,0:T(8,128)S(1)}, f32[1,512]{1,0:T(1,128)S(1)}) custom-call(bf16[1024,2048]{1,0:T(8,128)(2,1)S(1)} %get-tuple-element.85.refs_1_.refs_0_, f32[1024,512]{1,0:T(8,128)S(1)} %get-tuple-element.84.refs_1_, ...), custom_call_target="tpu_custom_call" | custom-call | flops 1 | bytes 1 | tf_op jit(solution)/shard_map/reverse/pallas_call | solution.py:586
  47.7 1.3 weights_out.1
  49.1 1.6 %collective-permute-start.6 = (f32[8,1024]{1,0:T(8,128)S(1)}, f32[8,1024]{1,0:T(8,128)S(1)}, u32[]{:S(2)}, u32[]{:S(2)}) collective-permute-start(f32[8,1024]{1,0:T(8,128)S(1)} %chip_outgoing.1.refs_4_), channel_id=1, source_target_pairs={{0,2},{1,3},{2,0},{3,1},{4,6},{5,7},{6,4},{7,5},{8,10},{9,11},{10,... | collective-permute-start | bytes 98312 | tf_op jit(solution)/shard_map/ppermute | solution.py:605
  50.7 0.5 collective-permute-start.7
  51.2 1.4 %collective-permute-start.8 = (f32[8,1024]{1,0:T(8,128)S(1)}, f32[8,1024]{1,0:T(8,128)S(1)}, u32[]{:S(2)}, u32[]{:S(2)}) collective-permute-start(f32[8,1024]{1,0:T(8,128)S(1)} %chip_outgoing.1.refs_4_), channel_id=1, source_target_pairs={{0,6},{1,7},{2,4},{3,5},{4,2},{5,3},{6,0},{7,1},{8,14},{9,15},{10,... | collective-permute-start | bytes 98312 | tf_op jit(solution)/shard_map/ppermute | solution.py:605
  52.6 0.9 first_core.1
  53.5 1.6 %collective-permute-start.13 = (bf16[2,256,512]{2,1,0:T(8,128)(2,1)S(1)}, bf16[2,256,512]{2,1,0:T(8,128)(2,1)S(1)}, u32[]{:S(2)}, u32[]{:S(2)}) collective-permute-start(bf16[2,256,512]{2,1,0:T(8,128)(2,1)S(1)} %get-tuple-element.99.refs_14_), channel_id=1, source_target_pairs={{0,2},{1,3},{2,0},{3,1},{4,6},{5,7},{6,4},{7,5},{8,10},{9,11},{10,... | collective-permute-start | bytes 1572872 | tf_op jit(solution)/shard_map/ppermute | solution.py:605
  55.1 0.5 collective-permute-start.14
  56.0 4.5 %back.1 = (bf16[1024,2048]{1,0:T(8,128)(2,1)S(1)}, f32[1,1024]{1,0:T(1,128)S(1)}, bf16[4,256,512]{2,1,0:T(8,128)(2,1)S(1)}, bf16[4,256,512]{2,1,0:T(8,128)(2,1)S(1)}) custom-call(f32[2,8,1024]{2,1,0:T(8,128)S(1)} %collective-permute-done.2.refs_1_.refs_0_, f32[2,8,1024]{2,1,0:T(8,128)S(1)} %collective-permute-done.3.refs_2_.refs_1_, ...), custom_call_target="tpu_custom_call" | custom-call | flops 10000000000 | bytes 1 | tf_op jit(solution)/shard_map/back/pallas_call | solution.py:586
  60.5 2.6 %gconv.1.refs_0_ = bf16[1024,512]{1,0:T(8,128)(2,1)S(1)} custom-call(bf16[1024,2048]{1,0:T(8,128)(2,1)S(1)} %get-tuple-element.106.refs_0_, bf16[512,2048]{1,0:T(8,128)(2,1)S(1)} %copy-done.2, f32[1,1024]{1,0:T(1,128)S(1)} %get-tuple-element.107.refs_2_.refs_9_), custom_call_target="tpu_custom_call" | custom-call | flops 1 | bytes 1 | tf_op jit(solution)/shard_map/gconv/pallas_call | solution.py:586
  63.1 1.3 collective-permute-start.15
  64.4 1.2 collective-permute-start.11
  65.7 0.6 collective-permute-done.15.refs_4_.refs_1_
  66.3 1.0 collective-permute-done.13.refs_1_
  67.3 1.0 collective-permute-done.14.refs_3_
  68.7 0.7 collective-permute-start.19
  69.4 1.4 %collective-permute-start.20 = (bf16[1,256,512]{2,1,0:T(8,128)(2,1)S(1)}, bf16[1,256,512]{2,1,0:T(8,128)(2,1)S(1)}, u32[]{:S(2)}, u32[]{:S(2)}) collective-permute-start(bf16[1,256,512]{2,1,0:T(8,128)(2,1)S(1)} %get-tuple-element.117), channel_id=1, source_target_pairs={{0,2},{1,3},{2,0},{3,1},{4,6},{5,7},{6,4},{7,5},{8,10},{9,11},{10,... | collective-permute-start | bytes 786440 | tf_op jit(solution)/shard_map/ppermute | solution.py:605
  70.7 0.7 second_core.1
  71.4 0.7 collective-permute-start.16
  72.1 1.4 %collective-permute-start.17 = (bf16[2,192,512]{2,1,0:T(8,128)(2,1)S(1)}, bf16[2,192,512]{2,1,0:T(8,128)(2,1)S(1)}, u32[]{:S(2)}, u32[]{:S(2)}) collective-permute-start(bf16[2,192,512]{2,1,0:T(8,128)(2,1)S(1)} %get-tuple-element.112), channel_id=1, source_target_pairs={{0,4},{1,5},{2,6},{3,7},{4,0},{5,1},{6,2},{7,3},{8,12},{9,13},{10,... | collective-permute-start | bytes 1179656 | tf_op jit(solution)/shard_map/ppermute | solution.py:605
  73.5 4.6 %tail.1 = (f32[8,128,512]{2,1,0:T(8,128)}, f32[8,512]{1,0:T(8,128)S(1)}) custom-call(bf16[1024,512]{1,0:T(8,128)(2,1)S(1)} %gconv.1.refs_0_, bf16[64,512]{1,0:T(8,128)(2,1)S(1)} %collective-permute-done.15.refs_4_.refs_1_, f32[4,1024,128]{2,1,0:T(8,128)S(1)} %get-tuple-element.79.refs_4_.refs_2_, bf16[1024,512]{1,0:T(8,128)(2,1)S(1)} %get-tuple-element.74.refs_0_.refs_3_, ...), custom_call_target="tpu_custom_call" | custom-call | flops 1 | bytes 1 | tf_op jit(solution)/shard_map/tail/pallas_call | solution.py:586
  78.8 1.7 %collective-permute-start.23 = (bf16[512,256]{1,0:T(8,128)(2,1)S(1)}, bf16[512,256]{1,0:T(8,128)(2,1)S(1)}, u32[]{:S(2)}, u32[]{:S(2)}) collective-permute-start(bf16[512,256]{1,0:T(8,128)(2,1)S(1)} %get-tuple-element.118.refs_6_), channel_id=1, source_target_pairs={{0,8},{8,0},{16,24},{24,16},{1,9},{9,1},{17,25},{25,17},{2,10},{10... | collective-permute-start | bytes 786440 | tf_op jit(solution)/shard_map/ppermute | solution.py:605
  80.5 1.2 collective-permute-done.18.refs_5_
  81.7 4.3 %collective-permute-done.16.refs_1_ = bf16[2,192,512]{2,1,0:T(8,128)(2,1)S(1)} collective-permute-done((bf16[2,192,512]{2,1,0:T(8,128)(2,1)S(1)}, bf16[2,192,512]{2,1,0:T(8,128)(2,1)S(1)}, u32[]{:S(2)}, u32[]{:S(2)}) %collective-permute-start.16) | collective-permute-done | bytes 393248 | tf_op jit(solution)/shard_map/ppermute | solution.py:605
  86.3 1.7 %collective-permute-start.21 = (bf16[1,192,512]{2,1,0:T(8,128)(2,1)S(1)}, bf16[1,192,512]{2,1,0:T(8,128)(2,1)S(1)}, u32[]{:S(2)}, u32[]{:S(2)}) collective-permute-start(bf16[1,192,512]{2,1,0:T(8,128)(2,1)S(1)} %get-tuple-element.119.refs_3_), channel_id=1, source_target_pairs={{0,4},{1,5},{2,6},{3,7},{4,0},{5,1},{6,2},{7,3},{8,12},{9,13},{10,... | collective-permute-start | bytes 589832 | tf_op jit(solution)/shard_map/ppermute | solution.py:605
  88.0 1.1 collective-permute-start.22
  89.1 1.0 collective-permute-start.24
  90.0 3.9 %result.1.refs_4_ = bf16[8,128,512]{2,1,0:T(8,128)(2,1)} custom-call(bf16[1024,2048]{1,0:T(8,128)(2,1)S(1)} %get-tuple-element.83.refs_2_.refs_0_, f32[1024,512]{1,0:T(8,128)S(1)} %get-tuple-element.84.refs_1_, bf16[2048,512]{1,0:T(8,128)(2,1)S(1)} %copy-done.1, bf16[1,192,512]{2,1,0:T(8,128)(2,1)S(1)} %get-tuple-element.119.refs_3_), custom_call_target="tpu_custom_call" | custom-call | flops 1 | bytes 1 | tf_op jit(solution)/shard_map/result/pallas_call | solution.py:586
  94.0 0.6 collective-permute-done.24.refs_3_
  94.6 1.2 copy-done.4
  96.0 2.7 %collective-permute-start.26 = (bf16[512,256]{1,0:T(8,128)(2,1)S(1)}, bf16[512,256]{1,0:T(8,128)(2,1)S(1)}, u32[]{:S(2)}, u32[]{:S(2)}) collective-permute-start(bf16[512,256]{1,0:T(8,128)(2,1)S(1)} %get-tuple-element.126.refs_4_.refs_0_), channel_id=1, source_target_pairs={{0,16},{8,24},{16,0},{24,8},{1,17},{9,25},{17,1},{25,9},{2,18},{10... | collective-permute-start | bytes 786440 | tf_op jit(solution)/shard_map/ppermute | solution.py:605
  98.9 1.6 %collective-permute-start.25 = (bf16[384,256]{1,0:T(8,128)(2,1)S(1)}, bf16[384,256]{1,0:T(8,128)(2,1)S(1)}, u32[]{:S(2)}, u32[]{:S(2)}) collective-permute-start(bf16[384,256]{1,0:T(8,128)(2,1)S(1)} %get-tuple-element.128.refs_4_), channel_id=1, source_target_pairs={{0,8},{8,0},{16,24},{24,16},{1,9},{9,1},{17,25},{25,17},{2,10},{10... | collective-permute-start | bytes 589832 | tf_op jit(solution)/shard_map/ppermute | solution.py:605
  100.9 3.3 %collective-permute-done.27.refs_3_ = f32[8,512]{1,0:T(8,128)S(1)} collective-permute-done((f32[8,512]{1,0:T(8,128)S(1)}, f32[8,512]{1,0:T(8,128)S(1)}, u32[]{:S(2)}, u32[]{:S(2)}) %collective-permute-start.27) | collective-permute-done | bytes 16416 | tf_op jit(solution)/shard_map/ppermute | solution.py:605
  104.3 5.0 %collective-permute-done.26.refs_1_ = bf16[512,256]{1,0:T(8,128)(2,1)S(1)} collective-permute-done((bf16[512,256]{1,0:T(8,128)(2,1)S(1)}, bf16[512,256]{1,0:T(8,128)(2,1)S(1)}, u32[]{:S(2)}, u32[]{:S(2)}) %collective-permute-start.26) | collective-permute-done | bytes 262176 | tf_op jit(solution)/shard_map/ppermute | solution.py:605
  109.5 0.8 collective-permute-start.29
  110.4 3.4 %collective-permute-start.28 = (bf16[384,256]{1,0:T(8,128)(2,1)S(1)}, bf16[384,256]{1,0:T(8,128)(2,1)S(1)}, u32[]{:S(2)}, u32[]{:S(2)}) collective-permute-start(bf16[384,256]{1,0:T(8,128)(2,1)S(1)} %second_last.1.refs_4_.refs_0_), channel_id=1, source_target_pairs={{0,16},{8,24},{16,0},{24,8},{1,17},{9,25},{17,1},{25,9},{2,18},{10... | collective-permute-start | bytes 589832 | tf_op jit(solution)/shard_map/ppermute | solution.py:605
  113.8 7.4 %collective-permute-done.30.refs_3_ = f32[8,512]{1,0:T(8,128)S(1)} collective-permute-done((f32[8,512]{1,0:T(8,128)S(1)}, f32[8,512]{1,0:T(8,128)S(1)}, u32[]{:S(2)}, u32[]{:S(2)}) %collective-permute-start.30) | collective-permute-done | bytes 16416 | tf_op jit(solution)/shard_map/ppermute | solution.py:605
  121.3 1.0 first_finish.1
  122.3 1.0 copy-done.8
  123.5 2.2 %collective-permute-start.31 = (bf16[384,256]{1,0:T(8,128)(2,1)S(1)}, bf16[384,256]{1,0:T(8,128)(2,1)S(1)}, u32[]{:S(2)}, u32[]{:S(2)}) collective-permute-start(bf16[384,256]{1,0:T(8,128)(2,1)S(1)} %second_total.1.refs_0_.refs_4_), channel_id=1, source_target_pairs={{0,8},{8,0},{16,24},{24,16},{1,9},{9,1},{17,25},{25,17},{2,10},{10... | collective-permute-start | bytes 589832 | tf_op jit(solution)/shard_map/ppermute | solution.py:605
  125.7 3.0 %collective-permute-start.32 = (f32[8,512]{1,0:T(8,128)S(1)}, f32[8,512]{1,0:T(8,128)S(1)}, u32[]{:S(2)}, u32[]{:S(2)}) collective-permute-start(f32[8,512]{1,0:T(8,128)S(1)} %get-tuple-element.133.refs_2_), channel_id=1, source_target_pairs={{0,16},{8,24},{16,0},{24,8},{1,17},{9,25},{17,1},{25,9},{2,18},{10... | collective-permute-start | bytes 49160 | tf_op jit(solution)/shard_map/ppermute | solution.py:605
  128.7 1.8 %collective-permute-done.32.refs_3_ = f32[8,512]{1,0:T(8,128)S(1)} collective-permute-done((f32[8,512]{1,0:T(8,128)S(1)}, f32[8,512]{1,0:T(8,128)S(1)}, u32[]{:S(2)}, u32[]{:S(2)}) %collective-permute-start.32) | collective-permute-done | bytes 16416 | tf_op jit(solution)/shard_map/ppermute | solution.py:605
  130.5 0.9 second_finish.1
  131.4 0.7 dynamic-slice_bitcast_fusion
  132.1 0.6 dynamic_slice.19
  132.7 0.6 fusion
  (66 shorter events, 3.7 us)
Async XLA Ops:
  0.6 1.2 copy-start.7
  1.9 0.7 copy-start.10
  2.6 0.7 copy-start.13
  3.2 10.5 %copy-start.9 = (f32[512,4]{0,1:T(4,128)S(1)}, f32[512,4]{0,1:T(4,128)}, u32[]{:S(2)}) copy-start(f32[512,4]{0,1:T(4,128)} %param.14) | copy-start | bytes 24580
  3.2 10.5 %copy-start.14 = (f32[1024]{0:T(1024)S(1)}, f32[1024]{0:T(1024)}, u32[]{:S(2)}) copy-start(f32[1024]{0:T(1024)} %param.15) | copy-start | bytes 12292
  6.5 7.3 %collective-permute-start = (bf16[64,512]{1,0:T(8,128)(2,1)S(1)}, bf16[64,512]{1,0:T(8,128)(2,1)S(1)}, u32[]{:S(2)}, u32[]{:S(2)}) collective-permute-start(bf16[64,512]{1,0:T(8,128)(2,1)S(1)} %get-tuple-element.75.refs_2_), channel_id=1, source_target_pairs={{0,1},{1,2},{2,3},{3,4},{4,5},{5,6},{6,7},{8,9},{9,10},{10,11},{11... | collective-permute-start | bytes 196616 | tf_op jit(solution)/shard_map/ppermute | solution.py:601
  8.8 1.6 %copy-start = (bf16[2048,512]{1,0:T(8,128)(2,1)S(1)}, bf16[2048,512]{1,0:T(8,128)(2,1)}, u32[]{:S(2)}) copy-start(bf16[2048,512]{1,0:T(8,128)(2,1)} %refs_2_.1) | copy-start | bytes 6291460
  10.4 1.2 copy-start.6
  11.7 2.1 %copy-start.2 = (bf16[512,2048]{1,0:T(8,128)(2,1)S(1)}, bf16[512,2048]{1,0:T(8,128)(2,1)}, u32[]{:S(2)}) copy-start(bf16[512,2048]{1,0:T(8,128)(2,1)} %refs_1_.7) | copy-start | bytes 6291460
  13.8 11.0 %copy-start.1 = (bf16[2048,512]{1,0:T(8,128)(2,1)S(1)}, bf16[2048,512]{1,0:T(8,128)(2,1)}, u32[]{:S(2)}) copy-start(bf16[2048,512]{1,0:T(8,128)(2,1)} %refs_2_.1) | copy-start | bytes 6291460
  17.6 3.6 %collective-permute-start.1 = (f32[2,8,1024]{2,1,0:T(8,128)S(1)}, f32[2,8,1024]{2,1,0:T(8,128)S(1)}, u32[]{:S(2)}, u32[]{:S(2)}) collective-permute-start(f32[2,8,1024]{2,1,0:T(8,128)S(1)} %get-tuple-element.78.refs_0_.refs_2_), channel_id=1, source_target_pairs={{0,1},{1,0},{2,3},{3,2},{4,5},{5,4},{6,7},{7,6},{8,9},{9,8},{10,11... | collective-permute-start | bytes 196616 | tf_op jit(solution)/shard_map/ppermute | solution.py:605
  21.2 7.3 %copy-start.3 = (bf16[512,2048]{1,0:T(8,128)(2,1)S(1)}, bf16[512,2048]{1,0:T(8,128)(2,1)}, u32[]{:S(2)}) copy-start(bf16[512,2048]{1,0:T(8,128)(2,1)} %refs_7_.1) | copy-start | bytes 6291460
  21.2 7.3 %copy-start.5 = (bf16[1024,512]{1,0:T(8,128)(2,1)S(1)}, bf16[1024,512]{1,0:T(8,128)(2,1)}, u32[]{:S(2)}) copy-start(bf16[1024,512]{1,0:T(8,128)(2,1)} %refs_6_.1) | copy-start | bytes 3145732
  21.2 7.3 %copy-start.12 = (f32[512]{0:T(512)S(1)}, f32[512]{0:T(512)}, u32[]{:S(2)}) copy-start(f32[512]{0:T(512)} %param.18) | copy-start | bytes 6148
  21.2 5.0 %collective-permute-start.2 = (f32[2,8,1024]{2,1,0:T(8,128)S(1)}, f32[2,8,1024]{2,1,0:T(8,128)S(1)}, u32[]{:S(2)}, u32[]{:S(2)}) collective-permute-start(f32[2,8,1024]{2,1,0:T(8,128)S(1)} %chip_totals.1.refs_2_), channel_id=1, source_target_pairs={{0,2},{1,3},{2,0},{3,1},{4,6},{5,7},{6,4},{7,5},{8,10},{9,11},{10,... | collective-permute-start | bytes 196616 | tf_op jit(solution)/shard_map/ppermute | solution.py:605
  22.8 5.7 %collective-permute-start.3 = (f32[2,8,1024]{2,1,0:T(8,128)S(1)}, f32[2,8,1024]{2,1,0:T(8,128)S(1)}, u32[]{:S(2)}, u32[]{:S(2)}) collective-permute-start(f32[2,8,1024]{2,1,0:T(8,128)S(1)} %chip_totals.1.refs_2_), channel_id=1, source_target_pairs={{0,4},{1,5},{2,6},{3,7},{4,0},{5,1},{6,2},{7,3},{8,12},{9,13},{10,... | collective-permute-start | bytes 196616 | tf_op jit(solution)/shard_map/ppermute | solution.py:605
  23.1 5.4 %collective-permute-start.4 = (f32[2,8,1024]{2,1,0:T(8,128)S(1)}, f32[2,8,1024]{2,1,0:T(8,128)S(1)}, u32[]{:S(2)}, u32[]{:S(2)}) collective-permute-start(f32[2,8,1024]{2,1,0:T(8,128)S(1)} %chip_totals.1.refs_2_), channel_id=1, source_target_pairs={{0,6},{1,7},{2,4},{3,5},{4,2},{5,3},{6,0},{7,1},{8,14},{9,15},{10,... | collective-permute-start | bytes 196616 | tf_op jit(solution)/shard_map/ppermute | solution.py:605
  41.9 10.7 %collective-permute-start.10 = (bf16[4,256,512]{2,1,0:T(8,128)(2,1)S(1)}, bf16[4,256,512]{2,1,0:T(8,128)(2,1)S(1)}, u32[]{:S(2)}, u32[]{:S(2)}) collective-permute-start(bf16[4,256,512]{2,1,0:T(8,128)(2,1)S(1)} %get-tuple-element.98), channel_id=1, source_target_pairs={{0,1},{1,0},{2,3},{3,2},{4,5},{5,4},{6,7},{7,6},{8,9},{9,8},{10,11... | collective-permute-start | bytes 3145736 | tf_op jit(solution)/shard_map/ppermute | solution.py:605
  42.0 10.7 %collective-permute-start.9 = (bf16[4,256,512]{2,1,0:T(8,128)(2,1)S(1)}, bf16[4,256,512]{2,1,0:T(8,128)(2,1)S(1)}, u32[]{:S(2)}, u32[]{:S(2)}) collective-permute-start(bf16[4,256,512]{2,1,0:T(8,128)(2,1)S(1)} %get-tuple-element.96), channel_id=1, source_target_pairs={{0,1},{1,0},{2,3},{3,2},{4,5},{5,4},{6,7},{7,6},{8,9},{9,8},{10,11... | collective-permute-start | bytes 3145736 | tf_op jit(solution)/shard_map/ppermute | solution.py:605
  47.6 1.5 %collective-permute-start.5 = (f32[8,1024]{1,0:T(8,128)S(1)}, f32[8,1024]{1,0:T(8,128)S(1)}, u32[]{:S(2)}, u32[]{:S(2)}) collective-permute-start(f32[8,1024]{1,0:T(8,128)S(1)} %get-tuple-element.88.refs_0_), channel_id=1, source_target_pairs={{0,1},{1,0},{2,3},{3,2},{4,5},{5,4},{6,7},{7,6},{8,9},{9,8},{10,11... | collective-permute-start | bytes 98312 | tf_op jit(solution)/shard_map/ppermute | solution.py:605
  49.1 6.6 %collective-permute-start.6 = (f32[8,1024]{1,0:T(8,128)S(1)}, f32[8,1024]{1,0:T(8,128)S(1)}, u32[]{:S(2)}, u32[]{:S(2)}) collective-permute-start(f32[8,1024]{1,0:T(8,128)S(1)} %chip_outgoing.1.refs_4_), channel_id=1, source_target_pairs={{0,2},{1,3},{2,0},{3,1},{4,6},{5,7},{6,4},{7,5},{8,10},{9,11},{10,... | collective-permute-start | bytes 98312 | tf_op jit(solution)/shard_map/ppermute | solution.py:605
  50.7 5.0 %collective-permute-start.7 = (f32[8,1024]{1,0:T(8,128)S(1)}, f32[8,1024]{1,0:T(8,128)S(1)}, u32[]{:S(2)}, u32[]{:S(2)}) collective-permute-start(f32[8,1024]{1,0:T(8,128)S(1)} %chip_outgoing.1.refs_4_), channel_id=1, source_target_pairs={{0,4},{1,5},{2,6},{3,7},{4,0},{5,1},{6,2},{7,3},{8,12},{9,13},{10,... | collective-permute-start | bytes 98312 | tf_op jit(solution)/shard_map/ppermute | solution.py:605
  51.2 4.8 %collective-permute-start.8 = (f32[8,1024]{1,0:T(8,128)S(1)}, f32[8,1024]{1,0:T(8,128)S(1)}, u32[]{:S(2)}, u32[]{:S(2)}) collective-permute-start(f32[8,1024]{1,0:T(8,128)S(1)} %chip_outgoing.1.refs_4_), channel_id=1, source_target_pairs={{0,6},{1,7},{2,4},{3,5},{4,2},{5,3},{6,0},{7,1},{8,14},{9,15},{10,... | collective-permute-start | bytes 98312 | tf_op jit(solution)/shard_map/ppermute | solution.py:605
  53.5 13.8 %collective-permute-start.13 = (bf16[2,256,512]{2,1,0:T(8,128)(2,1)S(1)}, bf16[2,256,512]{2,1,0:T(8,128)(2,1)S(1)}, u32[]{:S(2)}, u32[]{:S(2)}) collective-permute-start(bf16[2,256,512]{2,1,0:T(8,128)(2,1)S(1)} %get-tuple-element.99.refs_14_), channel_id=1, source_target_pairs={{0,2},{1,3},{2,0},{3,1},{4,6},{5,7},{6,4},{7,5},{8,10},{9,11},{10,... | collective-permute-start | bytes 1572872 | tf_op jit(solution)/shard_map/ppermute | solution.py:605
  55.1 13.1 %collective-permute-start.14 = (bf16[2,256,512]{2,1,0:T(8,128)(2,1)S(1)}, bf16[2,256,512]{2,1,0:T(8,128)(2,1)S(1)}, u32[]{:S(2)}, u32[]{:S(2)}) collective-permute-start(bf16[2,256,512]{2,1,0:T(8,128)(2,1)S(1)} %get-tuple-element.105), channel_id=1, source_target_pairs={{0,4},{1,5},{2,6},{3,7},{4,0},{5,1},{6,2},{7,3},{8,12},{9,13},{10,... | collective-permute-start | bytes 1572872 | tf_op jit(solution)/shard_map/ppermute | solution.py:605
  63.1 3.1 %collective-permute-start.15 = (bf16[64,512]{1,0:T(8,128)(2,1)S(1)}, bf16[64,512]{1,0:T(8,128)(2,1)S(1)}, u32[]{:S(2)}, u32[]{:S(2)}) collective-permute-start(bf16[64,512]{1,0:T(8,128)(2,1)S(1)} %slice.20), channel_id=1, source_target_pairs={{1,0},{2,1},{3,2},{4,3},{5,4},{6,5},{7,6},{9,8},{10,9},{11,10},{12... | collective-permute-start | bytes 196616 | tf_op jit(solution)/shard_map/ppermute | solution.py:601
  64.4 6.3 %collective-permute-start.11 = (bf16[4,256,512]{2,1,0:T(8,128)(2,1)S(1)}, bf16[4,256,512]{2,1,0:T(8,128)(2,1)S(1)}, u32[]{:S(2)}, u32[]{:S(2)}) collective-permute-start(bf16[4,256,512]{2,1,0:T(8,128)(2,1)S(1)} %get-tuple-element.101), channel_id=1, source_target_pairs={{0,1},{1,0},{2,3},{3,2},{4,5},{5,4},{6,7},{7,6},{8,9},{9,8},{10,11... | collective-permute-start | bytes 3145736 | tf_op jit(solution)/shard_map/ppermute | solution.py:605
  65.6 5.1 %collective-permute-start.12 = (bf16[4,128,512]{2,1,0:T(8,128)(2,1)S(1)}, bf16[4,128,512]{2,1,0:T(8,128)(2,1)S(1)}, u32[]{:S(2)}, u32[]{:S(2)}) collective-permute-start(bf16[4,128,512]{2,1,0:T(8,128)(2,1)S(1)} %get-tuple-element.102), channel_id=1, source_target_pairs={{0,1},{1,0},{2,3},{3,2},{4,5},{5,4},{6,7},{7,6},{8,9},{9,8},{10,11... | collective-permute-start | bytes 1572872 | tf_op jit(solution)/shard_map/ppermute | solution.py:605
  68.7 4.9 %copy-start.11 = (f32[512]{0:T(512)S(1)}, f32[512]{0:T(512)}, u32[]{:S(2)}) copy-start(f32[512]{0:T(512)} %param.13) | copy-start | bytes 6148
  68.7 9.5 %collective-permute-start.19 = (bf16[1,256,512]{2,1,0:T(8,128)(2,1)S(1)}, bf16[1,256,512]{2,1,0:T(8,128)(2,1)S(1)}, u32[]{:S(2)}, u32[]{:S(2)}) collective-permute-start(bf16[1,256,512]{2,1,0:T(8,128)(2,1)S(1)} %get-tuple-element.108.refs_4_), channel_id=1, source_target_pairs={{0,4},{1,5},{2,6},{3,7},{4,0},{5,1},{6,2},{7,3},{8,12},{9,13},{10,... | collective-permute-start | bytes 786440 | tf_op jit(solution)/shard_map/ppermute | solution.py:605
  69.4 9.2 %collective-permute-start.20 = (bf16[1,256,512]{2,1,0:T(8,128)(2,1)S(1)}, bf16[1,256,512]{2,1,0:T(8,128)(2,1)S(1)}, u32[]{:S(2)}, u32[]{:S(2)}) collective-permute-start(bf16[1,256,512]{2,1,0:T(8,128)(2,1)S(1)} %get-tuple-element.117), channel_id=1, source_target_pairs={{0,2},{1,3},{2,0},{3,1},{4,6},{5,7},{6,4},{7,5},{8,10},{9,11},{10,... | collective-permute-start | bytes 786440 | tf_op jit(solution)/shard_map/ppermute | solution.py:605
  71.4 14.6 %collective-permute-start.16 = (bf16[2,192,512]{2,1,0:T(8,128)(2,1)S(1)}, bf16[2,192,512]{2,1,0:T(8,128)(2,1)S(1)}, u32[]{:S(2)}, u32[]{:S(2)}) collective-permute-start(bf16[2,192,512]{2,1,0:T(8,128)(2,1)S(1)} %get-tuple-element.110.refs_10_), channel_id=1, source_target_pairs={{0,2},{1,3},{2,0},{3,1},{4,6},{5,7},{6,4},{7,5},{8,10},{9,11},{10,... | collective-permute-start | bytes 1179656 | tf_op jit(solution)/shard_map/ppermute | solution.py:605
  72.1 13.9 %collective-permute-start.17 = (bf16[2,192,512]{2,1,0:T(8,128)(2,1)S(1)}, bf16[2,192,512]{2,1,0:T(8,128)(2,1)S(1)}, u32[]{:S(2)}, u32[]{:S(2)}) collective-permute-start(bf16[2,192,512]{2,1,0:T(8,128)(2,1)S(1)} %get-tuple-element.112), channel_id=1, source_target_pairs={{0,4},{1,5},{2,6},{3,7},{4,0},{5,1},{6,2},{7,3},{8,12},{9,13},{10,... | collective-permute-start | bytes 1179656 | tf_op jit(solution)/shard_map/ppermute | solution.py:605
  78.8 15.1 %collective-permute-start.23 = (bf16[512,256]{1,0:T(8,128)(2,1)S(1)}, bf16[512,256]{1,0:T(8,128)(2,1)S(1)}, u32[]{:S(2)}, u32[]{:S(2)}) collective-permute-start(bf16[512,256]{1,0:T(8,128)(2,1)S(1)} %get-tuple-element.118.refs_6_), channel_id=1, source_target_pairs={{0,8},{8,0},{16,24},{24,16},{1,9},{9,1},{17,25},{25,17},{2,10},{10... | collective-permute-start | bytes 786440 | tf_op jit(solution)/shard_map/ppermute | solution.py:605
  80.5 1.2 collective-permute-start.18
  86.3 12.4 %collective-permute-start.21 = (bf16[1,192,512]{2,1,0:T(8,128)(2,1)S(1)}, bf16[1,192,512]{2,1,0:T(8,128)(2,1)S(1)}, u32[]{:S(2)}, u32[]{:S(2)}) collective-permute-start(bf16[1,192,512]{2,1,0:T(8,128)(2,1)S(1)} %get-tuple-element.119.refs_3_), channel_id=1, source_target_pairs={{0,4},{1,5},{2,6},{3,7},{4,0},{5,1},{6,2},{7,3},{8,12},{9,13},{10,... | collective-permute-start | bytes 589832 | tf_op jit(solution)/shard_map/ppermute | solution.py:605
  88.0 10.6 %collective-permute-start.22 = (bf16[1,192,512]{2,1,0:T(8,128)(2,1)S(1)}, bf16[1,192,512]{2,1,0:T(8,128)(2,1)S(1)}, u32[]{:S(2)}, u32[]{:S(2)}) collective-permute-start(bf16[1,192,512]{2,1,0:T(8,128)(2,1)S(1)} %get-tuple-element.123), channel_id=1, source_target_pairs={{0,2},{1,3},{2,0},{3,1},{4,6},{5,7},{6,4},{7,5},{8,10},{9,11},{10,... | collective-permute-start | bytes 589832 | tf_op jit(solution)/shard_map/ppermute | solution.py:605
  89.1 5.5 %collective-permute-start.24 = (f32[8,512]{1,0:T(8,128)S(1)}, f32[8,512]{1,0:T(8,128)S(1)}, u32[]{:S(2)}, u32[]{:S(2)}) collective-permute-start(f32[8,512]{1,0:T(8,128)S(1)} %get-tuple-element.125.refs_2_), channel_id=1, source_target_pairs={{0,2},{1,3},{2,0},{3,1},{4,6},{5,7},{6,4},{7,5},{8,10},{9,11},{10,... | collective-permute-start | bytes 49160 | tf_op jit(solution)/shard_map/ppermute | solution.py:605
  94.6 1.2 copy-start.4
  96.0 13.3 %collective-permute-start.26 = (bf16[512,256]{1,0:T(8,128)(2,1)S(1)}, bf16[512,256]{1,0:T(8,128)(2,1)S(1)}, u32[]{:S(2)}, u32[]{:S(2)}) collective-permute-start(bf16[512,256]{1,0:T(8,128)(2,1)S(1)} %get-tuple-element.126.refs_4_.refs_0_), channel_id=1, source_target_pairs={{0,16},{8,24},{16,0},{24,8},{1,17},{9,25},{17,1},{25,9},{2,18},{10... | collective-permute-start | bytes 786440 | tf_op jit(solution)/shard_map/ppermute | solution.py:605
  98.9 11.3 %collective-permute-start.25 = (bf16[384,256]{1,0:T(8,128)(2,1)S(1)}, bf16[384,256]{1,0:T(8,128)(2,1)S(1)}, u32[]{:S(2)}, u32[]{:S(2)}) collective-permute-start(bf16[384,256]{1,0:T(8,128)(2,1)S(1)} %get-tuple-element.128.refs_4_), channel_id=1, source_target_pairs={{0,8},{8,0},{16,24},{24,16},{1,9},{9,1},{17,25},{25,17},{2,10},{10... | collective-permute-start | bytes 589832 | tf_op jit(solution)/shard_map/ppermute | solution.py:605
  100.5 3.7 %collective-permute-start.27 = (f32[8,512]{1,0:T(8,128)S(1)}, f32[8,512]{1,0:T(8,128)S(1)}, u32[]{:S(2)}, u32[]{:S(2)}) collective-permute-start(f32[8,512]{1,0:T(8,128)S(1)} %get-tuple-element.129.refs_2_), channel_id=1, source_target_pairs={{0,4},{1,5},{2,6},{3,7},{4,0},{5,1},{6,2},{7,3},{8,12},{9,13},{10,... | collective-permute-start | bytes 49160 | tf_op jit(solution)/shard_map/ppermute | solution.py:605
  109.5 11.8 %collective-permute-start.29 = (bf16[512,256]{1,0:T(8,128)(2,1)S(1)}, bf16[512,256]{1,0:T(8,128)(2,1)S(1)}, u32[]{:S(2)}, u32[]{:S(2)}) collective-permute-start(bf16[512,256]{1,0:T(8,128)(2,1)S(1)} %get-tuple-element.130.refs_2_.refs_0_), channel_id=1, source_target_pairs={{0,8},{8,0},{16,24},{24,16},{1,9},{9,1},{17,25},{25,17},{2,10},{10... | collective-permute-start | bytes 786440 | tf_op jit(solution)/shard_map/ppermute | solution.py:605
  110.4 11.9 %collective-permute-start.28 = (bf16[384,256]{1,0:T(8,128)(2,1)S(1)}, bf16[384,256]{1,0:T(8,128)(2,1)S(1)}, u32[]{:S(2)}, u32[]{:S(2)}) collective-permute-start(bf16[384,256]{1,0:T(8,128)(2,1)S(1)} %second_last.1.refs_4_.refs_0_), channel_id=1, source_target_pairs={{0,16},{8,24},{16,0},{24,8},{1,17},{9,25},{17,1},{25,9},{2,18},{10... | collective-permute-start | bytes 589832 | tf_op jit(solution)/shard_map/ppermute | solution.py:605
  113.8 7.4 %collective-permute-start.30 = (f32[8,512]{1,0:T(8,128)S(1)}, f32[8,512]{1,0:T(8,128)S(1)}, u32[]{:S(2)}, u32[]{:S(2)}) collective-permute-start(f32[8,512]{1,0:T(8,128)S(1)} %get-tuple-element.131.refs_2_), channel_id=1, source_target_pairs={{0,8},{8,0},{16,24},{24,16},{1,9},{9,1},{17,25},{25,17},{2,10},{10... | collective-permute-start | bytes 49160 | tf_op jit(solution)/shard_map/ppermute | solution.py:605
  122.3 1.0 copy-start.8
  123.5 7.0 %collective-permute-start.31 = (bf16[384,256]{1,0:T(8,128)(2,1)S(1)}, bf16[384,256]{1,0:T(8,128)(2,1)S(1)}, u32[]{:S(2)}, u32[]{:S(2)}) collective-permute-start(bf16[384,256]{1,0:T(8,128)(2,1)S(1)} %second_total.1.refs_0_.refs_4_), channel_id=1, source_target_pairs={{0,8},{8,0},{16,24},{24,16},{1,9},{9,1},{17,25},{25,17},{2,10},{10... | collective-permute-start | bytes 589832 | tf_op jit(solution)/shard_map/ppermute | solution.py:605
  125.7 4.7 %collective-permute-start.32 = (f32[8,512]{1,0:T(8,128)S(1)}, f32[8,512]{1,0:T(8,128)S(1)}, u32[]{:S(2)}, u32[]{:S(2)}) collective-permute-start(f32[8,512]{1,0:T(8,128)S(1)} %get-tuple-element.133.refs_2_), channel_id=1, source_target_pairs={{0,16},{8,24},{16,0},{24,8},{1,17},{9,25},{17,1},{25,9},{2,18},{10... | collective-permute-start | bytes 49160 | tf_op jit(solution)/shard_map/ppermute | solution.py:605

commit v2 on v1

--- a/solution.py
+++ b/solution.py
@@ -10,9 +10,11 @@
 KW = 4
 EPS = 1e-05
 EDGE = 8
+SMALL = 16
 LANES = 128
-WORK = {"first_seq": 10**10, "back": 10**10}
-LIMITS = {"ingest": 2, "prepare": 3, "prepare_rest": 1, "front": 4, "forward": 3, "weights": 3, "reverse": 2, "back": 3, "gconv": 1, "tail": 10, "result": 4}
+FINAL = ("result", "inputs", "first_finish", "second_finish")
+WORK = dict.fromkeys(("ingest", "prepare", "front", "forward", "first_seq", "back", "chip_outgoing"), 10**10)
+LIMITS = {"ingest": 2, "prepare": 3, "prepare_rest": 1, "front": 4, "forward": 3, "weights": 3, "reverse": 2, "back": 3, "gconv": 1, "taps": 5, "inputs": 5, "result": 4}
 F32 = jnp.float32
 BF16 = jnp.bfloat16
 GELU_C = 0.7978845608028654
@@ -65,13 +67,16 @@
         buf[lane, rows, :] = values[:, lane * LANES : (lane + 1) * LANES]
 
 
-def ingest_kernel(x_ref, start_ref, gain_ref, xt_ref, normed_ref, edge_ref, keep_ref, x_buf, sems, *, steps):
+def ingest_kernel(x_ref, start_ref, gain_ref, xt_ref, normed_ref, edge_ref, keep_ref, x_buf, start_buf, gain_buf, sems, *, steps):
     batch, span, width = x_ref.shape
     size = steps * batch
     copies = [pltpu.make_async_copy(x_ref.at[row], x_buf.at[row], sems.at[row]) for row in range(batch)]
-    for copy in copies:
+    start_copy = pltpu.make_async_copy(start_ref, start_buf, sems.at[batch])
+    gain_copy = pltpu.make_async_copy(gain_ref, gain_buf, sems.at[batch + 1])
+    for copy in (start_copy, *copies, gain_copy):
         copy.start()
-    keep = 1.0 - start_ref[...].astype(F32)
+    start_copy.wait()
+    keep = 1.0 - start_buf[...].astype(F32)
     for token in range(span):
         keep_ref[token * batch : (token + 1) * batch, :] = jnp.broadcast_to(
             keep[:, token : token + 1], (batch, LANES)
@@ -79,11 +84,12 @@
     for row, copy in enumerate(copies):
         copy.wait()
         interleave(xt_ref, row, batch, x_buf[row])
+    gain_copy.wait()
 
     def chunk(index, carry):
         rows = rows_of(index, size)
         values = read(xt_ref, rows)
-        normed_ref[rows, :] = (values * rms(values) * gain_ref[...]).astype(BF16)
+        normed_ref[rows, :] = (values * rms(values) * gain_buf[...]).astype(BF16)
         return carry
 
     lax.fori_loop(0, span // steps, chunk, 0)
@@ -192,7 +198,7 @@
     chip_refs = refs[: chips - 1]
     (
         xt_ref, keep_ref, gate_ref, cand_ref, gact_ref, more_ref, gain_ref, w_out_ref, w_up_ref,
-        prev_ref, held_ref, mid_ref, nmid_ref, act_ref, gup_ref,
+        carry_ref, held_ref, mid_ref, nmid_ref, act_ref, gup_ref,
     ) = refs[chips - 1 :]
     batch, hidden = mate_ref.shape[1:]
     inner = w_up_ref.shape[1]
@@ -205,6 +211,7 @@
         state = from_chip(chip_refs, source, chip, 1)
         carry_in = jnp.where(source < chip, prod * carry_in + state, carry_in)
     carry_in = jnp.where(bit_of("seq", 0) == 1, mate_ref[0] * carry_in + mate_ref[1], carry_in)
+    carry_ref[...] = carry_in
     gain = gain_ref[...]
 
     def chunk(index, state):
@@ -215,7 +222,6 @@
             for side in range(2):
                 here = pl.ds(pl.multiple_of((index * steps + 2 * pair + side) * batch, batch), batch)
                 gate = gate_ref[here, :]
-                prev_ref[here, :] = state
                 decay = (1.0 - gate) * widen(keep_ref[here, :], hidden)
                 state = decay * state + gate * cand_ref[here, :]
                 out.append(state)
@@ -314,8 +320,8 @@
 def back_kernel(*refs, chips):
     chip_refs, out_refs = refs[: chips - 1], refs[chips - 1 : 2 * chips - 2]
     (
-        mate_ref, mate_out_ref, keep_ref, gate_ref, cand_ref, prev_ref, gheld_ref, conv_ref,
-        gproj_ref, gbias_ref, stay_ref, send_ref,
+        mate_ref, mate_out_ref, keep_ref, gate_ref, cand_ref, state_ref, held_ref, gheld_ref, conv_ref, w_in_ref,
+        gproj_ref, gbias_ref, edge_ref, stay_ref, send_ref,
     ) = refs[2 * chips - 2 :]
     batch, hidden = mate_out_ref.shape
     span = gate_ref.shape[0] // batch
@@ -332,6 +338,11 @@
         pair = span // 2 - 1 - offset
         logits = [None, None]
         cands = [None, None]
+        before = held_ref[rows_of(jnp.maximum(pair - 1, 0), 2 * batch), :].astype(F32)[batch:]
+        prevs = [
+            jnp.where(pair == 0, state_ref[...], before),
+            held_ref[rows_of(pair, 2 * batch), :].astype(F32)[:batch],
+        ]
         for side in (1, 0):
             here = pl.ds(pl.multiple_of((2 * pair + side) * batch, batch), batch)
             gate = gate_ref[here, :]
@@ -339,7 +350,7 @@
             gstate = gheld_ref[here, :] + arriving
             rest = 1.0 - gate
             cands[side] = gstate * gate
-            logits[side] = cands[side] * (cand_ref[here, :] - prev_ref[here, :] * keep) * rest
+            logits[side] = cands[side] * (cand_ref[here, :] - prevs[side] * keep) * rest
             arriving = rest * keep * gstate
             gbias = gbias + logits[side]
         both = rows_of(pair, 2 * batch)
@@ -351,6 +362,7 @@
         0, span // 2, two_steps, (carry_in, jnp.zeros((batch, hidden), F32)), unroll=4
     )
     gbias_ref[...] = jnp.sum(gbias, axis=0, keepdims=True)
+    edge_ref[...] = dot_nt(gproj_ref[: edge_ref.shape[0], :], w_in_ref[...]).astype(BF16)
     odd = bit_of("seq", 0) == 1
     wide_gradient(conv_ref, gproj_ref, stay_ref, send_ref, odd)
 
@@ -429,31 +441,40 @@
         base += half
 
 
-def split_sum_kernel(*refs, plan):
+def split_sum_kernel(*refs, plan, counts):
+    ins = 2 * sum(counts)
+    outs = refs[ins:]
+    source = 0
     for part, (which, axis) in enumerate(plan):
-        stay_ref, come_ref = refs[2 * part], refs[2 * part + 1]
-        out_stay, out_send = refs[2 * len(plan) + 2 * part], refs[2 * len(plan) + 2 * part + 1]
+        out_stay, out_send = outs[2 * part], outs[2 * part + 1]
         low = 1 << axis
-        for group in range(out_stay.shape[0]):
-            fixed = (group >> axis) * 2 * low + (group & (low - 1))
-            mine = fixed + low * bit_of("seq", which + 1)
-            other = fixed + low * (1 - bit_of("seq", which + 1))
-
-            def body(rows):
-                out_stay[group, rows, :] = stay_ref[mine, rows, :] + come_ref[mine, rows, :].astype(F32)
-                out_send[group, rows, :] = (
-                    stay_ref[other, rows, :] + come_ref[other, rows, :].astype(F32)
-                ).astype(BF16)
-
-            chunks(out_stay.shape[1], 16, body)
+        base = 0
+        for pair in range(counts[part]):
+            stay_ref, come_ref = refs[source], refs[source + 1]
+            source += 2
+            for group in range(out_stay.shape[0]):
+                fixed = (group >> axis) * 2 * low + (group & (low - 1))
+                mine = fixed + low * bit_of("seq", which + 1)
+                other = fixed + low * (1 - bit_of("seq", which + 1))
+
+                def body(rows):
+                    goal = pl.ds(pl.multiple_of(rows.start + base, 16), rows.size)
+                    out_stay[group, goal, :] = stay_ref[mine, rows, :].astype(F32) + come_ref[
+                        mine, rows, :
+                    ].astype(F32)
+                    out_send[group, goal, :] = (
+                        stay_ref[other, rows, :].astype(F32) + come_ref[other, rows, :].astype(F32)
+                    ).astype(BF16)
+
+                chunks(stay_ref.shape[1], 16, body)
+            base += stay_ref.shape[1]
 
 
 def join_sum_kernel(stay_a, come_a, stay_b, come_b, out_stay, out_send):
-    half = stay_a.shape[1]
     width = out_stay.shape[1]
     here = pl.ds(pl.multiple_of(bit_of("dp", 0) * width, width), width)
     there = pl.ds(pl.multiple_of((1 - bit_of("dp", 0)) * width, width), width)
-    for stay_ref, come_ref, base in ((stay_a, come_a, 0), (stay_b, come_b, half)):
+    for stay_ref, come_ref, base in ((stay_a, come_a, 0), (stay_b, come_b, stay_a.shape[1])):
 
         def body(rows):
             goal = pl.ds(pl.multiple_of(rows.start + base, 16), rows.size)
@@ -462,7 +483,7 @@
                 stay_ref[0, rows, there] + come_ref[0, rows, there].astype(F32)
             ).astype(BF16)
 
-        chunks(half, 16, body)
+        chunks(stay_ref.shape[1], 16, body)
 
 
 def column_sum_kernel(stay_ref, come_ref, out_stay, out_send, *, bit):
@@ -484,17 +505,17 @@
     chunks(out_ref.shape[0], 16, body)
 
 
-def tail_kernel(
-    gconv_ref, after_ref, xt_ref, normed_ref, halo_ref, gmid_ref, gain_ref, taps_ref, gnorm2_ref, gbias_ref,
-    ginput_ref, small_ref, norm_buf, gconv_buf, wide_buf,
+def taps_kernel(
+    gconv_ref, after_ref, xt_ref, normed_ref, halo_ref, taps_ref, gnorm2_ref, gbias_ref,
+    gnormed_ref, stay_ref, send_ref, norm_buf, gconv_buf,
     *, steps,
 ):
-    batch, span, width = ginput_ref.shape
+    tokens, width = gconv_ref.shape
+    batch = halo_ref.shape[0] // EDGE
     size = steps * batch
     lead = EDGE * batch
-    gain = gain_ref[...]
     norm_buf[:lead, :] = halo_ref[...].astype(F32)
-    gconv_buf[pl.ds(span * batch, after_ref.shape[0]), :] = after_ref[...].astype(F32)
+    gconv_buf[tokens : tokens + after_ref.shape[0], :] = after_ref[...].astype(F32)
 
     def spread(index, carry):
         rows = rows_of(index, size)
@@ -502,7 +523,7 @@
         gconv_buf[rows, :] = gconv_ref[rows, :].astype(F32)
         return carry
 
-    lax.fori_loop(0, span // steps, spread, 0)
+    lax.fori_loop(0, tokens // size, spread, 0)
 
     def chunk(index, carry):
         gnorm1, gtaps = carry
@@ -516,26 +537,48 @@
                 gnormed = gnormed + gconv_buf[later, :] * taps_ref[tap : tap + 1, :]
             earlier = pl.ds(pl.multiple_of(index * size + lead - tap * batch, 8), size)
             sums.append(gtaps[tap] + jnp.sum(norm_buf[earlier, :] * here, axis=0, keepdims=True))
+        gnormed_ref[rows, :] = gnormed
+        values = read(xt_ref, rows)
+        gnorm1 = gnorm1 + jnp.sum(gnormed * (values * rms(values)), axis=0, keepdims=True)
+        return gnorm1, tuple(sums)
+
+    zero = jnp.zeros((1, width), F32)
+    gnorm1, gtaps = lax.fori_loop(0, tokens // size, chunk, (zero, (zero,) * KW))
+    places = 2 * stay_ref.shape[0]
+    odd = bit_of("seq", 0) == 1
+    rows = []
+    for place in range(places):
+        parts = [
+            vector[:, place * (vector.shape[1] // places) : (place + 1) * (vector.shape[1] // places)]
+            for vector in (gnorm1, gnorm2_ref[...], *gtaps, gbias_ref[...])
+        ]
+        row = jnp.concatenate(parts, axis=1)
+        if row.shape[1] < width:
+            row = jnp.concatenate([row, jnp.zeros((1, width - row.shape[1]), F32)], axis=1)
+        rows.append(jnp.broadcast_to(row, (stay_ref.shape[1], width)))
+    for index in range(places // 2):
+        pair = rows[2 * index : 2 * index + 2]
+        stay_ref[index] = jnp.where(odd, pair[1], pair[0]).astype(BF16)
+        send_ref[index] = jnp.where(odd, pair[0], pair[1]).astype(BF16)
+
+
+def inputs_kernel(gnormed_ref, xt_ref, gmid_ref, gain_ref, ginput_ref, wide_buf, *, steps):
+    batch, span, width = ginput_ref.shape
+    gain = gain_ref[...]
+
+    def chunk(index, carry):
+        rows = rows_of(index, steps * batch)
         values = read(xt_ref, rows)
         scale = rms(values)
         unit = values * scale
-        gnorm1 = gnorm1 + jnp.sum(gnormed * unit, axis=0, keepdims=True)
-        pulled = gnormed * gain
+        pulled = gnormed_ref[rows, :] * gain
         ginput = gmid_ref[rows, :] + scale * (
             pulled - unit * jnp.mean(pulled * unit, axis=-1, keepdims=True)
         )
         write(wide_buf, rows, ginput)
-        return gnorm1, tuple(sums)
-
-    zero = jnp.zeros((1, width), F32)
-    gnorm1, gtaps = lax.fori_loop(0, span // steps, chunk, (zero, (zero,) * KW))
-    small_ref[0:1, :] = gnorm1
-    small_ref[1:2, :] = gnorm2_ref[...]
-    for tap in range(KW):
-        small_ref[2 + tap : 3 + tap, :] = gtaps[tap]
-    for part in range(gbias_ref.shape[1] // width):
-        row = 2 + KW + part
-        small_ref[row : row + 1, :] = gbias_ref[:, part * width : (part + 1) * width]
+        return carry
+
+    lax.fori_loop(0, span // steps, chunk, 0)
     for row in range(batch):
         ginput_ref[row] = deinterleave(wide_buf, row, batch, span)
 
@@ -543,50 +586,57 @@
 def finish_kernel(total_ref, come_ref, *outs, sizes):
     wide = total_ref.shape[1]
     width = 2 * wide
+    half = sum(sizes) // 2
+    if len(outs) > len(sizes):
+        low = bit_of("dp", 0) == 0
+        mine, other = [ref[half : half + SMALL, :].astype(F32) for ref in (total_ref, come_ref)]
+        row = jnp.concatenate([jnp.where(low, mine, other), jnp.where(low, other, mine)], axis=1)
+        column = 0
+        for out in outs[len(sizes) :]:
+            for line in range(out.shape[0]):
+                out[line : line + 1, :] = row[0:1, column : column + out.shape[1]]
+                column += out.shape[1]
     for source, bit in ((total_ref, bit_of("dp", 0)), (come_ref, 1 - bit_of("dp", 0))):
-        row = 0
-        for half in range(2):
+        for part_b in range(2):
+            row = part_b * (total_ref.shape[0] - half)
             for out, rows in zip(outs, sizes):
                 size = out.shape[0]
-                for start in range(half * rows // 2, (half + 1) * rows // 2, min(size, rows // 2)):
-                    count = min(size, rows // 2)
-                    part, low = start // size, start % size
+                count = min(size, rows // 2)
+                for start in range(part_b * rows // 2, (part_b + 1) * rows // 2, count):
+                    part, low_row = start // size, start % size
                     cols = pl.ds(pl.multiple_of(part * width + bit * wide, wide), wide)
-                    out[low : low + count, cols] = source[row : row + count, :].astype(F32)
+                    out[low_row : low_row + count, cols] = source[row : row + count, :].astype(F32)
                     row += count
 
 
 def call(
-    kernel, name, out_shapes, in_specs, args, scratch=(), limit=2, after=None, rider=None, work=1
+    kernel, name, out_shapes, in_specs, args, scratch=(), limit=2, after=(), work=1
 ):
     ins, outs = len(args), len(out_shapes)
 
     def body(*refs):
         inner = list(refs[:ins])
         rest = refs[ins:]
-        if rider is not None:
-            mine, other, rest = rest[0], rest[1], rest[2:]
-        if after is not None:
-            rest = rest[1:]
+        rest = rest[len(after) :]
         inner += rest[:outs]
         rest = rest[outs:]
-        if rider is not None:
-            rest[0][...] = mine[...] + other[...]
+        if name in FINAL:
+            rest[0][...] = jnp.zeros((8, LANES), F32)
             rest = rest[1:]
         kernel(*inner, *rest)
 
     args, in_specs, out_shapes = list(args), list(in_specs), list(out_shapes)
-    if rider is not None:
-        args += rider
-        in_specs += [VMEM_SPEC] * 2
-        out_shapes.append((rider[0].shape, rider[0].dtype))
-    if after is not None:
-        args.append(after)
-        in_specs.append(pl.BlockSpec(memory_space=pl.ANY))
+    if name in FINAL:
+        out_shapes.append(((8, LANES), F32))
+    args += after
+    in_specs += [pl.BlockSpec(memory_space=pl.ANY)] * len(after)
     return pl.pallas_call(
         body,
         name=name,
-        out_shape=[jax.ShapeDtypeStruct(shape, kind) for shape, kind in out_shapes],
+        out_shape=[
+            (pltpu.HBM if name in FINAL and index < outs else jax.ShapeDtypeStruct)(shape, kind)
+            for index, (shape, kind) in enumerate(out_shapes)
+        ],
         in_specs=in_specs,
         out_specs=[VMEM_SPEC] * len(out_shapes),
         scratch_shapes=list(scratch),
@@ -611,33 +661,18 @@
 
 class Order:
     def __init__(self):
-        self.last = None
-        self.small = None
-        self.come = None
-        self.hops = []
-        self.turn = 0
-
-    def ride(self, small, hops):
-        self.small, self.hops, self.turn = small, list(hops), 0
-        self.send()
-
-    def send(self):
-        self.come = swap(self.small, *self.hops.pop(0)) if self.hops else None
+        self.last = ()
 
     def call(self, *args, **kwargs):
-        self.turn += 1
-        rider = None if self.come is None or self.turn < 2 else [self.small, self.come]
         kwargs.setdefault("work", WORK.get(args[1], 1))
-        outs = list(call(*args, **kwargs, after=self.last, rider=rider))
-        if rider is not None:
-            self.small = outs.pop()
-            self.turn = 0
-            self.send()
-        self.last = min(outs, key=lambda out: out.size * out.dtype.itemsize)
+        outs = list(call(*args, **kwargs, after=self.last))
+        self.last = (min(outs, key=lambda out: out.size * out.dtype.itemsize),)
+        if args[1] in FINAL:
+            outs.pop()
         return outs
 
 
-def spread_sum(order, name, sources, out_shapes):
+def spread_sum(order, name, sources, out_shapes, late=()):
     places, _, width = sources[0][0].shape
     sizes = tuple(stay.shape[1] for stay, _ in sources)
     rows = sum(sizes)
@@ -646,8 +681,11 @@
     order_b = order_a[::-1]
     half = rows // 2
 
-    def shapes(count):
-        return [((count, half, width), F32), ((count, half, width), BF16)] * 2
+    def shapes(count, more=0):
+        out = []
+        for part in (half + more, half):
+            out += [((count, part, width), F32), ((count, part, width), BF16)]
+        return out
 
     stay_a, send_a, stay_b, send_b = order.call(
         functools.partial(core_sum_kernel, plan=(order_a[0], order_b[0])), name + "_core",
@@ -664,11 +702,15 @@
         for bits in (order_a, order_b):
             bit = bits[level + 1]
             plan.append((bit, bit - sum(done < bit for done in bits[: level + 1])))
+        sources = [stay_a, come_a, *(late if level == 0 else ()), stay_b, come_b]
+        more = SMALL if late else 0
         stay_a, send_a, stay_b, send_b = order.call(
-            functools.partial(split_sum_kernel, plan=tuple(plan)), name + "_seq",
-            shapes(places // 4 >> level), [VMEM_SPEC] * 4,
-            (stay_a, come_a, stay_b, come_b),
+            functools.partial(
+                split_sum_kernel, plan=tuple(plan), counts=(2 if late and level == 0 else 1, 1)
+            ),
+            name + "_seq", shapes(places // 4 >> level, more), [VMEM_SPEC] * len(sources), sources,
         )
+    rows += SMALL if late else 0
     depth = lax.axis_size("dp").bit_length() - 1
     wide = width // 2
     stay, send = order.call(
@@ -730,8 +772,12 @@
             ((lanes, tokens, LANES), F32), ((tokens, width), BF16), ((EDGE * batch, width), BF16),
             ((tokens, LANES), F32),
         ],
-        [pl.BlockSpec(memory_space=pltpu.HBM)] + [VMEM_SPEC] * 2, (inputs, doc_start, gain1),
-        [pltpu.VMEM((batch, span, width), BF16), pltpu.SemaphoreType.DMA((batch,))],
+        [pl.BlockSpec(memory_space=pltpu.HBM)] * 3,
+        [pltpu.with_memory_space_constraint(part, pltpu.HBM) for part in (inputs, doc_start, gain1)],
+        [
+            pltpu.VMEM((batch, span, width), BF16), pltpu.VMEM((batch, span), jnp.int32),
+            pltpu.VMEM((1, width), F32), pltpu.SemaphoreType.DMA((batch + 2,)),
+        ],
         limit=LIMITS["ingest"],
     )
     halo = shifted(edge, "seq", 1)
@@ -761,10 +807,10 @@
         functools.partial(prepare_rest_kernel, size=512, block=512), "prepare_rest",
         [((tokens, inner // 2), BF16)], [VMEM_SPEC] * 2, (gt, w_down), limit=LIMITS["prepare_rest"],
     )
-    prev, held, mid, nmid, act, gup = order.call(
+    state_in, held, mid, nmid, act, gup = order.call(
         functools.partial(forward_kernel, chips=chips, steps=64, block=512), "forward",
         [
-            ((tokens, hidden), F32), ((tokens, hidden), BF16), ((tokens, width), F32),
+            ((batch, hidden), F32), ((tokens, hidden), BF16), ((tokens, width), F32),
             ((tokens, width), BF16), ((tokens, inner), BF16), ((tokens, inner), BF16),
         ],
         [VMEM_SPEC] * (9 + chips),
@@ -804,46 +850,53 @@
         [(width // seq_count, inner), (up_rows, width)],
     )
     next(first)
-    gproj, gbias, stay_in, send_in = order.call(
+    gproj, gbias, gconv_edge, stay_in, send_in = order.call(
         functools.partial(back_kernel, chips=chips), "back",
-        [((tokens, 2 * hidden), BF16), ((1, hidden), F32)] + [((pairs, in_rows, width), BF16)] * 2,
-        [VMEM_SPEC] * (6 + 2 * chips),
+        [((tokens, 2 * hidden), BF16), ((1, hidden), F32), ((EDGE * batch, width), BF16)]
+        + [((pairs, in_rows, width), BF16)] * 2,
+        [VMEM_SPEC] * (8 + 2 * chips),
         (
-            *all_totals, *all_outgoing, mate_totals, mate_outgoing, keep, gate, cand, prev, gheld, conv_out,
+            *all_totals, *all_outgoing, mate_totals, mate_outgoing, keep, gate, cand, state_in, held, gheld, conv_out, w_in,
         ),
         limit=LIMITS["back"],
     )
+    after = shifted(gconv_edge, "seq", -1)
     come_in = swap(send_in, "seq", 0)
     (gconv,) = order.call(
         functools.partial(gconv_kernel, steps=64), "gconv", [((tokens, width), BF16)],
         [VMEM_SPEC] * 2, (gproj, w_in), limit=LIMITS["gconv"],
     )
-    after = shifted(gconv[: EDGE * batch], "seq", -1)
-    order.last = after
+    order.last = (*order.last, after)
+    late = []
+    share = width // seq_count
     second = spread_sum(
         order, "second", [(stay_in, come_in), (stay_out, come_out)],
-        [(width // seq_count, 2 * hidden), (out_rows, width)],
+        [
+            (share, 2 * hidden), (out_rows, width), (1, share), (1, share), (KW, share),
+            (1, hidden // seq_count),
+        ],
+        late,
     )
     next(first)
     next(second)
-    bias_rows = hidden // width
-    ginput, small = order.call(
-        functools.partial(tail_kernel, steps=16), "tail",
-        [((batch, span, width), F32), ((2 + KW + bias_rows, width), F32)],
-        [VMEM_SPEC] * 10,
-        (gconv, after, xt, normed, halo, gmid, gain1, taps, gnorm2, gbias),
+    gnormed, stay_small, send_small = order.call(
+        functools.partial(taps_kernel, steps=16), "taps",
+        [((tokens, width), F32)] + [((pairs, SMALL, width), BF16)] * 2, [VMEM_SPEC] * 8,
+        (gconv, after, xt, normed, halo, taps, gnorm2, gbias),
         [
             pltpu.VMEM((tokens + EDGE * batch, width), F32),
             pltpu.VMEM((tokens + EDGE * batch, width), F32),
-            pltpu.VMEM((lanes, tokens, LANES), F32),
         ],
-        limit=LIMITS["tail"],
-    )
-    order.ride(
-        small, [("seq", bit) for bit in range(seq_depth)] + [("dp", bit) for bit in range(dp_depth)]
-    )
+        limit=LIMITS["taps"],
+    )
+    come_small = swap(send_small, "seq", 0)
     next(first)
-    next(second)
+    stay_small, send_small = order.call(
+        functools.partial(split_sum_kernel, plan=((0, 0),), counts=(1,)), "small",
+        [((pairs // 2, SMALL, width), F32), ((pairs // 2, SMALL, width), BF16)], [VMEM_SPEC] * 2,
+        (stay_small, come_small),
+    )
+    late += [stay_small, swap(send_small, "seq", 1)]
     (result,) = order.call(
         functools.partial(result_kernel, steps=64), "result", [((batch, span, width), BF16)],
         [VMEM_SPEC] * 3, (act, mid, w_down), [pltpu.VMEM((lanes, tokens, LANES), F32)],
@@ -851,29 +904,25 @@
     )
     next(first)
     next(second)
+    next(second)
+    (ginput,) = order.call(
+        functools.partial(inputs_kernel, steps=16), "inputs", [((batch, span, width), F32)],
+        [VMEM_SPEC] * 4, (gnormed, xt, gmid, gain1), [pltpu.VMEM((lanes, tokens, LANES), F32)],
+        limit=LIMITS["inputs"],
+    )
     next(first)
     next(second)
     done = {}
     while len(done) < 2:
-        for part in (first, second):
+        for part in (second, first):
             if part not in done:
                 outs = next(part)
                 if outs is not None:
                     done[part] = outs
-    while order.come is not None:
-        order.small = order.small + order.come
-        order.send()
-    small = order.small
     gw_up, gw_down = done[first]
-    gw_in, gw_out = done[second]
-
-    def own(values):
-        size = values.shape[0] // seq_count
-        return lax.dynamic_slice_in_dim(values, seq_at * size, size, 0)
-
+    gw_in, gw_out, gnorm1, gnorm2, gtaps, gbias = done[second]
     return (
-        result, ginput, own(small[0]), own(jnp.transpose(small[2 : 2 + KW])),
-        own(small[2 + KW :].reshape(-1)), gw_in, gw_out, own(small[1]), gw_up, gw_down,
+        result, ginput, gnorm1[0], jnp.transpose(gtaps), gbias[0], gw_in, gw_out, gnorm2[0], gw_up, gw_down,
     )
 
 

time: 135 us -> 119 us (0.88); the launches traced: 133 us -> 119 us
  local copies, waits for them, and re-layouts: 9.55 us -> 0.05 us
  starting transfers between devices: 41.2 us -> 32.8 us
  Pallas kernels: 51.4 us -> 53.2 us
  waiting for transfers between devices: 30 us -> 31.7 us
    ppermute x31 -> x28, starting transfers between devices: 37.6 us -> 29 us  [swap_by(): lax.ppermute(block, axis, [(i, i ^ mask) for i in range(lax.axis_size(axi...]
    unnamed x32 -> x18, local copies, waits for them, and re-layouts: 7.71 us -> 0.05 us
    ppermute x31 -> x28, waiting for transfers between devices: 29.5 us -> 31.6 us  [swap_by(): lax.ppermute(block, axis, [(i, i ^ mask) for i in range(lax.axis_size(axi...]
    dynamic_slice x3 -> x0, local copies, waits for them, and re-layouts: 1.82 us -> none  [own(): return lax.dynamic_slice_in_dim(values, seq_at * size, size, 0)]
    pallas_call x26 -> x28, Pallas kernels: 51.4 us -> 53.2 us  [call(): pl.pallas_call(body, name=name, out_shape=[(pltpu.HBM if name in FINAL an...]
  transfers between devices with their start and end apart: 33 -> 30, of which waited for: 14 -> 14; matrix products, arithmetic and copies ran while one was open for 0% -> 0% of each run, Pallas kernels for 22% -> 27%
where the time goes in v2:
time: 119 us
  Pallas kernels  53.2 us (45%)
  starting transfers between devices  32.8 us (28%)
  waiting for transfers between devices  31.7 us (27%)
    pallas_call x28, Pallas kernels, call(): pl.pallas_call(body, name=name, out_shape=[(pltpu.HBM if name in FINAL an...  53.2 us
    ppermute x28, waiting for transfers between devices, swap_by(): lax.ppermute(block, axis, [(i, i ^ mask) for i in range(lax.axis_size(axi...  31.6 us
    ppermute x28, starting transfers between devices, swap_by(): lax.ppermute(block, axis, [(i, i ^ mask) for i in range(lax.axis_size(axi...  29 us
    ppermute x2, starting transfers between devices, shifted(): return lax.ppermute(block, axis, route)  3.78 us
  transfers between devices with their start and end apart: 30, of which 14 were waited for; matrix products, arithmetic and copies ran while one was open for 0% of the time, Pallas kernels for 27%

profile of v2, /device:TPU:0, one launch (start us, length us, event | category | flops | bytes accessed | tf_op | source)
XLA Modules:
  0.0 118.8 jit_solution(940815820767082162)
XLA Ops:
  0.7 2.7 %ingest.1 = (f32[4,1024,128]{2,1,0:T(8,128)S(1)}, bf16[1024,512]{1,0:T(8,128)(2,1)S(1)}, bf16[64,512]{1,0:T(8,128)(2,1)S(1)}, f32[1024,128]{1,0:T(8,128)S(1)}) custom-call(bf16[8,128,512]{2,1,0:T(8,128)(2,1)} %refs_0_.2, s32[8,128]{1,0:T(8,128)} %refs_1_.4, f32[1,512]{1,0:T(1,128)} %bitcast.12), custom_call_target="tpu_custom_call" | custom-call | flops 10000000000 | bytes 1 | tf_op jit(solution)/shard_map/ingest/pallas_call | solution.py:633
  3.4 2.5 %collective-permute-start = (bf16[64,512]{1,0:T(8,128)(2,1)S(1)}, bf16[64,512]{1,0:T(8,128)(2,1)S(1)}, u32[]{:S(2)}, u32[]{:S(2)}) collective-permute-start(bf16[64,512]{1,0:T(8,128)(2,1)S(1)} %get-tuple-element.81.refs_2_), channel_id=1, source_target_pairs={{0,1},{1,2},{2,3},{3,4},{4,5},{5,6},{6,7},{8,9},{9,10},{10,11},{11... | collective-permute-start | bytes 196616 | tf_op jit(solution)/shard_map/ppermute | solution.py:651
  6.0 2.1 %prepare.1 = (bf16[1024,512]{1,0:T(8,128)(2,1)S(1)}, bf16[1024,1024]{1,0:T(8,128)(2,1)S(1)}) custom-call(bf16[8,128,512]{2,1,0:T(8,128)(2,1)S(1)} %copy-done.7, bf16[2048,512]{1,0:T(8,128)(2,1)S(1)} %copy-done, bf16[64,512]{1,0:T(8,128)(2,1)S(1)} %get-tuple-element.81.refs_2_), custom_call_target="tpu_custom_call" | custom-call | flops 10000000000 | bytes 1 | tf_op jit(solution)/shard_map/prepare/pallas_call | solution.py:633
  8.1 3.8 %front.1 = (bf16[1024,512]{1,0:T(8,128)(2,1)S(1)}, f32[1024,1024]{1,0:T(8,128)S(1)}, f32[1024,1024]{1,0:T(8,128)S(1)}, f32[2,8,1024]{2,1,0:T(8,128)S(1)}) custom-call(bf16[1024,512]{1,0:T(8,128)(2,1)S(1)} %get-tuple-element.80.refs_0_.refs_3_, bf16[64,512]{1,0:T(8,128)(2,1)S(1)} %collective-permute-done.refs_1_.refs_4_, ...), custom_call_target="tpu_custom_call" | custom-call | flops 10000000000 | bytes 1 | tf_op jit(solution)/shard_map/front/pallas_call | solution.py:633
  11.9 2.7 %collective-permute-start.1 = (f32[2,8,1024]{2,1,0:T(8,128)S(1)}, f32[2,8,1024]{2,1,0:T(8,128)S(1)}, u32[]{:S(2)}, u32[]{:S(2)}) collective-permute-start(f32[2,8,1024]{2,1,0:T(8,128)S(1)} %get-tuple-element.84.refs_0_.refs_2_), channel_id=1, source_target_pairs={{0,1},{1,0},{2,3},{3,2},{4,5},{5,4},{6,7},{7,6},{8,9},{9,8},{10,11... | collective-permute-start | bytes 196616 | tf_op jit(solution)/shard_map/ppermute | solution.py:655
  14.6 0.9 collective-permute-done.1.refs_1_.refs_0_.refs_3_.refs_6_
  15.5 2.8 %collective-permute-start.4 = (f32[2,8,1024]{2,1,0:T(8,128)S(1)}, f32[2,8,1024]{2,1,0:T(8,128)S(1)}, u32[]{:S(2)}, u32[]{:S(2)}) collective-permute-start(f32[2,8,1024]{2,1,0:T(8,128)S(1)} %chip_totals.1.refs_2_), channel_id=1, source_target_pairs={{0,6},{1,7},{2,4},{3,5},{4,2},{5,3},{6,0},{7,1},{8,14},{9,15},{10,... | collective-permute-start | bytes 196616 | tf_op jit(solution)/shard_map/ppermute | solution.py:655
  18.3 0.5 collective-permute-start.3
  18.8 0.9 collective-permute-start.2
  19.8 1.5 %prepare_rest.1.refs_9_.refs_13_ = bf16[1024,1024]{1,0:T(8,128)(2,1)S(1)} custom-call(bf16[1024,512]{1,0:T(8,128)(2,1)S(1)} %get-tuple-element.83.refs_6_.refs_0_.refs_3_.refs_2_, bf16[2048,512]{1,0:T(8,128)(2,1)S(1)} %copy-done, f32[2,8,1024]{2,1,0:T(8,128)S(1)} %chip_totals.1.refs_2_), custom_call_target="tpu_custom_call" | custom-call | flops 1 | bytes 1 | tf_op jit(solution)/shard_map/prepare_rest/pallas_call | solution.py:633
  21.3 1.3 %collective-permute-done.3.refs_2_.refs_1_ = f32[2,8,1024]{2,1,0:T(8,128)S(1)} collective-permute-done((f32[2,8,1024]{2,1,0:T(8,128)S(1)}, f32[2,8,1024]{2,1,0:T(8,128)S(1)}, u32[]{:S(2)}, u32[]{:S(2)}) %collective-permute-start.3) | collective-permute-done | bytes 65568 | tf_op jit(solution)/shard_map/ppermute | solution.py:655
  22.6 0.7 collective-permute-done.2.refs_1_.refs_0_
  23.3 8.6 %forward.1 = (f32[8,1024]{1,0:T(8,128)S(1)}, bf16[1024,1024]{1,0:T(8,128)(2,1)S(1)}, f32[1024,512]{1,0:T(8,128)S(1)}, bf16[1024,512]{1,0:T(8,128)(2,1)S(1)}, bf1...) custom-call(f32[2,8,1024]{2,1,0:T(8,128)S(1)} %collective-permute-done.1.refs_1_.refs_0_.refs_3_.refs_6_, ...), custom_call_target="tpu_custom_call" | custom-call | flops 10000000000 | bytes 1 | tf_op jit(solution)/shard_map/forward/pallas_call | solution.py:633
  31.9 4.5 %weights.1 = (bf16[4,256,512]{2,1,0:T(8,128)(2,1)S(1)}, bf16[4,256,512]{2,1,0:T(8,128)(2,1)S(1)}, bf16[4,256,512]{2,1,0:T(8,128)(2,1)S(1)}, bf16[4,256,512]{2,1,0:T(8,128)(2,1)S(1)}) custom-call(bf16[1024,512]{1,0:T(8,128)(2,1)S(1)} %get-tuple-element.92.refs_0_, bf16[1024,2048]{1,0:T(8,128)(2,1)S(1)} %get-tuple-element.91.refs_1_.refs_0_, ...), custom_call_target="tpu_custom_call" | custom-call | flops 1 | bytes 1 | tf_op jit(solution)/shard_map/weights/pallas_call | solution.py:633
  36.5 0.5 collective-permute-start.10
  37.0 5.3 %reverse.1 = (f32[1024,512]{1,0:T(8,128)S(1)}, bf16[1024,512]{1,0:T(8,128)(2,1)S(1)}, f32[1024,1024]{1,0:T(8,128)S(1)}, f32[8,1024]{1,0:T(8,128)S(1)}, f32[1,512]{1,0:T(1,128)S(1)}) custom-call(bf16[1024,2048]{1,0:T(8,128)(2,1)S(1)} %get-tuple-element.91.refs_1_.refs_0_, f32[1024,512]{1,0:T(8,128)S(1)} %get-tuple-element.90.refs_1_, ...), custom_call_target="tpu_custom_call" | custom-call | flops 1 | bytes 1 | tf_op jit(solution)/shard_map/reverse/pallas_call | solution.py:633
  42.3 0.1 collective-permute-start.5
  42.4 1.3 %weights_out.1 = (bf16[4,128,512]{2,1,0:T(8,128)(2,1)S(1)}, bf16[4,128,512]{2,1,0:T(8,128)(2,1)S(1)}) custom-call(bf16[1024,1024]{1,0:T(8,128)(2,1)S(1)} %get-tuple-element.96.refs_0_.refs_12_, bf16[1024,512]{1,0:T(8,128)(2,1)S(1)} %get-tuple-element.97.refs_1_, f32[1,512]{1,0:T(1,128)S(1)} %get-tuple-element.98.refs_2_.refs_6_), custom_call_target="tpu_custom_call" | custom-call | flops 1 | bytes 1 | tf_op jit(solution)/shard_map/weights_out/pallas_call | solution.py:633
  43.8 2.3 %collective-permute-start.8 = (f32[8,1024]{1,0:T(8,128)S(1)}, f32[8,1024]{1,0:T(8,128)S(1)}, u32[]{:S(2)}, u32[]{:S(2)}) collective-permute-start(f32[8,1024]{1,0:T(8,128)S(1)} %chip_outgoing.1.refs_4_), channel_id=1, source_target_pairs={{0,6},{1,7},{2,4},{3,5},{4,2},{5,3},{6,0},{7,1},{8,14},{9,15},{10,... | collective-permute-start | bytes 98312 | tf_op jit(solution)/shard_map/ppermute | solution.py:655
  46.1 1.3 %collective-permute-start.6 = (f32[8,1024]{1,0:T(8,128)S(1)}, f32[8,1024]{1,0:T(8,128)S(1)}, u32[]{:S(2)}, u32[]{:S(2)}) collective-permute-start(f32[8,1024]{1,0:T(8,128)S(1)} %chip_outgoing.1.refs_4_), channel_id=1, source_target_pairs={{0,2},{1,3},{2,0},{3,1},{4,6},{5,7},{6,4},{7,5},{8,10},{9,11},{10,... | collective-permute-start | bytes 98312 | tf_op jit(solution)/shard_map/ppermute | solution.py:655
  47.3 0.9 first_core.1
  48.2 1.4 %collective-permute-start.15 = (bf16[2,256,512]{2,1,0:T(8,128)(2,1)S(1)}, bf16[2,256,512]{2,1,0:T(8,128)(2,1)S(1)}, u32[]{:S(2)}, u32[]{:S(2)}) collective-permute-start(bf16[2,256,512]{2,1,0:T(8,128)(2,1)S(1)} %get-tuple-element.114), channel_id=1, source_target_pairs={{0,4},{1,5},{2,6},{3,7},{4,0},{5,1},{6,2},{7,3},{8,12},{9,13},{10,... | collective-permute-start | bytes 1572872 | tf_op jit(solution)/shard_map/ppermute | solution.py:655
  49.6 1.4 %collective-permute-start.14 = (bf16[2,256,512]{2,1,0:T(8,128)(2,1)S(1)}, bf16[2,256,512]{2,1,0:T(8,128)(2,1)S(1)}, u32[]{:S(2)}, u32[]{:S(2)}) collective-permute-start(bf16[2,256,512]{2,1,0:T(8,128)(2,1)S(1)} %get-tuple-element.105.refs_16_), channel_id=1, source_target_pairs={{0,2},{1,3},{2,0},{3,1},{4,6},{5,7},{6,4},{7,5},{8,10},{9,11},{10,... | collective-permute-start | bytes 1572872 | tf_op jit(solution)/shard_map/ppermute | solution.py:655
  51.1 5.2 %back.1 = (bf16[1024,2048]{1,0:T(8,128)(2,1)S(1)}, f32[1,1024]{1,0:T(1,128)S(1)}, bf16[64,512]{1,0:T(8,128)(2,1)S(1)}, bf16[4,256,512]{2,1,0:T(8,128)(2,1)S(1)}, bf16[4,256,512]{2,1,0:T(8,128)(2,1)S(1)}) custom-call(f32[2,8,1024]{2,1,0:T(8,128)S(1)} %collective-permute-done.2.refs_1_.refs_0_, f32[2,8,1024]{2,1,0:T(8,128)S(1)} %collective-permute-done.3.refs_2_.refs_1_, ...), custom_call_target="tpu_custom_call" | custom-call | flops 10000000000 | bytes 1 | tf_op jit(solution)/shard_map/back/pallas_call | solution.py:633
  56.2 1.3 %collective-permute-start.11 = (bf16[64,512]{1,0:T(8,128)(2,1)S(1)}, bf16[64,512]{1,0:T(8,128)(2,1)S(1)}, u32[]{:S(2)}, u32[]{:S(2)}) collective-permute-start(bf16[64,512]{1,0:T(8,128)(2,1)S(1)} %get-tuple-element.108), channel_id=1, source_target_pairs={{1,0},{2,1},{3,2},{4,3},{5,4},{6,5},{7,6},{9,8},{10,9},{11,10},{12... | collective-permute-start | bytes 196616 | tf_op jit(solution)/shard_map/ppermute | solution.py:651
  57.5 1.2 %collective-permute-start.13 = (bf16[4,128,512]{2,1,0:T(8,128)(2,1)S(1)}, bf16[4,128,512]{2,1,0:T(8,128)(2,1)S(1)}, u32[]{:S(2)}, u32[]{:S(2)}) collective-permute-start(bf16[4,128,512]{2,1,0:T(8,128)(2,1)S(1)} %get-tuple-element.111), channel_id=1, source_target_pairs={{0,1},{1,0},{2,3},{3,2},{4,5},{5,4},{6,7},{7,6},{8,9},{9,8},{10,11... | collective-permute-start | bytes 1572872 | tf_op jit(solution)/shard_map/ppermute | solution.py:655
  58.7 0.1 collective-permute-start.12
  58.8 2.6 %gconv.1.refs_4_.refs_0_ = bf16[1024,512]{1,0:T(8,128)(2,1)S(1)} custom-call(bf16[1024,2048]{1,0:T(8,128)(2,1)S(1)} %get-tuple-element.106.refs_0_, bf16[512,2048]{1,0:T(8,128)(2,1)S(1)} %copy-done.2, f32[1,1024]{1,0:T(1,128)S(1)} %get-tuple-element.107.refs_2_.refs_7_), custom_call_target="tpu_custom_call" | custom-call | flops 1 | bytes 1 | tf_op jit(solution)/shard_map/gconv/pallas_call | solution.py:633
  61.4 0.3 collective-permute-done.15.refs_3_
  61.7 1.0 collective-permute-done.14.refs_1_
  62.8 0.4 first_seq.1
  63.2 1.5 %collective-permute-start.18 = (bf16[1,256,512]{2,1,0:T(8,128)(2,1)S(1)}, bf16[1,256,512]{2,1,0:T(8,128)(2,1)S(1)}, u32[]{:S(2)}, u32[]{:S(2)}) collective-permute-start(bf16[1,256,512]{2,1,0:T(8,128)(2,1)S(1)} %get-tuple-element.121), channel_id=1, source_target_pairs={{0,2},{1,3},{2,0},{3,1},{4,6},{5,7},{6,4},{7,5},{8,10},{9,11},{10,... | collective-permute-start | bytes 786440 | tf_op jit(solution)/shard_map/ppermute | solution.py:655
  64.7 0.4 collective-permute-start.17
  65.0 0.7 second_core.1
  65.7 1.7 %collective-permute-start.21 = (bf16[2,192,512]{2,1,0:T(8,128)(2,1)S(1)}, bf16[2,192,512]{2,1,0:T(8,128)(2,1)S(1)}, u32[]{:S(2)}, u32[]{:S(2)}) collective-permute-start(bf16[2,192,512]{2,1,0:T(8,128)(2,1)S(1)} %get-tuple-element.130), channel_id=1, source_target_pairs={{0,4},{1,5},{2,6},{3,7},{4,0},{5,1},{6,2},{7,3},{8,12},{9,13},{10,... | collective-permute-start | bytes 1179656 | tf_op jit(solution)/shard_map/ppermute | solution.py:655
  67.4 0.6 collective-permute-start.19
  68.0 2.8 %taps.1 = (f32[1024,512]{1,0:T(8,128)S(1)}, bf16[4,16,512]{2,1,0:T(8,128)(2,1)S(1)}, bf16[4,16,512]{2,1,0:T(8,128)(2,1)S(1)}) custom-call(bf16[1024,512]{1,0:T(8,128)(2,1)S(1)} %gconv.1.refs_4_.refs_0_, bf16[64,512]{1,0:T(8,128)(2,1)S(1)} %collective-permute-done.11.refs_5_.refs_1_, f32[4,1024,128]{2,1,0:T(8,128)S(1)} %get-tuple-element.85.refs_4_.refs_2_.refs_1_, ...), custom_call_target="tpu_custom_call" | custom-call | flops 1 | bytes 1 | tf_op jit(solution)/shard_map/taps/pallas_call | solution.py:633
  70.8 1.5 %collective-permute-done.18.refs_3_ = bf16[1,256,512]{2,1,0:T(8,128)(2,1)S(1)} collective-permute-done((bf16[1,256,512]{2,1,0:T(8,128)(2,1)S(1)}, bf16[1,256,512]{2,1,0:T(8,128)(2,1)S(1)}, u32[]{:S(2)}, u32[]{:S(2)}) %collective-permute-start.18) | collective-permute-done | bytes 262176 | tf_op jit(solution)/shard_map/ppermute | solution.py:655
  72.3 1.5 %collective-permute-done.17.refs_1_ = bf16[1,256,512]{2,1,0:T(8,128)(2,1)S(1)} collective-permute-done((bf16[1,256,512]{2,1,0:T(8,128)(2,1)S(1)}, bf16[1,256,512]{2,1,0:T(8,128)(2,1)S(1)}, u32[]{:S(2)}, u32[]{:S(2)}) %collective-permute-start.17) | collective-permute-done | bytes 262176 | tf_op jit(solution)/shard_map/ppermute | solution.py:655
  73.8 0.3 first_join.1
  74.1 1.7 %collective-permute-start.22 = (bf16[512,256]{1,0:T(8,128)(2,1)S(1)}, bf16[512,256]{1,0:T(8,128)(2,1)S(1)}, u32[]{:S(2)}, u32[]{:S(2)}) collective-permute-start(bf16[512,256]{1,0:T(8,128)(2,1)S(1)} %get-tuple-element.122.refs_2_), channel_id=1, source_target_pairs={{0,8},{8,0},{16,24},{24,16},{1,9},{9,1},{17,25},{25,17},{2,10},{10... | collective-permute-start | bytes 786440 | tf_op jit(solution)/shard_map/ppermute | solution.py:655
  75.8 1.3 %collective-permute-done.16.refs_1_ = bf16[4,16,512]{2,1,0:T(8,128)(2,1)S(1)} collective-permute-done((bf16[4,16,512]{2,1,0:T(8,128)(2,1)S(1)}, bf16[4,16,512]{2,1,0:T(8,128)(2,1)S(1)}, u32[]{:S(2)}, u32[]{:S(2)}) %collective-permute-start.16) | collective-permute-done | bytes 65568 | tf_op jit(solution)/shard_map/ppermute | solution.py:655
  77.1 0.6 collective-permute-start.20
  77.7 3.9 %result.1 = (bf16[8,128,512]{2,1,0:T(8,128)(2,1)}, f32[8,128]{1,0:T(8,128)S(1)}) custom-call(bf16[1024,2048]{1,0:T(8,128)(2,1)S(1)} %get-tuple-element.89.refs_2_.refs_0_, f32[1024,512]{1,0:T(8,128)S(1)} %get-tuple-element.90.refs_1_, bf16[2048,512]{1,0:T(8,128)(2,1)S(1)} %copy-done, bf16[2,16,512]{2,1,0:T(8,128)(2,1)S(1)} %get-tuple-element.123.refs_3_), custom_call_target="tpu_custom_call" | custom-call | flops 1 | bytes 1 | tf_op jit(solution)/shard_map/result/pallas_call | solution.py:633
  81.6 0.2 first_last.1.refs_6_.refs_0_
  81.9 0.3 second_seq.1
  82.2 0.8 collective-permute-start.23
  82.9 1.1 collective-permute-start.24
  84.1 2.6 %collective-permute-start.26 = (bf16[512,256]{1,0:T(8,128)(2,1)S(1)}, bf16[512,256]{1,0:T(8,128)(2,1)S(1)}, u32[]{:S(2)}, u32[]{:S(2)}) collective-permute-start(bf16[512,256]{1,0:T(8,128)(2,1)S(1)} %first_last.1.refs_6_.refs_0_), channel_id=1, source_target_pairs={{0,16},{8,24},{16,0},{24,8},{1,17},{9,25},{17,1},{25,9},{2,18},{10... | collective-permute-start | bytes 786440 | tf_op jit(solution)/shard_map/ppermute | solution.py:655
  86.7 2.7 %collective-permute-done.24.refs_3_ = bf16[1,192,512]{2,1,0:T(8,128)(2,1)S(1)} collective-permute-done((bf16[1,192,512]{2,1,0:T(8,128)(2,1)S(1)}, bf16[1,192,512]{2,1,0:T(8,128)(2,1)S(1)}, u32[]{:S(2)}, u32[]{:S(2)}) %collective-permute-start.24) | collective-permute-done | bytes 196640 | tf_op jit(solution)/shard_map/ppermute | solution.py:655
  89.3 0.2 second_join.1
  89.6 0.8 collective-permute-start.25
  90.4 3.6 %inputs.1 = (f32[8,128,512]{2,1,0:T(8,128)}, f32[8,128]{1,0:T(8,128)S(1)}) custom-call(f32[1024,512]{1,0:T(8,128)S(1)} %get-tuple-element.125.refs_0_, f32[4,1024,128]{2,1,0:T(8,128)S(1)} %get-tuple-element.85.refs_4_.refs_2_.refs_1_, f32[1024,512]{1,0:T(8,128)S(1)} %get-tuple-element.126.refs_2_, f32[1,512]{1,0:T(1,128)S(1)} %bitcast.13, ...), custom_call_target="tpu_custom_call" | custom-call | flops 1 | bytes 1 | tf_op jit(solution)/shard_map/inputs/pallas_call | solution.py:633
  93.9 4.2 %collective-permute-done.26.refs_1_ = bf16[512,256]{1,0:T(8,128)(2,1)S(1)} collective-permute-done((bf16[512,256]{1,0:T(8,128)(2,1)S(1)}, bf16[512,256]{1,0:T(8,128)(2,1)S(1)}, u32[]{:S(2)}, u32[]{:S(2)}) %collective-permute-start.26) | collective-permute-done | bytes 262176 | tf_op jit(solution)/shard_map/ppermute | solution.py:655
  98.1 0.2 first_total.1.refs_2_.refs_0_
  98.3 2.8 %collective-permute-done.25.refs_1_ = bf16[400,256]{1,0:T(8,128)(2,1)S(1)} collective-permute-done((bf16[400,256]{1,0:T(8,128)(2,1)S(1)}, bf16[400,256]{1,0:T(8,128)(2,1)S(1)}, u32[]{:S(2)}, u32[]{:S(2)}) %collective-permute-start.25) | collective-permute-done | bytes 204832 | tf_op jit(solution)/shard_map/ppermute | solution.py:655
  101.1 0.2 second_last.1.refs_0_.refs_2_
  101.3 1.9 %collective-permute-start.29 = (bf16[512,256]{1,0:T(8,128)(2,1)S(1)}, bf16[512,256]{1,0:T(8,128)(2,1)S(1)}, u32[]{:S(2)}, u32[]{:S(2)}) collective-permute-start(bf16[512,256]{1,0:T(8,128)(2,1)S(1)} %first_total.1.refs_2_.refs_0_), channel_id=1, source_target_pairs={{0,8},{8,0},{16,24},{24,16},{1,9},{9,1},{17,25},{25,17},{2,10},{10... | collective-permute-start | bytes 786440 | tf_op jit(solution)/shard_map/ppermute | solution.py:655
  103.2 8.1 %collective-permute-done.27.refs_1_ = bf16[400,256]{1,0:T(8,128)(2,1)S(1)} collective-permute-done((bf16[400,256]{1,0:T(8,128)(2,1)S(1)}, bf16[400,256]{1,0:T(8,128)(2,1)S(1)}, u32[]{:S(2)}, u32[]{:S(2)}) %collective-permute-start.27) | collective-permute-done | bytes 204832 | tf_op jit(solution)/shard_map/ppermute | solution.py:655
  111.3 0.1 second_total.1.refs_2_.refs_0_
  111.5 1.1 collective-permute-done.29.refs_1_
  112.6 1.0 first_finish.1
  113.7 4.1 %collective-permute-done.28.refs_1_ = bf16[400,256]{1,0:T(8,128)(2,1)S(1)} collective-permute-done((bf16[400,256]{1,0:T(8,128)(2,1)S(1)}, bf16[400,256]{1,0:T(8,128)(2,1)S(1)}, u32[]{:S(2)}, u32[]{:S(2)}) %collective-permute-start.28) | collective-permute-done | bytes 204832 | tf_op jit(solution)/shard_map/ppermute | solution.py:655
  117.8 0.9 second_finish.1
  (42 shorter events, 0.4 us)
Async XLA Ops:
  0.6 5.3 %copy-start = (bf16[2048,512]{1,0:T(8,128)(2,1)S(1)}, bf16[2048,512]{1,0:T(8,128)(2,1)}, u32[]{:S(2)}) copy-start(bf16[2048,512]{1,0:T(8,128)(2,1)} %refs_2_.1) | copy-start | bytes 6291460
  0.7 5.3 %copy-start.7 = (bf16[8,128,512]{2,1,0:T(8,128)(2,1)S(1)}, bf16[8,128,512]{2,1,0:T(8,128)(2,1)}, u32[]{:S(2)}) copy-start(bf16[8,128,512]{2,1,0:T(8,128)(2,1)} %refs_0_.3) | copy-start | bytes 3145732
  3.4 4.7 %copy-start.2 = (bf16[512,2048]{1,0:T(8,128)(2,1)S(1)}, bf16[512,2048]{1,0:T(8,128)(2,1)}, u32[]{:S(2)}) copy-start(bf16[512,2048]{1,0:T(8,128)(2,1)} %refs_1_.7) | copy-start | bytes 6291460
  3.4 4.7 %copy-start.4 = (f32[512,4]{0,1:T(4,128)S(1)}, f32[512,4]{0,1:T(4,128)}, u32[]{:S(2)}) copy-start(f32[512,4]{0,1:T(4,128)} %param.14) | copy-start | bytes 24580
  3.4 4.7 %copy-start.8 = (f32[1024]{0:T(1024)S(1)}, f32[1024]{0:T(1024)}, u32[]{:S(2)}) copy-start(f32[1024]{0:T(1024)} %param.15) | copy-start | bytes 12292
  3.4 4.6 %collective-permute-start = (bf16[64,512]{1,0:T(8,128)(2,1)S(1)}, bf16[64,512]{1,0:T(8,128)(2,1)S(1)}, u32[]{:S(2)}, u32[]{:S(2)}) collective-permute-start(bf16[64,512]{1,0:T(8,128)(2,1)S(1)} %get-tuple-element.81.refs_2_), channel_id=1, source_target_pairs={{0,1},{1,2},{2,3},{3,4},{4,5},{5,6},{6,7},{8,9},{9,10},{10,11},{11... | collective-permute-start | bytes 196616 | tf_op jit(solution)/shard_map/ppermute | solution.py:651
  11.9 3.6 %collective-permute-start.1 = (f32[2,8,1024]{2,1,0:T(8,128)S(1)}, f32[2,8,1024]{2,1,0:T(8,128)S(1)}, u32[]{:S(2)}, u32[]{:S(2)}) collective-permute-start(f32[2,8,1024]{2,1,0:T(8,128)S(1)} %get-tuple-element.84.refs_0_.refs_2_), channel_id=1, source_target_pairs={{0,1},{1,0},{2,3},{3,2},{4,5},{5,4},{6,7},{7,6},{8,9},{9,8},{10,11... | collective-permute-start | bytes 196616 | tf_op jit(solution)/shard_map/ppermute | solution.py:655
  15.5 7.8 %copy-start.1 = (bf16[512,2048]{1,0:T(8,128)(2,1)S(1)}, bf16[512,2048]{1,0:T(8,128)(2,1)}, u32[]{:S(2)}) copy-start(bf16[512,2048]{1,0:T(8,128)(2,1)} %refs_7_.1) | copy-start | bytes 6291460
  15.5 7.8 %copy-start.3 = (bf16[1024,512]{1,0:T(8,128)(2,1)S(1)}, bf16[1024,512]{1,0:T(8,128)(2,1)}, u32[]{:S(2)}) copy-start(bf16[1024,512]{1,0:T(8,128)(2,1)} %refs_6_.1) | copy-start | bytes 3145732
  15.5 7.8 %copy-start.5 = (f32[512]{0:T(512)S(1)}, f32[512]{0:T(512)}, u32[]{:S(2)}) copy-start(f32[512]{0:T(512)} %param.18) | copy-start | bytes 6148
  15.5 5.7 %collective-permute-start.4 = (f32[2,8,1024]{2,1,0:T(8,128)S(1)}, f32[2,8,1024]{2,1,0:T(8,128)S(1)}, u32[]{:S(2)}, u32[]{:S(2)}) collective-permute-start(f32[2,8,1024]{2,1,0:T(8,128)S(1)} %chip_totals.1.refs_2_), channel_id=1, source_target_pairs={{0,6},{1,7},{2,4},{3,5},{4,2},{5,3},{6,0},{7,1},{8,14},{9,15},{10,... | collective-permute-start | bytes 196616 | tf_op jit(solution)/shard_map/ppermute | solution.py:655
  18.3 4.3 %collective-permute-start.3 = (f32[2,8,1024]{2,1,0:T(8,128)S(1)}, f32[2,8,1024]{2,1,0:T(8,128)S(1)}, u32[]{:S(2)}, u32[]{:S(2)}) collective-permute-start(f32[2,8,1024]{2,1,0:T(8,128)S(1)} %chip_totals.1.refs_2_), channel_id=1, source_target_pairs={{0,4},{1,5},{2,6},{3,7},{4,0},{5,1},{6,2},{7,3},{8,12},{9,13},{10,... | collective-permute-start | bytes 196616 | tf_op jit(solution)/shard_map/ppermute | solution.py:655
  18.8 4.5 %collective-permute-start.2 = (f32[2,8,1024]{2,1,0:T(8,128)S(1)}, f32[2,8,1024]{2,1,0:T(8,128)S(1)}, u32[]{:S(2)}, u32[]{:S(2)}) collective-permute-start(f32[2,8,1024]{2,1,0:T(8,128)S(1)} %chip_totals.1.refs_2_), channel_id=1, source_target_pairs={{0,2},{1,3},{2,0},{3,1},{4,6},{5,7},{6,4},{7,5},{8,10},{9,11},{10,... | collective-permute-start | bytes 196616 | tf_op jit(solution)/shard_map/ppermute | solution.py:655
  36.4 10.9 %collective-permute-start.9 = (bf16[4,256,512]{2,1,0:T(8,128)(2,1)S(1)}, bf16[4,256,512]{2,1,0:T(8,128)(2,1)S(1)}, u32[]{:S(2)}, u32[]{:S(2)}) collective-permute-start(bf16[4,256,512]{2,1,0:T(8,128)(2,1)S(1)} %get-tuple-element.102), channel_id=1, source_target_pairs={{0,1},{1,0},{2,3},{3,2},{4,5},{5,4},{6,7},{7,6},{8,9},{9,8},{10,11... | collective-permute-start | bytes 3145736 | tf_op jit(solution)/shard_map/ppermute | solution.py:655
  36.5 10.8 %collective-permute-start.10 = (bf16[4,256,512]{2,1,0:T(8,128)(2,1)S(1)}, bf16[4,256,512]{2,1,0:T(8,128)(2,1)S(1)}, u32[]{:S(2)}, u32[]{:S(2)}) collective-permute-start(bf16[4,256,512]{2,1,0:T(8,128)(2,1)S(1)} %get-tuple-element.104), channel_id=1, source_target_pairs={{0,1},{1,0},{2,3},{3,2},{4,5},{5,4},{6,7},{7,6},{8,9},{9,8},{10,11... | collective-permute-start | bytes 3145736 | tf_op jit(solution)/shard_map/ppermute | solution.py:655
  42.3 1.5 %collective-permute-start.5 = (f32[8,1024]{1,0:T(8,128)S(1)}, f32[8,1024]{1,0:T(8,128)S(1)}, u32[]{:S(2)}, u32[]{:S(2)}) collective-permute-start(f32[8,1024]{1,0:T(8,128)S(1)} %get-tuple-element.95.refs_0_), channel_id=1, source_target_pairs={{0,1},{1,0},{2,3},{3,2},{4,5},{5,4},{6,7},{7,6},{8,9},{9,8},{10,11... | collective-permute-start | bytes 98312 | tf_op jit(solution)/shard_map/ppermute | solution.py:655
  43.8 7.3 %collective-permute-start.8 = (f32[8,1024]{1,0:T(8,128)S(1)}, f32[8,1024]{1,0:T(8,128)S(1)}, u32[]{:S(2)}, u32[]{:S(2)}) collective-permute-start(f32[8,1024]{1,0:T(8,128)S(1)} %chip_outgoing.1.refs_4_), channel_id=1, source_target_pairs={{0,6},{1,7},{2,4},{3,5},{4,2},{5,3},{6,0},{7,1},{8,14},{9,15},{10,... | collective-permute-start | bytes 98312 | tf_op jit(solution)/shard_map/ppermute | solution.py:655
  46.0 5.0 %collective-permute-start.7 = (f32[8,1024]{1,0:T(8,128)S(1)}, f32[8,1024]{1,0:T(8,128)S(1)}, u32[]{:S(2)}, u32[]{:S(2)}) collective-permute-start(f32[8,1024]{1,0:T(8,128)S(1)} %chip_outgoing.1.refs_4_), channel_id=1, source_target_pairs={{0,4},{1,5},{2,6},{3,7},{4,0},{5,1},{6,2},{7,3},{8,12},{9,13},{10,... | collective-permute-start | bytes 98312 | tf_op jit(solution)/shard_map/ppermute | solution.py:655
  46.1 5.0 %collective-permute-start.6 = (f32[8,1024]{1,0:T(8,128)S(1)}, f32[8,1024]{1,0:T(8,128)S(1)}, u32[]{:S(2)}, u32[]{:S(2)}) collective-permute-start(f32[8,1024]{1,0:T(8,128)S(1)} %chip_outgoing.1.refs_4_), channel_id=1, source_target_pairs={{0,2},{1,3},{2,0},{3,1},{4,6},{5,7},{6,4},{7,5},{8,10},{9,11},{10,... | collective-permute-start | bytes 98312 | tf_op jit(solution)/shard_map/ppermute | solution.py:655
  48.2 13.5 %collective-permute-start.15 = (bf16[2,256,512]{2,1,0:T(8,128)(2,1)S(1)}, bf16[2,256,512]{2,1,0:T(8,128)(2,1)S(1)}, u32[]{:S(2)}, u32[]{:S(2)}) collective-permute-start(bf16[2,256,512]{2,1,0:T(8,128)(2,1)S(1)} %get-tuple-element.114), channel_id=1, source_target_pairs={{0,4},{1,5},{2,6},{3,7},{4,0},{5,1},{6,2},{7,3},{8,12},{9,13},{10,... | collective-permute-start | bytes 1572872 | tf_op jit(solution)/shard_map/ppermute | solution.py:655
  49.6 13.2 %collective-permute-start.14 = (bf16[2,256,512]{2,1,0:T(8,128)(2,1)S(1)}, bf16[2,256,512]{2,1,0:T(8,128)(2,1)S(1)}, u32[]{:S(2)}, u32[]{:S(2)}) collective-permute-start(bf16[2,256,512]{2,1,0:T(8,128)(2,1)S(1)} %get-tuple-element.105.refs_16_), channel_id=1, source_target_pairs={{0,2},{1,3},{2,0},{3,1},{4,6},{5,7},{6,4},{7,5},{8,10},{9,11},{10,... | collective-permute-start | bytes 1572872 | tf_op jit(solution)/shard_map/ppermute | solution.py:655
  56.2 5.1 %collective-permute-start.11 = (bf16[64,512]{1,0:T(8,128)(2,1)S(1)}, bf16[64,512]{1,0:T(8,128)(2,1)S(1)}, u32[]{:S(2)}, u32[]{:S(2)}) collective-permute-start(bf16[64,512]{1,0:T(8,128)(2,1)S(1)} %get-tuple-element.108), channel_id=1, source_target_pairs={{1,0},{2,1},{3,2},{4,3},{5,4},{6,5},{7,6},{9,8},{10,9},{11,10},{12... | collective-permute-start | bytes 196616 | tf_op jit(solution)/shard_map/ppermute | solution.py:651
  57.5 7.5 %collective-permute-start.13 = (bf16[4,128,512]{2,1,0:T(8,128)(2,1)S(1)}, bf16[4,128,512]{2,1,0:T(8,128)(2,1)S(1)}, u32[]{:S(2)}, u32[]{:S(2)}) collective-permute-start(bf16[4,128,512]{2,1,0:T(8,128)(2,1)S(1)} %get-tuple-element.111), channel_id=1, source_target_pairs={{0,1},{1,0},{2,3},{3,2},{4,5},{5,4},{6,7},{7,6},{8,9},{9,8},{10,11... | collective-permute-start | bytes 1572872 | tf_op jit(solution)/shard_map/ppermute | solution.py:655
  58.7 6.3 %collective-permute-start.12 = (bf16[4,256,512]{2,1,0:T(8,128)(2,1)S(1)}, bf16[4,256,512]{2,1,0:T(8,128)(2,1)S(1)}, u32[]{:S(2)}, u32[]{:S(2)}) collective-permute-start(bf16[4,256,512]{2,1,0:T(8,128)(2,1)S(1)} %get-tuple-element.110), channel_id=1, source_target_pairs={{0,1},{1,0},{2,3},{3,2},{4,5},{5,4},{6,7},{7,6},{8,9},{9,8},{10,11... | collective-permute-start | bytes 3145736 | tf_op jit(solution)/shard_map/ppermute | solution.py:655
  63.2 9.2 %collective-permute-start.18 = (bf16[1,256,512]{2,1,0:T(8,128)(2,1)S(1)}, bf16[1,256,512]{2,1,0:T(8,128)(2,1)S(1)}, u32[]{:S(2)}, u32[]{:S(2)}) collective-permute-start(bf16[1,256,512]{2,1,0:T(8,128)(2,1)S(1)} %get-tuple-element.121), channel_id=1, source_target_pairs={{0,2},{1,3},{2,0},{3,1},{4,6},{5,7},{6,4},{7,5},{8,10},{9,11},{10,... | collective-permute-start | bytes 786440 | tf_op jit(solution)/shard_map/ppermute | solution.py:655
  64.7 9.2 %collective-permute-start.17 = (bf16[1,256,512]{2,1,0:T(8,128)(2,1)S(1)}, bf16[1,256,512]{2,1,0:T(8,128)(2,1)S(1)}, u32[]{:S(2)}, u32[]{:S(2)}) collective-permute-start(bf16[1,256,512]{2,1,0:T(8,128)(2,1)S(1)} %get-tuple-element.115.refs_4_), channel_id=1, source_target_pairs={{0,4},{1,5},{2,6},{3,7},{4,0},{5,1},{6,2},{7,3},{8,12},{9,13},{10,... | collective-permute-start | bytes 786440 | tf_op jit(solution)/shard_map/ppermute | solution.py:655
  65.7 16.1 %collective-permute-start.21 = (bf16[2,192,512]{2,1,0:T(8,128)(2,1)S(1)}, bf16[2,192,512]{2,1,0:T(8,128)(2,1)S(1)}, u32[]{:S(2)}, u32[]{:S(2)}) collective-permute-start(bf16[2,192,512]{2,1,0:T(8,128)(2,1)S(1)} %get-tuple-element.130), channel_id=1, source_target_pairs={{0,4},{1,5},{2,6},{3,7},{4,0},{5,1},{6,2},{7,3},{8,12},{9,13},{10,... | collective-permute-start | bytes 1179656 | tf_op jit(solution)/shard_map/ppermute | solution.py:655
  67.4 14.4 %collective-permute-start.19 = (bf16[2,192,512]{2,1,0:T(8,128)(2,1)S(1)}, bf16[2,192,512]{2,1,0:T(8,128)(2,1)S(1)}, u32[]{:S(2)}, u32[]{:S(2)}) collective-permute-start(bf16[2,192,512]{2,1,0:T(8,128)(2,1)S(1)} %get-tuple-element.116.refs_8_), channel_id=1, source_target_pairs={{0,2},{1,3},{2,0},{3,1},{4,6},{5,7},{6,4},{7,5},{8,10},{9,11},{10,... | collective-permute-start | bytes 1179656 | tf_op jit(solution)/shard_map/ppermute | solution.py:655
  74.1 7.5 %collective-permute-start.22 = (bf16[512,256]{1,0:T(8,128)(2,1)S(1)}, bf16[512,256]{1,0:T(8,128)(2,1)S(1)}, u32[]{:S(2)}, u32[]{:S(2)}) collective-permute-start(bf16[512,256]{1,0:T(8,128)(2,1)S(1)} %get-tuple-element.122.refs_2_), channel_id=1, source_target_pairs={{0,8},{8,0},{16,24},{24,16},{1,9},{9,1},{17,25},{25,17},{2,10},{10... | collective-permute-start | bytes 786440 | tf_op jit(solution)/shard_map/ppermute | solution.py:655
  75.8 1.3 %collective-permute-start.16 = (bf16[4,16,512]{2,1,0:T(8,128)(2,1)S(1)}, bf16[4,16,512]{2,1,0:T(8,128)(2,1)S(1)}, u32[]{:S(2)}, u32[]{:S(2)}) collective-permute-start(bf16[4,16,512]{2,1,0:T(8,128)(2,1)S(1)} %get-tuple-element.118), channel_id=1, source_target_pairs={{0,1},{1,0},{2,3},{3,2},{4,5},{5,4},{6,7},{7,6},{8,9},{9,8},{10,11... | collective-permute-start | bytes 196616 | tf_op jit(solution)/shard_map/ppermute | solution.py:655
  77.1 4.8 %collective-permute-start.20 = (bf16[2,16,512]{2,1,0:T(8,128)(2,1)S(1)}, bf16[2,16,512]{2,1,0:T(8,128)(2,1)S(1)}, u32[]{:S(2)}, u32[]{:S(2)}) collective-permute-start(bf16[2,16,512]{2,1,0:T(8,128)(2,1)S(1)} %get-tuple-element.123.refs_3_), channel_id=1, source_target_pairs={{0,2},{1,3},{2,0},{3,1},{4,6},{5,7},{6,4},{7,5},{8,10},{9,11},{10,... | collective-permute-start | bytes 98312 | tf_op jit(solution)/shard_map/ppermute | solution.py:655
  81.8 8.5 %copy-start.6 = (f32[512]{0:T(512)S(1)}, f32[512]{0:T(512)}, u32[]{:S(2)}) copy-start(f32[512]{0:T(512)} %param.13) | copy-start | bytes 6148
  82.2 7.2 %collective-permute-start.23 = (bf16[1,208,512]{2,1,0:T(8,128)(2,1)S(1)}, bf16[1,208,512]{2,1,0:T(8,128)(2,1)S(1)}, u32[]{:S(2)}, u32[]{:S(2)}) collective-permute-start(bf16[1,208,512]{2,1,0:T(8,128)(2,1)S(1)} %get-tuple-element.134), channel_id=1, source_target_pairs={{0,4},{1,5},{2,6},{3,7},{4,0},{5,1},{6,2},{7,3},{8,12},{9,13},{10,... | collective-permute-start | bytes 638984 | tf_op jit(solution)/shard_map/ppermute | solution.py:655
  82.9 6.4 %collective-permute-start.24 = (bf16[1,192,512]{2,1,0:T(8,128)(2,1)S(1)}, bf16[1,192,512]{2,1,0:T(8,128)(2,1)S(1)}, u32[]{:S(2)}, u32[]{:S(2)}) collective-permute-start(bf16[1,192,512]{2,1,0:T(8,128)(2,1)S(1)} %get-tuple-element.136.refs_4_), channel_id=1, source_target_pairs={{0,2},{1,3},{2,0},{3,1},{4,6},{5,7},{6,4},{7,5},{8,10},{9,11},{10,... | collective-permute-start | bytes 589832 | tf_op jit(solution)/shard_map/ppermute | solution.py:655
  84.1 14.0 %collective-permute-start.26 = (bf16[512,256]{1,0:T(8,128)(2,1)S(1)}, bf16[512,256]{1,0:T(8,128)(2,1)S(1)}, u32[]{:S(2)}, u32[]{:S(2)}) collective-permute-start(bf16[512,256]{1,0:T(8,128)(2,1)S(1)} %first_last.1.refs_6_.refs_0_), channel_id=1, source_target_pairs={{0,16},{8,24},{16,0},{24,8},{1,17},{9,25},{17,1},{25,9},{2,18},{10... | collective-permute-start | bytes 786440 | tf_op jit(solution)/shard_map/ppermute | solution.py:655
  89.6 11.5 %collective-permute-start.25 = (bf16[400,256]{1,0:T(8,128)(2,1)S(1)}, bf16[400,256]{1,0:T(8,128)(2,1)S(1)}, u32[]{:S(2)}, u32[]{:S(2)}) collective-permute-start(bf16[400,256]{1,0:T(8,128)(2,1)S(1)} %get-tuple-element.137.refs_4_), channel_id=1, source_target_pairs={{0,8},{8,0},{16,24},{24,16},{1,9},{9,1},{17,25},{25,17},{2,10},{10... | collective-permute-start | bytes 614408 | tf_op jit(solution)/shard_map/ppermute | solution.py:655
  101.2 10.0 %collective-permute-start.27 = (bf16[400,256]{1,0:T(8,128)(2,1)S(1)}, bf16[400,256]{1,0:T(8,128)(2,1)S(1)}, u32[]{:S(2)}, u32[]{:S(2)}) collective-permute-start(bf16[400,256]{1,0:T(8,128)(2,1)S(1)} %second_last.1.refs_0_.refs_2_), channel_id=1, source_target_pairs={{0,16},{8,24},{16,0},{24,8},{1,17},{9,25},{17,1},{25,9},{2,18},{10... | collective-permute-start | bytes 614408 | tf_op jit(solution)/shard_map/ppermute | solution.py:655
  101.3 11.3 %collective-permute-start.29 = (bf16[512,256]{1,0:T(8,128)(2,1)S(1)}, bf16[512,256]{1,0:T(8,128)(2,1)S(1)}, u32[]{:S(2)}, u32[]{:S(2)}) collective-permute-start(bf16[512,256]{1,0:T(8,128)(2,1)S(1)} %first_total.1.refs_2_.refs_0_), channel_id=1, source_target_pairs={{0,8},{8,0},{16,24},{24,16},{1,9},{9,1},{17,25},{25,17},{2,10},{10... | collective-permute-start | bytes 786440 | tf_op jit(solution)/shard_map/ppermute | solution.py:655
  111.4 6.4 %collective-permute-start.28 = (bf16[400,256]{1,0:T(8,128)(2,1)S(1)}, bf16[400,256]{1,0:T(8,128)(2,1)S(1)}, u32[]{:S(2)}, u32[]{:S(2)}) collective-permute-start(bf16[400,256]{1,0:T(8,128)(2,1)S(1)} %second_total.1.refs_2_.refs_0_), channel_id=1, source_target_pairs={{0,8},{8,0},{16,24},{24,16},{1,9},{9,1},{17,25},{25,17},{2,10},{10... | collective-permute-start | bytes 614408 | tf_op jit(solution)/shard_map/ppermute | solution.py:655

commit v3 on v2

--- a/solution.py
+++ b/solution.py
@@ -13,8 +13,8 @@
 SMALL = 16
 LANES = 128
 FINAL = ("result", "inputs", "first_finish", "second_finish")
-WORK = dict.fromkeys(("ingest", "prepare", "front", "forward", "first_seq", "back", "chip_outgoing"), 10**10)
-LIMITS = {"ingest": 2, "prepare": 3, "prepare_rest": 1, "front": 4, "forward": 3, "weights": 3, "reverse": 2, "back": 3, "gconv": 1, "taps": 5, "inputs": 5, "result": 4}
+WORK = {"second_join": 5 * 10**9, "result": 2000000000} | dict.fromkeys(("ingest", "prepare", "front", "forward", "first_seq", "back", "chip_outgoing"), 10**10)
+LIMITS = {"ingest": 2, "prepare": 3, "prepare_rest": 1, "front": 7, "forward": 6, "weights": 3, "reverse": 5, "back": 3, "gconv": 1, "taps": 5, "inputs": 5, "result": 4}
 F32 = jnp.float32
 BF16 = jnp.bfloat16
 GELU_C = 0.7978845608028654
@@ -788,7 +788,7 @@
         limit=LIMITS["prepare"],
     )
     conv_out, gate, cand, totals = order.call(
-        functools.partial(front_kernel, steps=64, block=512), "front",
+        functools.partial(front_kernel, steps=span, block=256), "front",
         [
             ((tokens, width), BF16), ((tokens, hidden), F32), ((tokens, hidden), F32),
             ((2, batch, hidden), F32),
@@ -808,7 +808,7 @@
         [((tokens, inner // 2), BF16)], [VMEM_SPEC] * 2, (gt, w_down), limit=LIMITS["prepare_rest"],
     )
     state_in, held, mid, nmid, act, gup = order.call(
-        functools.partial(forward_kernel, chips=chips, steps=64, block=512), "forward",
+        functools.partial(forward_kernel, chips=chips, steps=span, block=256), "forward",
         [
             ((batch, hidden), F32), ((tokens, hidden), BF16), ((tokens, width), F32),
             ((tokens, width), BF16), ((tokens, inner), BF16), ((tokens, inner), BF16),
@@ -824,7 +824,7 @@
     )
     come_up, come_down = swap(send_up, "seq", 0), swap(send_down, "seq", 0)
     gmid, gbranch, gheld, outgoing, gnorm2 = order.call(
-        functools.partial(reverse_kernel, steps=64), "reverse",
+        functools.partial(reverse_kernel, steps=span), "reverse",
         [
             ((tokens, width), F32), ((tokens, width), BF16), ((tokens, hidden), F32),
             ((batch, hidden), F32), ((1, width), F32),
@@ -902,8 +902,8 @@
         [VMEM_SPEC] * 3, (act, mid, w_down), [pltpu.VMEM((lanes, tokens, LANES), F32)],
         limit=LIMITS["result"],
     )
+    next(second)
     next(first)
-    next(second)
     next(second)
     (ginput,) = order.call(
         functools.partial(inputs_kernel, steps=16), "inputs", [((batch, span, width), F32)],

time: 119 us -> 116 us (0.975)
  waiting for transfers between devices: 31.7 us -> 25.6 us
  starting transfers between devices: 32.8 us -> 37.2 us
    ppermute x28, waiting for transfers between devices: 31.6 us -> 25.6 us  [swap_by(): lax.ppermute(block, axis, [(i, i ^ mask) for i in range(lax.axis_size(axi...]
    ppermute x28, starting transfers between devices: 29 us -> 33.4 us  [swap_by(): lax.ppermute(block, axis, [(i, i ^ mask) for i in range(lax.axis_size(axi...]
  transfers between devices with their start and end apart: 30 -> 30, of which waited for: 14 -> 15; matrix products, arithmetic and copies ran while one was open for 0% -> 0% of each run, Pallas kernels for 27% -> 28%
where the time goes in v3:
time: 116 us
  Pallas kernels  52.2 us (45%)
  starting transfers between devices  37.2 us (32%)
  waiting for transfers between devices  25.6 us (22%)
    pallas_call x28, Pallas kernels, call(): pl.pallas_call(body, name=name, out_shape=[(pltpu.HBM if name in FINAL an...  52.2 us
    ppermute x28, starting transfers between devices, swap_by(): lax.ppermute(block, axis, [(i, i ^ mask) for i in range(lax.axis_size(axi...  33.4 us
    ppermute x28, waiting for transfers between devices, swap_by(): lax.ppermute(block, axis, [(i, i ^ mask) for i in range(lax.axis_size(axi...  25.6 us
    ppermute x2, starting transfers between devices, shifted(): return lax.ppermute(block, axis, route)  3.78 us
  transfers between devices with their start and end apart: 30, of which 15 were waited for; matrix products, arithmetic and copies ran while one was open for 0% of the time, Pallas kernels for 28%

profile of v3, /device:TPU:0, one launch (start us, length us, event | category | flops | bytes accessed | tf_op | source)
XLA Modules:
  0.0 116.0 jit_solution(12271303337287900108)
XLA Ops:
  0.7 2.7 %ingest.1 = (f32[4,1024,128]{2,1,0:T(8,128)S(1)}, bf16[1024,512]{1,0:T(8,128)(2,1)S(1)}, bf16[64,512]{1,0:T(8,128)(2,1)S(1)}, f32[1024,128]{1,0:T(8,128)S(1)}) custom-call(bf16[8,128,512]{2,1,0:T(8,128)(2,1)} %refs_0_.2, s32[8,128]{1,0:T(8,128)} %refs_1_.4, f32[1,512]{1,0:T(1,128)} %bitcast.12), custom_call_target="tpu_custom_call" | custom-call | flops 10000000000 | bytes 1 | tf_op jit(solution)/shard_map/ingest/pallas_call | solution.py:633
  3.4 2.5 %collective-permute-start = (bf16[64,512]{1,0:T(8,128)(2,1)S(1)}, bf16[64,512]{1,0:T(8,128)(2,1)S(1)}, u32[]{:S(2)}, u32[]{:S(2)}) collective-permute-start(bf16[64,512]{1,0:T(8,128)(2,1)S(1)} %get-tuple-element.81.refs_2_), channel_id=1, source_target_pairs={{0,1},{1,2},{2,3},{3,4},{4,5},{5,6},{6,7},{8,9},{9,10},{10,11},{11... | collective-permute-start | bytes 196616 | tf_op jit(solution)/shard_map/ppermute | solution.py:651
  6.0 2.1 %prepare.1 = (bf16[1024,512]{1,0:T(8,128)(2,1)S(1)}, bf16[1024,1024]{1,0:T(8,128)(2,1)S(1)}) custom-call(bf16[8,128,512]{2,1,0:T(8,128)(2,1)S(1)} %copy-done.7, bf16[2048,512]{1,0:T(8,128)(2,1)S(1)} %copy-done, bf16[64,512]{1,0:T(8,128)(2,1)S(1)} %get-tuple-element.81.refs_2_), custom_call_target="tpu_custom_call" | custom-call | flops 10000000000 | bytes 1 | tf_op jit(solution)/shard_map/prepare/pallas_call | solution.py:633
  8.1 3.5 %front.1 = (bf16[1024,512]{1,0:T(8,128)(2,1)S(1)}, f32[1024,1024]{1,0:T(8,128)S(1)}, f32[1024,1024]{1,0:T(8,128)S(1)}, f32[2,8,1024]{2,1,0:T(8,128)S(1)}) custom-call(bf16[1024,512]{1,0:T(8,128)(2,1)S(1)} %get-tuple-element.80.refs_0_.refs_3_, bf16[64,512]{1,0:T(8,128)(2,1)S(1)} %collective-permute-done.refs_1_.refs_4_, ...), custom_call_target="tpu_custom_call" | custom-call | flops 10000000000 | bytes 1 | tf_op jit(solution)/shard_map/front/pallas_call | solution.py:633
  11.6 2.7 %collective-permute-start.1 = (f32[2,8,1024]{2,1,0:T(8,128)S(1)}, f32[2,8,1024]{2,1,0:T(8,128)S(1)}, u32[]{:S(2)}, u32[]{:S(2)}) collective-permute-start(f32[2,8,1024]{2,1,0:T(8,128)S(1)} %get-tuple-element.84.refs_0_.refs_2_), channel_id=1, source_target_pairs={{0,1},{1,0},{2,3},{3,2},{4,5},{5,4},{6,7},{7,6},{8,9},{9,8},{10,11... | collective-permute-start | bytes 196616 | tf_op jit(solution)/shard_map/ppermute | solution.py:655
  14.2 0.9 collective-permute-done.1.refs_1_.refs_0_.refs_3_.refs_6_
  15.2 2.8 %collective-permute-start.4 = (f32[2,8,1024]{2,1,0:T(8,128)S(1)}, f32[2,8,1024]{2,1,0:T(8,128)S(1)}, u32[]{:S(2)}, u32[]{:S(2)}) collective-permute-start(f32[2,8,1024]{2,1,0:T(8,128)S(1)} %chip_totals.1.refs_2_), channel_id=1, source_target_pairs={{0,6},{1,7},{2,4},{3,5},{4,2},{5,3},{6,0},{7,1},{8,14},{9,15},{10,... | collective-permute-start | bytes 196616 | tf_op jit(solution)/shard_map/ppermute | solution.py:655
  18.0 0.5 collective-permute-start.3
  18.5 0.9 collective-permute-start.2
  19.4 1.5 %prepare_rest.1.refs_9_.refs_13_ = bf16[1024,1024]{1,0:T(8,128)(2,1)S(1)} custom-call(bf16[1024,512]{1,0:T(8,128)(2,1)S(1)} %get-tuple-element.83.refs_6_.refs_0_.refs_3_.refs_2_, bf16[2048,512]{1,0:T(8,128)(2,1)S(1)} %copy-done, f32[2,8,1024]{2,1,0:T(8,128)S(1)} %chip_totals.1.refs_2_), custom_call_target="tpu_custom_call" | custom-call | flops 1 | bytes 1 | tf_op jit(solution)/shard_map/prepare_rest/pallas_call | solution.py:633
  20.9 1.3 %collective-permute-done.3.refs_2_.refs_1_ = f32[2,8,1024]{2,1,0:T(8,128)S(1)} collective-permute-done((f32[2,8,1024]{2,1,0:T(8,128)S(1)}, f32[2,8,1024]{2,1,0:T(8,128)S(1)}, u32[]{:S(2)}, u32[]{:S(2)}) %collective-permute-start.3) | collective-permute-done | bytes 65568 | tf_op jit(solution)/shard_map/ppermute | solution.py:655
  22.2 0.7 collective-permute-done.2.refs_1_.refs_0_
  22.9 8.0 %forward.1 = (f32[8,1024]{1,0:T(8,128)S(1)}, bf16[1024,1024]{1,0:T(8,128)(2,1)S(1)}, f32[1024,512]{1,0:T(8,128)S(1)}, bf16[1024,512]{1,0:T(8,128)(2,1)S(1)}, bf1...) custom-call(f32[2,8,1024]{2,1,0:T(8,128)S(1)} %collective-permute-done.1.refs_1_.refs_0_.refs_3_.refs_6_, ...), custom_call_target="tpu_custom_call" | custom-call | flops 10000000000 | bytes 1 | tf_op jit(solution)/shard_map/forward/pallas_call | solution.py:633
  30.9 4.6 %weights.1 = (bf16[4,256,512]{2,1,0:T(8,128)(2,1)S(1)}, bf16[4,256,512]{2,1,0:T(8,128)(2,1)S(1)}, bf16[4,256,512]{2,1,0:T(8,128)(2,1)S(1)}, bf16[4,256,512]{2,1,0:T(8,128)(2,1)S(1)}) custom-call(bf16[1024,512]{1,0:T(8,128)(2,1)S(1)} %get-tuple-element.92.refs_0_, bf16[1024,2048]{1,0:T(8,128)(2,1)S(1)} %get-tuple-element.91.refs_1_.refs_0_, ...), custom_call_target="tpu_custom_call" | custom-call | flops 1 | bytes 1 | tf_op jit(solution)/shard_map/weights/pallas_call | solution.py:633
  35.6 0.5 collective-permute-start.10
  36.1 5.1 %reverse.1 = (f32[1024,512]{1,0:T(8,128)S(1)}, bf16[1024,512]{1,0:T(8,128)(2,1)S(1)}, f32[1024,1024]{1,0:T(8,128)S(1)}, f32[8,1024]{1,0:T(8,128)S(1)}, f32[1,512]{1,0:T(1,128)S(1)}) custom-call(bf16[1024,2048]{1,0:T(8,128)(2,1)S(1)} %get-tuple-element.91.refs_1_.refs_0_, f32[1024,512]{1,0:T(8,128)S(1)} %get-tuple-element.90.refs_1_, ...), custom_call_target="tpu_custom_call" | custom-call | flops 1 | bytes 1 | tf_op jit(solution)/shard_map/reverse/pallas_call | solution.py:633
  41.3 1.3 %weights_out.1 = (bf16[4,128,512]{2,1,0:T(8,128)(2,1)S(1)}, bf16[4,128,512]{2,1,0:T(8,128)(2,1)S(1)}) custom-call(bf16[1024,1024]{1,0:T(8,128)(2,1)S(1)} %get-tuple-element.96.refs_0_.refs_12_, bf16[1024,512]{1,0:T(8,128)(2,1)S(1)} %get-tuple-element.97.refs_1_, f32[1,512]{1,0:T(1,128)S(1)} %get-tuple-element.98.refs_2_.refs_6_), custom_call_target="tpu_custom_call" | custom-call | flops 1 | bytes 1 | tf_op jit(solution)/shard_map/weights_out/pallas_call | solution.py:633
  42.7 2.3 %collective-permute-start.8 = (f32[8,1024]{1,0:T(8,128)S(1)}, f32[8,1024]{1,0:T(8,128)S(1)}, u32[]{:S(2)}, u32[]{:S(2)}) collective-permute-start(f32[8,1024]{1,0:T(8,128)S(1)} %chip_outgoing.1.refs_4_), channel_id=1, source_target_pairs={{0,6},{1,7},{2,4},{3,5},{4,2},{5,3},{6,0},{7,1},{8,14},{9,15},{10,... | collective-permute-start | bytes 98312 | tf_op jit(solution)/shard_map/ppermute | solution.py:655
  44.9 1.3 %collective-permute-start.6 = (f32[8,1024]{1,0:T(8,128)S(1)}, f32[8,1024]{1,0:T(8,128)S(1)}, u32[]{:S(2)}, u32[]{:S(2)}) collective-permute-start(f32[8,1024]{1,0:T(8,128)S(1)} %chip_outgoing.1.refs_4_), channel_id=1, source_target_pairs={{0,2},{1,3},{2,0},{3,1},{4,6},{5,7},{6,4},{7,5},{8,10},{9,11},{10,... | collective-permute-start | bytes 98312 | tf_op jit(solution)/shard_map/ppermute | solution.py:655
  46.2 0.9 first_core.1
  47.1 1.4 %collective-permute-start.15 = (bf16[2,256,512]{2,1,0:T(8,128)(2,1)S(1)}, bf16[2,256,512]{2,1,0:T(8,128)(2,1)S(1)}, u32[]{:S(2)}, u32[]{:S(2)}) collective-permute-start(bf16[2,256,512]{2,1,0:T(8,128)(2,1)S(1)} %get-tuple-element.114), channel_id=1, source_target_pairs={{0,4},{1,5},{2,6},{3,7},{4,0},{5,1},{6,2},{7,3},{8,12},{9,13},{10,... | collective-permute-start | bytes 1572872 | tf_op jit(solution)/shard_map/ppermute | solution.py:655
  48.5 1.4 %collective-permute-start.14 = (bf16[2,256,512]{2,1,0:T(8,128)(2,1)S(1)}, bf16[2,256,512]{2,1,0:T(8,128)(2,1)S(1)}, u32[]{:S(2)}, u32[]{:S(2)}) collective-permute-start(bf16[2,256,512]{2,1,0:T(8,128)(2,1)S(1)} %get-tuple-element.105.refs_16_), channel_id=1, source_target_pairs={{0,2},{1,3},{2,0},{3,1},{4,6},{5,7},{6,4},{7,5},{8,10},{9,11},{10,... | collective-permute-start | bytes 1572872 | tf_op jit(solution)/shard_map/ppermute | solution.py:655
  49.9 5.2 %back.1 = (bf16[1024,2048]{1,0:T(8,128)(2,1)S(1)}, f32[1,1024]{1,0:T(1,128)S(1)}, bf16[64,512]{1,0:T(8,128)(2,1)S(1)}, bf16[4,256,512]{2,1,0:T(8,128)(2,1)S(1)}, bf16[4,256,512]{2,1,0:T(8,128)(2,1)S(1)}) custom-call(f32[2,8,1024]{2,1,0:T(8,128)S(1)} %collective-permute-done.2.refs_1_.refs_0_, f32[2,8,1024]{2,1,0:T(8,128)S(1)} %collective-permute-done.3.refs_2_.refs_1_, ...), custom_call_target="tpu_custom_call" | custom-call | flops 10000000000 | bytes 1 | tf_op jit(solution)/shard_map/back/pallas_call | solution.py:633
  55.2 1.3 %collective-permute-start.11 = (bf16[64,512]{1,0:T(8,128)(2,1)S(1)}, bf16[64,512]{1,0:T(8,128)(2,1)S(1)}, u32[]{:S(2)}, u32[]{:S(2)}) collective-permute-start(bf16[64,512]{1,0:T(8,128)(2,1)S(1)} %get-tuple-element.108), channel_id=1, source_target_pairs={{1,0},{2,1},{3,2},{4,3},{5,4},{6,5},{7,6},{9,8},{10,9},{11,10},{12... | collective-permute-start | bytes 196616 | tf_op jit(solution)/shard_map/ppermute | solution.py:651
  56.5 1.2 %collective-permute-start.12 = (bf16[4,256,512]{2,1,0:T(8,128)(2,1)S(1)}, bf16[4,256,512]{2,1,0:T(8,128)(2,1)S(1)}, u32[]{:S(2)}, u32[]{:S(2)}) collective-permute-start(bf16[4,256,512]{2,1,0:T(8,128)(2,1)S(1)} %get-tuple-element.110), channel_id=1, source_target_pairs={{0,1},{1,0},{2,3},{3,2},{4,5},{5,4},{6,7},{7,6},{8,9},{9,8},{10,11... | collective-permute-start | bytes 3145736 | tf_op jit(solution)/shard_map/ppermute | solution.py:655
  57.7 2.6 %gconv.1.refs_4_.refs_0_ = bf16[1024,512]{1,0:T(8,128)(2,1)S(1)} custom-call(bf16[1024,2048]{1,0:T(8,128)(2,1)S(1)} %get-tuple-element.106.refs_0_, bf16[512,2048]{1,0:T(8,128)(2,1)S(1)} %copy-done.2, f32[1,1024]{1,0:T(1,128)S(1)} %get-tuple-element.107.refs_2_.refs_7_), custom_call_target="tpu_custom_call" | custom-call | flops 1 | bytes 1 | tf_op jit(solution)/shard_map/gconv/pallas_call | solution.py:633
  60.3 0.3 collective-permute-done.15.refs_3_
  60.6 1.0 collective-permute-done.14.refs_1_
  61.7 0.4 first_seq.1
  62.0 1.5 %collective-permute-start.18 = (bf16[1,256,512]{2,1,0:T(8,128)(2,1)S(1)}, bf16[1,256,512]{2,1,0:T(8,128)(2,1)S(1)}, u32[]{:S(2)}, u32[]{:S(2)}) collective-permute-start(bf16[1,256,512]{2,1,0:T(8,128)(2,1)S(1)} %get-tuple-element.121), channel_id=1, source_target_pairs={{0,2},{1,3},{2,0},{3,1},{4,6},{5,7},{6,4},{7,5},{8,10},{9,11},{10,... | collective-permute-start | bytes 786440 | tf_op jit(solution)/shard_map/ppermute | solution.py:655
  63.5 0.4 collective-permute-start.17
  63.9 0.7 second_core.1
  64.6 1.7 %collective-permute-start.21 = (bf16[2,192,512]{2,1,0:T(8,128)(2,1)S(1)}, bf16[2,192,512]{2,1,0:T(8,128)(2,1)S(1)}, u32[]{:S(2)}, u32[]{:S(2)}) collective-permute-start(bf16[2,192,512]{2,1,0:T(8,128)(2,1)S(1)} %get-tuple-element.130), channel_id=1, source_target_pairs={{0,4},{1,5},{2,6},{3,7},{4,0},{5,1},{6,2},{7,3},{8,12},{9,13},{10,... | collective-permute-start | bytes 1179656 | tf_op jit(solution)/shard_map/ppermute | solution.py:655
  66.3 0.6 collective-permute-start.19
  66.9 2.8 %taps.1 = (f32[1024,512]{1,0:T(8,128)S(1)}, bf16[4,16,512]{2,1,0:T(8,128)(2,1)S(1)}, bf16[4,16,512]{2,1,0:T(8,128)(2,1)S(1)}) custom-call(bf16[1024,512]{1,0:T(8,128)(2,1)S(1)} %gconv.1.refs_4_.refs_0_, bf16[64,512]{1,0:T(8,128)(2,1)S(1)} %collective-permute-done.11.refs_5_.refs_1_, f32[4,1024,128]{2,1,0:T(8,128)S(1)} %get-tuple-element.85.refs_4_.refs_2_.refs_1_, ...), custom_call_target="tpu_custom_call" | custom-call | flops 1 | bytes 1 | tf_op jit(solution)/shard_map/taps/pallas_call | solution.py:633
  69.8 1.4 %collective-permute-done.18.refs_3_ = bf16[1,256,512]{2,1,0:T(8,128)(2,1)S(1)} collective-permute-done((bf16[1,256,512]{2,1,0:T(8,128)(2,1)S(1)}, bf16[1,256,512]{2,1,0:T(8,128)(2,1)S(1)}, u32[]{:S(2)}, u32[]{:S(2)}) %collective-permute-start.18) | collective-permute-done | bytes 262176 | tf_op jit(solution)/shard_map/ppermute | solution.py:655
  71.2 1.5 %collective-permute-done.17.refs_1_ = bf16[1,256,512]{2,1,0:T(8,128)(2,1)S(1)} collective-permute-done((bf16[1,256,512]{2,1,0:T(8,128)(2,1)S(1)}, bf16[1,256,512]{2,1,0:T(8,128)(2,1)S(1)}, u32[]{:S(2)}, u32[]{:S(2)}) %collective-permute-start.17) | collective-permute-done | bytes 262176 | tf_op jit(solution)/shard_map/ppermute | solution.py:655
  72.7 0.3 first_join.1
  73.0 1.7 %collective-permute-start.24 = (bf16[512,256]{1,0:T(8,128)(2,1)S(1)}, bf16[512,256]{1,0:T(8,128)(2,1)S(1)}, u32[]{:S(2)}, u32[]{:S(2)}) collective-permute-start(bf16[512,256]{1,0:T(8,128)(2,1)S(1)} %get-tuple-element.122.refs_2_), channel_id=1, source_target_pairs={{0,8},{8,0},{16,24},{24,16},{1,9},{9,1},{17,25},{25,17},{2,10},{10... | collective-permute-start | bytes 786440 | tf_op jit(solution)/shard_map/ppermute | solution.py:655
  74.7 0.6 collective-permute-start.20
  75.3 3.9 %result.1 = (bf16[8,128,512]{2,1,0:T(8,128)(2,1)}, f32[8,128]{1,0:T(8,128)S(1)}) custom-call(bf16[1024,2048]{1,0:T(8,128)(2,1)S(1)} %get-tuple-element.89.refs_2_.refs_0_, f32[1024,512]{1,0:T(8,128)S(1)} %get-tuple-element.90.refs_1_, bf16[2048,512]{1,0:T(8,128)(2,1)S(1)} %copy-done, bf16[2,16,512]{2,1,0:T(8,128)(2,1)S(1)} %get-tuple-element.123.refs_3_), custom_call_target="tpu_custom_call" | custom-call | flops 2000000000 | bytes 1 | tf_op jit(solution)/shard_map/result/pallas_call | solution.py:633
  79.2 0.8 collective-permute-done.20.refs_3_
  80.0 0.2 collective-permute-done.21.refs_5_
  80.2 0.3 second_seq.1
  80.5 0.5 collective-permute-start.22
  81.0 1.0 collective-permute-start.23
  82.1 0.2 first_last.1.refs_4_.refs_0_
  82.3 2.6 %collective-permute-start.26 = (bf16[512,256]{1,0:T(8,128)(2,1)S(1)}, bf16[512,256]{1,0:T(8,128)(2,1)S(1)}, u32[]{:S(2)}, u32[]{:S(2)}) collective-permute-start(bf16[512,256]{1,0:T(8,128)(2,1)S(1)} %first_last.1.refs_4_.refs_0_), channel_id=1, source_target_pairs={{0,16},{8,24},{16,0},{24,8},{1,17},{9,25},{17,1},{25,9},{2,18},{10... | collective-permute-start | bytes 786440 | tf_op jit(solution)/shard_map/ppermute | solution.py:655
  84.9 2.4 %collective-permute-done.23.refs_3_ = bf16[1,192,512]{2,1,0:T(8,128)(2,1)S(1)} collective-permute-done((bf16[1,192,512]{2,1,0:T(8,128)(2,1)S(1)}, bf16[1,192,512]{2,1,0:T(8,128)(2,1)S(1)}, u32[]{:S(2)}, u32[]{:S(2)}) %collective-permute-start.23) | collective-permute-done | bytes 196640 | tf_op jit(solution)/shard_map/ppermute | solution.py:655
  87.3 0.2 second_join.1
  87.6 1.6 %collective-permute-start.25 = (bf16[400,256]{1,0:T(8,128)(2,1)S(1)}, bf16[400,256]{1,0:T(8,128)(2,1)S(1)}, u32[]{:S(2)}, u32[]{:S(2)}) collective-permute-start(bf16[400,256]{1,0:T(8,128)(2,1)S(1)} %get-tuple-element.137.refs_4_), channel_id=1, source_target_pairs={{0,8},{8,0},{16,24},{24,16},{1,9},{9,1},{17,25},{25,17},{2,10},{10... | collective-permute-start | bytes 614408 | tf_op jit(solution)/shard_map/ppermute | solution.py:655
  89.2 3.6 %inputs.1 = (f32[8,128,512]{2,1,0:T(8,128)}, f32[8,128]{1,0:T(8,128)S(1)}) custom-call(f32[1024,512]{1,0:T(8,128)S(1)} %get-tuple-element.125.refs_0_, f32[4,1024,128]{2,1,0:T(8,128)S(1)} %get-tuple-element.85.refs_4_.refs_2_.refs_1_, f32[1024,512]{1,0:T(8,128)S(1)} %get-tuple-element.126.refs_2_, f32[1,512]{1,0:T(1,128)S(1)} %bitcast.13, ...), custom_call_target="tpu_custom_call" | custom-call | flops 1 | bytes 1 | tf_op jit(solution)/shard_map/inputs/pallas_call | solution.py:633
  92.8 3.3 %collective-permute-done.26.refs_1_ = bf16[512,256]{1,0:T(8,128)(2,1)S(1)} collective-permute-done((bf16[512,256]{1,0:T(8,128)(2,1)S(1)}, bf16[512,256]{1,0:T(8,128)(2,1)S(1)}, u32[]{:S(2)}, u32[]{:S(2)}) %collective-permute-start.26) | collective-permute-done | bytes 262176 | tf_op jit(solution)/shard_map/ppermute | solution.py:655
  96.1 0.2 first_total.1.refs_2_.refs_0_
  96.2 1.5 %collective-permute-done.25.refs_1_ = bf16[400,256]{1,0:T(8,128)(2,1)S(1)} collective-permute-done((bf16[400,256]{1,0:T(8,128)(2,1)S(1)}, bf16[400,256]{1,0:T(8,128)(2,1)S(1)}, u32[]{:S(2)}, u32[]{:S(2)}) %collective-permute-start.25) | collective-permute-done | bytes 204832 | tf_op jit(solution)/shard_map/ppermute | solution.py:655
  97.8 0.2 second_last.1.refs_0_.refs_2_
  98.0 2.6 %collective-permute-start.27 = (bf16[400,256]{1,0:T(8,128)(2,1)S(1)}, bf16[400,256]{1,0:T(8,128)(2,1)S(1)}, u32[]{:S(2)}, u32[]{:S(2)}) collective-permute-start(bf16[400,256]{1,0:T(8,128)(2,1)S(1)} %second_last.1.refs_0_.refs_2_), channel_id=1, source_target_pairs={{0,16},{8,24},{16,0},{24,8},{1,17},{9,25},{17,1},{25,9},{2,18},{10... | collective-permute-start | bytes 614408 | tf_op jit(solution)/shard_map/ppermute | solution.py:655
  100.6 2.5 %collective-permute-start.29 = (bf16[512,256]{1,0:T(8,128)(2,1)S(1)}, bf16[512,256]{1,0:T(8,128)(2,1)S(1)}, u32[]{:S(2)}, u32[]{:S(2)}) collective-permute-start(bf16[512,256]{1,0:T(8,128)(2,1)S(1)} %first_total.1.refs_2_.refs_0_), channel_id=1, source_target_pairs={{0,8},{8,0},{16,24},{24,16},{1,9},{9,1},{17,25},{25,17},{2,10},{10... | collective-permute-start | bytes 786440 | tf_op jit(solution)/shard_map/ppermute | solution.py:655
  103.0 6.1 %collective-permute-done.27.refs_1_ = bf16[400,256]{1,0:T(8,128)(2,1)S(1)} collective-permute-done((bf16[400,256]{1,0:T(8,128)(2,1)S(1)}, bf16[400,256]{1,0:T(8,128)(2,1)S(1)}, u32[]{:S(2)}, u32[]{:S(2)}) %collective-permute-start.27) | collective-permute-done | bytes 204832 | tf_op jit(solution)/shard_map/ppermute | solution.py:655
  109.3 0.7 collective-permute-start.28
  110.0 0.4 collective-permute-done.29.refs_1_
  110.4 1.0 first_finish.1
  111.5 3.6 %collective-permute-done.28.refs_1_ = bf16[400,256]{1,0:T(8,128)(2,1)S(1)} collective-permute-done((bf16[400,256]{1,0:T(8,128)(2,1)S(1)}, bf16[400,256]{1,0:T(8,128)(2,1)S(1)}, u32[]{:S(2)}, u32[]{:S(2)}) %collective-permute-start.28) | collective-permute-done | bytes 204832 | tf_op jit(solution)/shard_map/ppermute | solution.py:655
  115.1 0.9 second_finish.1
  (42 shorter events, 0.6 us)
Async XLA Ops:
  0.6 5.3 %copy-start = (bf16[2048,512]{1,0:T(8,128)(2,1)S(1)}, bf16[2048,512]{1,0:T(8,128)(2,1)}, u32[]{:S(2)}) copy-start(bf16[2048,512]{1,0:T(8,128)(2,1)} %refs_2_.1) | copy-start | bytes 6291460
  0.7 5.3 %copy-start.7 = (bf16[8,128,512]{2,1,0:T(8,128)(2,1)S(1)}, bf16[8,128,512]{2,1,0:T(8,128)(2,1)}, u32[]{:S(2)}) copy-start(bf16[8,128,512]{2,1,0:T(8,128)(2,1)} %refs_0_.3) | copy-start | bytes 3145732
  3.4 4.7 %copy-start.2 = (bf16[512,2048]{1,0:T(8,128)(2,1)S(1)}, bf16[512,2048]{1,0:T(8,128)(2,1)}, u32[]{:S(2)}) copy-start(bf16[512,2048]{1,0:T(8,128)(2,1)} %refs_1_.7) | copy-start | bytes 6291460
  3.4 4.7 %copy-start.4 = (f32[512,4]{0,1:T(4,128)S(1)}, f32[512,4]{0,1:T(4,128)}, u32[]{:S(2)}) copy-start(f32[512,4]{0,1:T(4,128)} %param.14) | copy-start | bytes 24580
  3.4 4.7 %copy-start.8 = (f32[1024]{0:T(1024)S(1)}, f32[1024]{0:T(1024)}, u32[]{:S(2)}) copy-start(f32[1024]{0:T(1024)} %param.15) | copy-start | bytes 12292
  3.4 4.6 %collective-permute-start = (bf16[64,512]{1,0:T(8,128)(2,1)S(1)}, bf16[64,512]{1,0:T(8,128)(2,1)S(1)}, u32[]{:S(2)}, u32[]{:S(2)}) collective-permute-start(bf16[64,512]{1,0:T(8,128)(2,1)S(1)} %get-tuple-element.81.refs_2_), channel_id=1, source_target_pairs={{0,1},{1,2},{2,3},{3,4},{4,5},{5,6},{6,7},{8,9},{9,10},{10,11},{11... | collective-permute-start | bytes 196616 | tf_op jit(solution)/shard_map/ppermute | solution.py:651
  11.6 3.6 %collective-permute-start.1 = (f32[2,8,1024]{2,1,0:T(8,128)S(1)}, f32[2,8,1024]{2,1,0:T(8,128)S(1)}, u32[]{:S(2)}, u32[]{:S(2)}) collective-permute-start(f32[2,8,1024]{2,1,0:T(8,128)S(1)} %get-tuple-element.84.refs_0_.refs_2_), channel_id=1, source_target_pairs={{0,1},{1,0},{2,3},{3,2},{4,5},{5,4},{6,7},{7,6},{8,9},{9,8},{10,11... | collective-permute-start | bytes 196616 | tf_op jit(solution)/shard_map/ppermute | solution.py:655
  15.1 7.8 %copy-start.1 = (bf16[512,2048]{1,0:T(8,128)(2,1)S(1)}, bf16[512,2048]{1,0:T(8,128)(2,1)}, u32[]{:S(2)}) copy-start(bf16[512,2048]{1,0:T(8,128)(2,1)} %refs_7_.1) | copy-start | bytes 6291460
  15.2 7.8 %copy-start.3 = (bf16[1024,512]{1,0:T(8,128)(2,1)S(1)}, bf16[1024,512]{1,0:T(8,128)(2,1)}, u32[]{:S(2)}) copy-start(bf16[1024,512]{1,0:T(8,128)(2,1)} %refs_6_.1) | copy-start | bytes 3145732
  15.2 7.8 %copy-start.5 = (f32[512]{0:T(512)S(1)}, f32[512]{0:T(512)}, u32[]{:S(2)}) copy-start(f32[512]{0:T(512)} %param.18) | copy-start | bytes 6148
  15.2 5.7 %collective-permute-start.4 = (f32[2,8,1024]{2,1,0:T(8,128)S(1)}, f32[2,8,1024]{2,1,0:T(8,128)S(1)}, u32[]{:S(2)}, u32[]{:S(2)}) collective-permute-start(f32[2,8,1024]{2,1,0:T(8,128)S(1)} %chip_totals.1.refs_2_), channel_id=1, source_target_pairs={{0,6},{1,7},{2,4},{3,5},{4,2},{5,3},{6,0},{7,1},{8,14},{9,15},{10,... | collective-permute-start | bytes 196616 | tf_op jit(solution)/shard_map/ppermute | solution.py:655
  18.0 4.3 %collective-permute-start.3 = (f32[2,8,1024]{2,1,0:T(8,128)S(1)}, f32[2,8,1024]{2,1,0:T(8,128)S(1)}, u32[]{:S(2)}, u32[]{:S(2)}) collective-permute-start(f32[2,8,1024]{2,1,0:T(8,128)S(1)} %chip_totals.1.refs_2_), channel_id=1, source_target_pairs={{0,4},{1,5},{2,6},{3,7},{4,0},{5,1},{6,2},{7,3},{8,12},{9,13},{10,... | collective-permute-start | bytes 196616 | tf_op jit(solution)/shard_map/ppermute | solution.py:655
  18.5 4.5 %collective-permute-start.2 = (f32[2,8,1024]{2,1,0:T(8,128)S(1)}, f32[2,8,1024]{2,1,0:T(8,128)S(1)}, u32[]{:S(2)}, u32[]{:S(2)}) collective-permute-start(f32[2,8,1024]{2,1,0:T(8,128)S(1)} %chip_totals.1.refs_2_), channel_id=1, source_target_pairs={{0,2},{1,3},{2,0},{3,1},{4,6},{5,7},{6,4},{7,5},{8,10},{9,11},{10,... | collective-permute-start | bytes 196616 | tf_op jit(solution)/shard_map/ppermute | solution.py:655
  35.5 10.7 %collective-permute-start.9 = (bf16[4,256,512]{2,1,0:T(8,128)(2,1)S(1)}, bf16[4,256,512]{2,1,0:T(8,128)(2,1)S(1)}, u32[]{:S(2)}, u32[]{:S(2)}) collective-permute-start(bf16[4,256,512]{2,1,0:T(8,128)(2,1)S(1)} %get-tuple-element.102), channel_id=1, source_target_pairs={{0,1},{1,0},{2,3},{3,2},{4,5},{5,4},{6,7},{7,6},{8,9},{9,8},{10,11... | collective-permute-start | bytes 3145736 | tf_op jit(solution)/shard_map/ppermute | solution.py:655
  35.6 10.6 %collective-permute-start.10 = (bf16[4,256,512]{2,1,0:T(8,128)(2,1)S(1)}, bf16[4,256,512]{2,1,0:T(8,128)(2,1)S(1)}, u32[]{:S(2)}, u32[]{:S(2)}) collective-permute-start(bf16[4,256,512]{2,1,0:T(8,128)(2,1)S(1)} %get-tuple-element.104), channel_id=1, source_target_pairs={{0,1},{1,0},{2,3},{3,2},{4,5},{5,4},{6,7},{7,6},{8,9},{9,8},{10,11... | collective-permute-start | bytes 3145736 | tf_op jit(solution)/shard_map/ppermute | solution.py:655
  41.2 1.4 %collective-permute-start.5 = (f32[8,1024]{1,0:T(8,128)S(1)}, f32[8,1024]{1,0:T(8,128)S(1)}, u32[]{:S(2)}, u32[]{:S(2)}) collective-permute-start(f32[8,1024]{1,0:T(8,128)S(1)} %get-tuple-element.95.refs_0_), channel_id=1, source_target_pairs={{0,1},{1,0},{2,3},{3,2},{4,5},{5,4},{6,7},{7,6},{8,9},{9,8},{10,11... | collective-permute-start | bytes 98312 | tf_op jit(solution)/shard_map/ppermute | solution.py:655
  42.7 7.3 %collective-permute-start.8 = (f32[8,1024]{1,0:T(8,128)S(1)}, f32[8,1024]{1,0:T(8,128)S(1)}, u32[]{:S(2)}, u32[]{:S(2)}) collective-permute-start(f32[8,1024]{1,0:T(8,128)S(1)} %chip_outgoing.1.refs_4_), channel_id=1, source_target_pairs={{0,6},{1,7},{2,4},{3,5},{4,2},{5,3},{6,0},{7,1},{8,14},{9,15},{10,... | collective-permute-start | bytes 98312 | tf_op jit(solution)/shard_map/ppermute | solution.py:655
  44.9 5.0 %collective-permute-start.7 = (f32[8,1024]{1,0:T(8,128)S(1)}, f32[8,1024]{1,0:T(8,128)S(1)}, u32[]{:S(2)}, u32[]{:S(2)}) collective-permute-start(f32[8,1024]{1,0:T(8,128)S(1)} %chip_outgoing.1.refs_4_), channel_id=1, source_target_pairs={{0,4},{1,5},{2,6},{3,7},{4,0},{5,1},{6,2},{7,3},{8,12},{9,13},{10,... | collective-permute-start | bytes 98312 | tf_op jit(solution)/shard_map/ppermute | solution.py:655
  44.9 5.0 %collective-permute-start.6 = (f32[8,1024]{1,0:T(8,128)S(1)}, f32[8,1024]{1,0:T(8,128)S(1)}, u32[]{:S(2)}, u32[]{:S(2)}) collective-permute-start(f32[8,1024]{1,0:T(8,128)S(1)} %chip_outgoing.1.refs_4_), channel_id=1, source_target_pairs={{0,2},{1,3},{2,0},{3,1},{4,6},{5,7},{6,4},{7,5},{8,10},{9,11},{10,... | collective-permute-start | bytes 98312 | tf_op jit(solution)/shard_map/ppermute | solution.py:655
  47.1 13.5 %collective-permute-start.15 = (bf16[2,256,512]{2,1,0:T(8,128)(2,1)S(1)}, bf16[2,256,512]{2,1,0:T(8,128)(2,1)S(1)}, u32[]{:S(2)}, u32[]{:S(2)}) collective-permute-start(bf16[2,256,512]{2,1,0:T(8,128)(2,1)S(1)} %get-tuple-element.114), channel_id=1, source_target_pairs={{0,4},{1,5},{2,6},{3,7},{4,0},{5,1},{6,2},{7,3},{8,12},{9,13},{10,... | collective-permute-start | bytes 1572872 | tf_op jit(solution)/shard_map/ppermute | solution.py:655
  48.5 13.2 %collective-permute-start.14 = (bf16[2,256,512]{2,1,0:T(8,128)(2,1)S(1)}, bf16[2,256,512]{2,1,0:T(8,128)(2,1)S(1)}, u32[]{:S(2)}, u32[]{:S(2)}) collective-permute-start(bf16[2,256,512]{2,1,0:T(8,128)(2,1)S(1)} %get-tuple-element.105.refs_16_), channel_id=1, source_target_pairs={{0,2},{1,3},{2,0},{3,1},{4,6},{5,7},{6,4},{7,5},{8,10},{9,11},{10,... | collective-permute-start | bytes 1572872 | tf_op jit(solution)/shard_map/ppermute | solution.py:655
  55.2 5.1 %collective-permute-start.11 = (bf16[64,512]{1,0:T(8,128)(2,1)S(1)}, bf16[64,512]{1,0:T(8,128)(2,1)S(1)}, u32[]{:S(2)}, u32[]{:S(2)}) collective-permute-start(bf16[64,512]{1,0:T(8,128)(2,1)S(1)} %get-tuple-element.108), channel_id=1, source_target_pairs={{1,0},{2,1},{3,2},{4,3},{5,4},{6,5},{7,6},{9,8},{10,9},{11,10},{12... | collective-permute-start | bytes 196616 | tf_op jit(solution)/shard_map/ppermute | solution.py:651
  56.5 7.4 %collective-permute-start.12 = (bf16[4,256,512]{2,1,0:T(8,128)(2,1)S(1)}, bf16[4,256,512]{2,1,0:T(8,128)(2,1)S(1)}, u32[]{:S(2)}, u32[]{:S(2)}) collective-permute-start(bf16[4,256,512]{2,1,0:T(8,128)(2,1)S(1)} %get-tuple-element.110), channel_id=1, source_target_pairs={{0,1},{1,0},{2,3},{3,2},{4,5},{5,4},{6,7},{7,6},{8,9},{9,8},{10,11... | collective-permute-start | bytes 3145736 | tf_op jit(solution)/shard_map/ppermute | solution.py:655
  57.7 6.2 %collective-permute-start.13 = (bf16[4,128,512]{2,1,0:T(8,128)(2,1)S(1)}, bf16[4,128,512]{2,1,0:T(8,128)(2,1)S(1)}, u32[]{:S(2)}, u32[]{:S(2)}) collective-permute-start(bf16[4,128,512]{2,1,0:T(8,128)(2,1)S(1)} %get-tuple-element.111), channel_id=1, source_target_pairs={{0,1},{1,0},{2,3},{3,2},{4,5},{5,4},{6,7},{7,6},{8,9},{9,8},{10,11... | collective-permute-start | bytes 1572872 | tf_op jit(solution)/shard_map/ppermute | solution.py:655
  62.0 9.2 %collective-permute-start.18 = (bf16[1,256,512]{2,1,0:T(8,128)(2,1)S(1)}, bf16[1,256,512]{2,1,0:T(8,128)(2,1)S(1)}, u32[]{:S(2)}, u32[]{:S(2)}) collective-permute-start(bf16[1,256,512]{2,1,0:T(8,128)(2,1)S(1)} %get-tuple-element.121), channel_id=1, source_target_pairs={{0,2},{1,3},{2,0},{3,1},{4,6},{5,7},{6,4},{7,5},{8,10},{9,11},{10,... | collective-permute-start | bytes 786440 | tf_op jit(solution)/shard_map/ppermute | solution.py:655
  63.5 9.2 %collective-permute-start.17 = (bf16[1,256,512]{2,1,0:T(8,128)(2,1)S(1)}, bf16[1,256,512]{2,1,0:T(8,128)(2,1)S(1)}, u32[]{:S(2)}, u32[]{:S(2)}) collective-permute-start(bf16[1,256,512]{2,1,0:T(8,128)(2,1)S(1)} %get-tuple-element.115.refs_4_), channel_id=1, source_target_pairs={{0,4},{1,5},{2,6},{3,7},{4,0},{5,1},{6,2},{7,3},{8,12},{9,13},{10,... | collective-permute-start | bytes 786440 | tf_op jit(solution)/shard_map/ppermute | solution.py:655
  64.6 15.6 %collective-permute-start.21 = (bf16[2,192,512]{2,1,0:T(8,128)(2,1)S(1)}, bf16[2,192,512]{2,1,0:T(8,128)(2,1)S(1)}, u32[]{:S(2)}, u32[]{:S(2)}) collective-permute-start(bf16[2,192,512]{2,1,0:T(8,128)(2,1)S(1)} %get-tuple-element.130), channel_id=1, source_target_pairs={{0,4},{1,5},{2,6},{3,7},{4,0},{5,1},{6,2},{7,3},{8,12},{9,13},{10,... | collective-permute-start | bytes 1179656 | tf_op jit(solution)/shard_map/ppermute | solution.py:655
  66.3 13.9 %collective-permute-start.19 = (bf16[2,192,512]{2,1,0:T(8,128)(2,1)S(1)}, bf16[2,192,512]{2,1,0:T(8,128)(2,1)S(1)}, u32[]{:S(2)}, u32[]{:S(2)}) collective-permute-start(bf16[2,192,512]{2,1,0:T(8,128)(2,1)S(1)} %get-tuple-element.116.refs_8_), channel_id=1, source_target_pairs={{0,2},{1,3},{2,0},{3,1},{4,6},{5,7},{6,4},{7,5},{8,10},{9,11},{10,... | collective-permute-start | bytes 1179656 | tf_op jit(solution)/shard_map/ppermute | solution.py:655
  69.7 5.0 %collective-permute-start.16 = (bf16[4,16,512]{2,1,0:T(8,128)(2,1)S(1)}, bf16[4,16,512]{2,1,0:T(8,128)(2,1)S(1)}, u32[]{:S(2)}, u32[]{:S(2)}) collective-permute-start(bf16[4,16,512]{2,1,0:T(8,128)(2,1)S(1)} %get-tuple-element.118), channel_id=1, source_target_pairs={{0,1},{1,0},{2,3},{3,2},{4,5},{5,4},{6,7},{7,6},{8,9},{9,8},{10,11... | collective-permute-start | bytes 196616 | tf_op jit(solution)/shard_map/ppermute | solution.py:655
  73.0 9.1 %collective-permute-start.24 = (bf16[512,256]{1,0:T(8,128)(2,1)S(1)}, bf16[512,256]{1,0:T(8,128)(2,1)S(1)}, u32[]{:S(2)}, u32[]{:S(2)}) collective-permute-start(bf16[512,256]{1,0:T(8,128)(2,1)S(1)} %get-tuple-element.122.refs_2_), channel_id=1, source_target_pairs={{0,8},{8,0},{16,24},{24,16},{1,9},{9,1},{17,25},{25,17},{2,10},{10... | collective-permute-start | bytes 786440 | tf_op jit(solution)/shard_map/ppermute | solution.py:655
  74.7 5.3 %collective-permute-start.20 = (bf16[2,16,512]{2,1,0:T(8,128)(2,1)S(1)}, bf16[2,16,512]{2,1,0:T(8,128)(2,1)S(1)}, u32[]{:S(2)}, u32[]{:S(2)}) collective-permute-start(bf16[2,16,512]{2,1,0:T(8,128)(2,1)S(1)} %get-tuple-element.123.refs_3_), channel_id=1, source_target_pairs={{0,2},{1,3},{2,0},{3,1},{4,6},{5,7},{6,4},{7,5},{8,10},{9,11},{10,... | collective-permute-start | bytes 98312 | tf_op jit(solution)/shard_map/ppermute | solution.py:655
  80.5 6.8 %collective-permute-start.22 = (bf16[1,208,512]{2,1,0:T(8,128)(2,1)S(1)}, bf16[1,208,512]{2,1,0:T(8,128)(2,1)S(1)}, u32[]{:S(2)}, u32[]{:S(2)}) collective-permute-start(bf16[1,208,512]{2,1,0:T(8,128)(2,1)S(1)} %get-tuple-element.133), channel_id=1, source_target_pairs={{0,4},{1,5},{2,6},{3,7},{4,0},{5,1},{6,2},{7,3},{8,12},{9,13},{10,... | collective-permute-start | bytes 638984 | tf_op jit(solution)/shard_map/ppermute | solution.py:655
  81.0 6.3 %collective-permute-start.23 = (bf16[1,192,512]{2,1,0:T(8,128)(2,1)S(1)}, bf16[1,192,512]{2,1,0:T(8,128)(2,1)S(1)}, u32[]{:S(2)}, u32[]{:S(2)}) collective-permute-start(bf16[1,192,512]{2,1,0:T(8,128)(2,1)S(1)} %get-tuple-element.135.refs_2_), channel_id=1, source_target_pairs={{0,2},{1,3},{2,0},{3,1},{4,6},{5,7},{6,4},{7,5},{8,10},{9,11},{10,... | collective-permute-start | bytes 589832 | tf_op jit(solution)/shard_map/ppermute | solution.py:655
  82.3 13.8 %collective-permute-start.26 = (bf16[512,256]{1,0:T(8,128)(2,1)S(1)}, bf16[512,256]{1,0:T(8,128)(2,1)S(1)}, u32[]{:S(2)}, u32[]{:S(2)}) collective-permute-start(bf16[512,256]{1,0:T(8,128)(2,1)S(1)} %first_last.1.refs_4_.refs_0_), channel_id=1, source_target_pairs={{0,16},{8,24},{16,0},{24,8},{1,17},{9,25},{17,1},{25,9},{2,18},{10... | collective-permute-start | bytes 786440 | tf_op jit(solution)/shard_map/ppermute | solution.py:655
  87.3 1.9 %copy-start.6 = (f32[512]{0:T(512)S(1)}, f32[512]{0:T(512)}, u32[]{:S(2)}) copy-start(f32[512]{0:T(512)} %param.13) | copy-start | bytes 6148
  87.6 10.2 %collective-permute-start.25 = (bf16[400,256]{1,0:T(8,128)(2,1)S(1)}, bf16[400,256]{1,0:T(8,128)(2,1)S(1)}, u32[]{:S(2)}, u32[]{:S(2)}) collective-permute-start(bf16[400,256]{1,0:T(8,128)(2,1)S(1)} %get-tuple-element.137.refs_4_), channel_id=1, source_target_pairs={{0,8},{8,0},{16,24},{24,16},{1,9},{9,1},{17,25},{25,17},{2,10},{10... | collective-permute-start | bytes 614408 | tf_op jit(solution)/shard_map/ppermute | solution.py:655
  98.0 11.2 %collective-permute-start.27 = (bf16[400,256]{1,0:T(8,128)(2,1)S(1)}, bf16[400,256]{1,0:T(8,128)(2,1)S(1)}, u32[]{:S(2)}, u32[]{:S(2)}) collective-permute-start(bf16[400,256]{1,0:T(8,128)(2,1)S(1)} %second_last.1.refs_0_.refs_2_), channel_id=1, source_target_pairs={{0,16},{8,24},{16,0},{24,8},{1,17},{9,25},{17,1},{25,9},{2,18},{10... | collective-permute-start | bytes 614408 | tf_op jit(solution)/shard_map/ppermute | solution.py:655
  100.6 9.9 %collective-permute-start.29 = (bf16[512,256]{1,0:T(8,128)(2,1)S(1)}, bf16[512,256]{1,0:T(8,128)(2,1)S(1)}, u32[]{:S(2)}, u32[]{:S(2)}) collective-permute-start(bf16[512,256]{1,0:T(8,128)(2,1)S(1)} %first_total.1.refs_2_.refs_0_), channel_id=1, source_target_pairs={{0,8},{8,0},{16,24},{24,16},{1,9},{9,1},{17,25},{25,17},{2,10},{10... | collective-permute-start | bytes 786440 | tf_op jit(solution)/shard_map/ppermute | solution.py:655
  109.3 5.8 %collective-permute-start.28 = (bf16[400,256]{1,0:T(8,128)(2,1)S(1)}, bf16[400,256]{1,0:T(8,128)(2,1)S(1)}, u32[]{:S(2)}, u32[]{:S(2)}) collective-permute-start(bf16[400,256]{1,0:T(8,128)(2,1)S(1)} %second_total.1.refs_2_.refs_0_), channel_id=1, source_target_pairs={{0,8},{8,0},{16,24},{24,16},{1,9},{9,1},{17,25},{25,17},{2,10},{10... | collective-permute-start | bytes 614408 | tf_op jit(solution)/shard_map/ppermute | solution.py:655

commit v4 on v3

--- a/solution.py
+++ b/solution.py
@@ -14,7 +14,7 @@
 LANES = 128
 FINAL = ("result", "inputs", "first_finish", "second_finish")
 WORK = {"second_join": 5 * 10**9, "result": 2000000000} | dict.fromkeys(("ingest", "prepare", "front", "forward", "first_seq", "back", "chip_outgoing"), 10**10)
-LIMITS = {"ingest": 2, "prepare": 3, "prepare_rest": 1, "front": 7, "forward": 6, "weights": 3, "reverse": 5, "back": 3, "gconv": 1, "taps": 5, "inputs": 5, "result": 4}
+LIMITS = {"ingest": 4, "prepare": 6, "prepare_rest": 3, "front": 7, "forward": 6, "weights": 3, "reverse": 5, "back": 3, "gconv": 3, "taps": 5, "inputs": 7, "result": 7}
 F32 = jnp.float32
 BF16 = jnp.bfloat16
 GELU_C = 0.7978845608028654
@@ -150,7 +150,7 @@
 
 
 def front_kernel(
-    normed_ref, halo_ref, keep_ref, taps_ref, bias_ref, w_ref,
+    normed_ref, inside_ref, across_ref, keep_ref, taps_ref, bias_ref, w_ref,
     conv_ref, gate_ref, cand_ref, total_ref, norm_buf,
     *, steps, block,
 ):
@@ -159,7 +159,7 @@
     span = tokens // batch
     size = steps * batch
     lead = EDGE * batch
-    norm_buf[:lead, :] = halo_ref[...].astype(F32)
+    norm_buf[:lead, :] = pick_edge(inside_ref[...], across_ref[...], False)
 
     def chunk(index, carry):
         rows = rows_of(index, size)
@@ -506,7 +506,7 @@
 
 
 def taps_kernel(
-    gconv_ref, after_ref, xt_ref, normed_ref, halo_ref, taps_ref, gnorm2_ref, gbias_ref,
+    gconv_ref, after_ref, ahead_ref, xt_ref, normed_ref, halo_ref, across_ref, taps_ref, gnorm2_ref, gbias_ref,
     gnormed_ref, stay_ref, send_ref, norm_buf, gconv_buf,
     *, steps,
 ):
@@ -514,8 +514,8 @@
     batch = halo_ref.shape[0] // EDGE
     size = steps * batch
     lead = EDGE * batch
-    norm_buf[:lead, :] = halo_ref[...].astype(F32)
-    gconv_buf[tokens : tokens + after_ref.shape[0], :] = after_ref[...].astype(F32)
+    norm_buf[:lead, :] = pick_edge(halo_ref[...], across_ref[...], False)
+    gconv_buf[tokens : tokens + after_ref.shape[0], :] = pick_edge(after_ref[...], ahead_ref[...], True)
 
     def spread(index, carry):
         rows = rows_of(index, size)
@@ -645,10 +645,19 @@
     )(*args)
 
 
-def shifted(block, axis, distance):
-    devices = range(lax.axis_size(axis))
-    route = [(i - distance, i) for i in devices if i - distance in devices]
-    return lax.ppermute(block, axis, route)
+def neighbour(block, axis):
+    count = lax.axis_size(axis)
+    inside = swap_by(block, axis, 1)
+    across = lax.ppermute(block, axis, [(i, (i + 1 if i % 2 else i - 1) % count) for i in range(count)])
+    return inside, across
+
+
+def pick_edge(inside, across, ahead):
+    place = lax.axis_index("seq")
+    end = lax.axis_size("seq") - 1 if ahead else 0
+    odd = bit_of("seq", 0) == 1
+    value = jnp.where(odd != ahead, inside.astype(F32), across.astype(F32))
+    return jnp.where(place == end, jnp.zeros_like(value), value)
 
 
 def swap_by(block, axis, mask):
@@ -767,7 +776,7 @@
     order = Order()
 
     xt, normed, edge, keep = order.call(
-        functools.partial(ingest_kernel, steps=16), "ingest",
+        functools.partial(ingest_kernel, steps=span), "ingest",
         [
             ((lanes, tokens, LANES), F32), ((tokens, width), BF16), ((EDGE * batch, width), BF16),
             ((tokens, LANES), F32),
@@ -780,9 +789,9 @@
         ],
         limit=LIMITS["ingest"],
     )
-    halo = shifted(edge, "seq", 1)
+    halo = neighbour(edge, "seq")
     gt, gact = order.call(
-        functools.partial(prepare_kernel, steps=64, block=512), "prepare",
+        functools.partial(prepare_kernel, steps=span, block=256), "prepare",
         [((tokens, width), BF16), ((tokens, inner // 2), BF16)],
         [VMEM_SPEC] * 2, (out_grad, w_down), [pltpu.VMEM((lanes, tokens, LANES), F32)],
         limit=LIMITS["prepare"],
@@ -793,7 +802,7 @@
             ((tokens, width), BF16), ((tokens, hidden), F32), ((tokens, hidden), F32),
             ((2, batch, hidden), F32),
         ],
-        [VMEM_SPEC] * 6, (normed, halo, keep, taps, bias, w_in),
+        [VMEM_SPEC] * 7, (normed, *halo, keep, taps, bias, w_in),
         [pltpu.VMEM((tokens + EDGE * batch, width), F32)],
         limit=LIMITS["front"],
     )
@@ -804,7 +813,7 @@
     )
     all_totals = [swap_by(chip_totals, "seq", 2 * mask) for mask in range(1, chips)]
     (more,) = order.call(
-        functools.partial(prepare_rest_kernel, size=512, block=512), "prepare_rest",
+        functools.partial(prepare_rest_kernel, size=tokens, block=256), "prepare_rest",
         [((tokens, inner // 2), BF16)], [VMEM_SPEC] * 2, (gt, w_down), limit=LIMITS["prepare_rest"],
     )
     state_in, held, mid, nmid, act, gup = order.call(
@@ -860,13 +869,13 @@
         ),
         limit=LIMITS["back"],
     )
-    after = shifted(gconv_edge, "seq", -1)
+    after = neighbour(gconv_edge, "seq")
     come_in = swap(send_in, "seq", 0)
     (gconv,) = order.call(
-        functools.partial(gconv_kernel, steps=64), "gconv", [((tokens, width), BF16)],
+        functools.partial(gconv_kernel, steps=span), "gconv", [((tokens, width), BF16)],
         [VMEM_SPEC] * 2, (gproj, w_in), limit=LIMITS["gconv"],
     )
-    order.last = (*order.last, after)
+    order.last = (*order.last, *after)
     late = []
     share = width // seq_count
     second = spread_sum(
@@ -878,11 +887,10 @@
         late,
     )
     next(first)
-    next(second)
     gnormed, stay_small, send_small = order.call(
         functools.partial(taps_kernel, steps=16), "taps",
-        [((tokens, width), F32)] + [((pairs, SMALL, width), BF16)] * 2, [VMEM_SPEC] * 8,
-        (gconv, after, xt, normed, halo, taps, gnorm2, gbias),
+        [((tokens, width), F32)] + [((pairs, SMALL, width), BF16)] * 2, [VMEM_SPEC] * 10,
+        (gconv, *after, xt, normed, *halo, taps, gnorm2, gbias),
         [
             pltpu.VMEM((tokens + EDGE * batch, width), F32),
             pltpu.VMEM((tokens + EDGE * batch, width), F32),
@@ -890,6 +898,7 @@
         limit=LIMITS["taps"],
     )
     come_small = swap(send_small, "seq", 0)
+    next(second)
     next(first)
     stay_small, send_small = order.call(
         functools.partial(split_sum_kernel, plan=((0, 0),), counts=(1,)), "small",
@@ -898,7 +907,7 @@
     )
     late += [stay_small, swap(send_small, "seq", 1)]
     (result,) = order.call(
-        functools.partial(result_kernel, steps=64), "result", [((batch, span, width), BF16)],
+        functools.partial(result_kernel, steps=span), "result", [((batch, span, width), BF16)],
         [VMEM_SPEC] * 3, (act, mid, w_down), [pltpu.VMEM((lanes, tokens, LANES), F32)],
         limit=LIMITS["result"],
     )
@@ -906,7 +915,7 @@
     next(first)
     next(second)
     (ginput,) = order.call(
-        functools.partial(inputs_kernel, steps=16), "inputs", [((batch, span, width), F32)],
+        functools.partial(inputs_kernel, steps=64), "inputs", [((batch, span, width), F32)],
         [VMEM_SPEC] * 4, (gnormed, xt, gmid, gain1), [pltpu.VMEM((lanes, tokens, LANES), F32)],
         limit=LIMITS["inputs"],
     )

time: 116 us -> 114 us (0.983)
  Pallas kernels: 52.2 us -> 49.4 us
  waiting for transfers between devices: 25.6 us -> 28.3 us
  starting transfers between devices: 37.2 us -> 34.6 us
    ppermute x2, waiting for transfers between devices: 0.01 us -> 3.85 us  [neighbour(): lax.ppermute(block, axis, [(i, (i + 1 if i % 2 else i - 1) % count) for i...]
    pallas_call x28, Pallas kernels: 52.2 us -> 49.4 us  [call(): pl.pallas_call(body, name=name, out_shape=[(pltpu.HBM if name in FINAL an...]
    ppermute x28 -> x30, starting transfers between devices: 33.4 us -> 31 us  [swap_by(): lax.ppermute(block, axis, [(i, i ^ mask) for i in range(lax.axis_size(axi...]
    ppermute x28 -> x30, waiting for transfers between devices: 25.6 us -> 24.5 us  [swap_by(): lax.ppermute(block, axis, [(i, i ^ mask) for i in range(lax.axis_size(axi...]
  transfers between devices with their start and end apart: 30 -> 32, of which waited for: 15 -> 15; matrix products, arithmetic and copies ran while one was open for 0% -> 0% of each run, Pallas kernels for 28% -> 27%
where the time goes in v4:
time: 114 us; the launch traced here: 113 us
  Pallas kernels  49.4 us (43%)
  starting transfers between devices  34.6 us (30%)
  waiting for transfers between devices  28.3 us (25%)
    pallas_call x28, Pallas kernels, call(): pl.pallas_call(body, name=name, out_shape=[(pltpu.HBM if name in FINAL an...  49.4 us
    ppermute x30, starting transfers between devices, swap_by(): lax.ppermute(block, axis, [(i, i ^ mask) for i in range(lax.axis_size(axi...  31 us
    ppermute x30, waiting for transfers between devices, swap_by(): lax.ppermute(block, axis, [(i, i ^ mask) for i in range(lax.axis_size(axi...  24.5 us
    ppermute x2, waiting for transfers between devices, neighbour(): lax.ppermute(block, axis, [(i, (i + 1 if i % 2 else i - 1) % count) for i...  3.85 us
    ppermute x2, starting transfers between devices, neighbour(): lax.ppermute(block, axis, [(i, (i + 1 if i % 2 else i - 1) % count) for i...  3.67 us
  transfers between devices with their start and end apart: 32, of which 15 were waited for; matrix products, arithmetic and copies ran while one was open for 0% of the time, Pallas kernels for 27%

profile of v4, /device:TPU:0, one launch (start us, length us, event | category | flops | bytes accessed | tf_op | source)
XLA Modules:
  0.0 113.4 jit_solution(14038028411094536223)
XLA Ops:
  0.7 2.1 %ingest.1 = (f32[4,1024,128]{2,1,0:T(8,128)S(1)}, bf16[1024,512]{1,0:T(8,128)(2,1)S(1)}, bf16[64,512]{1,0:T(8,128)(2,1)S(1)}, f32[1024,128]{1,0:T(8,128)S(1)}) custom-call(bf16[8,128,512]{2,1,0:T(8,128)(2,1)} %refs_0_.2, s32[8,128]{1,0:T(8,128)} %refs_1_.4, f32[1,512]{1,0:T(1,128)} %bitcast.12), custom_call_target="tpu_custom_call" | custom-call | flops 10000000000 | bytes 1 | tf_op jit(solution)/shard_map/ingest/pallas_call | solution.py:633
  2.8 3.4 %collective-permute-start.1 = (bf16[64,512]{1,0:T(8,128)(2,1)S(1)}, bf16[64,512]{1,0:T(8,128)(2,1)S(1)}, u32[]{:S(2)}, u32[]{:S(2)}) collective-permute-start(bf16[64,512]{1,0:T(8,128)(2,1)S(1)} %get-tuple-element.81.refs_2_), channel_id=1, source_target_pairs={{0,7},{1,2},{2,1},{3,4},{4,3},{5,6},{6,5},{7,0},{8,15},{9,10},{10,... | collective-permute-start | bytes 196616 | tf_op jit(solution)/shard_map/ppermute | solution.py:651
  6.3 1.4 %prepare.1 = (bf16[1024,512]{1,0:T(8,128)(2,1)S(1)}, bf16[1024,1024]{1,0:T(8,128)(2,1)S(1)}) custom-call(bf16[8,128,512]{2,1,0:T(8,128)(2,1)S(1)} %copy-done.7, bf16[2048,512]{1,0:T(8,128)(2,1)S(1)} %copy-done, bf16[64,512]{1,0:T(8,128)(2,1)S(1)} %get-tuple-element.81.refs_2_), custom_call_target="tpu_custom_call" | custom-call | flops 10000000000 | bytes 1 | tf_op jit(solution)/shard_map/prepare/pallas_call | solution.py:633
  7.6 0.6 collective-permute-done.1.refs_2_.refs_6_
  8.2 3.5 %front.1 = (bf16[1024,512]{1,0:T(8,128)(2,1)S(1)}, f32[1024,1024]{1,0:T(8,128)S(1)}, f32[1024,1024]{1,0:T(8,128)S(1)}, f32[2,8,1024]{2,1,0:T(8,128)S(1)}) custom-call(bf16[1024,512]{1,0:T(8,128)(2,1)S(1)} %get-tuple-element.80.refs_0_.refs_4_, bf16[64,512]{1,0:T(8,128)(2,1)S(1)} %collective-permute-done.refs_1_.refs_5_, ...), custom_call_target="tpu_custom_call" | custom-call | flops 10000000000 | bytes 1 | tf_op jit(solution)/shard_map/front/pallas_call | solution.py:633
  11.8 1.2 %collective-permute-done.2.refs_1_.refs_0_.refs_3_.refs_6_ = f32[2,8,1024]{2,1,0:T(8,128)S(1)} collective-permute-done((f32[2,8,1024]{2,1,0:T(8,128)S(1)}, f32[2,8,1024]{2,1,0:T(8,128)S(1)}, u32[]{:S(2)}, u32[]{:S(2)}) %collective-permute-start.2) | collective-permute-done | bytes 65568 | tf_op jit(solution)/shard_map/ppermute | solution.py:664
  13.1 3.0 %collective-permute-start.5 = (f32[2,8,1024]{2,1,0:T(8,128)S(1)}, f32[2,8,1024]{2,1,0:T(8,128)S(1)}, u32[]{:S(2)}, u32[]{:S(2)}) collective-permute-start(f32[2,8,1024]{2,1,0:T(8,128)S(1)} %chip_totals.1.refs_2_), channel_id=1, source_target_pairs={{0,6},{1,7},{2,4},{3,5},{4,2},{5,3},{6,0},{7,1},{8,14},{9,15},{10,... | collective-permute-start | bytes 196616 | tf_op jit(solution)/shard_map/ppermute | solution.py:664
  16.1 0.9 collective-permute-start.4
  17.0 1.3 %prepare_rest.1.refs_9_.refs_13_ = bf16[1024,1024]{1,0:T(8,128)(2,1)S(1)} custom-call(bf16[1024,512]{1,0:T(8,128)(2,1)S(1)} %get-tuple-element.83.refs_7_.refs_0_.refs_3_.refs_2_, bf16[2048,512]{1,0:T(8,128)(2,1)S(1)} %copy-done, f32[2,8,1024]{2,1,0:T(8,128)S(1)} %chip_totals.1.refs_2_), custom_call_target="tpu_custom_call" | custom-call | flops 1 | bytes 1 | tf_op jit(solution)/shard_map/prepare_rest/pallas_call | solution.py:633
  18.3 0.3 collective-permute-done.5.refs_3_.refs_2_
  18.6 1.8 %collective-permute-done.4.refs_2_.refs_1_ = f32[2,8,1024]{2,1,0:T(8,128)S(1)} collective-permute-done((f32[2,8,1024]{2,1,0:T(8,128)S(1)}, f32[2,8,1024]{2,1,0:T(8,128)S(1)}, u32[]{:S(2)}, u32[]{:S(2)}) %collective-permute-start.4) | collective-permute-done | bytes 65568 | tf_op jit(solution)/shard_map/ppermute | solution.py:664
  20.4 0.9 collective-permute-done.3.refs_1_.refs_0_
  21.2 8.0 %forward.1 = (f32[8,1024]{1,0:T(8,128)S(1)}, bf16[1024,1024]{1,0:T(8,128)(2,1)S(1)}, f32[1024,512]{1,0:T(8,128)S(1)}, bf16[1024,512]{1,0:T(8,128)(2,1)S(1)}, bf1...) custom-call(f32[2,8,1024]{2,1,0:T(8,128)S(1)} %collective-permute-done.2.refs_1_.refs_0_.refs_3_.refs_6_, ...), custom_call_target="tpu_custom_call" | custom-call | flops 10000000000 | bytes 1 | tf_op jit(solution)/shard_map/forward/pallas_call | solution.py:633
  29.2 4.6 %weights.1 = (bf16[4,256,512]{2,1,0:T(8,128)(2,1)S(1)}, bf16[4,256,512]{2,1,0:T(8,128)(2,1)S(1)}, bf16[4,256,512]{2,1,0:T(8,128)(2,1)S(1)}, bf16[4,256,512]{2,1,0:T(8,128)(2,1)S(1)}) custom-call(bf16[1024,512]{1,0:T(8,128)(2,1)S(1)} %get-tuple-element.92.refs_0_, bf16[1024,2048]{1,0:T(8,128)(2,1)S(1)} %get-tuple-element.91.refs_1_.refs_0_, ...), custom_call_target="tpu_custom_call" | custom-call | flops 1 | bytes 1 | tf_op jit(solution)/shard_map/weights/pallas_call | solution.py:633
  33.9 0.5 collective-permute-start.11
  34.4 5.1 %reverse.1 = (f32[1024,512]{1,0:T(8,128)S(1)}, bf16[1024,512]{1,0:T(8,128)(2,1)S(1)}, f32[1024,1024]{1,0:T(8,128)S(1)}, f32[8,1024]{1,0:T(8,128)S(1)}, f32[1,512]{1,0:T(1,128)S(1)}) custom-call(bf16[1024,2048]{1,0:T(8,128)(2,1)S(1)} %get-tuple-element.91.refs_1_.refs_0_, f32[1024,512]{1,0:T(8,128)S(1)} %get-tuple-element.90.refs_1_, ...), custom_call_target="tpu_custom_call" | custom-call | flops 1 | bytes 1 | tf_op jit(solution)/shard_map/reverse/pallas_call | solution.py:633
  39.7 1.3 %weights_out.1 = (bf16[4,128,512]{2,1,0:T(8,128)(2,1)S(1)}, bf16[4,128,512]{2,1,0:T(8,128)(2,1)S(1)}) custom-call(bf16[1024,1024]{1,0:T(8,128)(2,1)S(1)} %get-tuple-element.96.refs_0_.refs_12_, bf16[1024,512]{1,0:T(8,128)(2,1)S(1)} %get-tuple-element.97.refs_1_, f32[1,512]{1,0:T(1,128)S(1)} %get-tuple-element.98.refs_2_.refs_8_), custom_call_target="tpu_custom_call" | custom-call | flops 1 | bytes 1 | tf_op jit(solution)/shard_map/weights_out/pallas_call | solution.py:633
  41.0 1.4 %collective-permute-start.9 = (f32[8,1024]{1,0:T(8,128)S(1)}, f32[8,1024]{1,0:T(8,128)S(1)}, u32[]{:S(2)}, u32[]{:S(2)}) collective-permute-start(f32[8,1024]{1,0:T(8,128)S(1)} %chip_outgoing.1.refs_4_), channel_id=1, source_target_pairs={{0,6},{1,7},{2,4},{3,5},{4,2},{5,3},{6,0},{7,1},{8,14},{9,15},{10,... | collective-permute-start | bytes 98312 | tf_op jit(solution)/shard_map/ppermute | solution.py:664
  42.4 1.0 collective-permute-start.8
  43.4 1.1 collective-permute-start.7
  44.5 0.9 first_core.1
  45.4 1.2 %collective-permute-start.15 = (bf16[2,256,512]{2,1,0:T(8,128)(2,1)S(1)}, bf16[2,256,512]{2,1,0:T(8,128)(2,1)S(1)}, u32[]{:S(2)}, u32[]{:S(2)}) collective-permute-start(bf16[2,256,512]{2,1,0:T(8,128)(2,1)S(1)} %get-tuple-element.111), channel_id=1, source_target_pairs={{0,4},{1,5},{2,6},{3,7},{4,0},{5,1},{6,2},{7,3},{8,12},{9,13},{10,... | collective-permute-start | bytes 1572872 | tf_op jit(solution)/shard_map/ppermute | solution.py:664
  46.6 0.8 collective-permute-start.14
  47.4 5.3 %back.1 = (bf16[1024,2048]{1,0:T(8,128)(2,1)S(1)}, f32[1,1024]{1,0:T(1,128)S(1)}, bf16[64,512]{1,0:T(8,128)(2,1)S(1)}, bf16[4,256,512]{2,1,0:T(8,128)(2,1)S(1)}, bf16[4,256,512]{2,1,0:T(8,128)(2,1)S(1)}) custom-call(f32[2,8,1024]{2,1,0:T(8,128)S(1)} %collective-permute-done.3.refs_1_.refs_0_, f32[2,8,1024]{2,1,0:T(8,128)S(1)} %collective-permute-done.4.refs_2_.refs_1_, ...), custom_call_target="tpu_custom_call" | custom-call | flops 10000000000 | bytes 1 | tf_op jit(solution)/shard_map/back/pallas_call | solution.py:633
  52.7 0.3 collective-permute-start.13
  53.0 1.2 %collective-permute-start.12 = (bf16[64,512]{1,0:T(8,128)(2,1)S(1)}, bf16[64,512]{1,0:T(8,128)(2,1)S(1)}, u32[]{:S(2)}, u32[]{:S(2)}) collective-permute-start(bf16[64,512]{1,0:T(8,128)(2,1)S(1)} %get-tuple-element.108), channel_id=1, source_target_pairs={{0,1},{1,0},{2,3},{3,2},{4,5},{5,4},{6,7},{7,6},{8,9},{9,8},{10,11... | collective-permute-start | bytes 196616 | tf_op jit(solution)/shard_map/ppermute | solution.py:664
  54.2 2.4 %gconv.1.refs_4_.refs_0_ = bf16[1024,512]{1,0:T(8,128)(2,1)S(1)} custom-call(bf16[1024,2048]{1,0:T(8,128)(2,1)S(1)} %get-tuple-element.106.refs_0_, bf16[512,2048]{1,0:T(8,128)(2,1)S(1)} %copy-done.2, f32[1,1024]{1,0:T(1,128)S(1)} %get-tuple-element.107.refs_2_.refs_9_), custom_call_target="tpu_custom_call" | custom-call | flops 1 | bytes 1 | tf_op jit(solution)/shard_map/gconv/pallas_call | solution.py:633
  56.5 3.3 %collective-permute-done.13.refs_6_.refs_2_ = bf16[64,512]{1,0:T(8,128)(2,1)S(1)} collective-permute-done((bf16[64,512]{1,0:T(8,128)(2,1)S(1)}, bf16[64,512]{1,0:T(8,128)(2,1)S(1)}, u32[]{:S(2)}, u32[]{:S(2)}) %collective-permute-start.13) | collective-permute-done | bytes 65568 | tf_op jit(solution)/shard_map/ppermute | solution.py:651
  59.8 1.2 %collective-permute-start.20 = (bf16[4,128,512]{2,1,0:T(8,128)(2,1)S(1)}, bf16[4,128,512]{2,1,0:T(8,128)(2,1)S(1)}, u32[]{:S(2)}, u32[]{:S(2)}) collective-permute-start(bf16[4,128,512]{2,1,0:T(8,128)(2,1)S(1)} %get-tuple-element.120), channel_id=1, source_target_pairs={{0,1},{1,0},{2,3},{3,2},{4,5},{5,4},{6,7},{7,6},{8,9},{9,8},{10,11... | collective-permute-start | bytes 1572872 | tf_op jit(solution)/shard_map/ppermute | solution.py:664
  61.0 0.4 first_seq.1
  61.4 1.3 %collective-permute-start.18 = (bf16[1,256,512]{2,1,0:T(8,128)(2,1)S(1)}, bf16[1,256,512]{2,1,0:T(8,128)(2,1)S(1)}, u32[]{:S(2)}, u32[]{:S(2)}) collective-permute-start(bf16[1,256,512]{2,1,0:T(8,128)(2,1)S(1)} %get-tuple-element.117), channel_id=1, source_target_pairs={{0,2},{1,3},{2,0},{3,1},{4,6},{5,7},{6,4},{7,5},{8,10},{9,11},{10,... | collective-permute-start | bytes 786440 | tf_op jit(solution)/shard_map/ppermute | solution.py:664
  62.7 1.0 collective-permute-start.17
  63.7 2.8 %taps.1 = (f32[1024,512]{1,0:T(8,128)S(1)}, bf16[4,16,512]{2,1,0:T(8,128)(2,1)S(1)}, bf16[4,16,512]{2,1,0:T(8,128)(2,1)S(1)}) custom-call(bf16[1024,512]{1,0:T(8,128)(2,1)S(1)} %gconv.1.refs_4_.refs_0_, bf16[64,512]{1,0:T(8,128)(2,1)S(1)} %collective-permute-done.12.refs_5_.refs_1_, bf16[64,512]{1,0:T(8,128)(2,1)S(1)} %collective-permute-done.13.refs_6_.refs_2_, ...), custom_call_target="tpu_custom_call" | custom-call | flops 1 | bytes 1 | tf_op jit(solution)/shard_map/taps/pallas_call | solution.py:633
  66.6 0.7 second_core.1
  67.3 1.1 collective-permute-start.23
  68.4 0.8 collective-permute-start.21
  69.2 0.6 collective-permute-done.18.refs_3_
  69.7 2.2 %collective-permute-done.17.refs_1_ = bf16[1,256,512]{2,1,0:T(8,128)(2,1)S(1)} collective-permute-done((bf16[1,256,512]{2,1,0:T(8,128)(2,1)S(1)}, bf16[1,256,512]{2,1,0:T(8,128)(2,1)S(1)}, u32[]{:S(2)}, u32[]{:S(2)}) %collective-permute-start.17) | collective-permute-done | bytes 262176 | tf_op jit(solution)/shard_map/ppermute | solution.py:664
  71.9 0.3 first_join.1
  72.2 1.7 %collective-permute-start.26 = (bf16[512,256]{1,0:T(8,128)(2,1)S(1)}, bf16[512,256]{1,0:T(8,128)(2,1)S(1)}, u32[]{:S(2)}, u32[]{:S(2)}) collective-permute-start(bf16[512,256]{1,0:T(8,128)(2,1)S(1)} %get-tuple-element.122.refs_2_), channel_id=1, source_target_pairs={{0,8},{8,0},{16,24},{24,16},{1,9},{9,1},{17,25},{25,17},{2,10},{10... | collective-permute-start | bytes 786440 | tf_op jit(solution)/shard_map/ppermute | solution.py:664
  74.0 0.8 collective-permute-start.22
  74.8 3.5 %result.1 = (bf16[8,128,512]{2,1,0:T(8,128)(2,1)}, f32[8,128]{1,0:T(8,128)S(1)}) custom-call(bf16[1024,2048]{1,0:T(8,128)(2,1)S(1)} %get-tuple-element.89.refs_2_.refs_0_, f32[1024,512]{1,0:T(8,128)S(1)} %get-tuple-element.90.refs_1_, bf16[2048,512]{1,0:T(8,128)(2,1)S(1)} %copy-done, bf16[2,16,512]{2,1,0:T(8,128)(2,1)S(1)} %get-tuple-element.123.refs_3_), custom_call_target="tpu_custom_call" | custom-call | flops 2000000000 | bytes 1 | tf_op jit(solution)/shard_map/result/pallas_call | solution.py:633
  78.3 0.9 collective-permute-done.22.refs_3_
  79.3 0.3 second_seq.1
  79.6 1.1 collective-permute-start.24
  80.6 0.8 collective-permute-start.25
  81.5 0.2 first_last.1.refs_4_.refs_0_
  81.7 2.7 %collective-permute-start.28 = (bf16[512,256]{1,0:T(8,128)(2,1)S(1)}, bf16[512,256]{1,0:T(8,128)(2,1)S(1)}, u32[]{:S(2)}, u32[]{:S(2)}) collective-permute-start(bf16[512,256]{1,0:T(8,128)(2,1)S(1)} %first_last.1.refs_4_.refs_0_), channel_id=1, source_target_pairs={{0,16},{8,24},{16,0},{24,8},{1,17},{9,25},{17,1},{25,9},{2,18},{10... | collective-permute-start | bytes 786440 | tf_op jit(solution)/shard_map/ppermute | solution.py:664
  84.3 2.0 %collective-permute-done.25.refs_3_ = bf16[1,192,512]{2,1,0:T(8,128)(2,1)S(1)} collective-permute-done((bf16[1,192,512]{2,1,0:T(8,128)(2,1)S(1)}, bf16[1,192,512]{2,1,0:T(8,128)(2,1)S(1)}, u32[]{:S(2)}, u32[]{:S(2)}) %collective-permute-start.25) | collective-permute-done | bytes 196640 | tf_op jit(solution)/shard_map/ppermute | solution.py:664
  86.3 0.2 second_join.1
  86.6 1.6 %collective-permute-start.27 = (bf16[400,256]{1,0:T(8,128)(2,1)S(1)}, bf16[400,256]{1,0:T(8,128)(2,1)S(1)}, u32[]{:S(2)}, u32[]{:S(2)}) collective-permute-start(bf16[400,256]{1,0:T(8,128)(2,1)S(1)} %get-tuple-element.137.refs_4_), channel_id=1, source_target_pairs={{0,8},{8,0},{16,24},{24,16},{1,9},{9,1},{17,25},{25,17},{2,10},{10... | collective-permute-start | bytes 614408 | tf_op jit(solution)/shard_map/ppermute | solution.py:664
  88.2 2.7 %inputs.1 = (f32[8,128,512]{2,1,0:T(8,128)}, f32[8,128]{1,0:T(8,128)S(1)}) custom-call(f32[1024,512]{1,0:T(8,128)S(1)} %get-tuple-element.125.refs_0_, f32[4,1024,128]{2,1,0:T(8,128)S(1)} %get-tuple-element.85.refs_4_.refs_3_.refs_1_, f32[1024,512]{1,0:T(8,128)S(1)} %get-tuple-element.126.refs_2_, f32[1,512]{1,0:T(1,128)S(1)} %bitcast.13, ...), custom_call_target="tpu_custom_call" | custom-call | flops 1 | bytes 1 | tf_op jit(solution)/shard_map/inputs/pallas_call | solution.py:633
  90.9 3.8 %collective-permute-done.28.refs_1_ = bf16[512,256]{1,0:T(8,128)(2,1)S(1)} collective-permute-done((bf16[512,256]{1,0:T(8,128)(2,1)S(1)}, bf16[512,256]{1,0:T(8,128)(2,1)S(1)}, u32[]{:S(2)}, u32[]{:S(2)}) %collective-permute-start.28) | collective-permute-done | bytes 262176 | tf_op jit(solution)/shard_map/ppermute | solution.py:664
  94.7 0.2 first_total.1.refs_2_.refs_0_
  94.9 1.4 %collective-permute-done.27.refs_1_ = bf16[400,256]{1,0:T(8,128)(2,1)S(1)} collective-permute-done((bf16[400,256]{1,0:T(8,128)(2,1)S(1)}, bf16[400,256]{1,0:T(8,128)(2,1)S(1)}, u32[]{:S(2)}, u32[]{:S(2)}) %collective-permute-start.27) | collective-permute-done | bytes 204832 | tf_op jit(solution)/shard_map/ppermute | solution.py:664
  96.3 0.2 second_last.1.refs_0_.refs_2_
  96.5 2.1 %collective-permute-start.29 = (bf16[400,256]{1,0:T(8,128)(2,1)S(1)}, bf16[400,256]{1,0:T(8,128)(2,1)S(1)}, u32[]{:S(2)}, u32[]{:S(2)}) collective-permute-start(bf16[400,256]{1,0:T(8,128)(2,1)S(1)} %second_last.1.refs_0_.refs_2_), channel_id=1, source_target_pairs={{0,16},{8,24},{16,0},{24,8},{1,17},{9,25},{17,1},{25,9},{2,18},{10... | collective-permute-start | bytes 614408 | tf_op jit(solution)/shard_map/ppermute | solution.py:664
  98.6 2.5 %collective-permute-start.31 = (bf16[512,256]{1,0:T(8,128)(2,1)S(1)}, bf16[512,256]{1,0:T(8,128)(2,1)S(1)}, u32[]{:S(2)}, u32[]{:S(2)}) collective-permute-start(bf16[512,256]{1,0:T(8,128)(2,1)S(1)} %first_total.1.refs_2_.refs_0_), channel_id=1, source_target_pairs={{0,8},{8,0},{16,24},{24,16},{1,9},{9,1},{17,25},{25,17},{2,10},{10... | collective-permute-start | bytes 786440 | tf_op jit(solution)/shard_map/ppermute | solution.py:664
  101.1 5.4 %collective-permute-done.29.refs_1_ = bf16[400,256]{1,0:T(8,128)(2,1)S(1)} collective-permute-done((bf16[400,256]{1,0:T(8,128)(2,1)S(1)}, bf16[400,256]{1,0:T(8,128)(2,1)S(1)}, u32[]{:S(2)}, u32[]{:S(2)}) %collective-permute-start.29) | collective-permute-done | bytes 204832 | tf_op jit(solution)/shard_map/ppermute | solution.py:664
  106.6 0.8 collective-permute-start.30
  107.5 1.1 collective-permute-done.31.refs_1_
  108.6 1.0 first_finish.1
  109.6 2.9 %collective-permute-done.30.refs_1_ = bf16[400,256]{1,0:T(8,128)(2,1)S(1)} collective-permute-done((bf16[400,256]{1,0:T(8,128)(2,1)S(1)}, bf16[400,256]{1,0:T(8,128)(2,1)S(1)}, u32[]{:S(2)}, u32[]{:S(2)}) %collective-permute-start.30) | collective-permute-done | bytes 204832 | tf_op jit(solution)/shard_map/ppermute | solution.py:664
  112.5 0.9 second_finish.1
  (46 shorter events, 0.6 us)
Async XLA Ops:
  0.6 5.6 %copy-start = (bf16[2048,512]{1,0:T(8,128)(2,1)S(1)}, bf16[2048,512]{1,0:T(8,128)(2,1)}, u32[]{:S(2)}) copy-start(bf16[2048,512]{1,0:T(8,128)(2,1)} %refs_2_.1) | copy-start | bytes 6291460
  0.7 5.6 %copy-start.7 = (bf16[8,128,512]{2,1,0:T(8,128)(2,1)S(1)}, bf16[8,128,512]{2,1,0:T(8,128)(2,1)}, u32[]{:S(2)}) copy-start(bf16[8,128,512]{2,1,0:T(8,128)(2,1)} %refs_0_.3) | copy-start | bytes 3145732
  2.8 5.4 %copy-start.2 = (bf16[512,2048]{1,0:T(8,128)(2,1)S(1)}, bf16[512,2048]{1,0:T(8,128)(2,1)}, u32[]{:S(2)}) copy-start(bf16[512,2048]{1,0:T(8,128)(2,1)} %refs_1_.7) | copy-start | bytes 6291460
  2.8 5.4 %copy-start.4 = (f32[512,4]{0,1:T(4,128)S(1)}, f32[512,4]{0,1:T(4,128)}, u32[]{:S(2)}) copy-start(f32[512,4]{0,1:T(4,128)} %param.14) | copy-start | bytes 24580
  2.8 5.4 %copy-start.8 = (f32[1024]{0:T(1024)S(1)}, f32[1024]{0:T(1024)}, u32[]{:S(2)}) copy-start(f32[1024]{0:T(1024)} %param.15) | copy-start | bytes 12292
  2.8 5.3 %collective-permute-start.1 = (bf16[64,512]{1,0:T(8,128)(2,1)S(1)}, bf16[64,512]{1,0:T(8,128)(2,1)S(1)}, u32[]{:S(2)}, u32[]{:S(2)}) collective-permute-start(bf16[64,512]{1,0:T(8,128)(2,1)S(1)} %get-tuple-element.81.refs_2_), channel_id=1, source_target_pairs={{0,7},{1,2},{2,1},{3,4},{4,3},{5,6},{6,5},{7,0},{8,15},{9,10},{10,... | collective-permute-start | bytes 196616 | tf_op jit(solution)/shard_map/ppermute | solution.py:651
  6.2 2.0 %collective-permute-start = (bf16[64,512]{1,0:T(8,128)(2,1)S(1)}, bf16[64,512]{1,0:T(8,128)(2,1)S(1)}, u32[]{:S(2)}, u32[]{:S(2)}) collective-permute-start(bf16[64,512]{1,0:T(8,128)(2,1)S(1)} %get-tuple-element.81.refs_2_), channel_id=1, source_target_pairs={{0,1},{1,0},{2,3},{3,2},{4,5},{5,4},{6,7},{7,6},{8,9},{9,8},{10,11... | collective-permute-start | bytes 196616 | tf_op jit(solution)/shard_map/ppermute | solution.py:664
  11.7 1.3 %collective-permute-start.2 = (f32[2,8,1024]{2,1,0:T(8,128)S(1)}, f32[2,8,1024]{2,1,0:T(8,128)S(1)}, u32[]{:S(2)}, u32[]{:S(2)}) collective-permute-start(f32[2,8,1024]{2,1,0:T(8,128)S(1)} %get-tuple-element.84.refs_0_.refs_2_), channel_id=1, source_target_pairs={{0,1},{1,0},{2,3},{3,2},{4,5},{5,4},{6,7},{7,6},{8,9},{9,8},{10,11... | collective-permute-start | bytes 196616 | tf_op jit(solution)/shard_map/ppermute | solution.py:664
  13.0 8.2 %copy-start.1 = (bf16[512,2048]{1,0:T(8,128)(2,1)S(1)}, bf16[512,2048]{1,0:T(8,128)(2,1)}, u32[]{:S(2)}) copy-start(bf16[512,2048]{1,0:T(8,128)(2,1)} %refs_7_.1) | copy-start | bytes 6291460
  13.0 8.2 %copy-start.3 = (bf16[1024,512]{1,0:T(8,128)(2,1)S(1)}, bf16[1024,512]{1,0:T(8,128)(2,1)}, u32[]{:S(2)}) copy-start(bf16[1024,512]{1,0:T(8,128)(2,1)} %refs_6_.3) | copy-start | bytes 3145732
  13.0 8.2 %copy-start.5 = (f32[512]{0:T(512)S(1)}, f32[512]{0:T(512)}, u32[]{:S(2)}) copy-start(f32[512]{0:T(512)} %param.18) | copy-start | bytes 6148
  13.1 5.5 %collective-permute-start.5 = (f32[2,8,1024]{2,1,0:T(8,128)S(1)}, f32[2,8,1024]{2,1,0:T(8,128)S(1)}, u32[]{:S(2)}, u32[]{:S(2)}) collective-permute-start(f32[2,8,1024]{2,1,0:T(8,128)S(1)} %chip_totals.1.refs_2_), channel_id=1, source_target_pairs={{0,6},{1,7},{2,4},{3,5},{4,2},{5,3},{6,0},{7,1},{8,14},{9,15},{10,... | collective-permute-start | bytes 196616 | tf_op jit(solution)/shard_map/ppermute | solution.py:664
  16.1 4.3 %collective-permute-start.4 = (f32[2,8,1024]{2,1,0:T(8,128)S(1)}, f32[2,8,1024]{2,1,0:T(8,128)S(1)}, u32[]{:S(2)}, u32[]{:S(2)}) collective-permute-start(f32[2,8,1024]{2,1,0:T(8,128)S(1)} %chip_totals.1.refs_2_), channel_id=1, source_target_pairs={{0,4},{1,5},{2,6},{3,7},{4,0},{5,1},{6,2},{7,3},{8,12},{9,13},{10,... | collective-permute-start | bytes 196616 | tf_op jit(solution)/shard_map/ppermute | solution.py:664
  17.0 4.3 %collective-permute-start.3 = (f32[2,8,1024]{2,1,0:T(8,128)S(1)}, f32[2,8,1024]{2,1,0:T(8,128)S(1)}, u32[]{:S(2)}, u32[]{:S(2)}) collective-permute-start(f32[2,8,1024]{2,1,0:T(8,128)S(1)} %chip_totals.1.refs_2_), channel_id=1, source_target_pairs={{0,2},{1,3},{2,0},{3,1},{4,6},{5,7},{6,4},{7,5},{8,10},{9,11},{10,... | collective-permute-start | bytes 196616 | tf_op jit(solution)/shard_map/ppermute | solution.py:664
  33.9 10.7 %collective-permute-start.10 = (bf16[4,256,512]{2,1,0:T(8,128)(2,1)S(1)}, bf16[4,256,512]{2,1,0:T(8,128)(2,1)S(1)}, u32[]{:S(2)}, u32[]{:S(2)}) collective-permute-start(bf16[4,256,512]{2,1,0:T(8,128)(2,1)S(1)} %get-tuple-element.102), channel_id=1, source_target_pairs={{0,1},{1,0},{2,3},{3,2},{4,5},{5,4},{6,7},{7,6},{8,9},{9,8},{10,11... | collective-permute-start | bytes 3145736 | tf_op jit(solution)/shard_map/ppermute | solution.py:664
  33.9 10.6 %collective-permute-start.11 = (bf16[4,256,512]{2,1,0:T(8,128)(2,1)S(1)}, bf16[4,256,512]{2,1,0:T(8,128)(2,1)S(1)}, u32[]{:S(2)}, u32[]{:S(2)}) collective-permute-start(bf16[4,256,512]{2,1,0:T(8,128)(2,1)S(1)} %get-tuple-element.104), channel_id=1, source_target_pairs={{0,1},{1,0},{2,3},{3,2},{4,5},{5,4},{6,7},{7,6},{8,9},{9,8},{10,11... | collective-permute-start | bytes 3145736 | tf_op jit(solution)/shard_map/ppermute | solution.py:664
  39.5 1.4 %collective-permute-start.6 = (f32[8,1024]{1,0:T(8,128)S(1)}, f32[8,1024]{1,0:T(8,128)S(1)}, u32[]{:S(2)}, u32[]{:S(2)}) collective-permute-start(f32[8,1024]{1,0:T(8,128)S(1)} %get-tuple-element.95.refs_0_), channel_id=1, source_target_pairs={{0,1},{1,0},{2,3},{3,2},{4,5},{5,4},{6,7},{7,6},{8,9},{9,8},{10,11... | collective-permute-start | bytes 98312 | tf_op jit(solution)/shard_map/ppermute | solution.py:664
  41.0 6.4 %collective-permute-start.9 = (f32[8,1024]{1,0:T(8,128)S(1)}, f32[8,1024]{1,0:T(8,128)S(1)}, u32[]{:S(2)}, u32[]{:S(2)}) collective-permute-start(f32[8,1024]{1,0:T(8,128)S(1)} %chip_outgoing.1.refs_4_), channel_id=1, source_target_pairs={{0,6},{1,7},{2,4},{3,5},{4,2},{5,3},{6,0},{7,1},{8,14},{9,15},{10,... | collective-permute-start | bytes 98312 | tf_op jit(solution)/shard_map/ppermute | solution.py:664
  42.4 5.0 %collective-permute-start.8 = (f32[8,1024]{1,0:T(8,128)S(1)}, f32[8,1024]{1,0:T(8,128)S(1)}, u32[]{:S(2)}, u32[]{:S(2)}) collective-permute-start(f32[8,1024]{1,0:T(8,128)S(1)} %chip_outgoing.1.refs_4_), channel_id=1, source_target_pairs={{0,4},{1,5},{2,6},{3,7},{4,0},{5,1},{6,2},{7,3},{8,12},{9,13},{10,... | collective-permute-start | bytes 98312 | tf_op jit(solution)/shard_map/ppermute | solution.py:664
  43.4 4.0 %collective-permute-start.7 = (f32[8,1024]{1,0:T(8,128)S(1)}, f32[8,1024]{1,0:T(8,128)S(1)}, u32[]{:S(2)}, u32[]{:S(2)}) collective-permute-start(f32[8,1024]{1,0:T(8,128)S(1)} %chip_outgoing.1.refs_4_), channel_id=1, source_target_pairs={{0,2},{1,3},{2,0},{3,1},{4,6},{5,7},{6,4},{7,5},{8,10},{9,11},{10,... | collective-permute-start | bytes 98312 | tf_op jit(solution)/shard_map/ppermute | solution.py:664
  45.4 15.6 %collective-permute-start.15 = (bf16[2,256,512]{2,1,0:T(8,128)(2,1)S(1)}, bf16[2,256,512]{2,1,0:T(8,128)(2,1)S(1)}, u32[]{:S(2)}, u32[]{:S(2)}) collective-permute-start(bf16[2,256,512]{2,1,0:T(8,128)(2,1)S(1)} %get-tuple-element.111), channel_id=1, source_target_pairs={{0,4},{1,5},{2,6},{3,7},{4,0},{5,1},{6,2},{7,3},{8,12},{9,13},{10,... | collective-permute-start | bytes 1572872 | tf_op jit(solution)/shard_map/ppermute | solution.py:664
  46.6 14.4 %collective-permute-start.14 = (bf16[2,256,512]{2,1,0:T(8,128)(2,1)S(1)}, bf16[2,256,512]{2,1,0:T(8,128)(2,1)S(1)}, u32[]{:S(2)}, u32[]{:S(2)}) collective-permute-start(bf16[2,256,512]{2,1,0:T(8,128)(2,1)S(1)} %get-tuple-element.105.refs_16_), channel_id=1, source_target_pairs={{0,2},{1,3},{2,0},{3,1},{4,6},{5,7},{6,4},{7,5},{8,10},{9,11},{10,... | collective-permute-start | bytes 1572872 | tf_op jit(solution)/shard_map/ppermute | solution.py:664
  52.7 7.1 %collective-permute-start.13 = (bf16[64,512]{1,0:T(8,128)(2,1)S(1)}, bf16[64,512]{1,0:T(8,128)(2,1)S(1)}, u32[]{:S(2)}, u32[]{:S(2)}) collective-permute-start(bf16[64,512]{1,0:T(8,128)(2,1)S(1)} %get-tuple-element.108), channel_id=1, source_target_pairs={{0,7},{1,2},{2,1},{3,4},{4,3},{5,6},{6,5},{7,0},{8,15},{9,10},{10,... | collective-permute-start | bytes 196616 | tf_op jit(solution)/shard_map/ppermute | solution.py:651
  53.0 8.0 %collective-permute-start.12 = (bf16[64,512]{1,0:T(8,128)(2,1)S(1)}, bf16[64,512]{1,0:T(8,128)(2,1)S(1)}, u32[]{:S(2)}, u32[]{:S(2)}) collective-permute-start(bf16[64,512]{1,0:T(8,128)(2,1)S(1)} %get-tuple-element.108), channel_id=1, source_target_pairs={{0,1},{1,0},{2,3},{3,2},{4,5},{5,4},{6,7},{7,6},{8,9},{9,8},{10,11... | collective-permute-start | bytes 196616 | tf_op jit(solution)/shard_map/ppermute | solution.py:664
  54.2 12.4 %collective-permute-start.19 = (bf16[4,256,512]{2,1,0:T(8,128)(2,1)S(1)}, bf16[4,256,512]{2,1,0:T(8,128)(2,1)S(1)}, u32[]{:S(2)}, u32[]{:S(2)}) collective-permute-start(bf16[4,256,512]{2,1,0:T(8,128)(2,1)S(1)} %get-tuple-element.119), channel_id=1, source_target_pairs={{0,1},{1,0},{2,3},{3,2},{4,5},{5,4},{6,7},{7,6},{8,9},{9,8},{10,11... | collective-permute-start | bytes 3145736 | tf_op jit(solution)/shard_map/ppermute | solution.py:664
  59.8 6.8 %collective-permute-start.20 = (bf16[4,128,512]{2,1,0:T(8,128)(2,1)S(1)}, bf16[4,128,512]{2,1,0:T(8,128)(2,1)S(1)}, u32[]{:S(2)}, u32[]{:S(2)}) collective-permute-start(bf16[4,128,512]{2,1,0:T(8,128)(2,1)S(1)} %get-tuple-element.120), channel_id=1, source_target_pairs={{0,1},{1,0},{2,3},{3,2},{4,5},{5,4},{6,7},{7,6},{8,9},{9,8},{10,11... | collective-permute-start | bytes 1572872 | tf_op jit(solution)/shard_map/ppermute | solution.py:664
  61.4 8.3 %collective-permute-start.18 = (bf16[1,256,512]{2,1,0:T(8,128)(2,1)S(1)}, bf16[1,256,512]{2,1,0:T(8,128)(2,1)S(1)}, u32[]{:S(2)}, u32[]{:S(2)}) collective-permute-start(bf16[1,256,512]{2,1,0:T(8,128)(2,1)S(1)} %get-tuple-element.117), channel_id=1, source_target_pairs={{0,2},{1,3},{2,0},{3,1},{4,6},{5,7},{6,4},{7,5},{8,10},{9,11},{10,... | collective-permute-start | bytes 786440 | tf_op jit(solution)/shard_map/ppermute | solution.py:664
  62.7 9.2 %collective-permute-start.17 = (bf16[1,256,512]{2,1,0:T(8,128)(2,1)S(1)}, bf16[1,256,512]{2,1,0:T(8,128)(2,1)S(1)}, u32[]{:S(2)}, u32[]{:S(2)}) collective-permute-start(bf16[1,256,512]{2,1,0:T(8,128)(2,1)S(1)} %get-tuple-element.112.refs_10_), channel_id=1, source_target_pairs={{0,4},{1,5},{2,6},{3,7},{4,0},{5,1},{6,2},{7,3},{8,12},{9,13},{10,... | collective-permute-start | bytes 786440 | tf_op jit(solution)/shard_map/ppermute | solution.py:664
  67.3 12.0 %collective-permute-start.23 = (bf16[2,192,512]{2,1,0:T(8,128)(2,1)S(1)}, bf16[2,192,512]{2,1,0:T(8,128)(2,1)S(1)}, u32[]{:S(2)}, u32[]{:S(2)}) collective-permute-start(bf16[2,192,512]{2,1,0:T(8,128)(2,1)S(1)} %get-tuple-element.130), channel_id=1, source_target_pairs={{0,4},{1,5},{2,6},{3,7},{4,0},{5,1},{6,2},{7,3},{8,12},{9,13},{10,... | collective-permute-start | bytes 1179656 | tf_op jit(solution)/shard_map/ppermute | solution.py:664
  68.4 10.9 %collective-permute-start.21 = (bf16[2,192,512]{2,1,0:T(8,128)(2,1)S(1)}, bf16[2,192,512]{2,1,0:T(8,128)(2,1)S(1)}, u32[]{:S(2)}, u32[]{:S(2)}) collective-permute-start(bf16[2,192,512]{2,1,0:T(8,128)(2,1)S(1)} %get-tuple-element.121.refs_4_), channel_id=1, source_target_pairs={{0,2},{1,3},{2,0},{3,1},{4,6},{5,7},{6,4},{7,5},{8,10},{9,11},{10,... | collective-permute-start | bytes 1179656 | tf_op jit(solution)/shard_map/ppermute | solution.py:664
  69.2 4.8 %collective-permute-start.16 = (bf16[4,16,512]{2,1,0:T(8,128)(2,1)S(1)}, bf16[4,16,512]{2,1,0:T(8,128)(2,1)S(1)}, u32[]{:S(2)}, u32[]{:S(2)}) collective-permute-start(bf16[4,16,512]{2,1,0:T(8,128)(2,1)S(1)} %get-tuple-element.114), channel_id=1, source_target_pairs={{0,1},{1,0},{2,3},{3,2},{4,5},{5,4},{6,7},{7,6},{8,9},{9,8},{10,11... | collective-permute-start | bytes 196616 | tf_op jit(solution)/shard_map/ppermute | solution.py:664
  72.2 9.2 %collective-permute-start.26 = (bf16[512,256]{1,0:T(8,128)(2,1)S(1)}, bf16[512,256]{1,0:T(8,128)(2,1)S(1)}, u32[]{:S(2)}, u32[]{:S(2)}) collective-permute-start(bf16[512,256]{1,0:T(8,128)(2,1)S(1)} %get-tuple-element.122.refs_2_), channel_id=1, source_target_pairs={{0,8},{8,0},{16,24},{24,16},{1,9},{9,1},{17,25},{25,17},{2,10},{10... | collective-permute-start | bytes 786440 | tf_op jit(solution)/shard_map/ppermute | solution.py:664
  74.0 5.3 %collective-permute-start.22 = (bf16[2,16,512]{2,1,0:T(8,128)(2,1)S(1)}, bf16[2,16,512]{2,1,0:T(8,128)(2,1)S(1)}, u32[]{:S(2)}, u32[]{:S(2)}) collective-permute-start(bf16[2,16,512]{2,1,0:T(8,128)(2,1)S(1)} %get-tuple-element.123.refs_3_), channel_id=1, source_target_pairs={{0,2},{1,3},{2,0},{3,1},{4,6},{5,7},{6,4},{7,5},{8,10},{9,11},{10,... | collective-permute-start | bytes 98312 | tf_op jit(solution)/shard_map/ppermute | solution.py:664
  79.6 6.7 %collective-permute-start.24 = (bf16[1,208,512]{2,1,0:T(8,128)(2,1)S(1)}, bf16[1,208,512]{2,1,0:T(8,128)(2,1)S(1)}, u32[]{:S(2)}, u32[]{:S(2)}) collective-permute-start(bf16[1,208,512]{2,1,0:T(8,128)(2,1)S(1)} %get-tuple-element.133), channel_id=1, source_target_pairs={{0,4},{1,5},{2,6},{3,7},{4,0},{5,1},{6,2},{7,3},{8,12},{9,13},{10,... | collective-permute-start | bytes 638984 | tf_op jit(solution)/shard_map/ppermute | solution.py:664
  80.6 5.7 %collective-permute-start.25 = (bf16[1,192,512]{2,1,0:T(8,128)(2,1)S(1)}, bf16[1,192,512]{2,1,0:T(8,128)(2,1)S(1)}, u32[]{:S(2)}, u32[]{:S(2)}) collective-permute-start(bf16[1,192,512]{2,1,0:T(8,128)(2,1)S(1)} %get-tuple-element.135.refs_2_), channel_id=1, source_target_pairs={{0,2},{1,3},{2,0},{3,1},{4,6},{5,7},{6,4},{7,5},{8,10},{9,11},{10,... | collective-permute-start | bytes 589832 | tf_op jit(solution)/shard_map/ppermute | solution.py:664
  81.7 13.1 %collective-permute-start.28 = (bf16[512,256]{1,0:T(8,128)(2,1)S(1)}, bf16[512,256]{1,0:T(8,128)(2,1)S(1)}, u32[]{:S(2)}, u32[]{:S(2)}) collective-permute-start(bf16[512,256]{1,0:T(8,128)(2,1)S(1)} %first_last.1.refs_4_.refs_0_), channel_id=1, source_target_pairs={{0,16},{8,24},{16,0},{24,8},{1,17},{9,25},{17,1},{25,9},{2,18},{10... | collective-permute-start | bytes 786440 | tf_op jit(solution)/shard_map/ppermute | solution.py:664
  86.3 1.9 %copy-start.6 = (f32[512]{0:T(512)S(1)}, f32[512]{0:T(512)}, u32[]{:S(2)}) copy-start(f32[512]{0:T(512)} %param.13) | copy-start | bytes 6148
  86.6 9.8 %collective-permute-start.27 = (bf16[400,256]{1,0:T(8,128)(2,1)S(1)}, bf16[400,256]{1,0:T(8,128)(2,1)S(1)}, u32[]{:S(2)}, u32[]{:S(2)}) collective-permute-start(bf16[400,256]{1,0:T(8,128)(2,1)S(1)} %get-tuple-element.137.refs_4_), channel_id=1, source_target_pairs={{0,8},{8,0},{16,24},{24,16},{1,9},{9,1},{17,25},{25,17},{2,10},{10... | collective-permute-start | bytes 614408 | tf_op jit(solution)/shard_map/ppermute | solution.py:664
  96.5 10.0 %collective-permute-start.29 = (bf16[400,256]{1,0:T(8,128)(2,1)S(1)}, bf16[400,256]{1,0:T(8,128)(2,1)S(1)}, u32[]{:S(2)}, u32[]{:S(2)}) collective-permute-start(bf16[400,256]{1,0:T(8,128)(2,1)S(1)} %second_last.1.refs_0_.refs_2_), channel_id=1, source_target_pairs={{0,16},{8,24},{16,0},{24,8},{1,17},{9,25},{17,1},{25,9},{2,18},{10... | collective-permute-start | bytes 614408 | tf_op jit(solution)/shard_map/ppermute | solution.py:664
  98.6 9.9 %collective-permute-start.31 = (bf16[512,256]{1,0:T(8,128)(2,1)S(1)}, bf16[512,256]{1,0:T(8,128)(2,1)S(1)}, u32[]{:S(2)}, u32[]{:S(2)}) collective-permute-start(bf16[512,256]{1,0:T(8,128)(2,1)S(1)} %first_total.1.refs_2_.refs_0_), channel_id=1, source_target_pairs={{0,8},{8,0},{16,24},{24,16},{1,9},{9,1},{17,25},{25,17},{2,10},{10... | collective-permute-start | bytes 786440 | tf_op jit(solution)/shard_map/ppermute | solution.py:664
  106.6 5.8 %collective-permute-start.30 = (bf16[400,256]{1,0:T(8,128)(2,1)S(1)}, bf16[400,256]{1,0:T(8,128)(2,1)S(1)}, u32[]{:S(2)}, u32[]{:S(2)}) collective-permute-start(bf16[400,256]{1,0:T(8,128)(2,1)S(1)} %second_total.1.refs_2_.refs_0_), channel_id=1, source_target_pairs={{0,8},{8,0},{16,24},{24,16},{1,9},{9,1},{17,25},{25,17},{2,10},{10... | collective-permute-start | bytes 614408 | tf_op jit(solution)/shard_map/ppermute | solution.py:664

commit v5 on v4

--- a/solution.py
+++ b/solution.py
@@ -875,7 +875,7 @@
         functools.partial(gconv_kernel, steps=span), "gconv", [((tokens, width), BF16)],
         [VMEM_SPEC] * 2, (gproj, w_in), limit=LIMITS["gconv"],
     )
-    order.last = (*order.last, *after)
+    order.last = (*order.last, after[0])
     late = []
     share = width // seq_count
     second = spread_sum(

time: 114 us -> 111 us (0.974)
  waiting for transfers between devices: 28.3 us -> 26 us
    ppermute x2, waiting for transfers between devices: 3.85 us -> 0.56 us  [neighbour(): lax.ppermute(block, axis, [(i, (i + 1 if i % 2 else i - 1) % count) for i...]
    ppermute x30, starting transfers between devices: 31 us -> 29.4 us  [swap_by(): lax.ppermute(block, axis, [(i, i ^ mask) for i in range(lax.axis_size(axi...]
    ppermute x2, starting transfers between devices: 3.67 us -> 5.09 us  [neighbour(): lax.ppermute(block, axis, [(i, (i + 1 if i % 2 else i - 1) % count) for i...]
  transfers between devices with their start and end apart: 32 -> 32, of which waited for: 15 -> 14; matrix products, arithmetic and copies ran while one was open for 0% -> 0% of each run, Pallas kernels for 27% -> 27%
where the time goes in v5:
time: 111 us
  Pallas kernels  49.4 us (45%)
  starting transfers between devices  34.5 us (31%)
  waiting for transfers between devices  26 us (23%)
    pallas_call x28, Pallas kernels, call(): pl.pallas_call(body, name=name, out_shape=[(pltpu.HBM if name in FINAL an...  49.4 us
    ppermute x30, starting transfers between devices, swap_by(): lax.ppermute(block, axis, [(i, i ^ mask) for i in range(lax.axis_size(axi...  29.4 us
    ppermute x30, waiting for transfers between devices, swap_by(): lax.ppermute(block, axis, [(i, i ^ mask) for i in range(lax.axis_size(axi...  25.4 us
    ppermute x2, starting transfers between devices, neighbour(): lax.ppermute(block, axis, [(i, (i + 1 if i % 2 else i - 1) % count) for i...  5.09 us
  transfers between devices with their start and end apart: 32, of which 14 were waited for; matrix products, arithmetic and copies ran while one was open for 0% of the time, Pallas kernels for 27%

profile of v5, /device:TPU:0, one launch (start us, length us, event | category | flops | bytes accessed | tf_op | source)
XLA Modules:
  0.0 110.9 jit_solution(10705008134748314729)
XLA Ops:
  0.7 2.1 %ingest.1 = (f32[4,1024,128]{2,1,0:T(8,128)S(1)}, bf16[1024,512]{1,0:T(8,128)(2,1)S(1)}, bf16[64,512]{1,0:T(8,128)(2,1)S(1)}, f32[1024,128]{1,0:T(8,128)S(1)}) custom-call(bf16[8,128,512]{2,1,0:T(8,128)(2,1)} %refs_0_.2, s32[8,128]{1,0:T(8,128)} %refs_1_.4, f32[1,512]{1,0:T(1,128)} %bitcast.12), custom_call_target="tpu_custom_call" | custom-call | flops 10000000000 | bytes 1 | tf_op jit(solution)/shard_map/ingest/pallas_call | solution.py:633
  2.8 3.4 %collective-permute-start.1 = (bf16[64,512]{1,0:T(8,128)(2,1)S(1)}, bf16[64,512]{1,0:T(8,128)(2,1)S(1)}, u32[]{:S(2)}, u32[]{:S(2)}) collective-permute-start(bf16[64,512]{1,0:T(8,128)(2,1)S(1)} %get-tuple-element.81.refs_2_), channel_id=1, source_target_pairs={{0,7},{1,2},{2,1},{3,4},{4,3},{5,6},{6,5},{7,0},{8,15},{9,10},{10,... | collective-permute-start | bytes 196616 | tf_op jit(solution)/shard_map/ppermute | solution.py:651
  6.3 1.4 %prepare.1 = (bf16[1024,512]{1,0:T(8,128)(2,1)S(1)}, bf16[1024,1024]{1,0:T(8,128)(2,1)S(1)}) custom-call(bf16[8,128,512]{2,1,0:T(8,128)(2,1)S(1)} %copy-done.7, bf16[2048,512]{1,0:T(8,128)(2,1)S(1)} %copy-done, bf16[64,512]{1,0:T(8,128)(2,1)S(1)} %get-tuple-element.81.refs_2_), custom_call_target="tpu_custom_call" | custom-call | flops 10000000000 | bytes 1 | tf_op jit(solution)/shard_map/prepare/pallas_call | solution.py:633
  7.6 0.6 collective-permute-done.1.refs_2_.refs_6_
  8.2 3.5 %front.1 = (bf16[1024,512]{1,0:T(8,128)(2,1)S(1)}, f32[1024,1024]{1,0:T(8,128)S(1)}, f32[1024,1024]{1,0:T(8,128)S(1)}, f32[2,8,1024]{2,1,0:T(8,128)S(1)}) custom-call(bf16[1024,512]{1,0:T(8,128)(2,1)S(1)} %get-tuple-element.80.refs_0_.refs_4_, bf16[64,512]{1,0:T(8,128)(2,1)S(1)} %collective-permute-done.refs_1_.refs_5_, ...), custom_call_target="tpu_custom_call" | custom-call | flops 10000000000 | bytes 1 | tf_op jit(solution)/shard_map/front/pallas_call | solution.py:633
  11.7 0.1 collective-permute-start.2
  11.8 1.2 %collective-permute-done.2.refs_1_.refs_0_.refs_3_.refs_6_ = f32[2,8,1024]{2,1,0:T(8,128)S(1)} collective-permute-done((f32[2,8,1024]{2,1,0:T(8,128)S(1)}, f32[2,8,1024]{2,1,0:T(8,128)S(1)}, u32[]{:S(2)}, u32[]{:S(2)}) %collective-permute-start.2) | collective-permute-done | bytes 65568 | tf_op jit(solution)/shard_map/ppermute | solution.py:664
  13.1 3.0 %collective-permute-start.5 = (f32[2,8,1024]{2,1,0:T(8,128)S(1)}, f32[2,8,1024]{2,1,0:T(8,128)S(1)}, u32[]{:S(2)}, u32[]{:S(2)}) collective-permute-start(f32[2,8,1024]{2,1,0:T(8,128)S(1)} %chip_totals.1.refs_2_), channel_id=1, source_target_pairs={{0,6},{1,7},{2,4},{3,5},{4,2},{5,3},{6,0},{7,1},{8,14},{9,15},{10,... | collective-permute-start | bytes 196616 | tf_op jit(solution)/shard_map/ppermute | solution.py:664
  16.1 0.9 collective-permute-start.4
  17.0 1.3 %prepare_rest.1.refs_9_.refs_13_ = bf16[1024,1024]{1,0:T(8,128)(2,1)S(1)} custom-call(bf16[1024,512]{1,0:T(8,128)(2,1)S(1)} %get-tuple-element.83.refs_7_.refs_0_.refs_3_.refs_2_, bf16[2048,512]{1,0:T(8,128)(2,1)S(1)} %copy-done, f32[2,8,1024]{2,1,0:T(8,128)S(1)} %chip_totals.1.refs_2_), custom_call_target="tpu_custom_call" | custom-call | flops 1 | bytes 1 | tf_op jit(solution)/shard_map/prepare_rest/pallas_call | solution.py:633
  18.3 0.3 collective-permute-done.5.refs_3_.refs_2_
  18.6 1.8 %collective-permute-done.4.refs_2_.refs_1_ = f32[2,8,1024]{2,1,0:T(8,128)S(1)} collective-permute-done((f32[2,8,1024]{2,1,0:T(8,128)S(1)}, f32[2,8,1024]{2,1,0:T(8,128)S(1)}, u32[]{:S(2)}, u32[]{:S(2)}) %collective-permute-start.4) | collective-permute-done | bytes 65568 | tf_op jit(solution)/shard_map/ppermute | solution.py:664
  20.4 0.9 collective-permute-done.3.refs_1_.refs_0_
  21.2 8.0 %forward.1 = (f32[8,1024]{1,0:T(8,128)S(1)}, bf16[1024,1024]{1,0:T(8,128)(2,1)S(1)}, f32[1024,512]{1,0:T(8,128)S(1)}, bf16[1024,512]{1,0:T(8,128)(2,1)S(1)}, bf1...) custom-call(f32[2,8,1024]{2,1,0:T(8,128)S(1)} %collective-permute-done.2.refs_1_.refs_0_.refs_3_.refs_6_, ...), custom_call_target="tpu_custom_call" | custom-call | flops 10000000000 | bytes 1 | tf_op jit(solution)/shard_map/forward/pallas_call | solution.py:633
  29.2 4.6 %weights.1 = (bf16[4,256,512]{2,1,0:T(8,128)(2,1)S(1)}, bf16[4,256,512]{2,1,0:T(8,128)(2,1)S(1)}, bf16[4,256,512]{2,1,0:T(8,128)(2,1)S(1)}, bf16[4,256,512]{2,1,0:T(8,128)(2,1)S(1)}) custom-call(bf16[1024,512]{1,0:T(8,128)(2,1)S(1)} %get-tuple-element.92.refs_0_, bf16[1024,2048]{1,0:T(8,128)(2,1)S(1)} %get-tuple-element.91.refs_1_.refs_0_, ...), custom_call_target="tpu_custom_call" | custom-call | flops 1 | bytes 1 | tf_op jit(solution)/shard_map/weights/pallas_call | solution.py:633
  33.9 0.5 collective-permute-start.11
  34.4 5.1 %reverse.1 = (f32[1024,512]{1,0:T(8,128)S(1)}, bf16[1024,512]{1,0:T(8,128)(2,1)S(1)}, f32[1024,1024]{1,0:T(8,128)S(1)}, f32[8,1024]{1,0:T(8,128)S(1)}, f32[1,512]{1,0:T(1,128)S(1)}) custom-call(bf16[1024,2048]{1,0:T(8,128)(2,1)S(1)} %get-tuple-element.91.refs_1_.refs_0_, f32[1024,512]{1,0:T(8,128)S(1)} %get-tuple-element.90.refs_1_, ...), custom_call_target="tpu_custom_call" | custom-call | flops 1 | bytes 1 | tf_op jit(solution)/shard_map/reverse/pallas_call | solution.py:633
  39.5 0.1 collective-permute-start.6
  39.7 1.3 %weights_out.1 = (bf16[4,128,512]{2,1,0:T(8,128)(2,1)S(1)}, bf16[4,128,512]{2,1,0:T(8,128)(2,1)S(1)}) custom-call(bf16[1024,1024]{1,0:T(8,128)(2,1)S(1)} %get-tuple-element.96.refs_0_.refs_12_, bf16[1024,512]{1,0:T(8,128)(2,1)S(1)} %get-tuple-element.97.refs_1_, f32[1,512]{1,0:T(1,128)S(1)} %get-tuple-element.98.refs_2_.refs_8_), custom_call_target="tpu_custom_call" | custom-call | flops 1 | bytes 1 | tf_op jit(solution)/shard_map/weights_out/pallas_call | solution.py:633
  41.0 1.4 %collective-permute-start.9 = (f32[8,1024]{1,0:T(8,128)S(1)}, f32[8,1024]{1,0:T(8,128)S(1)}, u32[]{:S(2)}, u32[]{:S(2)}) collective-permute-start(f32[8,1024]{1,0:T(8,128)S(1)} %chip_outgoing.1.refs_4_), channel_id=1, source_target_pairs={{0,6},{1,7},{2,4},{3,5},{4,2},{5,3},{6,0},{7,1},{8,14},{9,15},{10,... | collective-permute-start | bytes 98312 | tf_op jit(solution)/shard_map/ppermute | solution.py:664
  42.4 1.0 collective-permute-start.8
  43.4 1.1 %collective-permute-start.7 = (f32[8,1024]{1,0:T(8,128)S(1)}, f32[8,1024]{1,0:T(8,128)S(1)}, u32[]{:S(2)}, u32[]{:S(2)}) collective-permute-start(f32[8,1024]{1,0:T(8,128)S(1)} %chip_outgoing.1.refs_4_), channel_id=1, source_target_pairs={{0,2},{1,3},{2,0},{3,1},{4,6},{5,7},{6,4},{7,5},{8,10},{9,11},{10,... | collective-permute-start | bytes 98312 | tf_op jit(solution)/shard_map/ppermute | solution.py:664
  44.5 0.9 first_core.1
  45.4 1.2 %collective-permute-start.15 = (bf16[2,256,512]{2,1,0:T(8,128)(2,1)S(1)}, bf16[2,256,512]{2,1,0:T(8,128)(2,1)S(1)}, u32[]{:S(2)}, u32[]{:S(2)}) collective-permute-start(bf16[2,256,512]{2,1,0:T(8,128)(2,1)S(1)} %get-tuple-element.111), channel_id=1, source_target_pairs={{0,4},{1,5},{2,6},{3,7},{4,0},{5,1},{6,2},{7,3},{8,12},{9,13},{10,... | collective-permute-start | bytes 1572872 | tf_op jit(solution)/shard_map/ppermute | solution.py:664
  46.6 0.8 collective-permute-start.14
  47.4 5.3 %back.1 = (bf16[1024,2048]{1,0:T(8,128)(2,1)S(1)}, f32[1,1024]{1,0:T(1,128)S(1)}, bf16[64,512]{1,0:T(8,128)(2,1)S(1)}, bf16[4,256,512]{2,1,0:T(8,128)(2,1)S(1)}, bf16[4,256,512]{2,1,0:T(8,128)(2,1)S(1)}) custom-call(f32[2,8,1024]{2,1,0:T(8,128)S(1)} %collective-permute-done.3.refs_1_.refs_0_, f32[2,8,1024]{2,1,0:T(8,128)S(1)} %collective-permute-done.4.refs_2_.refs_1_, ...), custom_call_target="tpu_custom_call" | custom-call | flops 10000000000 | bytes 1 | tf_op jit(solution)/shard_map/back/pallas_call | solution.py:633
  52.8 0.5 collective-permute-start.19
  53.4 2.4 %gconv.1.refs_4_.refs_0_ = bf16[1024,512]{1,0:T(8,128)(2,1)S(1)} custom-call(bf16[1024,2048]{1,0:T(8,128)(2,1)S(1)} %get-tuple-element.106.refs_0_, bf16[512,2048]{1,0:T(8,128)(2,1)S(1)} %copy-done.2, f32[1,1024]{1,0:T(1,128)S(1)} %get-tuple-element.107.refs_2_.refs_9_), custom_call_target="tpu_custom_call" | custom-call | flops 1 | bytes 1 | tf_op jit(solution)/shard_map/gconv/pallas_call | solution.py:633
  55.8 1.7 %collective-permute-start.13 = (bf16[64,512]{1,0:T(8,128)(2,1)S(1)}, bf16[64,512]{1,0:T(8,128)(2,1)S(1)}, u32[]{:S(2)}, u32[]{:S(2)}) collective-permute-start(bf16[64,512]{1,0:T(8,128)(2,1)S(1)} %get-tuple-element.108), channel_id=1, source_target_pairs={{0,7},{1,2},{2,1},{3,4},{4,3},{5,6},{6,5},{7,0},{8,15},{9,10},{10,... | collective-permute-start | bytes 196616 | tf_op jit(solution)/shard_map/ppermute | solution.py:651
  57.4 1.5 %collective-permute-done.15.refs_3_ = bf16[2,256,512]{2,1,0:T(8,128)(2,1)S(1)} collective-permute-done((bf16[2,256,512]{2,1,0:T(8,128)(2,1)S(1)}, bf16[2,256,512]{2,1,0:T(8,128)(2,1)S(1)}, u32[]{:S(2)}, u32[]{:S(2)}) %collective-permute-start.15) | collective-permute-done | bytes 524320 | tf_op jit(solution)/shard_map/ppermute | solution.py:664
  58.9 1.4 %collective-permute-done.14.refs_1_ = bf16[2,256,512]{2,1,0:T(8,128)(2,1)S(1)} collective-permute-done((bf16[2,256,512]{2,1,0:T(8,128)(2,1)S(1)}, bf16[2,256,512]{2,1,0:T(8,128)(2,1)S(1)}, u32[]{:S(2)}, u32[]{:S(2)}) %collective-permute-start.14) | collective-permute-done | bytes 524320 | tf_op jit(solution)/shard_map/ppermute | solution.py:664
  60.3 0.4 first_seq.1
  60.7 0.8 collective-permute-start.18
  61.5 1.1 %collective-permute-start.17 = (bf16[1,256,512]{2,1,0:T(8,128)(2,1)S(1)}, bf16[1,256,512]{2,1,0:T(8,128)(2,1)S(1)}, u32[]{:S(2)}, u32[]{:S(2)}) collective-permute-start(bf16[1,256,512]{2,1,0:T(8,128)(2,1)S(1)} %get-tuple-element.112.refs_10_), channel_id=1, source_target_pairs={{0,4},{1,5},{2,6},{3,7},{4,0},{5,1},{6,2},{7,3},{8,12},{9,13},{10,... | collective-permute-start | bytes 786440 | tf_op jit(solution)/shard_map/ppermute | solution.py:664
  62.6 2.8 %taps.1 = (f32[1024,512]{1,0:T(8,128)S(1)}, bf16[4,16,512]{2,1,0:T(8,128)(2,1)S(1)}, bf16[4,16,512]{2,1,0:T(8,128)(2,1)S(1)}) custom-call(bf16[1024,512]{1,0:T(8,128)(2,1)S(1)} %gconv.1.refs_4_.refs_0_, bf16[64,512]{1,0:T(8,128)(2,1)S(1)} %collective-permute-done.12.refs_5_.refs_1_, bf16[64,512]{1,0:T(8,128)(2,1)S(1)} %collective-permute-done.13.refs_2_, ...), custom_call_target="tpu_custom_call" | custom-call | flops 1 | bytes 1 | tf_op jit(solution)/shard_map/taps/pallas_call | solution.py:633
  65.4 0.7 second_core.1
  66.1 1.0 collective-permute-start.23
  67.1 1.3 %collective-permute-start.21 = (bf16[2,192,512]{2,1,0:T(8,128)(2,1)S(1)}, bf16[2,192,512]{2,1,0:T(8,128)(2,1)S(1)}, u32[]{:S(2)}, u32[]{:S(2)}) collective-permute-start(bf16[2,192,512]{2,1,0:T(8,128)(2,1)S(1)} %get-tuple-element.121.refs_4_), channel_id=1, source_target_pairs={{0,2},{1,3},{2,0},{3,1},{4,6},{5,7},{6,4},{7,5},{8,10},{9,11},{10,... | collective-permute-start | bytes 1179656 | tf_op jit(solution)/shard_map/ppermute | solution.py:664
  68.4 0.3 first_join.1
  68.7 1.6 %collective-permute-start.26 = (bf16[512,256]{1,0:T(8,128)(2,1)S(1)}, bf16[512,256]{1,0:T(8,128)(2,1)S(1)}, u32[]{:S(2)}, u32[]{:S(2)}) collective-permute-start(bf16[512,256]{1,0:T(8,128)(2,1)S(1)} %get-tuple-element.122.refs_2_), channel_id=1, source_target_pairs={{0,8},{8,0},{16,24},{24,16},{1,9},{9,1},{17,25},{25,17},{2,10},{10... | collective-permute-start | bytes 786440 | tf_op jit(solution)/shard_map/ppermute | solution.py:664
  70.3 1.2 %collective-permute-start.22 = (bf16[2,16,512]{2,1,0:T(8,128)(2,1)S(1)}, bf16[2,16,512]{2,1,0:T(8,128)(2,1)S(1)}, u32[]{:S(2)}, u32[]{:S(2)}) collective-permute-start(bf16[2,16,512]{2,1,0:T(8,128)(2,1)S(1)} %get-tuple-element.123.refs_3_), channel_id=1, source_target_pairs={{0,2},{1,3},{2,0},{3,1},{4,6},{5,7},{6,4},{7,5},{8,10},{9,11},{10,... | collective-permute-start | bytes 98312 | tf_op jit(solution)/shard_map/ppermute | solution.py:664
  71.5 3.5 %result.1 = (bf16[8,128,512]{2,1,0:T(8,128)(2,1)}, f32[8,128]{1,0:T(8,128)S(1)}) custom-call(bf16[1024,2048]{1,0:T(8,128)(2,1)S(1)} %get-tuple-element.89.refs_2_.refs_0_, f32[1024,512]{1,0:T(8,128)S(1)} %get-tuple-element.90.refs_1_, bf16[2048,512]{1,0:T(8,128)(2,1)S(1)} %copy-done, bf16[2,16,512]{2,1,0:T(8,128)(2,1)S(1)} %get-tuple-element.123.refs_3_), custom_call_target="tpu_custom_call" | custom-call | flops 2000000000 | bytes 1 | tf_op jit(solution)/shard_map/result/pallas_call | solution.py:633
  75.1 2.2 %collective-permute-done.22.refs_3_ = bf16[2,16,512]{2,1,0:T(8,128)(2,1)S(1)} collective-permute-done((bf16[2,16,512]{2,1,0:T(8,128)(2,1)S(1)}, bf16[2,16,512]{2,1,0:T(8,128)(2,1)S(1)}, u32[]{:S(2)}, u32[]{:S(2)}) %collective-permute-start.22) | collective-permute-done | bytes 32800 | tf_op jit(solution)/shard_map/ppermute | solution.py:664
  77.3 0.3 second_seq.1
  77.6 1.2 %collective-permute-start.24 = (bf16[1,208,512]{2,1,0:T(8,128)(2,1)S(1)}, bf16[1,208,512]{2,1,0:T(8,128)(2,1)S(1)}, u32[]{:S(2)}, u32[]{:S(2)}) collective-permute-start(bf16[1,208,512]{2,1,0:T(8,128)(2,1)S(1)} %get-tuple-element.133), channel_id=1, source_target_pairs={{0,4},{1,5},{2,6},{3,7},{4,0},{5,1},{6,2},{7,3},{8,12},{9,13},{10,... | collective-permute-start | bytes 638984 | tf_op jit(solution)/shard_map/ppermute | solution.py:664
  78.7 1.0 collective-permute-start.25
  79.7 0.2 first_last.1.refs_4_.refs_0_
  79.9 2.8 %collective-permute-start.28 = (bf16[512,256]{1,0:T(8,128)(2,1)S(1)}, bf16[512,256]{1,0:T(8,128)(2,1)S(1)}, u32[]{:S(2)}, u32[]{:S(2)}) collective-permute-start(bf16[512,256]{1,0:T(8,128)(2,1)S(1)} %first_last.1.refs_4_.refs_0_), channel_id=1, source_target_pairs={{0,16},{8,24},{16,0},{24,8},{1,17},{9,25},{17,1},{25,9},{2,18},{10... | collective-permute-start | bytes 786440 | tf_op jit(solution)/shard_map/ppermute | solution.py:664
  82.7 1.7 %collective-permute-done.25.refs_3_ = bf16[1,192,512]{2,1,0:T(8,128)(2,1)S(1)} collective-permute-done((bf16[1,192,512]{2,1,0:T(8,128)(2,1)S(1)}, bf16[1,192,512]{2,1,0:T(8,128)(2,1)S(1)}, u32[]{:S(2)}, u32[]{:S(2)}) %collective-permute-start.25) | collective-permute-done | bytes 196640 | tf_op jit(solution)/shard_map/ppermute | solution.py:664
  84.4 0.2 second_join.1
  84.7 1.6 %collective-permute-start.27 = (bf16[400,256]{1,0:T(8,128)(2,1)S(1)}, bf16[400,256]{1,0:T(8,128)(2,1)S(1)}, u32[]{:S(2)}, u32[]{:S(2)}) collective-permute-start(bf16[400,256]{1,0:T(8,128)(2,1)S(1)} %get-tuple-element.137.refs_4_), channel_id=1, source_target_pairs={{0,8},{8,0},{16,24},{24,16},{1,9},{9,1},{17,25},{25,17},{2,10},{10... | collective-permute-start | bytes 614408 | tf_op jit(solution)/shard_map/ppermute | solution.py:664
  86.3 2.7 %inputs.1 = (f32[8,128,512]{2,1,0:T(8,128)}, f32[8,128]{1,0:T(8,128)S(1)}) custom-call(f32[1024,512]{1,0:T(8,128)S(1)} %get-tuple-element.125.refs_0_, f32[4,1024,128]{2,1,0:T(8,128)S(1)} %get-tuple-element.85.refs_4_.refs_3_.refs_1_, f32[1024,512]{1,0:T(8,128)S(1)} %get-tuple-element.126.refs_2_, f32[1,512]{1,0:T(1,128)S(1)} %bitcast.13, ...), custom_call_target="tpu_custom_call" | custom-call | flops 1 | bytes 1 | tf_op jit(solution)/shard_map/inputs/pallas_call | solution.py:633
  89.0 3.3 %collective-permute-done.28.refs_1_ = bf16[512,256]{1,0:T(8,128)(2,1)S(1)} collective-permute-done((bf16[512,256]{1,0:T(8,128)(2,1)S(1)}, bf16[512,256]{1,0:T(8,128)(2,1)S(1)}, u32[]{:S(2)}, u32[]{:S(2)}) %collective-permute-start.28) | collective-permute-done | bytes 262176 | tf_op jit(solution)/shard_map/ppermute | solution.py:664
  92.3 0.2 first_total.1.refs_2_.refs_0_
  92.5 0.5 collective-permute-done.27.refs_1_
  93.0 0.2 second_last.1.refs_0_.refs_2_
  93.2 2.5 %collective-permute-start.29 = (bf16[400,256]{1,0:T(8,128)(2,1)S(1)}, bf16[400,256]{1,0:T(8,128)(2,1)S(1)}, u32[]{:S(2)}, u32[]{:S(2)}) collective-permute-start(bf16[400,256]{1,0:T(8,128)(2,1)S(1)} %second_last.1.refs_0_.refs_2_), channel_id=1, source_target_pairs={{0,16},{8,24},{16,0},{24,8},{1,17},{9,25},{17,1},{25,9},{2,18},{10... | collective-permute-start | bytes 614408 | tf_op jit(solution)/shard_map/ppermute | solution.py:664
  95.7 2.5 %collective-permute-start.31 = (bf16[512,256]{1,0:T(8,128)(2,1)S(1)}, bf16[512,256]{1,0:T(8,128)(2,1)S(1)}, u32[]{:S(2)}, u32[]{:S(2)}) collective-permute-start(bf16[512,256]{1,0:T(8,128)(2,1)S(1)} %first_total.1.refs_2_.refs_0_), channel_id=1, source_target_pairs={{0,8},{8,0},{16,24},{24,16},{1,9},{9,1},{17,25},{25,17},{2,10},{10... | collective-permute-start | bytes 786440 | tf_op jit(solution)/shard_map/ppermute | solution.py:664
  98.2 5.8 %collective-permute-done.29.refs_1_ = bf16[400,256]{1,0:T(8,128)(2,1)S(1)} collective-permute-done((bf16[400,256]{1,0:T(8,128)(2,1)S(1)}, bf16[400,256]{1,0:T(8,128)(2,1)S(1)}, u32[]{:S(2)}, u32[]{:S(2)}) %collective-permute-start.29) | collective-permute-done | bytes 204832 | tf_op jit(solution)/shard_map/ppermute | solution.py:664
  104.0 0.1 second_total.1.refs_2_.refs_0_
  104.2 1.2 %collective-permute-done.31.refs_1_ = bf16[512,256]{1,0:T(8,128)(2,1)S(1)} collective-permute-done((bf16[512,256]{1,0:T(8,128)(2,1)S(1)}, bf16[512,256]{1,0:T(8,128)(2,1)S(1)}, u32[]{:S(2)}, u32[]{:S(2)}) %collective-permute-start.31) | collective-permute-done | bytes 262176 | tf_op jit(solution)/shard_map/ppermute | solution.py:664
  105.4 1.0 first_finish.1
  106.4 3.5 %collective-permute-done.30.refs_1_ = bf16[400,256]{1,0:T(8,128)(2,1)S(1)} collective-permute-done((bf16[400,256]{1,0:T(8,128)(2,1)S(1)}, bf16[400,256]{1,0:T(8,128)(2,1)S(1)}, u32[]{:S(2)}, u32[]{:S(2)}) %collective-permute-start.30) | collective-permute-done | bytes 204832 | tf_op jit(solution)/shard_map/ppermute | solution.py:664
  110.0 0.9 second_finish.1
  (46 shorter events, 0.4 us)
Async XLA Ops:
  0.6 5.6 %copy-start = (bf16[2048,512]{1,0:T(8,128)(2,1)S(1)}, bf16[2048,512]{1,0:T(8,128)(2,1)}, u32[]{:S(2)}) copy-start(bf16[2048,512]{1,0:T(8,128)(2,1)} %refs_2_.1) | copy-start | bytes 6291460
  0.7 5.6 %copy-start.7 = (bf16[8,128,512]{2,1,0:T(8,128)(2,1)S(1)}, bf16[8,128,512]{2,1,0:T(8,128)(2,1)}, u32[]{:S(2)}) copy-start(bf16[8,128,512]{2,1,0:T(8,128)(2,1)} %refs_0_.3) | copy-start | bytes 3145732
  2.8 5.4 %copy-start.2 = (bf16[512,2048]{1,0:T(8,128)(2,1)S(1)}, bf16[512,2048]{1,0:T(8,128)(2,1)}, u32[]{:S(2)}) copy-start(bf16[512,2048]{1,0:T(8,128)(2,1)} %refs_1_.7) | copy-start | bytes 6291460
  2.8 5.4 %copy-start.4 = (f32[512,4]{0,1:T(4,128)S(1)}, f32[512,4]{0,1:T(4,128)}, u32[]{:S(2)}) copy-start(f32[512,4]{0,1:T(4,128)} %param.14) | copy-start | bytes 24580
  2.8 5.4 %copy-start.8 = (f32[1024]{0:T(1024)S(1)}, f32[1024]{0:T(1024)}, u32[]{:S(2)}) copy-start(f32[1024]{0:T(1024)} %param.15) | copy-start | bytes 12292
  2.8 5.3 %collective-permute-start.1 = (bf16[64,512]{1,0:T(8,128)(2,1)S(1)}, bf16[64,512]{1,0:T(8,128)(2,1)S(1)}, u32[]{:S(2)}, u32[]{:S(2)}) collective-permute-start(bf16[64,512]{1,0:T(8,128)(2,1)S(1)} %get-tuple-element.81.refs_2_), channel_id=1, source_target_pairs={{0,7},{1,2},{2,1},{3,4},{4,3},{5,6},{6,5},{7,0},{8,15},{9,10},{10,... | collective-permute-start | bytes 196616 | tf_op jit(solution)/shard_map/ppermute | solution.py:651
  6.2 2.0 %collective-permute-start = (bf16[64,512]{1,0:T(8,128)(2,1)S(1)}, bf16[64,512]{1,0:T(8,128)(2,1)S(1)}, u32[]{:S(2)}, u32[]{:S(2)}) collective-permute-start(bf16[64,512]{1,0:T(8,128)(2,1)S(1)} %get-tuple-element.81.refs_2_), channel_id=1, source_target_pairs={{0,1},{1,0},{2,3},{3,2},{4,5},{5,4},{6,7},{7,6},{8,9},{9,8},{10,11... | collective-permute-start | bytes 196616 | tf_op jit(solution)/shard_map/ppermute | solution.py:664
  11.7 1.3 %collective-permute-start.2 = (f32[2,8,1024]{2,1,0:T(8,128)S(1)}, f32[2,8,1024]{2,1,0:T(8,128)S(1)}, u32[]{:S(2)}, u32[]{:S(2)}) collective-permute-start(f32[2,8,1024]{2,1,0:T(8,128)S(1)} %get-tuple-element.84.refs_0_.refs_2_), channel_id=1, source_target_pairs={{0,1},{1,0},{2,3},{3,2},{4,5},{5,4},{6,7},{7,6},{8,9},{9,8},{10,11... | collective-permute-start | bytes 196616 | tf_op jit(solution)/shard_map/ppermute | solution.py:664
  13.0 8.2 %copy-start.1 = (bf16[512,2048]{1,0:T(8,128)(2,1)S(1)}, bf16[512,2048]{1,0:T(8,128)(2,1)}, u32[]{:S(2)}) copy-start(bf16[512,2048]{1,0:T(8,128)(2,1)} %refs_7_.1) | copy-start | bytes 6291460
  13.0 8.2 %copy-start.3 = (bf16[1024,512]{1,0:T(8,128)(2,1)S(1)}, bf16[1024,512]{1,0:T(8,128)(2,1)}, u32[]{:S(2)}) copy-start(bf16[1024,512]{1,0:T(8,128)(2,1)} %refs_6_.3) | copy-start | bytes 3145732
  13.0 8.2 %copy-start.5 = (f32[512]{0:T(512)S(1)}, f32[512]{0:T(512)}, u32[]{:S(2)}) copy-start(f32[512]{0:T(512)} %param.18) | copy-start | bytes 6148
  13.1 5.5 %collective-permute-start.5 = (f32[2,8,1024]{2,1,0:T(8,128)S(1)}, f32[2,8,1024]{2,1,0:T(8,128)S(1)}, u32[]{:S(2)}, u32[]{:S(2)}) collective-permute-start(f32[2,8,1024]{2,1,0:T(8,128)S(1)} %chip_totals.1.refs_2_), channel_id=1, source_target_pairs={{0,6},{1,7},{2,4},{3,5},{4,2},{5,3},{6,0},{7,1},{8,14},{9,15},{10,... | collective-permute-start | bytes 196616 | tf_op jit(solution)/shard_map/ppermute | solution.py:664
  16.1 4.3 %collective-permute-start.4 = (f32[2,8,1024]{2,1,0:T(8,128)S(1)}, f32[2,8,1024]{2,1,0:T(8,128)S(1)}, u32[]{:S(2)}, u32[]{:S(2)}) collective-permute-start(f32[2,8,1024]{2,1,0:T(8,128)S(1)} %chip_totals.1.refs_2_), channel_id=1, source_target_pairs={{0,4},{1,5},{2,6},{3,7},{4,0},{5,1},{6,2},{7,3},{8,12},{9,13},{10,... | collective-permute-start | bytes 196616 | tf_op jit(solution)/shard_map/ppermute | solution.py:664
  17.0 4.3 %collective-permute-start.3 = (f32[2,8,1024]{2,1,0:T(8,128)S(1)}, f32[2,8,1024]{2,1,0:T(8,128)S(1)}, u32[]{:S(2)}, u32[]{:S(2)}) collective-permute-start(f32[2,8,1024]{2,1,0:T(8,128)S(1)} %chip_totals.1.refs_2_), channel_id=1, source_target_pairs={{0,2},{1,3},{2,0},{3,1},{4,6},{5,7},{6,4},{7,5},{8,10},{9,11},{10,... | collective-permute-start | bytes 196616 | tf_op jit(solution)/shard_map/ppermute | solution.py:664
  33.9 10.7 %collective-permute-start.10 = (bf16[4,256,512]{2,1,0:T(8,128)(2,1)S(1)}, bf16[4,256,512]{2,1,0:T(8,128)(2,1)S(1)}, u32[]{:S(2)}, u32[]{:S(2)}) collective-permute-start(bf16[4,256,512]{2,1,0:T(8,128)(2,1)S(1)} %get-tuple-element.102), channel_id=1, source_target_pairs={{0,1},{1,0},{2,3},{3,2},{4,5},{5,4},{6,7},{7,6},{8,9},{9,8},{10,11... | collective-permute-start | bytes 3145736 | tf_op jit(solution)/shard_map/ppermute | solution.py:664
  33.9 10.6 %collective-permute-start.11 = (bf16[4,256,512]{2,1,0:T(8,128)(2,1)S(1)}, bf16[4,256,512]{2,1,0:T(8,128)(2,1)S(1)}, u32[]{:S(2)}, u32[]{:S(2)}) collective-permute-start(bf16[4,256,512]{2,1,0:T(8,128)(2,1)S(1)} %get-tuple-element.104), channel_id=1, source_target_pairs={{0,1},{1,0},{2,3},{3,2},{4,5},{5,4},{6,7},{7,6},{8,9},{9,8},{10,11... | collective-permute-start | bytes 3145736 | tf_op jit(solution)/shard_map/ppermute | solution.py:664
  39.5 1.4 %collective-permute-start.6 = (f32[8,1024]{1,0:T(8,128)S(1)}, f32[8,1024]{1,0:T(8,128)S(1)}, u32[]{:S(2)}, u32[]{:S(2)}) collective-permute-start(f32[8,1024]{1,0:T(8,128)S(1)} %get-tuple-element.95.refs_0_), channel_id=1, source_target_pairs={{0,1},{1,0},{2,3},{3,2},{4,5},{5,4},{6,7},{7,6},{8,9},{9,8},{10,11... | collective-permute-start | bytes 98312 | tf_op jit(solution)/shard_map/ppermute | solution.py:664
  41.0 6.4 %collective-permute-start.9 = (f32[8,1024]{1,0:T(8,128)S(1)}, f32[8,1024]{1,0:T(8,128)S(1)}, u32[]{:S(2)}, u32[]{:S(2)}) collective-permute-start(f32[8,1024]{1,0:T(8,128)S(1)} %chip_outgoing.1.refs_4_), channel_id=1, source_target_pairs={{0,6},{1,7},{2,4},{3,5},{4,2},{5,3},{6,0},{7,1},{8,14},{9,15},{10,... | collective-permute-start | bytes 98312 | tf_op jit(solution)/shard_map/ppermute | solution.py:664
  42.4 5.0 %collective-permute-start.8 = (f32[8,1024]{1,0:T(8,128)S(1)}, f32[8,1024]{1,0:T(8,128)S(1)}, u32[]{:S(2)}, u32[]{:S(2)}) collective-permute-start(f32[8,1024]{1,0:T(8,128)S(1)} %chip_outgoing.1.refs_4_), channel_id=1, source_target_pairs={{0,4},{1,5},{2,6},{3,7},{4,0},{5,1},{6,2},{7,3},{8,12},{9,13},{10,... | collective-permute-start | bytes 98312 | tf_op jit(solution)/shard_map/ppermute | solution.py:664
  43.4 4.0 %collective-permute-start.7 = (f32[8,1024]{1,0:T(8,128)S(1)}, f32[8,1024]{1,0:T(8,128)S(1)}, u32[]{:S(2)}, u32[]{:S(2)}) collective-permute-start(f32[8,1024]{1,0:T(8,128)S(1)} %chip_outgoing.1.refs_4_), channel_id=1, source_target_pairs={{0,2},{1,3},{2,0},{3,1},{4,6},{5,7},{6,4},{7,5},{8,10},{9,11},{10,... | collective-permute-start | bytes 98312 | tf_op jit(solution)/shard_map/ppermute | solution.py:664
  45.4 13.5 %collective-permute-start.15 = (bf16[2,256,512]{2,1,0:T(8,128)(2,1)S(1)}, bf16[2,256,512]{2,1,0:T(8,128)(2,1)S(1)}, u32[]{:S(2)}, u32[]{:S(2)}) collective-permute-start(bf16[2,256,512]{2,1,0:T(8,128)(2,1)S(1)} %get-tuple-element.111), channel_id=1, source_target_pairs={{0,4},{1,5},{2,6},{3,7},{4,0},{5,1},{6,2},{7,3},{8,12},{9,13},{10,... | collective-permute-start | bytes 1572872 | tf_op jit(solution)/shard_map/ppermute | solution.py:664
  46.6 13.6 %collective-permute-start.14 = (bf16[2,256,512]{2,1,0:T(8,128)(2,1)S(1)}, bf16[2,256,512]{2,1,0:T(8,128)(2,1)S(1)}, u32[]{:S(2)}, u32[]{:S(2)}) collective-permute-start(bf16[2,256,512]{2,1,0:T(8,128)(2,1)S(1)} %get-tuple-element.105.refs_16_), channel_id=1, source_target_pairs={{0,2},{1,3},{2,0},{3,1},{4,6},{5,7},{6,4},{7,5},{8,10},{9,11},{10,... | collective-permute-start | bytes 1572872 | tf_op jit(solution)/shard_map/ppermute | solution.py:664
  52.7 3.0 %collective-permute-start.12 = (bf16[64,512]{1,0:T(8,128)(2,1)S(1)}, bf16[64,512]{1,0:T(8,128)(2,1)S(1)}, u32[]{:S(2)}, u32[]{:S(2)}) collective-permute-start(bf16[64,512]{1,0:T(8,128)(2,1)S(1)} %get-tuple-element.108), channel_id=1, source_target_pairs={{0,1},{1,0},{2,3},{3,2},{4,5},{5,4},{6,7},{7,6},{8,9},{9,8},{10,11... | collective-permute-start | bytes 196616 | tf_op jit(solution)/shard_map/ppermute | solution.py:664
  52.8 12.6 %collective-permute-start.19 = (bf16[4,256,512]{2,1,0:T(8,128)(2,1)S(1)}, bf16[4,256,512]{2,1,0:T(8,128)(2,1)S(1)}, u32[]{:S(2)}, u32[]{:S(2)}) collective-permute-start(bf16[4,256,512]{2,1,0:T(8,128)(2,1)S(1)} %get-tuple-element.119), channel_id=1, source_target_pairs={{0,1},{1,0},{2,3},{3,2},{4,5},{5,4},{6,7},{7,6},{8,9},{9,8},{10,11... | collective-permute-start | bytes 3145736 | tf_op jit(solution)/shard_map/ppermute | solution.py:664
  53.3 12.1 %collective-permute-start.20 = (bf16[4,128,512]{2,1,0:T(8,128)(2,1)S(1)}, bf16[4,128,512]{2,1,0:T(8,128)(2,1)S(1)}, u32[]{:S(2)}, u32[]{:S(2)}) collective-permute-start(bf16[4,128,512]{2,1,0:T(8,128)(2,1)S(1)} %get-tuple-element.120), channel_id=1, source_target_pairs={{0,1},{1,0},{2,3},{3,2},{4,5},{5,4},{6,7},{7,6},{8,9},{9,8},{10,11... | collective-permute-start | bytes 1572872 | tf_op jit(solution)/shard_map/ppermute | solution.py:664
  55.8 6.8 %collective-permute-start.13 = (bf16[64,512]{1,0:T(8,128)(2,1)S(1)}, bf16[64,512]{1,0:T(8,128)(2,1)S(1)}, u32[]{:S(2)}, u32[]{:S(2)}) collective-permute-start(bf16[64,512]{1,0:T(8,128)(2,1)S(1)} %get-tuple-element.108), channel_id=1, source_target_pairs={{0,7},{1,2},{2,1},{3,4},{4,3},{5,6},{6,5},{7,0},{8,15},{9,10},{10,... | collective-permute-start | bytes 196616 | tf_op jit(solution)/shard_map/ppermute | solution.py:651
  60.7 7.7 %collective-permute-start.18 = (bf16[1,256,512]{2,1,0:T(8,128)(2,1)S(1)}, bf16[1,256,512]{2,1,0:T(8,128)(2,1)S(1)}, u32[]{:S(2)}, u32[]{:S(2)}) collective-permute-start(bf16[1,256,512]{2,1,0:T(8,128)(2,1)S(1)} %get-tuple-element.117), channel_id=1, source_target_pairs={{0,2},{1,3},{2,0},{3,1},{4,6},{5,7},{6,4},{7,5},{8,10},{9,11},{10,... | collective-permute-start | bytes 786440 | tf_op jit(solution)/shard_map/ppermute | solution.py:664
  61.5 7.0 %collective-permute-start.17 = (bf16[1,256,512]{2,1,0:T(8,128)(2,1)S(1)}, bf16[1,256,512]{2,1,0:T(8,128)(2,1)S(1)}, u32[]{:S(2)}, u32[]{:S(2)}) collective-permute-start(bf16[1,256,512]{2,1,0:T(8,128)(2,1)S(1)} %get-tuple-element.112.refs_10_), channel_id=1, source_target_pairs={{0,4},{1,5},{2,6},{3,7},{4,0},{5,1},{6,2},{7,3},{8,12},{9,13},{10,... | collective-permute-start | bytes 786440 | tf_op jit(solution)/shard_map/ppermute | solution.py:664
  66.1 11.1 %collective-permute-start.23 = (bf16[2,192,512]{2,1,0:T(8,128)(2,1)S(1)}, bf16[2,192,512]{2,1,0:T(8,128)(2,1)S(1)}, u32[]{:S(2)}, u32[]{:S(2)}) collective-permute-start(bf16[2,192,512]{2,1,0:T(8,128)(2,1)S(1)} %get-tuple-element.130), channel_id=1, source_target_pairs={{0,4},{1,5},{2,6},{3,7},{4,0},{5,1},{6,2},{7,3},{8,12},{9,13},{10,... | collective-permute-start | bytes 1179656 | tf_op jit(solution)/shard_map/ppermute | solution.py:664
  67.1 10.2 %collective-permute-start.21 = (bf16[2,192,512]{2,1,0:T(8,128)(2,1)S(1)}, bf16[2,192,512]{2,1,0:T(8,128)(2,1)S(1)}, u32[]{:S(2)}, u32[]{:S(2)}) collective-permute-start(bf16[2,192,512]{2,1,0:T(8,128)(2,1)S(1)} %get-tuple-element.121.refs_4_), channel_id=1, source_target_pairs={{0,2},{1,3},{2,0},{3,1},{4,6},{5,7},{6,4},{7,5},{8,10},{9,11},{10,... | collective-permute-start | bytes 1179656 | tf_op jit(solution)/shard_map/ppermute | solution.py:664
  68.4 1.9 %collective-permute-start.16 = (bf16[4,16,512]{2,1,0:T(8,128)(2,1)S(1)}, bf16[4,16,512]{2,1,0:T(8,128)(2,1)S(1)}, u32[]{:S(2)}, u32[]{:S(2)}) collective-permute-start(bf16[4,16,512]{2,1,0:T(8,128)(2,1)S(1)} %get-tuple-element.114), channel_id=1, source_target_pairs={{0,1},{1,0},{2,3},{3,2},{4,5},{5,4},{6,7},{7,6},{8,9},{9,8},{10,11... | collective-permute-start | bytes 196616 | tf_op jit(solution)/shard_map/ppermute | solution.py:664
  68.7 10.9 %collective-permute-start.26 = (bf16[512,256]{1,0:T(8,128)(2,1)S(1)}, bf16[512,256]{1,0:T(8,128)(2,1)S(1)}, u32[]{:S(2)}, u32[]{:S(2)}) collective-permute-start(bf16[512,256]{1,0:T(8,128)(2,1)S(1)} %get-tuple-element.122.refs_2_), channel_id=1, source_target_pairs={{0,8},{8,0},{16,24},{24,16},{1,9},{9,1},{17,25},{25,17},{2,10},{10... | collective-permute-start | bytes 786440 | tf_op jit(solution)/shard_map/ppermute | solution.py:664
  70.3 6.9 %collective-permute-start.22 = (bf16[2,16,512]{2,1,0:T(8,128)(2,1)S(1)}, bf16[2,16,512]{2,1,0:T(8,128)(2,1)S(1)}, u32[]{:S(2)}, u32[]{:S(2)}) collective-permute-start(bf16[2,16,512]{2,1,0:T(8,128)(2,1)S(1)} %get-tuple-element.123.refs_3_), channel_id=1, source_target_pairs={{0,2},{1,3},{2,0},{3,1},{4,6},{5,7},{6,4},{7,5},{8,10},{9,11},{10,... | collective-permute-start | bytes 98312 | tf_op jit(solution)/shard_map/ppermute | solution.py:664
  77.6 6.9 %collective-permute-start.24 = (bf16[1,208,512]{2,1,0:T(8,128)(2,1)S(1)}, bf16[1,208,512]{2,1,0:T(8,128)(2,1)S(1)}, u32[]{:S(2)}, u32[]{:S(2)}) collective-permute-start(bf16[1,208,512]{2,1,0:T(8,128)(2,1)S(1)} %get-tuple-element.133), channel_id=1, source_target_pairs={{0,4},{1,5},{2,6},{3,7},{4,0},{5,1},{6,2},{7,3},{8,12},{9,13},{10,... | collective-permute-start | bytes 638984 | tf_op jit(solution)/shard_map/ppermute | solution.py:664
  78.7 5.7 %collective-permute-start.25 = (bf16[1,192,512]{2,1,0:T(8,128)(2,1)S(1)}, bf16[1,192,512]{2,1,0:T(8,128)(2,1)S(1)}, u32[]{:S(2)}, u32[]{:S(2)}) collective-permute-start(bf16[1,192,512]{2,1,0:T(8,128)(2,1)S(1)} %get-tuple-element.135.refs_2_), channel_id=1, source_target_pairs={{0,2},{1,3},{2,0},{3,1},{4,6},{5,7},{6,4},{7,5},{8,10},{9,11},{10,... | collective-permute-start | bytes 589832 | tf_op jit(solution)/shard_map/ppermute | solution.py:664
  79.9 12.4 %collective-permute-start.28 = (bf16[512,256]{1,0:T(8,128)(2,1)S(1)}, bf16[512,256]{1,0:T(8,128)(2,1)S(1)}, u32[]{:S(2)}, u32[]{:S(2)}) collective-permute-start(bf16[512,256]{1,0:T(8,128)(2,1)S(1)} %first_last.1.refs_4_.refs_0_), channel_id=1, source_target_pairs={{0,16},{8,24},{16,0},{24,8},{1,17},{9,25},{17,1},{25,9},{2,18},{10... | collective-permute-start | bytes 786440 | tf_op jit(solution)/shard_map/ppermute | solution.py:664
  84.4 1.9 %copy-start.6 = (f32[512]{0:T(512)S(1)}, f32[512]{0:T(512)}, u32[]{:S(2)}) copy-start(f32[512]{0:T(512)} %param.13) | copy-start | bytes 6148
  84.7 8.4 %collective-permute-start.27 = (bf16[400,256]{1,0:T(8,128)(2,1)S(1)}, bf16[400,256]{1,0:T(8,128)(2,1)S(1)}, u32[]{:S(2)}, u32[]{:S(2)}) collective-permute-start(bf16[400,256]{1,0:T(8,128)(2,1)S(1)} %get-tuple-element.137.refs_4_), channel_id=1, source_target_pairs={{0,8},{8,0},{16,24},{24,16},{1,9},{9,1},{17,25},{25,17},{2,10},{10... | collective-permute-start | bytes 614408 | tf_op jit(solution)/shard_map/ppermute | solution.py:664
  93.2 10.8 %collective-permute-start.29 = (bf16[400,256]{1,0:T(8,128)(2,1)S(1)}, bf16[400,256]{1,0:T(8,128)(2,1)S(1)}, u32[]{:S(2)}, u32[]{:S(2)}) collective-permute-start(bf16[400,256]{1,0:T(8,128)(2,1)S(1)} %second_last.1.refs_0_.refs_2_), channel_id=1, source_target_pairs={{0,16},{8,24},{16,0},{24,8},{1,17},{9,25},{17,1},{25,9},{2,18},{10... | collective-permute-start | bytes 614408 | tf_op jit(solution)/shard_map/ppermute | solution.py:664
  95.7 9.7 %collective-permute-start.31 = (bf16[512,256]{1,0:T(8,128)(2,1)S(1)}, bf16[512,256]{1,0:T(8,128)(2,1)S(1)}, u32[]{:S(2)}, u32[]{:S(2)}) collective-permute-start(bf16[512,256]{1,0:T(8,128)(2,1)S(1)} %first_total.1.refs_2_.refs_0_), channel_id=1, source_target_pairs={{0,8},{8,0},{16,24},{24,16},{1,9},{9,1},{17,25},{25,17},{2,10},{10... | collective-permute-start | bytes 786440 | tf_op jit(solution)/shard_map/ppermute | solution.py:664
  104.1 5.8 %collective-permute-start.30 = (bf16[400,256]{1,0:T(8,128)(2,1)S(1)}, bf16[400,256]{1,0:T(8,128)(2,1)S(1)}, u32[]{:S(2)}, u32[]{:S(2)}) collective-permute-start(bf16[400,256]{1,0:T(8,128)(2,1)S(1)} %second_total.1.refs_2_.refs_0_), channel_id=1, source_target_pairs={{0,8},{8,0},{16,24},{24,16},{1,9},{9,1},{17,25},{25,17},{2,10},{10... | collective-permute-start | bytes 614408 | tf_op jit(solution)/shard_map/ppermute | solution.py:664

commit v6 on v5

--- a/solution.py
+++ b/solution.py
@@ -13,7 +13,7 @@
 SMALL = 16
 LANES = 128
 FINAL = ("result", "inputs", "first_finish", "second_finish")
-WORK = {"second_join": 5 * 10**9, "result": 2000000000} | dict.fromkeys(("ingest", "prepare", "front", "forward", "first_seq", "back", "chip_outgoing"), 10**10)
+WORK = {"second_core": 10**9, "second_join": 5 * 10**9, "result": 2000000000} | dict.fromkeys(("ingest", "prepare", "front", "forward", "first_seq", "back", "chip_outgoing"), 10**10)
 LIMITS = {"ingest": 4, "prepare": 6, "prepare_rest": 3, "front": 7, "forward": 6, "weights": 3, "reverse": 5, "back": 3, "gconv": 3, "taps": 5, "inputs": 7, "result": 7}
 F32 = jnp.float32
 BF16 = jnp.bfloat16
@@ -184,7 +184,7 @@
             decay = (1.0 - gate) * widen(keep_ref[here, :], hidden)
             return decay * prod, decay * state + gate * cand_ref[here, :]
 
-        return lax.fori_loop(0, steps, step, carry, unroll=8)
+        return lax.fori_loop(0, steps, step, carry, unroll=16)
 
     first = (jnp.ones((batch, hidden), F32), jnp.zeros((batch, hidden), F32))
     prod, state = lax.fori_loop(0, span // steps, chunk, first)
@@ -229,7 +229,7 @@
             held_ref[both, :] = jnp.concatenate(out, axis=0).astype(BF16)
             return state
 
-        state = lax.fori_loop(0, steps // 2, two_steps, state, unroll=4)
+        state = lax.fori_loop(0, steps // 2, two_steps, state, unroll=8)
         middle = read(xt_ref, rows) + dot(held_ref[rows, :], w_out_ref[...])
         mid_ref[rows, :] = middle
         nmid = (middle * rms(middle) * gain).astype(BF16)
@@ -238,7 +238,7 @@
             cols = slice(part * block, (part + 1) * block)
             up = dot(nmid, w_up_ref[:, cols])
             square = up * up
-            half = 0.5 + 0.5 * jnp.tanh(up * (GELU_C + (GELU_C * GELU_A) * square))
+            half = jax.nn.sigmoid(up * (2.0 * GELU_C + (2.0 * GELU_C * GELU_A) * square))
             act = up * half
             slope = half + act * (1.0 - half) * (2.0 * GELU_C + (6.0 * GELU_C * GELU_A) * square)
             act_ref[rows, cols] = act.astype(BF16)
@@ -309,7 +309,7 @@
             decay = (1.0 - gate_ref[here, :]) * widen(keep_ref[here, :], hidden)
             return decay * (gheld_ref[here, :] + arriving)
 
-        return lax.fori_loop(0, steps, back, arriving, unroll=8), gnorm2
+        return lax.fori_loop(0, steps, back, arriving, unroll=16), gnorm2
 
     first = (jnp.zeros((batch, hidden), F32), jnp.zeros((1, width), F32))
     outgoing, gnorm2 = lax.fori_loop(0, span // steps, chunk, first)
@@ -359,7 +359,7 @@
         return arriving, gbias
 
     _, gbias = lax.fori_loop(
-        0, span // 2, two_steps, (carry_in, jnp.zeros((batch, hidden), F32)), unroll=4
+        0, span // 2, two_steps, (carry_in, jnp.zeros((batch, hidden), F32)), unroll=8
     )
     gbias_ref[...] = jnp.sum(gbias, axis=0, keepdims=True)
     edge_ref[...] = dot_nt(gproj_ref[: edge_ref.shape[0], :], w_in_ref[...]).astype(BF16)

time: 111 us -> 111 us (level)
  no operation moved by 1% of the time
where the time goes in v6:
time: 111 us; the launch traced here: 110 us
  Pallas kernels  49.1 us (44%)
  starting transfers between devices  34.6 us (31%)
  waiting for transfers between devices  25.8 us (23%)
    pallas_call x28, Pallas kernels, call(): pl.pallas_call(body, name=name, out_shape=[(pltpu.HBM if name in FINAL an...  49.1 us
    ppermute x30, starting transfers between devices, swap_by(): lax.ppermute(block, axis, [(i, i ^ mask) for i in range(lax.axis_size(axi...  29.5 us
    ppermute x30, waiting for transfers between devices, swap_by(): lax.ppermute(block, axis, [(i, i ^ mask) for i in range(lax.axis_size(axi...  25.2 us
    ppermute x2, starting transfers between devices, neighbour(): lax.ppermute(block, axis, [(i, (i + 1 if i % 2 else i - 1) % count) for i...  5.09 us
  transfers between devices with their start and end apart: 32, of which 14 were waited for; matrix products, arithmetic and copies ran while one was open for 0% of the time, Pallas kernels for 27%

profile of v6, /device:TPU:0, one launch (start us, length us, event | category | flops | bytes accessed | tf_op | source)
XLA Modules:
  0.0 110.5 jit_solution(14628247562252333680)
XLA Ops:
  0.7 2.1 %ingest.1 = (f32[4,1024,128]{2,1,0:T(8,128)S(1)}, bf16[1024,512]{1,0:T(8,128)(2,1)S(1)}, bf16[64,512]{1,0:T(8,128)(2,1)S(1)}, f32[1024,128]{1,0:T(8,128)S(1)}) custom-call(bf16[8,128,512]{2,1,0:T(8,128)(2,1)} %refs_0_.2, s32[8,128]{1,0:T(8,128)} %refs_1_.4, f32[1,512]{1,0:T(1,128)} %bitcast.12), custom_call_target="tpu_custom_call" | custom-call | flops 10000000000 | bytes 1 | tf_op jit(solution)/shard_map/ingest/pallas_call | solution.py:633
  2.8 3.4 %collective-permute-start.1 = (bf16[64,512]{1,0:T(8,128)(2,1)S(1)}, bf16[64,512]{1,0:T(8,128)(2,1)S(1)}, u32[]{:S(2)}, u32[]{:S(2)}) collective-permute-start(bf16[64,512]{1,0:T(8,128)(2,1)S(1)} %get-tuple-element.81.refs_2_), channel_id=1, source_target_pairs={{0,7},{1,2},{2,1},{3,4},{4,3},{5,6},{6,5},{7,0},{8,15},{9,10},{10,... | collective-permute-start | bytes 196616 | tf_op jit(solution)/shard_map/ppermute | solution.py:651
  6.3 1.4 %prepare.1 = (bf16[1024,512]{1,0:T(8,128)(2,1)S(1)}, bf16[1024,1024]{1,0:T(8,128)(2,1)S(1)}) custom-call(bf16[8,128,512]{2,1,0:T(8,128)(2,1)S(1)} %copy-done.7, bf16[2048,512]{1,0:T(8,128)(2,1)S(1)} %copy-done, bf16[64,512]{1,0:T(8,128)(2,1)S(1)} %get-tuple-element.81.refs_2_), custom_call_target="tpu_custom_call" | custom-call | flops 10000000000 | bytes 1 | tf_op jit(solution)/shard_map/prepare/pallas_call | solution.py:633
  7.6 0.6 collective-permute-done.1.refs_2_.refs_6_
  8.2 3.4 %front.1 = (bf16[1024,512]{1,0:T(8,128)(2,1)S(1)}, f32[1024,1024]{1,0:T(8,128)S(1)}, f32[1024,1024]{1,0:T(8,128)S(1)}, f32[2,8,1024]{2,1,0:T(8,128)S(1)}) custom-call(bf16[1024,512]{1,0:T(8,128)(2,1)S(1)} %get-tuple-element.80.refs_0_.refs_4_, bf16[64,512]{1,0:T(8,128)(2,1)S(1)} %collective-permute-done.refs_1_.refs_5_, ...), custom_call_target="tpu_custom_call" | custom-call | flops 10000000000 | bytes 1 | tf_op jit(solution)/shard_map/front/pallas_call | solution.py:633
  11.6 0.1 collective-permute-start.2
  11.7 1.2 %collective-permute-done.2.refs_1_.refs_0_.refs_3_.refs_6_ = f32[2,8,1024]{2,1,0:T(8,128)S(1)} collective-permute-done((f32[2,8,1024]{2,1,0:T(8,128)S(1)}, f32[2,8,1024]{2,1,0:T(8,128)S(1)}, u32[]{:S(2)}, u32[]{:S(2)}) %collective-permute-start.2) | collective-permute-done | bytes 65568 | tf_op jit(solution)/shard_map/ppermute | solution.py:664
  13.0 3.0 %collective-permute-start.5 = (f32[2,8,1024]{2,1,0:T(8,128)S(1)}, f32[2,8,1024]{2,1,0:T(8,128)S(1)}, u32[]{:S(2)}, u32[]{:S(2)}) collective-permute-start(f32[2,8,1024]{2,1,0:T(8,128)S(1)} %chip_totals.1.refs_2_), channel_id=1, source_target_pairs={{0,6},{1,7},{2,4},{3,5},{4,2},{5,3},{6,0},{7,1},{8,14},{9,15},{10,... | collective-permute-start | bytes 196616 | tf_op jit(solution)/shard_map/ppermute | solution.py:664
  16.0 0.9 collective-permute-start.4
  16.9 1.3 %prepare_rest.1.refs_9_.refs_13_ = bf16[1024,1024]{1,0:T(8,128)(2,1)S(1)} custom-call(bf16[1024,512]{1,0:T(8,128)(2,1)S(1)} %get-tuple-element.83.refs_7_.refs_0_.refs_3_.refs_2_, bf16[2048,512]{1,0:T(8,128)(2,1)S(1)} %copy-done, f32[2,8,1024]{2,1,0:T(8,128)S(1)} %chip_totals.1.refs_2_), custom_call_target="tpu_custom_call" | custom-call | flops 1 | bytes 1 | tf_op jit(solution)/shard_map/prepare_rest/pallas_call | solution.py:633
  18.2 0.3 collective-permute-done.5.refs_3_.refs_2_
  18.5 1.8 %collective-permute-done.4.refs_2_.refs_1_ = f32[2,8,1024]{2,1,0:T(8,128)S(1)} collective-permute-done((f32[2,8,1024]{2,1,0:T(8,128)S(1)}, f32[2,8,1024]{2,1,0:T(8,128)S(1)}, u32[]{:S(2)}, u32[]{:S(2)}) %collective-permute-start.4) | collective-permute-done | bytes 65568 | tf_op jit(solution)/shard_map/ppermute | solution.py:664
  20.3 0.9 collective-permute-done.3.refs_1_.refs_0_
  21.2 7.7 %forward.1 = (f32[8,1024]{1,0:T(8,128)S(1)}, bf16[1024,1024]{1,0:T(8,128)(2,1)S(1)}, f32[1024,512]{1,0:T(8,128)S(1)}, bf16[1024,512]{1,0:T(8,128)(2,1)S(1)}, bf1...) custom-call(f32[2,8,1024]{2,1,0:T(8,128)S(1)} %collective-permute-done.2.refs_1_.refs_0_.refs_3_.refs_6_, ...), custom_call_target="tpu_custom_call" | custom-call | flops 10000000000 | bytes 1 | tf_op jit(solution)/shard_map/forward/pallas_call | solution.py:633
  28.9 4.6 %weights.1 = (bf16[4,256,512]{2,1,0:T(8,128)(2,1)S(1)}, bf16[4,256,512]{2,1,0:T(8,128)(2,1)S(1)}, bf16[4,256,512]{2,1,0:T(8,128)(2,1)S(1)}, bf16[4,256,512]{2,1,0:T(8,128)(2,1)S(1)}) custom-call(bf16[1024,512]{1,0:T(8,128)(2,1)S(1)} %get-tuple-element.92.refs_0_, bf16[1024,2048]{1,0:T(8,128)(2,1)S(1)} %get-tuple-element.91.refs_1_.refs_0_, ...), custom_call_target="tpu_custom_call" | custom-call | flops 1 | bytes 1 | tf_op jit(solution)/shard_map/weights/pallas_call | solution.py:633
  33.6 0.5 collective-permute-start.11
  34.1 5.0 %reverse.1 = (f32[1024,512]{1,0:T(8,128)S(1)}, bf16[1024,512]{1,0:T(8,128)(2,1)S(1)}, f32[1024,1024]{1,0:T(8,128)S(1)}, f32[8,1024]{1,0:T(8,128)S(1)}, f32[1,512]{1,0:T(1,128)S(1)}) custom-call(bf16[1024,2048]{1,0:T(8,128)(2,1)S(1)} %get-tuple-element.91.refs_1_.refs_0_, f32[1024,512]{1,0:T(8,128)S(1)} %get-tuple-element.90.refs_1_, ...), custom_call_target="tpu_custom_call" | custom-call | flops 1 | bytes 1 | tf_op jit(solution)/shard_map/reverse/pallas_call | solution.py:633
  39.1 0.1 collective-permute-start.6
  39.2 1.3 %weights_out.1 = (bf16[4,128,512]{2,1,0:T(8,128)(2,1)S(1)}, bf16[4,128,512]{2,1,0:T(8,128)(2,1)S(1)}) custom-call(bf16[1024,1024]{1,0:T(8,128)(2,1)S(1)} %get-tuple-element.96.refs_0_.refs_12_, bf16[1024,512]{1,0:T(8,128)(2,1)S(1)} %get-tuple-element.97.refs_1_, f32[1,512]{1,0:T(1,128)S(1)} %get-tuple-element.98.refs_2_.refs_8_), custom_call_target="tpu_custom_call" | custom-call | flops 1 | bytes 1 | tf_op jit(solution)/shard_map/weights_out/pallas_call | solution.py:633
  40.6 1.4 %collective-permute-start.9 = (f32[8,1024]{1,0:T(8,128)S(1)}, f32[8,1024]{1,0:T(8,128)S(1)}, u32[]{:S(2)}, u32[]{:S(2)}) collective-permute-start(f32[8,1024]{1,0:T(8,128)S(1)} %chip_outgoing.1.refs_4_), channel_id=1, source_target_pairs={{0,6},{1,7},{2,4},{3,5},{4,2},{5,3},{6,0},{7,1},{8,14},{9,15},{10,... | collective-permute-start | bytes 98312 | tf_op jit(solution)/shard_map/ppermute | solution.py:664
  42.0 1.0 collective-permute-start.8
  43.0 1.1 %collective-permute-start.7 = (f32[8,1024]{1,0:T(8,128)S(1)}, f32[8,1024]{1,0:T(8,128)S(1)}, u32[]{:S(2)}, u32[]{:S(2)}) collective-permute-start(f32[8,1024]{1,0:T(8,128)S(1)} %chip_outgoing.1.refs_4_), channel_id=1, source_target_pairs={{0,2},{1,3},{2,0},{3,1},{4,6},{5,7},{6,4},{7,5},{8,10},{9,11},{10,... | collective-permute-start | bytes 98312 | tf_op jit(solution)/shard_map/ppermute | solution.py:664
  44.1 0.9 first_core.1
  45.0 1.2 %collective-permute-start.15 = (bf16[2,256,512]{2,1,0:T(8,128)(2,1)S(1)}, bf16[2,256,512]{2,1,0:T(8,128)(2,1)S(1)}, u32[]{:S(2)}, u32[]{:S(2)}) collective-permute-start(bf16[2,256,512]{2,1,0:T(8,128)(2,1)S(1)} %get-tuple-element.111), channel_id=1, source_target_pairs={{0,4},{1,5},{2,6},{3,7},{4,0},{5,1},{6,2},{7,3},{8,12},{9,13},{10,... | collective-permute-start | bytes 1572872 | tf_op jit(solution)/shard_map/ppermute | solution.py:664
  46.2 0.8 collective-permute-start.14
  47.0 5.3 %back.1 = (bf16[1024,2048]{1,0:T(8,128)(2,1)S(1)}, f32[1,1024]{1,0:T(1,128)S(1)}, bf16[64,512]{1,0:T(8,128)(2,1)S(1)}, bf16[4,256,512]{2,1,0:T(8,128)(2,1)S(1)}, bf16[4,256,512]{2,1,0:T(8,128)(2,1)S(1)}) custom-call(f32[2,8,1024]{2,1,0:T(8,128)S(1)} %collective-permute-done.3.refs_1_.refs_0_, f32[2,8,1024]{2,1,0:T(8,128)S(1)} %collective-permute-done.4.refs_2_.refs_1_, ...), custom_call_target="tpu_custom_call" | custom-call | flops 10000000000 | bytes 1 | tf_op jit(solution)/shard_map/back/pallas_call | solution.py:633
  52.4 0.5 collective-permute-start.12
  53.0 2.4 %gconv.1.refs_4_.refs_0_ = bf16[1024,512]{1,0:T(8,128)(2,1)S(1)} custom-call(bf16[1024,2048]{1,0:T(8,128)(2,1)S(1)} %get-tuple-element.106.refs_0_, bf16[512,2048]{1,0:T(8,128)(2,1)S(1)} %copy-done.2, f32[1,1024]{1,0:T(1,128)S(1)} %get-tuple-element.107.refs_2_.refs_9_), custom_call_target="tpu_custom_call" | custom-call | flops 1 | bytes 1 | tf_op jit(solution)/shard_map/gconv/pallas_call | solution.py:633
  55.4 1.7 %collective-permute-start.13 = (bf16[64,512]{1,0:T(8,128)(2,1)S(1)}, bf16[64,512]{1,0:T(8,128)(2,1)S(1)}, u32[]{:S(2)}, u32[]{:S(2)}) collective-permute-start(bf16[64,512]{1,0:T(8,128)(2,1)S(1)} %get-tuple-element.108), channel_id=1, source_target_pairs={{0,7},{1,2},{2,1},{3,4},{4,3},{5,6},{6,5},{7,0},{8,15},{9,10},{10,... | collective-permute-start | bytes 196616 | tf_op jit(solution)/shard_map/ppermute | solution.py:651
  57.1 1.4 %collective-permute-done.15.refs_3_ = bf16[2,256,512]{2,1,0:T(8,128)(2,1)S(1)} collective-permute-done((bf16[2,256,512]{2,1,0:T(8,128)(2,1)S(1)}, bf16[2,256,512]{2,1,0:T(8,128)(2,1)S(1)}, u32[]{:S(2)}, u32[]{:S(2)}) %collective-permute-start.15) | collective-permute-done | bytes 524320 | tf_op jit(solution)/shard_map/ppermute | solution.py:664
  58.5 1.3 %collective-permute-done.14.refs_1_ = bf16[2,256,512]{2,1,0:T(8,128)(2,1)S(1)} collective-permute-done((bf16[2,256,512]{2,1,0:T(8,128)(2,1)S(1)}, bf16[2,256,512]{2,1,0:T(8,128)(2,1)S(1)}, u32[]{:S(2)}, u32[]{:S(2)}) %collective-permute-start.14) | collective-permute-done | bytes 524320 | tf_op jit(solution)/shard_map/ppermute | solution.py:664
  59.8 0.4 first_seq.1
  60.2 0.8 collective-permute-start.18
  61.0 1.1 %collective-permute-start.17 = (bf16[1,256,512]{2,1,0:T(8,128)(2,1)S(1)}, bf16[1,256,512]{2,1,0:T(8,128)(2,1)S(1)}, u32[]{:S(2)}, u32[]{:S(2)}) collective-permute-start(bf16[1,256,512]{2,1,0:T(8,128)(2,1)S(1)} %get-tuple-element.112.refs_10_), channel_id=1, source_target_pairs={{0,4},{1,5},{2,6},{3,7},{4,0},{5,1},{6,2},{7,3},{8,12},{9,13},{10,... | collective-permute-start | bytes 786440 | tf_op jit(solution)/shard_map/ppermute | solution.py:664
  62.2 2.8 %taps.1 = (f32[1024,512]{1,0:T(8,128)S(1)}, bf16[4,16,512]{2,1,0:T(8,128)(2,1)S(1)}, bf16[4,16,512]{2,1,0:T(8,128)(2,1)S(1)}) custom-call(bf16[1024,512]{1,0:T(8,128)(2,1)S(1)} %gconv.1.refs_4_.refs_0_, bf16[64,512]{1,0:T(8,128)(2,1)S(1)} %collective-permute-done.12.refs_5_.refs_1_, bf16[64,512]{1,0:T(8,128)(2,1)S(1)} %collective-permute-done.13.refs_2_, ...), custom_call_target="tpu_custom_call" | custom-call | flops 1 | bytes 1 | tf_op jit(solution)/shard_map/taps/pallas_call | solution.py:633
  65.0 0.7 second_core.1
  65.7 0.9 collective-permute-start.23
  66.7 1.3 %collective-permute-start.21 = (bf16[2,192,512]{2,1,0:T(8,128)(2,1)S(1)}, bf16[2,192,512]{2,1,0:T(8,128)(2,1)S(1)}, u32[]{:S(2)}, u32[]{:S(2)}) collective-permute-start(bf16[2,192,512]{2,1,0:T(8,128)(2,1)S(1)} %get-tuple-element.121.refs_4_), channel_id=1, source_target_pairs={{0,2},{1,3},{2,0},{3,1},{4,6},{5,7},{6,4},{7,5},{8,10},{9,11},{10,... | collective-permute-start | bytes 1179656 | tf_op jit(solution)/shard_map/ppermute | solution.py:664
  67.9 0.3 first_join.1
  68.3 1.6 %collective-permute-start.26 = (bf16[512,256]{1,0:T(8,128)(2,1)S(1)}, bf16[512,256]{1,0:T(8,128)(2,1)S(1)}, u32[]{:S(2)}, u32[]{:S(2)}) collective-permute-start(bf16[512,256]{1,0:T(8,128)(2,1)S(1)} %get-tuple-element.122.refs_2_), channel_id=1, source_target_pairs={{0,8},{8,0},{16,24},{24,16},{1,9},{9,1},{17,25},{25,17},{2,10},{10... | collective-permute-start | bytes 786440 | tf_op jit(solution)/shard_map/ppermute | solution.py:664
  69.9 1.2 %collective-permute-start.22 = (bf16[2,16,512]{2,1,0:T(8,128)(2,1)S(1)}, bf16[2,16,512]{2,1,0:T(8,128)(2,1)S(1)}, u32[]{:S(2)}, u32[]{:S(2)}) collective-permute-start(bf16[2,16,512]{2,1,0:T(8,128)(2,1)S(1)} %get-tuple-element.123.refs_3_), channel_id=1, source_target_pairs={{0,2},{1,3},{2,0},{3,1},{4,6},{5,7},{6,4},{7,5},{8,10},{9,11},{10,... | collective-permute-start | bytes 98312 | tf_op jit(solution)/shard_map/ppermute | solution.py:664
  71.1 3.5 %result.1 = (bf16[8,128,512]{2,1,0:T(8,128)(2,1)}, f32[8,128]{1,0:T(8,128)S(1)}) custom-call(bf16[1024,2048]{1,0:T(8,128)(2,1)S(1)} %get-tuple-element.89.refs_2_.refs_0_, f32[1024,512]{1,0:T(8,128)S(1)} %get-tuple-element.90.refs_1_, bf16[2048,512]{1,0:T(8,128)(2,1)S(1)} %copy-done, bf16[2,16,512]{2,1,0:T(8,128)(2,1)S(1)} %get-tuple-element.123.refs_3_), custom_call_target="tpu_custom_call" | custom-call | flops 2000000000 | bytes 1 | tf_op jit(solution)/shard_map/result/pallas_call | solution.py:633
  74.6 2.2 %collective-permute-done.22.refs_3_ = bf16[2,16,512]{2,1,0:T(8,128)(2,1)S(1)} collective-permute-done((bf16[2,16,512]{2,1,0:T(8,128)(2,1)S(1)}, bf16[2,16,512]{2,1,0:T(8,128)(2,1)S(1)}, u32[]{:S(2)}, u32[]{:S(2)}) %collective-permute-start.22) | collective-permute-done | bytes 32800 | tf_op jit(solution)/shard_map/ppermute | solution.py:664
  76.9 0.3 second_seq.1
  77.1 1.2 %collective-permute-start.24 = (bf16[1,208,512]{2,1,0:T(8,128)(2,1)S(1)}, bf16[1,208,512]{2,1,0:T(8,128)(2,1)S(1)}, u32[]{:S(2)}, u32[]{:S(2)}) collective-permute-start(bf16[1,208,512]{2,1,0:T(8,128)(2,1)S(1)} %get-tuple-element.133), channel_id=1, source_target_pairs={{0,4},{1,5},{2,6},{3,7},{4,0},{5,1},{6,2},{7,3},{8,12},{9,13},{10,... | collective-permute-start | bytes 638984 | tf_op jit(solution)/shard_map/ppermute | solution.py:664
  78.4 0.9 collective-permute-start.25
  79.3 0.2 first_last.1.refs_4_.refs_0_
  79.5 2.8 %collective-permute-start.28 = (bf16[512,256]{1,0:T(8,128)(2,1)S(1)}, bf16[512,256]{1,0:T(8,128)(2,1)S(1)}, u32[]{:S(2)}, u32[]{:S(2)}) collective-permute-start(bf16[512,256]{1,0:T(8,128)(2,1)S(1)} %first_last.1.refs_4_.refs_0_), channel_id=1, source_target_pairs={{0,16},{8,24},{16,0},{24,8},{1,17},{9,25},{17,1},{25,9},{2,18},{10... | collective-permute-start | bytes 786440 | tf_op jit(solution)/shard_map/ppermute | solution.py:664
  82.3 1.8 %collective-permute-done.25.refs_3_ = bf16[1,192,512]{2,1,0:T(8,128)(2,1)S(1)} collective-permute-done((bf16[1,192,512]{2,1,0:T(8,128)(2,1)S(1)}, bf16[1,192,512]{2,1,0:T(8,128)(2,1)S(1)}, u32[]{:S(2)}, u32[]{:S(2)}) %collective-permute-start.25) | collective-permute-done | bytes 196640 | tf_op jit(solution)/shard_map/ppermute | solution.py:664
  84.0 0.2 second_join.1
  84.3 1.7 %collective-permute-start.27 = (bf16[400,256]{1,0:T(8,128)(2,1)S(1)}, bf16[400,256]{1,0:T(8,128)(2,1)S(1)}, u32[]{:S(2)}, u32[]{:S(2)}) collective-permute-start(bf16[400,256]{1,0:T(8,128)(2,1)S(1)} %get-tuple-element.137.refs_4_), channel_id=1, source_target_pairs={{0,8},{8,0},{16,24},{24,16},{1,9},{9,1},{17,25},{25,17},{2,10},{10... | collective-permute-start | bytes 614408 | tf_op jit(solution)/shard_map/ppermute | solution.py:664
  85.9 2.7 %inputs.1 = (f32[8,128,512]{2,1,0:T(8,128)}, f32[8,128]{1,0:T(8,128)S(1)}) custom-call(f32[1024,512]{1,0:T(8,128)S(1)} %get-tuple-element.125.refs_0_, f32[4,1024,128]{2,1,0:T(8,128)S(1)} %get-tuple-element.85.refs_4_.refs_3_.refs_1_, f32[1024,512]{1,0:T(8,128)S(1)} %get-tuple-element.126.refs_2_, f32[1,512]{1,0:T(1,128)S(1)} %bitcast.13, ...), custom_call_target="tpu_custom_call" | custom-call | flops 1 | bytes 1 | tf_op jit(solution)/shard_map/inputs/pallas_call | solution.py:633
  88.7 3.2 %collective-permute-done.28.refs_1_ = bf16[512,256]{1,0:T(8,128)(2,1)S(1)} collective-permute-done((bf16[512,256]{1,0:T(8,128)(2,1)S(1)}, bf16[512,256]{1,0:T(8,128)(2,1)S(1)}, u32[]{:S(2)}, u32[]{:S(2)}) %collective-permute-start.28) | collective-permute-done | bytes 262176 | tf_op jit(solution)/shard_map/ppermute | solution.py:664
  91.8 0.2 first_total.1.refs_2_.refs_0_
  92.0 0.6 collective-permute-done.27.refs_1_
  92.6 0.2 second_last.1.refs_0_.refs_2_
  92.8 2.5 %collective-permute-start.29 = (bf16[400,256]{1,0:T(8,128)(2,1)S(1)}, bf16[400,256]{1,0:T(8,128)(2,1)S(1)}, u32[]{:S(2)}, u32[]{:S(2)}) collective-permute-start(bf16[400,256]{1,0:T(8,128)(2,1)S(1)} %second_last.1.refs_0_.refs_2_), channel_id=1, source_target_pairs={{0,16},{8,24},{16,0},{24,8},{1,17},{9,25},{17,1},{25,9},{2,18},{10... | collective-permute-start | bytes 614408 | tf_op jit(solution)/shard_map/ppermute | solution.py:664
  95.3 2.5 %collective-permute-start.31 = (bf16[512,256]{1,0:T(8,128)(2,1)S(1)}, bf16[512,256]{1,0:T(8,128)(2,1)S(1)}, u32[]{:S(2)}, u32[]{:S(2)}) collective-permute-start(bf16[512,256]{1,0:T(8,128)(2,1)S(1)} %first_total.1.refs_2_.refs_0_), channel_id=1, source_target_pairs={{0,8},{8,0},{16,24},{24,16},{1,9},{9,1},{17,25},{25,17},{2,10},{10... | collective-permute-start | bytes 786440 | tf_op jit(solution)/shard_map/ppermute | solution.py:664
  97.8 5.8 %collective-permute-done.29.refs_1_ = bf16[400,256]{1,0:T(8,128)(2,1)S(1)} collective-permute-done((bf16[400,256]{1,0:T(8,128)(2,1)S(1)}, bf16[400,256]{1,0:T(8,128)(2,1)S(1)}, u32[]{:S(2)}, u32[]{:S(2)}) %collective-permute-start.29) | collective-permute-done | bytes 204832 | tf_op jit(solution)/shard_map/ppermute | solution.py:664
  103.6 0.1 second_total.1.refs_2_.refs_0_
  103.8 1.1 %collective-permute-done.31.refs_1_ = bf16[512,256]{1,0:T(8,128)(2,1)S(1)} collective-permute-done((bf16[512,256]{1,0:T(8,128)(2,1)S(1)}, bf16[512,256]{1,0:T(8,128)(2,1)S(1)}, u32[]{:S(2)}, u32[]{:S(2)}) %collective-permute-start.31) | collective-permute-done | bytes 262176 | tf_op jit(solution)/shard_map/ppermute | solution.py:664
  104.9 1.0 first_finish.1
  106.0 3.6 %collective-permute-done.30.refs_1_ = bf16[400,256]{1,0:T(8,128)(2,1)S(1)} collective-permute-done((bf16[400,256]{1,0:T(8,128)(2,1)S(1)}, bf16[400,256]{1,0:T(8,128)(2,1)S(1)}, u32[]{:S(2)}, u32[]{:S(2)}) %collective-permute-start.30) | collective-permute-done | bytes 204832 | tf_op jit(solution)/shard_map/ppermute | solution.py:664
  109.5 0.9 second_finish.1
  (46 shorter events, 0.4 us)
Async XLA Ops:
  0.6 5.6 %copy-start = (bf16[2048,512]{1,0:T(8,128)(2,1)S(1)}, bf16[2048,512]{1,0:T(8,128)(2,1)}, u32[]{:S(2)}) copy-start(bf16[2048,512]{1,0:T(8,128)(2,1)} %refs_2_.1) | copy-start | bytes 6291460
  0.7 5.6 %copy-start.7 = (bf16[8,128,512]{2,1,0:T(8,128)(2,1)S(1)}, bf16[8,128,512]{2,1,0:T(8,128)(2,1)}, u32[]{:S(2)}) copy-start(bf16[8,128,512]{2,1,0:T(8,128)(2,1)} %refs_0_.3) | copy-start | bytes 3145732
  2.8 5.4 %copy-start.2 = (bf16[512,2048]{1,0:T(8,128)(2,1)S(1)}, bf16[512,2048]{1,0:T(8,128)(2,1)}, u32[]{:S(2)}) copy-start(bf16[512,2048]{1,0:T(8,128)(2,1)} %refs_1_.7) | copy-start | bytes 6291460
  2.8 5.4 %copy-start.4 = (f32[512,4]{0,1:T(4,128)S(1)}, f32[512,4]{0,1:T(4,128)}, u32[]{:S(2)}) copy-start(f32[512,4]{0,1:T(4,128)} %param.14) | copy-start | bytes 24580
  2.8 5.4 %copy-start.8 = (f32[1024]{0:T(1024)S(1)}, f32[1024]{0:T(1024)}, u32[]{:S(2)}) copy-start(f32[1024]{0:T(1024)} %param.15) | copy-start | bytes 12292
  2.8 5.3 %collective-permute-start.1 = (bf16[64,512]{1,0:T(8,128)(2,1)S(1)}, bf16[64,512]{1,0:T(8,128)(2,1)S(1)}, u32[]{:S(2)}, u32[]{:S(2)}) collective-permute-start(bf16[64,512]{1,0:T(8,128)(2,1)S(1)} %get-tuple-element.81.refs_2_), channel_id=1, source_target_pairs={{0,7},{1,2},{2,1},{3,4},{4,3},{5,6},{6,5},{7,0},{8,15},{9,10},{10,... | collective-permute-start | bytes 196616 | tf_op jit(solution)/shard_map/ppermute | solution.py:651
  6.2 2.0 %collective-permute-start = (bf16[64,512]{1,0:T(8,128)(2,1)S(1)}, bf16[64,512]{1,0:T(8,128)(2,1)S(1)}, u32[]{:S(2)}, u32[]{:S(2)}) collective-permute-start(bf16[64,512]{1,0:T(8,128)(2,1)S(1)} %get-tuple-element.81.refs_2_), channel_id=1, source_target_pairs={{0,1},{1,0},{2,3},{3,2},{4,5},{5,4},{6,7},{7,6},{8,9},{9,8},{10,11... | collective-permute-start | bytes 196616 | tf_op jit(solution)/shard_map/ppermute | solution.py:664
  11.6 1.3 %collective-permute-start.2 = (f32[2,8,1024]{2,1,0:T(8,128)S(1)}, f32[2,8,1024]{2,1,0:T(8,128)S(1)}, u32[]{:S(2)}, u32[]{:S(2)}) collective-permute-start(f32[2,8,1024]{2,1,0:T(8,128)S(1)} %get-tuple-element.84.refs_0_.refs_2_), channel_id=1, source_target_pairs={{0,1},{1,0},{2,3},{3,2},{4,5},{5,4},{6,7},{7,6},{8,9},{9,8},{10,11... | collective-permute-start | bytes 196616 | tf_op jit(solution)/shard_map/ppermute | solution.py:664
  13.0 8.2 %copy-start.1 = (bf16[512,2048]{1,0:T(8,128)(2,1)S(1)}, bf16[512,2048]{1,0:T(8,128)(2,1)}, u32[]{:S(2)}) copy-start(bf16[512,2048]{1,0:T(8,128)(2,1)} %refs_7_.1) | copy-start | bytes 6291460
  13.0 8.2 %copy-start.3 = (bf16[1024,512]{1,0:T(8,128)(2,1)S(1)}, bf16[1024,512]{1,0:T(8,128)(2,1)}, u32[]{:S(2)}) copy-start(bf16[1024,512]{1,0:T(8,128)(2,1)} %refs_6_.3) | copy-start | bytes 3145732
  13.0 8.2 %copy-start.5 = (f32[512]{0:T(512)S(1)}, f32[512]{0:T(512)}, u32[]{:S(2)}) copy-start(f32[512]{0:T(512)} %param.18) | copy-start | bytes 6148
  13.0 5.5 %collective-permute-start.5 = (f32[2,8,1024]{2,1,0:T(8,128)S(1)}, f32[2,8,1024]{2,1,0:T(8,128)S(1)}, u32[]{:S(2)}, u32[]{:S(2)}) collective-permute-start(f32[2,8,1024]{2,1,0:T(8,128)S(1)} %chip_totals.1.refs_2_), channel_id=1, source_target_pairs={{0,6},{1,7},{2,4},{3,5},{4,2},{5,3},{6,0},{7,1},{8,14},{9,15},{10,... | collective-permute-start | bytes 196616 | tf_op jit(solution)/shard_map/ppermute | solution.py:664
  16.0 4.3 %collective-permute-start.4 = (f32[2,8,1024]{2,1,0:T(8,128)S(1)}, f32[2,8,1024]{2,1,0:T(8,128)S(1)}, u32[]{:S(2)}, u32[]{:S(2)}) collective-permute-start(f32[2,8,1024]{2,1,0:T(8,128)S(1)} %chip_totals.1.refs_2_), channel_id=1, source_target_pairs={{0,4},{1,5},{2,6},{3,7},{4,0},{5,1},{6,2},{7,3},{8,12},{9,13},{10,... | collective-permute-start | bytes 196616 | tf_op jit(solution)/shard_map/ppermute | solution.py:664
  16.9 4.3 %collective-permute-start.3 = (f32[2,8,1024]{2,1,0:T(8,128)S(1)}, f32[2,8,1024]{2,1,0:T(8,128)S(1)}, u32[]{:S(2)}, u32[]{:S(2)}) collective-permute-start(f32[2,8,1024]{2,1,0:T(8,128)S(1)} %chip_totals.1.refs_2_), channel_id=1, source_target_pairs={{0,2},{1,3},{2,0},{3,1},{4,6},{5,7},{6,4},{7,5},{8,10},{9,11},{10,... | collective-permute-start | bytes 196616 | tf_op jit(solution)/shard_map/ppermute | solution.py:664
  33.5 10.6 %collective-permute-start.10 = (bf16[4,256,512]{2,1,0:T(8,128)(2,1)S(1)}, bf16[4,256,512]{2,1,0:T(8,128)(2,1)S(1)}, u32[]{:S(2)}, u32[]{:S(2)}) collective-permute-start(bf16[4,256,512]{2,1,0:T(8,128)(2,1)S(1)} %get-tuple-element.102), channel_id=1, source_target_pairs={{0,1},{1,0},{2,3},{3,2},{4,5},{5,4},{6,7},{7,6},{8,9},{9,8},{10,11... | collective-permute-start | bytes 3145736 | tf_op jit(solution)/shard_map/ppermute | solution.py:664
  33.6 10.6 %collective-permute-start.11 = (bf16[4,256,512]{2,1,0:T(8,128)(2,1)S(1)}, bf16[4,256,512]{2,1,0:T(8,128)(2,1)S(1)}, u32[]{:S(2)}, u32[]{:S(2)}) collective-permute-start(bf16[4,256,512]{2,1,0:T(8,128)(2,1)S(1)} %get-tuple-element.104), channel_id=1, source_target_pairs={{0,1},{1,0},{2,3},{3,2},{4,5},{5,4},{6,7},{7,6},{8,9},{9,8},{10,11... | collective-permute-start | bytes 3145736 | tf_op jit(solution)/shard_map/ppermute | solution.py:664
  39.1 1.4 %collective-permute-start.6 = (f32[8,1024]{1,0:T(8,128)S(1)}, f32[8,1024]{1,0:T(8,128)S(1)}, u32[]{:S(2)}, u32[]{:S(2)}) collective-permute-start(f32[8,1024]{1,0:T(8,128)S(1)} %get-tuple-element.95.refs_0_), channel_id=1, source_target_pairs={{0,1},{1,0},{2,3},{3,2},{4,5},{5,4},{6,7},{7,6},{8,9},{9,8},{10,11... | collective-permute-start | bytes 98312 | tf_op jit(solution)/shard_map/ppermute | solution.py:664
  40.6 6.4 %collective-permute-start.9 = (f32[8,1024]{1,0:T(8,128)S(1)}, f32[8,1024]{1,0:T(8,128)S(1)}, u32[]{:S(2)}, u32[]{:S(2)}) collective-permute-start(f32[8,1024]{1,0:T(8,128)S(1)} %chip_outgoing.1.refs_4_), channel_id=1, source_target_pairs={{0,6},{1,7},{2,4},{3,5},{4,2},{5,3},{6,0},{7,1},{8,14},{9,15},{10,... | collective-permute-start | bytes 98312 | tf_op jit(solution)/shard_map/ppermute | solution.py:664
  42.0 5.0 %collective-permute-start.8 = (f32[8,1024]{1,0:T(8,128)S(1)}, f32[8,1024]{1,0:T(8,128)S(1)}, u32[]{:S(2)}, u32[]{:S(2)}) collective-permute-start(f32[8,1024]{1,0:T(8,128)S(1)} %chip_outgoing.1.refs_4_), channel_id=1, source_target_pairs={{0,4},{1,5},{2,6},{3,7},{4,0},{5,1},{6,2},{7,3},{8,12},{9,13},{10,... | collective-permute-start | bytes 98312 | tf_op jit(solution)/shard_map/ppermute | solution.py:664
  43.0 4.0 %collective-permute-start.7 = (f32[8,1024]{1,0:T(8,128)S(1)}, f32[8,1024]{1,0:T(8,128)S(1)}, u32[]{:S(2)}, u32[]{:S(2)}) collective-permute-start(f32[8,1024]{1,0:T(8,128)S(1)} %chip_outgoing.1.refs_4_), channel_id=1, source_target_pairs={{0,2},{1,3},{2,0},{3,1},{4,6},{5,7},{6,4},{7,5},{8,10},{9,11},{10,... | collective-permute-start | bytes 98312 | tf_op jit(solution)/shard_map/ppermute | solution.py:664
  45.0 13.5 %collective-permute-start.15 = (bf16[2,256,512]{2,1,0:T(8,128)(2,1)S(1)}, bf16[2,256,512]{2,1,0:T(8,128)(2,1)S(1)}, u32[]{:S(2)}, u32[]{:S(2)}) collective-permute-start(bf16[2,256,512]{2,1,0:T(8,128)(2,1)S(1)} %get-tuple-element.111), channel_id=1, source_target_pairs={{0,4},{1,5},{2,6},{3,7},{4,0},{5,1},{6,2},{7,3},{8,12},{9,13},{10,... | collective-permute-start | bytes 1572872 | tf_op jit(solution)/shard_map/ppermute | solution.py:664
  46.2 13.6 %collective-permute-start.14 = (bf16[2,256,512]{2,1,0:T(8,128)(2,1)S(1)}, bf16[2,256,512]{2,1,0:T(8,128)(2,1)S(1)}, u32[]{:S(2)}, u32[]{:S(2)}) collective-permute-start(bf16[2,256,512]{2,1,0:T(8,128)(2,1)S(1)} %get-tuple-element.105.refs_16_), channel_id=1, source_target_pairs={{0,2},{1,3},{2,0},{3,1},{4,6},{5,7},{6,4},{7,5},{8,10},{9,11},{10,... | collective-permute-start | bytes 1572872 | tf_op jit(solution)/shard_map/ppermute | solution.py:664
  52.4 12.6 %collective-permute-start.19 = (bf16[4,256,512]{2,1,0:T(8,128)(2,1)S(1)}, bf16[4,256,512]{2,1,0:T(8,128)(2,1)S(1)}, u32[]{:S(2)}, u32[]{:S(2)}) collective-permute-start(bf16[4,256,512]{2,1,0:T(8,128)(2,1)S(1)} %get-tuple-element.119), channel_id=1, source_target_pairs={{0,1},{1,0},{2,3},{3,2},{4,5},{5,4},{6,7},{7,6},{8,9},{9,8},{10,11... | collective-permute-start | bytes 3145736 | tf_op jit(solution)/shard_map/ppermute | solution.py:664
  52.4 2.9 %collective-permute-start.12 = (bf16[64,512]{1,0:T(8,128)(2,1)S(1)}, bf16[64,512]{1,0:T(8,128)(2,1)S(1)}, u32[]{:S(2)}, u32[]{:S(2)}) collective-permute-start(bf16[64,512]{1,0:T(8,128)(2,1)S(1)} %get-tuple-element.108), channel_id=1, source_target_pairs={{0,1},{1,0},{2,3},{3,2},{4,5},{5,4},{6,7},{7,6},{8,9},{9,8},{10,11... | collective-permute-start | bytes 196616 | tf_op jit(solution)/shard_map/ppermute | solution.py:664
  52.9 12.1 %collective-permute-start.20 = (bf16[4,128,512]{2,1,0:T(8,128)(2,1)S(1)}, bf16[4,128,512]{2,1,0:T(8,128)(2,1)S(1)}, u32[]{:S(2)}, u32[]{:S(2)}) collective-permute-start(bf16[4,128,512]{2,1,0:T(8,128)(2,1)S(1)} %get-tuple-element.120), channel_id=1, source_target_pairs={{0,1},{1,0},{2,3},{3,2},{4,5},{5,4},{6,7},{7,6},{8,9},{9,8},{10,11... | collective-permute-start | bytes 1572872 | tf_op jit(solution)/shard_map/ppermute | solution.py:664
  55.4 6.8 %collective-permute-start.13 = (bf16[64,512]{1,0:T(8,128)(2,1)S(1)}, bf16[64,512]{1,0:T(8,128)(2,1)S(1)}, u32[]{:S(2)}, u32[]{:S(2)}) collective-permute-start(bf16[64,512]{1,0:T(8,128)(2,1)S(1)} %get-tuple-element.108), channel_id=1, source_target_pairs={{0,7},{1,2},{2,1},{3,4},{4,3},{5,6},{6,5},{7,0},{8,15},{9,10},{10,... | collective-permute-start | bytes 196616 | tf_op jit(solution)/shard_map/ppermute | solution.py:651
  60.2 7.7 %collective-permute-start.18 = (bf16[1,256,512]{2,1,0:T(8,128)(2,1)S(1)}, bf16[1,256,512]{2,1,0:T(8,128)(2,1)S(1)}, u32[]{:S(2)}, u32[]{:S(2)}) collective-permute-start(bf16[1,256,512]{2,1,0:T(8,128)(2,1)S(1)} %get-tuple-element.117), channel_id=1, source_target_pairs={{0,2},{1,3},{2,0},{3,1},{4,6},{5,7},{6,4},{7,5},{8,10},{9,11},{10,... | collective-permute-start | bytes 786440 | tf_op jit(solution)/shard_map/ppermute | solution.py:664
  61.0 6.9 %collective-permute-start.17 = (bf16[1,256,512]{2,1,0:T(8,128)(2,1)S(1)}, bf16[1,256,512]{2,1,0:T(8,128)(2,1)S(1)}, u32[]{:S(2)}, u32[]{:S(2)}) collective-permute-start(bf16[1,256,512]{2,1,0:T(8,128)(2,1)S(1)} %get-tuple-element.112.refs_10_), channel_id=1, source_target_pairs={{0,4},{1,5},{2,6},{3,7},{4,0},{5,1},{6,2},{7,3},{8,12},{9,13},{10,... | collective-permute-start | bytes 786440 | tf_op jit(solution)/shard_map/ppermute | solution.py:664
  65.7 11.1 %collective-permute-start.23 = (bf16[2,192,512]{2,1,0:T(8,128)(2,1)S(1)}, bf16[2,192,512]{2,1,0:T(8,128)(2,1)S(1)}, u32[]{:S(2)}, u32[]{:S(2)}) collective-permute-start(bf16[2,192,512]{2,1,0:T(8,128)(2,1)S(1)} %get-tuple-element.130), channel_id=1, source_target_pairs={{0,4},{1,5},{2,6},{3,7},{4,0},{5,1},{6,2},{7,3},{8,12},{9,13},{10,... | collective-permute-start | bytes 1179656 | tf_op jit(solution)/shard_map/ppermute | solution.py:664
  66.7 10.2 %collective-permute-start.21 = (bf16[2,192,512]{2,1,0:T(8,128)(2,1)S(1)}, bf16[2,192,512]{2,1,0:T(8,128)(2,1)S(1)}, u32[]{:S(2)}, u32[]{:S(2)}) collective-permute-start(bf16[2,192,512]{2,1,0:T(8,128)(2,1)S(1)} %get-tuple-element.121.refs_4_), channel_id=1, source_target_pairs={{0,2},{1,3},{2,0},{3,1},{4,6},{5,7},{6,4},{7,5},{8,10},{9,11},{10,... | collective-permute-start | bytes 1179656 | tf_op jit(solution)/shard_map/ppermute | solution.py:664
  67.9 1.9 %collective-permute-start.16 = (bf16[4,16,512]{2,1,0:T(8,128)(2,1)S(1)}, bf16[4,16,512]{2,1,0:T(8,128)(2,1)S(1)}, u32[]{:S(2)}, u32[]{:S(2)}) collective-permute-start(bf16[4,16,512]{2,1,0:T(8,128)(2,1)S(1)} %get-tuple-element.114), channel_id=1, source_target_pairs={{0,1},{1,0},{2,3},{3,2},{4,5},{5,4},{6,7},{7,6},{8,9},{9,8},{10,11... | collective-permute-start | bytes 196616 | tf_op jit(solution)/shard_map/ppermute | solution.py:664
  68.3 11.0 %collective-permute-start.26 = (bf16[512,256]{1,0:T(8,128)(2,1)S(1)}, bf16[512,256]{1,0:T(8,128)(2,1)S(1)}, u32[]{:S(2)}, u32[]{:S(2)}) collective-permute-start(bf16[512,256]{1,0:T(8,128)(2,1)S(1)} %get-tuple-element.122.refs_2_), channel_id=1, source_target_pairs={{0,8},{8,0},{16,24},{24,16},{1,9},{9,1},{17,25},{25,17},{2,10},{10... | collective-permute-start | bytes 786440 | tf_op jit(solution)/shard_map/ppermute | solution.py:664
  69.9 6.9 %collective-permute-start.22 = (bf16[2,16,512]{2,1,0:T(8,128)(2,1)S(1)}, bf16[2,16,512]{2,1,0:T(8,128)(2,1)S(1)}, u32[]{:S(2)}, u32[]{:S(2)}) collective-permute-start(bf16[2,16,512]{2,1,0:T(8,128)(2,1)S(1)} %get-tuple-element.123.refs_3_), channel_id=1, source_target_pairs={{0,2},{1,3},{2,0},{3,1},{4,6},{5,7},{6,4},{7,5},{8,10},{9,11},{10,... | collective-permute-start | bytes 98312 | tf_op jit(solution)/shard_map/ppermute | solution.py:664
  77.1 6.9 %collective-permute-start.24 = (bf16[1,208,512]{2,1,0:T(8,128)(2,1)S(1)}, bf16[1,208,512]{2,1,0:T(8,128)(2,1)S(1)}, u32[]{:S(2)}, u32[]{:S(2)}) collective-permute-start(bf16[1,208,512]{2,1,0:T(8,128)(2,1)S(1)} %get-tuple-element.133), channel_id=1, source_target_pairs={{0,4},{1,5},{2,6},{3,7},{4,0},{5,1},{6,2},{7,3},{8,12},{9,13},{10,... | collective-permute-start | bytes 638984 | tf_op jit(solution)/shard_map/ppermute | solution.py:664
  78.4 5.7 %collective-permute-start.25 = (bf16[1,192,512]{2,1,0:T(8,128)(2,1)S(1)}, bf16[1,192,512]{2,1,0:T(8,128)(2,1)S(1)}, u32[]{:S(2)}, u32[]{:S(2)}) collective-permute-start(bf16[1,192,512]{2,1,0:T(8,128)(2,1)S(1)} %get-tuple-element.135.refs_2_), channel_id=1, source_target_pairs={{0,2},{1,3},{2,0},{3,1},{4,6},{5,7},{6,4},{7,5},{8,10},{9,11},{10,... | collective-permute-start | bytes 589832 | tf_op jit(solution)/shard_map/ppermute | solution.py:664
  79.5 12.3 %collective-permute-start.28 = (bf16[512,256]{1,0:T(8,128)(2,1)S(1)}, bf16[512,256]{1,0:T(8,128)(2,1)S(1)}, u32[]{:S(2)}, u32[]{:S(2)}) collective-permute-start(bf16[512,256]{1,0:T(8,128)(2,1)S(1)} %first_last.1.refs_4_.refs_0_), channel_id=1, source_target_pairs={{0,16},{8,24},{16,0},{24,8},{1,17},{9,25},{17,1},{25,9},{2,18},{10... | collective-permute-start | bytes 786440 | tf_op jit(solution)/shard_map/ppermute | solution.py:664
  84.0 1.9 %copy-start.6 = (f32[512]{0:T(512)S(1)}, f32[512]{0:T(512)}, u32[]{:S(2)}) copy-start(f32[512]{0:T(512)} %param.13) | copy-start | bytes 6148
  84.3 8.3 %collective-permute-start.27 = (bf16[400,256]{1,0:T(8,128)(2,1)S(1)}, bf16[400,256]{1,0:T(8,128)(2,1)S(1)}, u32[]{:S(2)}, u32[]{:S(2)}) collective-permute-start(bf16[400,256]{1,0:T(8,128)(2,1)S(1)} %get-tuple-element.137.refs_4_), channel_id=1, source_target_pairs={{0,8},{8,0},{16,24},{24,16},{1,9},{9,1},{17,25},{25,17},{2,10},{10... | collective-permute-start | bytes 614408 | tf_op jit(solution)/shard_map/ppermute | solution.py:664
  92.8 10.8 %collective-permute-start.29 = (bf16[400,256]{1,0:T(8,128)(2,1)S(1)}, bf16[400,256]{1,0:T(8,128)(2,1)S(1)}, u32[]{:S(2)}, u32[]{:S(2)}) collective-permute-start(bf16[400,256]{1,0:T(8,128)(2,1)S(1)} %second_last.1.refs_0_.refs_2_), channel_id=1, source_target_pairs={{0,16},{8,24},{16,0},{24,8},{1,17},{9,25},{17,1},{25,9},{2,18},{10... | collective-permute-start | bytes 614408 | tf_op jit(solution)/shard_map/ppermute | solution.py:664
  95.3 9.7 %collective-permute-start.31 = (bf16[512,256]{1,0:T(8,128)(2,1)S(1)}, bf16[512,256]{1,0:T(8,128)(2,1)S(1)}, u32[]{:S(2)}, u32[]{:S(2)}) collective-permute-start(bf16[512,256]{1,0:T(8,128)(2,1)S(1)} %first_total.1.refs_2_.refs_0_), channel_id=1, source_target_pairs={{0,8},{8,0},{16,24},{24,16},{1,9},{9,1},{17,25},{25,17},{2,10},{10... | collective-permute-start | bytes 786440 | tf_op jit(solution)/shard_map/ppermute | solution.py:664
  103.7 5.8 %collective-permute-start.30 = (bf16[400,256]{1,0:T(8,128)(2,1)S(1)}, bf16[400,256]{1,0:T(8,128)(2,1)S(1)}, u32[]{:S(2)}, u32[]{:S(2)}) collective-permute-start(bf16[400,256]{1,0:T(8,128)(2,1)S(1)} %second_total.1.refs_2_.refs_0_), channel_id=1, source_target_pairs={{0,8},{8,0},{16,24},{24,16},{1,9},{9,1},{17,25},{25,17},{2,10},{10... | collective-permute-start | bytes 614408 | tf_op jit(solution)/shard_map/ppermute | solution.py:664
